TPU v7x, 128 devices: a whole 4x4x4 slice. The times are simulated.
128 devices in a mesh: segment: 8 (over x, core), wide: 16 (over z, y).
Axes of the slice: x: 4, y: 4, z: 4, core: 2. Of those that a mesh axis runs over, the one named last changes fastest.
Arguments:
- prompt_states: bfloat16 [4, 256, 8192], P(None, None, 'wide')
- norm_gain: bfloat16 [8, 8192], P('segment', 'wide'), may hold values from 0.29882812 to 3
- w_latent: bfloat16 [8, 8192, 512], P('segment', 'wide'), may hold values from -0.0625 to 0.0625
- w_back: bfloat16 [8, 512, 8192], P('segment', None, 'wide'), may hold values from -0.25 to 0.25
- page_lists: int32 [8, 8, 1], replicated, may hold values from 0 to 7; in each aligned block of 8 rows (0 to 7, 8 to 15, ..., all dimensions but the last counted through in order) at most 2 rows name the same one
- queries: bfloat16 [128, 8, 64, 512], P('segment', None, 'wide'), may hold values from -64 to 64
- new_latent: bfloat16 [128, 8, 512], P('segment'), may hold values from -6 to 6
- context_lengths: int32 [128, 8], P('segment'), may hold values from 0 to 256
Outputs:
- attended: bfloat16 [128, 8, 64, 512], P('segment', None, 'wide')
Inputs may be any that keep to these rules, and one draw needn't show every extreme that they name: Page p of layer l is sent to decode owner page_lists[l, p, 0]; no owner receives more than 2 pages of one layer, and exactly 2 in some layers.
All inputs are finite; a program needn't handle non-finite values.
Results may differ from a plain program's by a relative error of at most 0.03.
Values may be sent and summed in bfloat16 or wider, within the bound.
No kernel may reach another device: no remote copies, remote signals or barrier semaphores. Data moves between devices by JAX's collectives and lax.ppermute only.
A program may use at most 64 MiB of HBM per device.

v0:
```python
import jax
import jax.numpy as jnp
from jax import lax
from jax.sharding import PartitionSpec as P

PAGE = 128


eps_norm = 1e-06
score_scale = 192.0 ** (-0.5)


def passed_along(x, axis, by):
    length = lax.axis_size(axis)
    pairs = [(i, i + by) for i in range(length) if 0 <= i + by < length]
    return lax.ppermute(x, axis, pairs)


def page_ranks(targets):
    count = targets.shape[-1]
    order = jnp.arange(count, dtype=jnp.int32)
    earlier = order[None, :] < order[:, None]
    same = targets[..., :, None] == targets[..., None, :]
    return jnp.sum((same & earlier).astype(jnp.int32), axis=-1)


def latent_layer(state, gain, w_lat, w_out):
    wide_size = lax.axis_size("wide")
    values = state.astype(jnp.float32)
    squares = lax.psum(jnp.sum(values * values, axis=1), "wide")
    inverse_rms = lax.rsqrt(squares / (state.shape[1] * wide_size) + eps_norm)
    normed = (values * inverse_rms[:, None] * gain.astype(jnp.float32)[None, :]).astype(
        jnp.bfloat16
    )
    partial_term = jnp.dot(normed, w_lat, preferred_element_type=jnp.float32)
    latent = lax.psum(partial_term, "wide").astype(jnp.bfloat16)
    activated = jax.nn.silu(latent.astype(jnp.float32)).astype(jnp.bfloat16)
    update = jnp.dot(activated, w_out, preferred_element_type=jnp.float32)
    return ((values + update).astype(jnp.bfloat16), latent)


def decode_block(owner_queries, keys, owner_new, limit):
    positions = jnp.arange(keys.shape[1], dtype=jnp.int32)
    readable = positions[None, None, :] < limit[:, :, None]
    scores = (
        jnp.einsum("rlhc,lkc->rlhk", owner_queries, keys, preferred_element_type=jnp.float32)
        * score_scale
    )
    scores = jnp.where(readable[:, :, None, :], scores, -jnp.inf)
    own_score = (
        jnp.einsum("rlhc,rlc->rlh", owner_queries, owner_new, preferred_element_type=jnp.float32)
        * score_scale
    )
    top = jnp.maximum(jnp.max(scores, axis=-1), own_score)
    weights = jnp.exp(scores - top[..., None])
    own_weight = jnp.exp(own_score - top)
    total = jnp.sum(weights, axis=-1) + own_weight
    numer = jnp.einsum(
        "rlhk,lkc->rlhc", weights.astype(jnp.bfloat16), keys, preferred_element_type=jnp.float32
    )
    numer = numer + own_weight[..., None] * owner_new.astype(jnp.float32)[:, :, None, :]
    return (numer / total[..., None]).astype(jnp.bfloat16)


def shards(
    prompt_states, norm_gain, w_latent, w_back, page_lists, queries, new_latent, context_lengths
):
    phases = lax.axis_size("segment")
    position = lax.axis_index("segment")
    batches, tok_rows, local_width = prompt_states.shape
    local_layers = w_latent.shape[0]
    latent_width = w_latent.shape[2]
    all_layers = local_layers * phases
    page_count = batches * tok_rows // PAGE
    capacity = max(2, (2 * page_count + phases - 1) // phases)
    steps_total = batches + phases - 1

    def advance(step, carry):
        inbound, stored = carry
        step = jnp.asarray(step).astype(jnp.int32)
        batch_index = step - position
        active = (batch_index >= 0) & (batch_index < batches)
        first_input = lax.dynamic_index_in_dim(
            prompt_states, jnp.clip(step, 0, batches - 1), 0, keepdims=False
        )
        state = jnp.where(position == 0, first_input, inbound)
        latents = []
        state, latent = latent_layer(state, norm_gain[0], w_latent[0], w_back[0])
        latents.append(latent)
        latents = jnp.stack(latents)
        slot_index = jnp.clip(batch_index, 0, batches - 1)
        previous = lax.dynamic_index_in_dim(stored, slot_index, 1, keepdims=False)
        written = jnp.where(active, latents, previous)
        stored = lax.dynamic_update_slice_in_dim(stored, written[:, None], slot_index, 1)
        inbound = passed_along(state, "segment", 1)
        return (inbound, stored)

    start_inbound = jnp.zeros((tok_rows, local_width), jnp.bfloat16)
    start_stored = jnp.zeros((local_layers, batches, tok_rows, latent_width), jnp.bfloat16)
    _, stored = lax.fori_loop(0, steps_total, advance, (start_inbound, start_stored))
    pages = stored.reshape(local_layers, page_count, PAGE, latent_width)
    targets = page_lists[:, :, 0]
    local_targets = lax.dynamic_slice_in_dim(targets, position * local_layers, local_layers, 0)
    local_rank = page_ranks(local_targets)
    owner_ids = jnp.arange(phases, dtype=jnp.int32)
    slot_ids = jnp.arange(capacity, dtype=jnp.int32)
    chosen = (
        (local_targets[:, None, None, :] == owner_ids[None, :, None, None])
        & (local_rank[:, None, None, :] == slot_ids[None, None, :, None])
    ).astype(jnp.bfloat16)
    outgoing = jnp.einsum(
        "lojp,lptc->oljtc", chosen, pages, preferred_element_type=jnp.float32
    ).astype(jnp.bfloat16)
    received = lax.all_to_all(outgoing, "segment", split_axis=0, concat_axis=0, tiled=True)
    keys = received.reshape(all_layers, capacity * PAGE, latent_width)
    counts = jnp.sum((targets == position).astype(jnp.int32), axis=1)
    limit = jnp.minimum(context_lengths, counts[None, :] * PAGE)
    return decode_block(queries, keys, new_latent, limit)


def solution(mesh):
    in_specs = (
        P(None, None, "wide"),
        P("segment", "wide"),
        P("segment", "wide", None),
        P("segment", None, "wide"),
        P(),
        P("segment", None, "wide", None),
        P("segment", None, None),
        P("segment", None),
    )
    out_specs = P("segment", None, "wide", None)
    return jax.shard_map(shards, mesh=mesh, in_specs=in_specs, out_specs=out_specs, check_vma=False)
```

profile of v0, /device:TPU:0, one launch (start us, length us, event | category | flops | bytes accessed | tf_op | source)
XLA Modules:
  0.0 1406.6 jit_solution(5530155793887246631)
XLA Ops:
  1.0 1340.9 %while.16 = (s32[]{:T(128)}, bf16[256,512]{1,0:T(8,128)(2,1)S(1)}, bf16[1,4,256,512]{3,2,1,0:T(8,128)(2,1)S(1)}, pred[]{:T(512)}, bf16[4,256,512]{2,1,0:T(8,128)...) while((s32[]{:T(128)}, bf16[256,512]{1,0:T(8,128)(2,1)S(1)}, ...), condition=%wide.region_4.5_spmd, body=%wide.region_0.4_spmd.sunk | while | flops 270926848 | bytes 8662304 | solution.py:100
  1.1 1.2 fusion.54
  2.2 42.0 %psum.26 = f32[256]{0:T(256)S(1)} all-reduce(f32[256]{0:T(256)S(1)} %get-tuple-element.264), channel_id=1, replica_groups=mesh['segment'=8,'wide'=16] {'wide'}, use_global_device_ids=true, to_apply=%region_2.2 | all-reduce | flops 256 | bytes 2048 | tf_op jit(solution)/shard_map/while/body/eval_jaxpr/psum | solution.py:30
  45.0 1.4 fusion.55
  46.3 74.9 %all-reduce.1 = bf16[256,512]{1,0:T(8,128)(2,1)S(1)} all-reduce(f32[256,512]{1,0:T(8,128)S(1)} %fusion.55), channel_id=1, replica_groups=mesh['segment'=8,'wide'=16] {'wide'}, use_global_device_ids=true, to_apply=%region_3.3 | all-reduce | flops 131072 | bytes 786432 | tf_op jit(solution)/shard_map/while/body/eval_jaxpr/psum | solution.py:36
  121.6 1.3 collective-permute-start
  123.0 1.0 collective-permute-done
  124.0 1.2 fusion.54
  125.2 38.0 %psum.26 = f32[256]{0:T(256)S(1)} all-reduce(f32[256]{0:T(256)S(1)} %get-tuple-element.264), channel_id=1, replica_groups=mesh['segment'=8,'wide'=16] {'wide'}, use_global_device_ids=true, to_apply=%region_2.2 | all-reduce | flops 256 | bytes 2048 | tf_op jit(solution)/shard_map/while/body/eval_jaxpr/psum | solution.py:30
  163.9 1.4 fusion.55
  165.3 75.1 %all-reduce.1 = bf16[256,512]{1,0:T(8,128)(2,1)S(1)} all-reduce(f32[256,512]{1,0:T(8,128)S(1)} %fusion.55), channel_id=1, replica_groups=mesh['segment'=8,'wide'=16] {'wide'}, use_global_device_ids=true, to_apply=%region_3.3 | all-reduce | flops 131072 | bytes 786432 | tf_op jit(solution)/shard_map/while/body/eval_jaxpr/psum | solution.py:36
  240.8 1.3 collective-permute-start
  243.2 1.2 fusion.54
  244.4 37.8 %psum.26 = f32[256]{0:T(256)S(1)} all-reduce(f32[256]{0:T(256)S(1)} %get-tuple-element.264), channel_id=1, replica_groups=mesh['segment'=8,'wide'=16] {'wide'}, use_global_device_ids=true, to_apply=%region_2.2 | all-reduce | flops 256 | bytes 2048 | tf_op jit(solution)/shard_map/while/body/eval_jaxpr/psum | solution.py:30
  282.8 1.4 fusion.55
  284.2 75.0 %all-reduce.1 = bf16[256,512]{1,0:T(8,128)(2,1)S(1)} all-reduce(f32[256,512]{1,0:T(8,128)S(1)} %fusion.55), channel_id=1, replica_groups=mesh['segment'=8,'wide'=16] {'wide'}, use_global_device_ids=true, to_apply=%region_3.3 | all-reduce | flops 131072 | bytes 786432 | tf_op jit(solution)/shard_map/while/body/eval_jaxpr/psum | solution.py:36
  359.6 1.3 collective-permute-start
  361.0 1.0 collective-permute-done
  362.0 1.2 fusion.54
  363.2 37.8 %psum.26 = f32[256]{0:T(256)S(1)} all-reduce(f32[256]{0:T(256)S(1)} %get-tuple-element.264), channel_id=1, replica_groups=mesh['segment'=8,'wide'=16] {'wide'}, use_global_device_ids=true, to_apply=%region_2.2 | all-reduce | flops 256 | bytes 2048 | tf_op jit(solution)/shard_map/while/body/eval_jaxpr/psum | solution.py:30
  401.7 1.4 fusion.55
  403.1 75.0 %all-reduce.1 = bf16[256,512]{1,0:T(8,128)(2,1)S(1)} all-reduce(f32[256,512]{1,0:T(8,128)S(1)} %fusion.55), channel_id=1, replica_groups=mesh['segment'=8,'wide'=16] {'wide'}, use_global_device_ids=true, to_apply=%region_3.3 | all-reduce | flops 131072 | bytes 786432 | tf_op jit(solution)/shard_map/while/body/eval_jaxpr/psum | solution.py:36
  478.5 1.3 collective-permute-start
  479.9 1.0 collective-permute-done
  480.9 1.2 fusion.54
  482.1 37.6 %psum.26 = f32[256]{0:T(256)S(1)} all-reduce(f32[256]{0:T(256)S(1)} %get-tuple-element.264), channel_id=1, replica_groups=mesh['segment'=8,'wide'=16] {'wide'}, use_global_device_ids=true, to_apply=%region_2.2 | all-reduce | flops 256 | bytes 2048 | tf_op jit(solution)/shard_map/while/body/eval_jaxpr/psum | solution.py:30
  520.4 1.4 fusion.55
  521.7 75.5 %all-reduce.1 = bf16[256,512]{1,0:T(8,128)(2,1)S(1)} all-reduce(f32[256,512]{1,0:T(8,128)S(1)} %fusion.55), channel_id=1, replica_groups=mesh['segment'=8,'wide'=16] {'wide'}, use_global_device_ids=true, to_apply=%region_3.3 | all-reduce | flops 131072 | bytes 786432 | tf_op jit(solution)/shard_map/while/body/eval_jaxpr/psum | solution.py:36
  597.5 1.3 collective-permute-start
  599.0 1.0 collective-permute-done
  600.0 1.2 fusion.54
  601.2 37.2 %psum.26 = f32[256]{0:T(256)S(1)} all-reduce(f32[256]{0:T(256)S(1)} %get-tuple-element.264), channel_id=1, replica_groups=mesh['segment'=8,'wide'=16] {'wide'}, use_global_device_ids=true, to_apply=%region_2.2 | all-reduce | flops 256 | bytes 2048 | tf_op jit(solution)/shard_map/while/body/eval_jaxpr/psum | solution.py:30
  639.1 1.4 fusion.55
  640.5 75.4 %all-reduce.1 = bf16[256,512]{1,0:T(8,128)(2,1)S(1)} all-reduce(f32[256,512]{1,0:T(8,128)S(1)} %fusion.55), channel_id=1, replica_groups=mesh['segment'=8,'wide'=16] {'wide'}, use_global_device_ids=true, to_apply=%region_3.3 | all-reduce | flops 131072 | bytes 786432 | tf_op jit(solution)/shard_map/while/body/eval_jaxpr/psum | solution.py:36
  716.2 5.0 collective-permute-start
  722.3 1.2 fusion.54
  723.5 38.0 %psum.26 = f32[256]{0:T(256)S(1)} all-reduce(f32[256]{0:T(256)S(1)} %get-tuple-element.264), channel_id=1, replica_groups=mesh['segment'=8,'wide'=16] {'wide'}, use_global_device_ids=true, to_apply=%region_2.2 | all-reduce | flops 256 | bytes 2048 | tf_op jit(solution)/shard_map/while/body/eval_jaxpr/psum | solution.py:30
  762.2 1.4 fusion.55
  763.6 74.9 %all-reduce.1 = bf16[256,512]{1,0:T(8,128)(2,1)S(1)} all-reduce(f32[256,512]{1,0:T(8,128)S(1)} %fusion.55), channel_id=1, replica_groups=mesh['segment'=8,'wide'=16] {'wide'}, use_global_device_ids=true, to_apply=%region_3.3 | all-reduce | flops 131072 | bytes 786432 | tf_op jit(solution)/shard_map/while/body/eval_jaxpr/psum | solution.py:36
  838.8 6.8 collective-permute-start
  846.7 1.2 fusion.54
  847.9 37.1 %psum.26 = f32[256]{0:T(256)S(1)} all-reduce(f32[256]{0:T(256)S(1)} %get-tuple-element.264), channel_id=1, replica_groups=mesh['segment'=8,'wide'=16] {'wide'}, use_global_device_ids=true, to_apply=%region_2.2 | all-reduce | flops 256 | bytes 2048 | tf_op jit(solution)/shard_map/while/body/eval_jaxpr/psum | solution.py:30
  885.7 1.4 fusion.55
  887.1 75.5 %all-reduce.1 = bf16[256,512]{1,0:T(8,128)(2,1)S(1)} all-reduce(f32[256,512]{1,0:T(8,128)S(1)} %fusion.55), channel_id=1, replica_groups=mesh['segment'=8,'wide'=16] {'wide'}, use_global_device_ids=true, to_apply=%region_3.3 | all-reduce | flops 131072 | bytes 786432 | tf_op jit(solution)/shard_map/while/body/eval_jaxpr/psum | solution.py:36
  963.0 6.5 collective-permute-start
  970.6 1.2 fusion.54
  971.8 37.1 %psum.26 = f32[256]{0:T(256)S(1)} all-reduce(f32[256]{0:T(256)S(1)} %get-tuple-element.264), channel_id=1, replica_groups=mesh['segment'=8,'wide'=16] {'wide'}, use_global_device_ids=true, to_apply=%region_2.2 | all-reduce | flops 256 | bytes 2048 | tf_op jit(solution)/shard_map/while/body/eval_jaxpr/psum | solution.py:30
  1009.6 1.4 fusion.55
  1011.0 75.5 %all-reduce.1 = bf16[256,512]{1,0:T(8,128)(2,1)S(1)} all-reduce(f32[256,512]{1,0:T(8,128)S(1)} %fusion.55), channel_id=1, replica_groups=mesh['segment'=8,'wide'=16] {'wide'}, use_global_device_ids=true, to_apply=%region_3.3 | all-reduce | flops 131072 | bytes 786432 | tf_op jit(solution)/shard_map/while/body/eval_jaxpr/psum | solution.py:36
  1086.8 6.7 collective-permute-start
  1094.6 1.2 fusion.54
  1095.8 36.8 %psum.26 = f32[256]{0:T(256)S(1)} all-reduce(f32[256]{0:T(256)S(1)} %get-tuple-element.264), channel_id=1, replica_groups=mesh['segment'=8,'wide'=16] {'wide'}, use_global_device_ids=true, to_apply=%region_2.2 | all-reduce | flops 256 | bytes 2048 | tf_op jit(solution)/shard_map/while/body/eval_jaxpr/psum | solution.py:30
  1133.3 1.4 fusion.55
  1134.7 75.8 %all-reduce.1 = bf16[256,512]{1,0:T(8,128)(2,1)S(1)} all-reduce(f32[256,512]{1,0:T(8,128)S(1)} %fusion.55), channel_id=1, replica_groups=mesh['segment'=8,'wide'=16] {'wide'}, use_global_device_ids=true, to_apply=%region_3.3 | all-reduce | flops 131072 | bytes 786432 | tf_op jit(solution)/shard_map/while/body/eval_jaxpr/psum | solution.py:36
  1210.9 5.9 collective-permute-start
  1218.0 1.2 fusion.54
  1219.2 37.1 %psum.26 = f32[256]{0:T(256)S(1)} all-reduce(f32[256]{0:T(256)S(1)} %get-tuple-element.264), channel_id=1, replica_groups=mesh['segment'=8,'wide'=16] {'wide'}, use_global_device_ids=true, to_apply=%region_2.2 | all-reduce | flops 256 | bytes 2048 | tf_op jit(solution)/shard_map/while/body/eval_jaxpr/psum | solution.py:30
  1257.0 1.4 fusion.55
  1258.4 75.6 %all-reduce.1 = bf16[256,512]{1,0:T(8,128)(2,1)S(1)} all-reduce(f32[256,512]{1,0:T(8,128)S(1)} %fusion.55), channel_id=1, replica_groups=mesh['segment'=8,'wide'=16] {'wide'}, use_global_device_ids=true, to_apply=%region_3.3 | all-reduce | flops 131072 | bytes 786432 | tf_op jit(solution)/shard_map/while/body/eval_jaxpr/psum | solution.py:36
  1334.3 6.5 collective-permute-start
  1342.8 3.0 copy.25
  1345.7 30.2 %all-to-all-start = ((bf16[8,1,2,128,512]{4,2,3,1,0:T(2,128)(2,1)}), bf16[8,1,2,128,512]{4,2,3,1,0:T(2,128)(2,1)S(1)}, u32[]{:S(2)}, u32[]{:S(2)}) async-start(bf16[8,1,2,128,512]{4,2,3,1,0:T(2,128)(2,1)} %copy.25), calls=%async_computation | async-start | bytes 4194304 | tf_op jit(solution)/shard_map/all_to_all | solution.py:114
  1377.2 26.0 %all-to-all-done = bf16[8,1,2,128,512]{4,2,3,1,0:T(2,128)(2,1)S(1)} async-done(((bf16[8,1,2,128,512]{4,2,3,1,0:T(2,128)(2,1)}), bf16[8,1,2,128,512]{4,2,3,1,0:T(2,128)(2,1)S(1)}, u32[]{:S(2)}, u32[]{:S(2)}) %all-to-all-start) | async-done | bytes 2097184 | tf_op jit(solution)/shard_map/all_to_all | solution.py:114
  1405.4 1.2 copy.29
  (112 shorter events, 24.6 us)
Async XLA Ops:
  0.0 1376.1 %copy-start = (bf16[16,8,4,512]{3,2,1,0:T(4,128)(2,1)S(1)}, bf16[16,8,4,512]{3,2,1,0:T(4,128)(2,1)}, u32[]{:S(2)}) copy-start(bf16[16,8,4,512]{3,2,1,0:T(4,128)(2,1)} %param.15) | copy-start | bytes 1572868
  1.0 120.2 %copy-start.4 = (bf16[1,512,512]{2,1,0:T(8,128)(2,1)S(1)}, bf16[1,512,512]{2,1,0:T(8,128)(2,1)}, u32[]{:S(2)}) copy-start(bf16[1,512,512]{2,1,0:T(8,128)(2,1)} %get-tuple-element.298) | copy-start | bytes 1572868 | tf_op jit(solution)/shard_map/while
  121.6 2.4 collective-permute-start
  124.0 116.4 %copy-start.4 = (bf16[1,512,512]{2,1,0:T(8,128)(2,1)S(1)}, bf16[1,512,512]{2,1,0:T(8,128)(2,1)}, u32[]{:S(2)}) copy-start(bf16[1,512,512]{2,1,0:T(8,128)(2,1)} %get-tuple-element.298) | copy-start | bytes 1572868 | tf_op jit(solution)/shard_map/while
  240.8 2.4 collective-permute-start
  243.2 116.0 %copy-start.4 = (bf16[1,512,512]{2,1,0:T(8,128)(2,1)S(1)}, bf16[1,512,512]{2,1,0:T(8,128)(2,1)}, u32[]{:S(2)}) copy-start(bf16[1,512,512]{2,1,0:T(8,128)(2,1)} %get-tuple-element.298) | copy-start | bytes 1572868 | tf_op jit(solution)/shard_map/while
  359.6 2.4 collective-permute-start
  362.0 116.1 %copy-start.4 = (bf16[1,512,512]{2,1,0:T(8,128)(2,1)S(1)}, bf16[1,512,512]{2,1,0:T(8,128)(2,1)}, u32[]{:S(2)}) copy-start(bf16[1,512,512]{2,1,0:T(8,128)(2,1)} %get-tuple-element.298) | copy-start | bytes 1572868 | tf_op jit(solution)/shard_map/while
  478.5 2.4 collective-permute-start
  480.9 116.3 %copy-start.4 = (bf16[1,512,512]{2,1,0:T(8,128)(2,1)S(1)}, bf16[1,512,512]{2,1,0:T(8,128)(2,1)}, u32[]{:S(2)}) copy-start(bf16[1,512,512]{2,1,0:T(8,128)(2,1)} %get-tuple-element.298) | copy-start | bytes 1572868 | tf_op jit(solution)/shard_map/while
  597.5 2.4 collective-permute-start
  600.0 115.9 %copy-start.4 = (bf16[1,512,512]{2,1,0:T(8,128)(2,1)S(1)}, bf16[1,512,512]{2,1,0:T(8,128)(2,1)}, u32[]{:S(2)}) copy-start(bf16[1,512,512]{2,1,0:T(8,128)(2,1)} %get-tuple-element.298) | copy-start | bytes 1572868 | tf_op jit(solution)/shard_map/while
  716.2 6.1 collective-permute-start
  722.3 116.2 %copy-start.4 = (bf16[1,512,512]{2,1,0:T(8,128)(2,1)S(1)}, bf16[1,512,512]{2,1,0:T(8,128)(2,1)}, u32[]{:S(2)}) copy-start(bf16[1,512,512]{2,1,0:T(8,128)(2,1)} %get-tuple-element.298) | copy-start | bytes 1572868 | tf_op jit(solution)/shard_map/while
  838.8 7.9 collective-permute-start
  846.7 115.9 %copy-start.4 = (bf16[1,512,512]{2,1,0:T(8,128)(2,1)S(1)}, bf16[1,512,512]{2,1,0:T(8,128)(2,1)}, u32[]{:S(2)}) copy-start(bf16[1,512,512]{2,1,0:T(8,128)(2,1)} %get-tuple-element.298) | copy-start | bytes 1572868 | tf_op jit(solution)/shard_map/while
  963.0 7.7 collective-permute-start
  970.6 115.8 %copy-start.4 = (bf16[1,512,512]{2,1,0:T(8,128)(2,1)S(1)}, bf16[1,512,512]{2,1,0:T(8,128)(2,1)}, u32[]{:S(2)}) copy-start(bf16[1,512,512]{2,1,0:T(8,128)(2,1)} %get-tuple-element.298) | copy-start | bytes 1572868 | tf_op jit(solution)/shard_map/while
  1086.8 7.8 collective-permute-start
  1094.6 116.0 %copy-start.4 = (bf16[1,512,512]{2,1,0:T(8,128)(2,1)S(1)}, bf16[1,512,512]{2,1,0:T(8,128)(2,1)}, u32[]{:S(2)}) copy-start(bf16[1,512,512]{2,1,0:T(8,128)(2,1)} %get-tuple-element.298) | copy-start | bytes 1572868 | tf_op jit(solution)/shard_map/while
  1210.9 7.1 collective-permute-start
  1218.0 116.0 %copy-start.4 = (bf16[1,512,512]{2,1,0:T(8,128)(2,1)S(1)}, bf16[1,512,512]{2,1,0:T(8,128)(2,1)}, u32[]{:S(2)}) copy-start(bf16[1,512,512]{2,1,0:T(8,128)(2,1)} %get-tuple-element.298) | copy-start | bytes 1572868 | tf_op jit(solution)/shard_map/while
  1334.3 7.7 collective-permute-start
  1345.7 30.2 %copy-start.1 = (bf16[16,8,512]{2,1,0:T(8,128)(2,1)S(1)}, bf16[16,8,512]{2,1,0:T(8,128)(2,1)}, u32[]{:S(2)}) copy-start(bf16[16,8,512]{2,1,0:T(8,128)(2,1)} %param.16) | copy-start | bytes 393220
  1345.7 57.4 %all-to-all-start = ((bf16[8,1,2,128,512]{4,2,3,1,0:T(2,128)(2,1)}), bf16[8,1,2,128,512]{4,2,3,1,0:T(2,128)(2,1)S(1)}, u32[]{:S(2)}, u32[]{:S(2)}) async-start(bf16[8,1,2,128,512]{4,2,3,1,0:T(2,128)(2,1)} %copy.25), calls=%async_computation | async-start | bytes 4194304 | tf_op jit(solution)/shard_map/all_to_all | solution.py:114
  1376.0 0.8 copy-start.2
  1376.0 1.0 copy-start.3
where the time goes:
time: 1410 us
  blocking collectives  1240 us (88%)
  starting transfers between devices  74.2 us (5%)
  waiting for transfers between devices  37 us (3%)
  other arithmetic  22.4 us (2%)
  matrix products  21.6 us (2%)
    psum x11, blocking collectives, latent_layer(): latent = lax.psum(partial_term, 'wide').astype(jnp.bfloat16)  828 us
    psum x11, blocking collectives, latent_layer(): squares = lax.psum(jnp.sum(values * values, axis=1), 'wide')  417 us
    ppermute x11, starting transfers between devices, passed_along(): return lax.ppermute(x, axis, pairs)  43.9 us
    all_to_all x1, starting transfers between devices, shards(): lax.all_to_all(outgoing, 'segment', split_axis=0, concat_axis=0, tiled=True)  30.2 us
  transfers between devices with their start and end apart: 12, of which 12 were waited for; matrix products, arithmetic and copies ran while one was open for 0% of the time, Pallas kernels for 0%

commit v1 on v0

v1 whole, which is shorter than its diff:
```python
import jax
import jax.numpy as jnp
from jax import lax
from jax.sharding import PartitionSpec as P

PAGE = 128
LANES = 128

eps_norm = 1e-06
score_scale = 192.0 ** (-0.5)

GROUPS = ((0,), (1,), (2,), (3,), (4,), (5,), (6,), (7,))


def dot(a, b):
    return jnp.dot(a, b, preferred_element_type=jnp.float32)


def dot_t(a, b):
    return lax.dot_general(a, b, (((1,), (1,)), ((), ())), preferred_element_type=jnp.float32)


def square_columns(state):
    values = state.astype(jnp.float32)
    squares = jnp.sum(values * values, axis=1, keepdims=True)
    high = squares.astype(jnp.bfloat16)
    low = (squares - high.astype(jnp.float32)).astype(jnp.bfloat16)
    column = lax.broadcasted_iota(jnp.int32, (state.shape[0], LANES), 1)
    return jnp.where(column == 0, high, jnp.where(column == 1, low, jnp.zeros_like(low)))


def scatter_sum(parts, axis):
    size = lax.axis_size(axis)
    rows = parts.shape[0] // size
    sent = parts.reshape(size, rows, parts.shape[1])
    received = lax.all_to_all(sent, axis, 0, 0, tiled=True)
    return jnp.sum(received.astype(jnp.float32), axis=0)


def gathered(block, axis):
    size = lax.axis_size(axis)
    sent = jnp.broadcast_to(block[None], (size,) + block.shape)
    return lax.all_to_all(sent, axis, 0, 0, tiled=True)


def silu(latent):
    return jax.nn.silu(latent.astype(jnp.float32)).astype(jnp.bfloat16)


def decode_block(owner_queries, keys, owner_new, limit):
    positions = jnp.arange(keys.shape[1], dtype=jnp.int32)
    readable = positions[None, None, :] < limit[:, :, None]
    scores = (
        jnp.einsum("rlhc,lkc->rlhk", owner_queries, keys, preferred_element_type=jnp.float32)
        * score_scale
    )
    scores = jnp.where(readable[:, :, None, :], scores, -jnp.inf)
    own_score = (
        jnp.einsum("rlhc,rlc->rlh", owner_queries, owner_new, preferred_element_type=jnp.float32)
        * score_scale
    )
    top = jnp.maximum(jnp.max(scores, axis=-1), own_score)
    weights = jnp.exp(scores - top[..., None])
    own_weight = jnp.exp(own_score - top)
    total = jnp.sum(weights, axis=-1) + own_weight
    numer = jnp.einsum(
        "rlhk,lkc->rlhc", weights.astype(jnp.bfloat16), keys, preferred_element_type=jnp.float32
    )
    numer = numer + own_weight[..., None] * owner_new.astype(jnp.float32)[:, :, None, :]
    return (numer / total[..., None]).astype(jnp.bfloat16)


def shards(
    prompt_states, norm_gain, w_latent, w_back, page_lists, queries, new_latent, context_lengths
):
    segments = lax.axis_size("segment")
    wide_size = lax.axis_size("wide")
    position = lax.axis_index("segment")
    core = position % 2
    batches, tok_rows, local_width = prompt_states.shape
    width = local_width * wide_size
    tokens = batches * tok_rows
    mine = tokens // segments
    layers = segments
    lat = w_latent.shape[2]

    gained = (
        w_latent[0].astype(jnp.float32) * norm_gain[0].astype(jnp.float32)[:, None]
    ).astype(jnp.bfloat16)
    back = w_back[0]

    first = lax.all_gather(jnp.where(core == 0, back, gained), "segment", axis=0)
    second = lax.all_gather(jnp.where(core == 0, gained, back), "segment", axis=0)

    def latent_weight(layer):
        return (second if layer % 2 == 0 else first)[layer]

    def back_weight(layer):
        return (first if layer % 2 == 0 else second)[layer]

    states = prompt_states.reshape(tokens, local_width)
    state = lax.dynamic_slice_in_dim(states, position * mine, mine, 0)
    lent = lax.ppermute(gained, "segment", [(0, 1)])
    home_weight = jnp.where(position == 0, gained, lent)
    by_core = states.reshape(segments // 2, 2, mine, local_width)
    turn = lax.dynamic_index_in_dim(by_core, core, 1, keepdims=False)
    home = dot(turn.reshape(tokens // 2, local_width), home_weight).astype(jnp.bfloat16)
    home = home.reshape(segments // 2, mine, lat)
    product = jnp.where(position < 2, home[0], jnp.zeros_like(home[0]))
    for hop in range(1, segments // 2):
        product = product + lax.ppermute(
            home[hop], "segment", [(0, 2 * hop), (1, 2 * hop + 1)]
        )

    pages = []
    for number, group in enumerate(GROUPS):
        last = number == len(GROUPS) - 1
        (layer,) = group
        if number > 0:
            update = dot(activated, back_weight(layer - 1))
            state = (state.astype(jnp.float32) + update).astype(jnp.bfloat16)
            product = dot(state, latent_weight(layer)).astype(jnp.bfloat16)
        summed = scatter_sum(jnp.concatenate([product, square_columns(state)], axis=1), "wide")
        squares = summed[:, lat : lat + 1] + summed[:, lat + 1 : lat + 2]
        inverse_rms = lax.rsqrt(squares / width + eps_norm)
        latent = (summed[:, :lat] * inverse_rms).astype(jnp.bfloat16)
        if not last:
            whole = gathered(latent, "wide").reshape(mine, lat)
            activated = silu(whole)
            pages.append(lax.all_gather(whole, "segment", axis=0))

    targets = page_lists[:, :, 0]
    owned = targets == position
    counts = jnp.sum(owned.astype(jnp.int32), axis=1)
    order = jnp.arange(targets.shape[1], dtype=jnp.int32)[None, :]
    none = targets.shape[1]
    slot0 = jnp.min(jnp.where(owned, order, none), axis=1)
    slot1 = jnp.min(jnp.where(owned & (order > slot0[:, None]), order, none), axis=1)
    slot0 = jnp.minimum(slot0, none - 1)
    slot1 = jnp.minimum(slot1, none - 1)

    keys = []
    for layer in range(layers - 1):
        here = pages[layer]
        keys.append(jnp.concatenate([here[slot0[layer]], here[slot1[layer]]], axis=0))
    spread = gathered(latent, "segment")
    chosen = jnp.concatenate(
        [spread[slot0[layers - 1]], spread[slot1[layers - 1]]], axis=1
    )
    ends = gathered(chosen, "wide").reshape(mine, 2 * lat)
    keys.append(jnp.concatenate([ends[:, :lat], ends[:, lat:]], axis=0))
    keys = jnp.stack(keys)
    limit = jnp.minimum(context_lengths, counts[None, :] * PAGE)
    return decode_block(queries, keys, new_latent, limit)


def solution(mesh):
    in_specs = (
        P(None, None, "wide"),
        P("segment", "wide"),
        P("segment", "wide", None),
        P("segment", None, "wide"),
        P(),
        P("segment", None, "wide", None),
        P("segment", None, None),
        P("segment", None),
    )
    out_specs = P("segment", None, "wide", None)
    return jax.shard_map(shards, mesh=mesh, in_specs=in_specs, out_specs=out_specs, check_vma=False)
```

time: 1410 us -> 300 us (0.21)
  blocking collectives: 1240 us -> 51.5 us
  waiting for transfers between devices: 37 us -> 89.2 us
  between operations: 0.12 us -> 45.4 us
    psum x22 -> x0, blocking collectives: 1240 us -> none  [the longest x11 828 us: latent_layer(): latent = lax.psum(partial_term, 'wide').astype(jnp.bfloat16)]
    all_to_all x0 -> x4, blocking collectives: none -> 51.5 us  [the longest x3 33.1 us: gathered(): return lax.all_to_all(sent, axis, 0, 0, tiled=True)]
    all_to_all x1 -> x13, waiting for transfers between devices: 26 us -> 75.1 us  [the longest x7 44.8 us: scatter_sum(): received = lax.all_to_all(sent, axis, 0, 0, tiled=True)]
    ppermute x11 -> x4, starting transfers between devices: 43.9 us -> 6.42 us  [the longest x3 5.1 us: shards(): lax.ppermute(home[hop], 'segment', [(0, 2 * hop), (1, 2 * hop + 1)])]
    all_to_all x1 -> x13, starting transfers between devices: 30.2 us -> 54.8 us  [the longest x7 30 us: scatter_sum(): received = lax.all_to_all(sent, axis, 0, 0, tiled=True)]
  transfers between devices with their start and end apart: 12 -> 26, of which waited for: 12 -> 15; matrix products, arithmetic and copies ran while one was open for 0% -> 14% of each run, Pallas kernels for 0% -> 0%
where the time goes in v1:
time: 300 us; the launch traced here: 298 us
  waiting for transfers between devices  89.2 us (30%)
  starting transfers between devices  61.5 us (20%)
  blocking collectives  51.5 us (17%)
  between operations  45.4 us (15%)
  matrix products  21.4 us (7%)
  local copies, waits for them, and re-layouts  15 us (5%)
  other arithmetic  13.7 us (5%)
    all_to_all x7, waiting for transfers between devices, scatter_sum(): received = lax.all_to_all(sent, axis, 0, 0, tiled=True)  44.8 us
    all_to_all x3, blocking collectives, gathered(): return lax.all_to_all(sent, axis, 0, 0, tiled=True)  33.1 us
    all_to_all x6, waiting for transfers between devices, gathered(): return lax.all_to_all(sent, axis, 0, 0, tiled=True)  30.2 us
    all_to_all x7, starting transfers between devices, scatter_sum(): received = lax.all_to_all(sent, axis, 0, 0, tiled=True)  30 us
    all_to_all x6, starting transfers between devices, gathered(): return lax.all_to_all(sent, axis, 0, 0, tiled=True)  24.8 us
    dot_general x15, matrix products, dot(): return jnp.dot(a, b, preferred_element_type=jnp.float32)  19.4 us
    all_to_all x1, blocking collectives, scatter_sum(): received = lax.all_to_all(sent, axis, 0, 0, tiled=True)  18.4 us
    squeeze x7, local copies, waits for them, and re-layouts, shards(): here[slot0[layer]]  6.96 us
  transfers between devices with their start and end apart: 26, of which 15 were waited for; matrix products, arithmetic and copies ran while one was open for 14% of the time, Pallas kernels for 0%

profile of v1, /device:TPU:0, one launch (start us, length us, event | category | flops | bytes accessed | tf_op | source)
XLA Modules:
  0.0 297.7 jit_solution(3167302584156595920)
XLA Ops:
  6.5 0.8 convert_element_type.545
  7.3 2.5 broadcast_select_fusion
  9.9 0.7 all-gather.16.cloned.1.call-update
  10.6 1.2 fusion.33
  11.8 1.3 collective-permute-start
  13.4 1.3 collective-permute-done
  15.2 1.6 collective-permute-start.1
  16.8 2.2 collective-permute-start.2
  19.0 1.3 collective-permute-start.3
  20.6 2.4 collective-permute-done.2
  23.3 18.4 %all_to_all.85 = bf16[16,8,640]{2,1,0:T(8,128)(2,1)S(1)} all-to-all(bf16[16,8,640]{2,1,0:T(8,128)(2,1)S(1)} %bitcast.264), channel_id=1, replica_groups=mesh['segment'=8,'wide'=16] {'wide'}, dimensions={0} | all-to-all | bytes 327680 | tf_op jit(solution)/shard_map/all_to_all | solution.py:36
  42.0 11.0 %all_to_all.86 = bf16[16,8,512]{2,1,0:T(8,128)(2,1)S(1)} all-to-all(bf16[16,8,512]{2,1,0:T(8,128)(2,1)S(1)} %broadcast_in_dim.227), channel_id=1, replica_groups=mesh['segment'=8,'wide'=16] {'wide'}, dimensions={0} | all-to-all | bytes 262144 | tf_op jit(solution)/shard_map/all_to_all | solution.py:43
  53.1 1.4 fusion.45
  54.7 1.3 convolution_convert_fusion.7
  56.0 0.7 maximum_bitcast_fusion.8
  56.7 3.5 %all-to-all-start.2 = ((bf16[16,8,640]{2,1,0:T(8,128)(2,1)}), bf16[16,8,640]{2,1,0:T(8,128)(2,1)S(1)}, u32[]{:S(2)}, u32[]{:S(2)}) async-start(bf16[16,8,640]{2,1,0:T(8,128)(2,1)} %maximum_bitcast_fusion.8), calls=%async_computation.2 | async-start | bytes 327680 | tf_op jit(solution)/shard_map/all_to_all | solution.py:36
  61.0 7.4 %all-to-all-done.2 = bf16[16,8,640]{2,1,0:T(8,128)(2,1)S(1)} async-done(((bf16[16,8,640]{2,1,0:T(8,128)(2,1)}), bf16[16,8,640]{2,1,0:T(8,128)(2,1)S(1)}, u32[]{:S(2)}, u32[]{:S(2)}) %all-to-all-start.2) | async-done | bytes 163872 | tf_op jit(solution)/shard_map/all_to_all | solution.py:36
  69.3 3.5 %all-to-all-start.3 = ((bf16[16,8,512]{2,1,0:T(8,128)(2,1)}), bf16[16,8,512]{2,1,0:T(8,128)(2,1)S(1)}, u32[]{:S(2)}, u32[]{:S(2)}) async-start(bf16[16,8,512]{2,1,0:T(8,128)(2,1)} %broadcast_in_dim.234), calls=%async_computation.3 | async-start | bytes 262144 | tf_op jit(solution)/shard_map/all_to_all | solution.py:43
  72.9 6.2 %all-gather.16.cloned.1.call-done = bf16[8,512,512]{2,1,0:T(8,128)(2,1)} async-done(((bf16[1,512,512]{2,1,0:T(8,128)(2,1)}), bf16[8,512,512]{2,1,0:T(8,128)(2,1)}) %all-gather.16.cloned.1.call-update) | async-done | bytes 4194320 | tf_op jit(solution)/shard_map/all_gather | solution.py:93
  79.1 1.7 all-to-all-done.3
  80.8 1.4 fusion.50
  82.5 1.3 convolution_convert_fusion.6
  84.4 5.3 %all-to-all-start.4 = ((bf16[16,8,640]{2,1,0:T(8,128)(2,1)}), bf16[16,8,640]{2,1,0:T(8,128)(2,1)S(1)}, u32[]{:S(2)}, u32[]{:S(2)}) async-start(bf16[16,8,640]{2,1,0:T(8,128)(2,1)} %maximum_bitcast_fusion.9), calls=%async_computation.4 | async-start | bytes 327680 | tf_op jit(solution)/shard_map/all_to_all | solution.py:36
  90.3 7.6 %all-to-all-done.4 = bf16[16,8,640]{2,1,0:T(8,128)(2,1)S(1)} async-done(((bf16[16,8,640]{2,1,0:T(8,128)(2,1)}), bf16[16,8,640]{2,1,0:T(8,128)(2,1)S(1)}, u32[]{:S(2)}, u32[]{:S(2)}) %all-to-all-start.4) | async-done | bytes 163872 | tf_op jit(solution)/shard_map/all_to_all | solution.py:36
  98.2 11.0 %all_to_all.87 = bf16[16,8,512]{2,1,0:T(8,128)(2,1)S(1)} all-to-all(bf16[16,8,512]{2,1,0:T(8,128)(2,1)S(1)} %broadcast_in_dim.237), channel_id=1, replica_groups=mesh['segment'=8,'wide'=16] {'wide'}, dimensions={0} | all-to-all | bytes 262144 | tf_op jit(solution)/shard_map/all_to_all | solution.py:43
  109.2 1.4 fusion.55
  110.9 1.3 convolution_convert_fusion.5
  112.9 3.5 %all-to-all-start.6 = ((bf16[16,8,640]{2,1,0:T(8,128)(2,1)}), bf16[16,8,640]{2,1,0:T(8,128)(2,1)S(1)}, u32[]{:S(2)}, u32[]{:S(2)}) async-start(bf16[16,8,640]{2,1,0:T(8,128)(2,1)} %maximum_bitcast_fusion.10), calls=%async_computation.6 | async-start | bytes 327680 | tf_op jit(solution)/shard_map/all_to_all | solution.py:36
  117.0 7.5 %all-to-all-done.6 = bf16[16,8,640]{2,1,0:T(8,128)(2,1)S(1)} async-done(((bf16[16,8,640]{2,1,0:T(8,128)(2,1)}), bf16[16,8,640]{2,1,0:T(8,128)(2,1)S(1)}, u32[]{:S(2)}, u32[]{:S(2)}) %all-to-all-start.6) | async-done | bytes 163872 | tf_op jit(solution)/shard_map/all_to_all | solution.py:36
  124.8 11.0 %all_to_all.88 = bf16[16,8,512]{2,1,0:T(8,128)(2,1)S(1)} all-to-all(bf16[16,8,512]{2,1,0:T(8,128)(2,1)S(1)} %broadcast_in_dim.240), channel_id=1, replica_groups=mesh['segment'=8,'wide'=16] {'wide'}, dimensions={0} | all-to-all | bytes 262144 | tf_op jit(solution)/shard_map/all_to_all | solution.py:43
  135.9 1.4 fusion.60
  137.5 1.3 convolution_convert_fusion.4
  139.5 3.5 %all-to-all-start.8 = ((bf16[16,8,640]{2,1,0:T(8,128)(2,1)}), bf16[16,8,640]{2,1,0:T(8,128)(2,1)S(1)}, u32[]{:S(2)}, u32[]{:S(2)}) async-start(bf16[16,8,640]{2,1,0:T(8,128)(2,1)} %maximum_bitcast_fusion.11), calls=%async_computation.8 | async-start | bytes 327680 | tf_op jit(solution)/shard_map/all_to_all | solution.py:36
  143.6 7.5 %all-to-all-done.8 = bf16[16,8,640]{2,1,0:T(8,128)(2,1)S(1)} async-done(((bf16[16,8,640]{2,1,0:T(8,128)(2,1)}), bf16[16,8,640]{2,1,0:T(8,128)(2,1)S(1)}, u32[]{:S(2)}, u32[]{:S(2)}) %all-to-all-start.8) | async-done | bytes 163872 | tf_op jit(solution)/shard_map/all_to_all | solution.py:36
  152.1 3.5 %all-to-all-start.9 = ((bf16[16,8,512]{2,1,0:T(8,128)(2,1)}), bf16[16,8,512]{2,1,0:T(8,128)(2,1)S(1)}, u32[]{:S(2)}, u32[]{:S(2)}) async-start(bf16[16,8,512]{2,1,0:T(8,128)(2,1)} %broadcast_in_dim.243), calls=%async_computation.9 | async-start | bytes 262144 | tf_op jit(solution)/shard_map/all_to_all | solution.py:43
  155.7 7.9 %all-to-all-done.9 = bf16[16,8,512]{2,1,0:T(8,128)(2,1)S(1)} async-done(((bf16[16,8,512]{2,1,0:T(8,128)(2,1)}), bf16[16,8,512]{2,1,0:T(8,128)(2,1)S(1)}, u32[]{:S(2)}, u32[]{:S(2)}) %all-to-all-start.9) | async-done | bytes 131104 | tf_op jit(solution)/shard_map/all_to_all | solution.py:43
  163.6 1.4 fusion.65
  165.3 1.3 convolution_convert_fusion.3
  167.2 3.5 %all-to-all-start.10 = ((bf16[16,8,640]{2,1,0:T(8,128)(2,1)}), bf16[16,8,640]{2,1,0:T(8,128)(2,1)S(1)}, u32[]{:S(2)}, u32[]{:S(2)}) async-start(bf16[16,8,640]{2,1,0:T(8,128)(2,1)} %maximum_bitcast_fusion.12), calls=%async_computation.10 | async-start | bytes 327680 | tf_op jit(solution)/shard_map/all_to_all | solution.py:36
  171.5 7.4 %all-to-all-done.10 = bf16[16,8,640]{2,1,0:T(8,128)(2,1)S(1)} async-done(((bf16[16,8,640]{2,1,0:T(8,128)(2,1)}), bf16[16,8,640]{2,1,0:T(8,128)(2,1)S(1)}, u32[]{:S(2)}, u32[]{:S(2)}) %all-to-all-start.10) | async-done | bytes 163872 | tf_op jit(solution)/shard_map/all_to_all | solution.py:36
  179.9 3.5 %all-to-all-start.11 = ((bf16[16,8,512]{2,1,0:T(8,128)(2,1)}), bf16[16,8,512]{2,1,0:T(8,128)(2,1)S(1)}, u32[]{:S(2)}, u32[]{:S(2)}) async-start(bf16[16,8,512]{2,1,0:T(8,128)(2,1)} %broadcast_in_dim.246), calls=%async_computation.11 | async-start | bytes 262144 | tf_op jit(solution)/shard_map/all_to_all | solution.py:43
  205.8 1.4 fusion.70
  207.5 1.3 convolution_convert_fusion.2
  209.5 7.2 %all-to-all-start.12 = ((bf16[16,8,640]{2,1,0:T(8,128)(2,1)}), bf16[16,8,640]{2,1,0:T(8,128)(2,1)S(1)}, u32[]{:S(2)}, u32[]{:S(2)}) async-start(bf16[16,8,640]{2,1,0:T(8,128)(2,1)} %maximum_bitcast_fusion.13), calls=%async_computation.12 | async-start | bytes 327680 | tf_op jit(solution)/shard_map/all_to_all | solution.py:36
  228.9 7.2 %all-to-all-start.13 = ((bf16[16,8,512]{2,1,0:T(8,128)(2,1)}), bf16[16,8,512]{2,1,0:T(8,128)(2,1)S(1)}, u32[]{:S(2)}, u32[]{:S(2)}) async-start(bf16[16,8,512]{2,1,0:T(8,128)(2,1)} %broadcast_in_dim.249), calls=%async_computation.13 | async-start | bytes 262144 | tf_op jit(solution)/shard_map/all_to_all | solution.py:43
  236.2 7.9 %all-to-all-done.13 = bf16[16,8,512]{2,1,0:T(8,128)(2,1)S(1)} async-done(((bf16[16,8,512]{2,1,0:T(8,128)(2,1)}), bf16[16,8,512]{2,1,0:T(8,128)(2,1)S(1)}, u32[]{:S(2)}, u32[]{:S(2)}) %all-to-all-start.13) | async-done | bytes 131104 | tf_op jit(solution)/shard_map/all_to_all | solution.py:43
  244.1 1.4 multiply_reduce_fusion
  245.7 1.3 convolution_convert_fusion.1
  247.7 3.5 %all-to-all-start.14 = ((bf16[16,8,640]{2,1,0:T(8,128)(2,1)}), bf16[16,8,640]{2,1,0:T(8,128)(2,1)S(1)}, u32[]{:S(2)}, u32[]{:S(2)}) async-start(bf16[16,8,640]{2,1,0:T(8,128)(2,1)} %maximum_bitcast_fusion.14), calls=%async_computation.14 | async-start | bytes 327680 | tf_op jit(solution)/shard_map/all_to_all | solution.py:36
  252.0 7.4 %all-to-all-done.14 = bf16[16,8,640]{2,1,0:T(8,128)(2,1)S(1)} async-done(((bf16[16,8,640]{2,1,0:T(8,128)(2,1)}), bf16[16,8,640]{2,1,0:T(8,128)(2,1)S(1)}, u32[]{:S(2)}, u32[]{:S(2)}) %all-to-all-start.14) | async-done | bytes 163872 | tf_op jit(solution)/shard_map/all_to_all | solution.py:36
  260.3 3.5 %all-to-all-start.15 = ((bf16[8,8,512]{2,1,0:T(8,128)(2,1)}), bf16[8,8,512]{2,1,0:T(8,128)(2,1)S(1)}, u32[]{:S(2)}, u32[]{:S(2)}) async-start(bf16[8,8,512]{2,1,0:T(8,128)(2,1)} %broadcast_in_dim.252), calls=%async_computation.15 | async-start | bytes 131072 | tf_op jit(solution)/shard_map/all_to_all | solution.py:43
  263.8 1.0 dynamic-slice_bitcast_fusion.13
  264.8 5.1 %all-to-all-done.15 = bf16[8,8,512]{2,1,0:T(8,128)(2,1)S(1)} async-done(((bf16[8,8,512]{2,1,0:T(8,128)(2,1)}), bf16[8,8,512]{2,1,0:T(8,128)(2,1)S(1)}, u32[]{:S(2)}, u32[]{:S(2)}) %all-to-all-start.15) | async-done | bytes 65568 | tf_op jit(solution)/shard_map/all_to_all | solution.py:43
  269.9 0.7 broadcast_in_dim.253
  270.6 3.5 %all-to-all-start.16 = ((bf16[16,8,1024]{2,1,0:T(8,128)(2,1)}), bf16[16,8,1024]{2,1,0:T(8,128)(2,1)S(1)}, u32[]{:S(2)}, u32[]{:S(2)}) async-start(bf16[16,8,1024]{2,1,0:T(8,128)(2,1)} %broadcast_in_dim.253), calls=%async_computation.16 | async-start | bytes 524288 | tf_op jit(solution)/shard_map/all_to_all | solution.py:43
  274.2 1.0 dynamic-slice_bitcast_fusion.11
  275.2 7.6 %all-to-all-done.16 = bf16[16,8,1024]{2,1,0:T(8,128)(2,1)S(1)} async-done(((bf16[16,8,1024]{2,1,0:T(8,128)(2,1)}), bf16[16,8,1024]{2,1,0:T(8,128)(2,1)S(1)}, u32[]{:S(2)}, u32[]{:S(2)}) %all-to-all-start.16) | async-done | bytes 262176 | tf_op jit(solution)/shard_map/all_to_all | solution.py:43
  282.9 1.0 dynamic-slice_bitcast_fusion.9
  284.0 1.0 dynamic-slice_bitcast_fusion.7
  285.0 1.0 dynamic-slice_bitcast_fusion.5
  286.1 1.0 dynamic-slice_bitcast_fusion.3
  287.1 1.0 dynamic-slice_bitcast_fusion.1
  288.2 0.9 fusion.173
  289.9 1.2 copy.71
  (148 shorter events, 20.0 us)
Async XLA Ops:
  6.5 210.1 %copy-start = (bf16[16,8,4,512]{3,2,1,0:T(4,128)(2,1)S(1)}, bf16[16,8,4,512]{3,2,1,0:T(4,128)(2,1)}, u32[]{:S(2)}) copy-start(bf16[16,8,4,512]{3,2,1,0:T(4,128)(2,1)} %param.13) | copy-start | bytes 1572868
  6.5 6.6 %copy-start.8 = (bf16[4,256,512]{2,1,0:T(8,128)(2,1)S(1)}, bf16[4,256,512]{2,1,0:T(8,128)(2,1)}, u32[]{:S(2)}) copy-start(bf16[4,256,512]{2,1,0:T(8,128)(2,1)} %param.8) | copy-start | bytes 3145732
  6.5 46.5 %all-gather.12.cloned.1.call-start = ((), (), s32[]{:S(2)}) async-start(), calls=%async_computation.18 | async-start | bytes 4718592 | tf_op jit(solution)/shard_map/all_gather | solution.py:92
  9.9 69.2 %all-gather.16.cloned.1.call-start = ((), (), s32[]{:S(2)}) async-start(), calls=%async_computation.20 | async-start | bytes 4718592 | tf_op jit(solution)/shard_map/all_gather | solution.py:93
  11.8 2.8 collective-permute-start
  15.2 5.4 %collective-permute-start.1 = (bf16[128,512]{0,1:T(8,128)(2,1)S(1)}, bf16[128,512]{0,1:T(8,128)(2,1)S(1)}, u32[]{:S(2)}, u32[]{:S(2)}) collective-permute-start(bf16[128,512]{0,1:T(8,128)(2,1)S(1)} %get-tuple-element.27), channel_id=1, source_target_pairs={{0,32},{16,48},{1,33},{17,49},{2,34},{18,50},{3,35},{19,51},{4,36}... | collective-permute-start | bytes 393224 | tf_op jit(solution)/shard_map/ppermute | solution.py:111
  16.8 6.2 %collective-permute-start.2 = (bf16[128,512]{0,1:T(8,128)(2,1)S(1)}, bf16[128,512]{0,1:T(8,128)(2,1)S(1)}, u32[]{:S(2)}, u32[]{:S(2)}) collective-permute-start(bf16[128,512]{0,1:T(8,128)(2,1)S(1)} %get-tuple-element.29), channel_id=1, source_target_pairs={{0,64},{16,80},{1,65},{17,81},{2,66},{18,82},{3,67},{19,83},{4,68}... | collective-permute-start | bytes 393224 | tf_op jit(solution)/shard_map/ppermute | solution.py:111
  19.0 4.0 %collective-permute-start.3 = (bf16[128,512]{0,1:T(8,128)(2,1)S(1)}, bf16[128,512]{0,1:T(8,128)(2,1)S(1)}, u32[]{:S(2)}, u32[]{:S(2)}) collective-permute-start(bf16[128,512]{0,1:T(8,128)(2,1)S(1)} %get-tuple-element.28), channel_id=1, source_target_pairs={{0,96},{16,112},{1,97},{17,113},{2,98},{18,114},{3,99},{19,115},{4... | collective-permute-start | bytes 393224 | tf_op jit(solution)/shard_map/ppermute | solution.py:111
  53.1 7.2 %copy-start.1 = (bf16[16,8,512]{2,1,0:T(8,128)(2,1)}, bf16[16,8,512]{2,1,0:T(8,128)(2,1)S(1)}, u32[]{:S(2)}) copy-start(bf16[16,8,512]{2,1,0:T(8,128)(2,1)S(1)} %all_to_all.86) | copy-start | bytes 393220
  56.7 11.7 %all-to-all-start.2 = ((bf16[16,8,640]{2,1,0:T(8,128)(2,1)}), bf16[16,8,640]{2,1,0:T(8,128)(2,1)S(1)}, u32[]{:S(2)}, u32[]{:S(2)}) async-start(bf16[16,8,640]{2,1,0:T(8,128)(2,1)} %maximum_bitcast_fusion.8), calls=%async_computation.2 | async-start | bytes 327680 | tf_op jit(solution)/shard_map/all_to_all | solution.py:36
  60.2 203.6 %all-gather.10.cloned.1.call-start = ((), (), s32[]{:S(2)}) async-start(), calls=%async_computation.17 | async-start | bytes 1179648 | tf_op jit(solution)/shard_map/all_gather | solution.py:130
  69.3 11.5 %all-to-all-start.3 = ((bf16[16,8,512]{2,1,0:T(8,128)(2,1)}), bf16[16,8,512]{2,1,0:T(8,128)(2,1)S(1)}, u32[]{:S(2)}, u32[]{:S(2)}) async-start(bf16[16,8,512]{2,1,0:T(8,128)(2,1)} %broadcast_in_dim.234), calls=%async_computation.3 | async-start | bytes 262144 | tf_op jit(solution)/shard_map/all_to_all | solution.py:43
  80.8 8.9 %copy-start.2 = (bf16[16,8,512]{2,1,0:T(8,128)(2,1)}, bf16[16,8,512]{2,1,0:T(8,128)(2,1)S(1)}, u32[]{:S(2)}) copy-start(bf16[16,8,512]{2,1,0:T(8,128)(2,1)S(1)} %all-to-all-done.3) | copy-start | bytes 393220
  84.4 13.4 %all-to-all-start.4 = ((bf16[16,8,640]{2,1,0:T(8,128)(2,1)}), bf16[16,8,640]{2,1,0:T(8,128)(2,1)S(1)}, u32[]{:S(2)}, u32[]{:S(2)}) async-start(bf16[16,8,640]{2,1,0:T(8,128)(2,1)} %maximum_bitcast_fusion.9), calls=%async_computation.4 | async-start | bytes 327680 | tf_op jit(solution)/shard_map/all_to_all | solution.py:36
  89.7 184.5 %all-gather.14.cloned.1.call-start = ((), (), s32[]{:S(2)}) async-start(), calls=%async_computation.19 | async-start | bytes 1179648 | tf_op jit(solution)/shard_map/all_gather | solution.py:130
  98.2 44.9 %copy-start.10 = (s32[8,8,1]{1,2,0:T(1,128)S(1)}, s32[8,8,1]{1,2,0:T(1,128)}, u32[]{:S(2)}) copy-start(s32[8,8,1]{1,2,0:T(1,128)} %param.12) | copy-start | bytes 772
  109.2 7.2 %copy-start.3 = (bf16[16,8,512]{2,1,0:T(8,128)(2,1)}, bf16[16,8,512]{2,1,0:T(8,128)(2,1)S(1)}, u32[]{:S(2)}) copy-start(bf16[16,8,512]{2,1,0:T(8,128)(2,1)S(1)} %all_to_all.87) | copy-start | bytes 393220
  112.9 11.7 %all-to-all-start.6 = ((bf16[16,8,640]{2,1,0:T(8,128)(2,1)}), bf16[16,8,640]{2,1,0:T(8,128)(2,1)S(1)}, u32[]{:S(2)}, u32[]{:S(2)}) async-start(bf16[16,8,640]{2,1,0:T(8,128)(2,1)} %maximum_bitcast_fusion.10), calls=%async_computation.6 | async-start | bytes 327680 | tf_op jit(solution)/shard_map/all_to_all | solution.py:36
  116.4 166.5 %all-gather.18.cloned.1.call-start = ((), (), s32[]{:S(2)}) async-start(), calls=%async_computation.21 | async-start | bytes 1179648 | tf_op jit(solution)/shard_map/all_gather | solution.py:130
  135.9 7.5 %copy-start.4 = (bf16[16,8,512]{2,1,0:T(8,128)(2,1)}, bf16[16,8,512]{2,1,0:T(8,128)(2,1)S(1)}, u32[]{:S(2)}) copy-start(bf16[16,8,512]{2,1,0:T(8,128)(2,1)S(1)} %all_to_all.88) | copy-start | bytes 393220
  135.9 69.9 %copy-start.9 = (bf16[16,8,512]{2,1,0:T(8,128)(2,1)S(1)}, bf16[16,8,512]{2,1,0:T(8,128)(2,1)}, u32[]{:S(2)}) copy-start(bf16[16,8,512]{2,1,0:T(8,128)(2,1)} %param.14) | copy-start | bytes 393220
  139.5 11.7 %all-to-all-start.8 = ((bf16[16,8,640]{2,1,0:T(8,128)(2,1)}), bf16[16,8,640]{2,1,0:T(8,128)(2,1)S(1)}, u32[]{:S(2)}, u32[]{:S(2)}) async-start(bf16[16,8,640]{2,1,0:T(8,128)(2,1)} %maximum_bitcast_fusion.11), calls=%async_computation.8 | async-start | bytes 327680 | tf_op jit(solution)/shard_map/all_to_all | solution.py:36
  143.0 140.9 %all-gather.20.cloned.1.call-start = ((), (), s32[]{:S(2)}) async-start(), calls=%async_computation.22 | async-start | bytes 1179648 | tf_op jit(solution)/shard_map/all_gather | solution.py:130
  152.1 11.5 %all-to-all-start.9 = ((bf16[16,8,512]{2,1,0:T(8,128)(2,1)}), bf16[16,8,512]{2,1,0:T(8,128)(2,1)S(1)}, u32[]{:S(2)}, u32[]{:S(2)}) async-start(bf16[16,8,512]{2,1,0:T(8,128)(2,1)} %broadcast_in_dim.243), calls=%async_computation.9 | async-start | bytes 262144 | tf_op jit(solution)/shard_map/all_to_all | solution.py:43
  163.6 7.2 %copy-start.5 = (bf16[16,8,512]{2,1,0:T(8,128)(2,1)}, bf16[16,8,512]{2,1,0:T(8,128)(2,1)S(1)}, u32[]{:S(2)}) copy-start(bf16[16,8,512]{2,1,0:T(8,128)(2,1)S(1)} %all-to-all-done.9) | copy-start | bytes 393220
  167.2 11.7 %all-to-all-start.10 = ((bf16[16,8,640]{2,1,0:T(8,128)(2,1)}), bf16[16,8,640]{2,1,0:T(8,128)(2,1)S(1)}, u32[]{:S(2)}, u32[]{:S(2)}) async-start(bf16[16,8,640]{2,1,0:T(8,128)(2,1)} %maximum_bitcast_fusion.12), calls=%async_computation.10 | async-start | bytes 327680 | tf_op jit(solution)/shard_map/all_to_all | solution.py:36
  170.8 65.3 %copy-start.11 = (s32[16,8]{0,1:T(8,128)S(1)}, s32[16,8]{0,1:T(8,128)}, u32[]{:S(2)}) copy-start(s32[16,8]{0,1:T(8,128)} %param.15) | copy-start | bytes 1540
  170.8 114.2 %all-gather.22.cloned.1.call-start = ((), (), s32[]{:S(2)}) async-start(), calls=%async_computation.23 | async-start | bytes 1179648 | tf_op jit(solution)/shard_map/all_gather | solution.py:130
  179.9 25.9 %all-to-all-start.11 = ((bf16[16,8,512]{2,1,0:T(8,128)(2,1)}), bf16[16,8,512]{2,1,0:T(8,128)(2,1)S(1)}, u32[]{:S(2)}, u32[]{:S(2)}) async-start(bf16[16,8,512]{2,1,0:T(8,128)(2,1)} %broadcast_in_dim.246), calls=%async_computation.11 | async-start | bytes 262144 | tf_op jit(solution)/shard_map/all_to_all | solution.py:43
  205.8 22.0 %copy-start.6 = (bf16[16,8,512]{2,1,0:T(8,128)(2,1)}, bf16[16,8,512]{2,1,0:T(8,128)(2,1)S(1)}, u32[]{:S(2)}) copy-start(bf16[16,8,512]{2,1,0:T(8,128)(2,1)S(1)} %all-to-all-done.11) | copy-start | bytes 393220
  209.5 18.4 %all-to-all-start.12 = ((bf16[16,8,640]{2,1,0:T(8,128)(2,1)}), bf16[16,8,640]{2,1,0:T(8,128)(2,1)S(1)}, u32[]{:S(2)}, u32[]{:S(2)}) async-start(bf16[16,8,640]{2,1,0:T(8,128)(2,1)} %maximum_bitcast_fusion.13), calls=%async_computation.12 | async-start | bytes 327680 | tf_op jit(solution)/shard_map/all_to_all | solution.py:36
  216.6 69.4 %all-gather.24.cloned.1.call-start = ((), (), s32[]{:S(2)}) async-start(), calls=%async_computation.24 | async-start | bytes 1179648 | tf_op jit(solution)/shard_map/all_gather | solution.py:130
  228.9 15.2 %all-to-all-start.13 = ((bf16[16,8,512]{2,1,0:T(8,128)(2,1)}), bf16[16,8,512]{2,1,0:T(8,128)(2,1)S(1)}, u32[]{:S(2)}, u32[]{:S(2)}) async-start(bf16[16,8,512]{2,1,0:T(8,128)(2,1)} %broadcast_in_dim.249), calls=%async_computation.13 | async-start | bytes 262144 | tf_op jit(solution)/shard_map/all_to_all | solution.py:43
  244.1 7.3 %copy-start.7 = (bf16[16,8,512]{2,1,0:T(8,128)(2,1)}, bf16[16,8,512]{2,1,0:T(8,128)(2,1)S(1)}, u32[]{:S(2)}) copy-start(bf16[16,8,512]{2,1,0:T(8,128)(2,1)S(1)} %all-to-all-done.13) | copy-start | bytes 393220
  247.7 11.7 %all-to-all-start.14 = ((bf16[16,8,640]{2,1,0:T(8,128)(2,1)}), bf16[16,8,640]{2,1,0:T(8,128)(2,1)S(1)}, u32[]{:S(2)}, u32[]{:S(2)}) async-start(bf16[16,8,640]{2,1,0:T(8,128)(2,1)} %maximum_bitcast_fusion.14), calls=%async_computation.14 | async-start | bytes 327680 | tf_op jit(solution)/shard_map/all_to_all | solution.py:36
  251.2 35.9 %all-gather.26.cloned.1.call-start = ((), (), s32[]{:S(2)}) async-start(), calls=%async_computation.25 | async-start | bytes 1179648 | tf_op jit(solution)/shard_map/all_gather | solution.py:130
  260.3 9.6 %all-to-all-start.15 = ((bf16[8,8,512]{2,1,0:T(8,128)(2,1)}), bf16[8,8,512]{2,1,0:T(8,128)(2,1)S(1)}, u32[]{:S(2)}, u32[]{:S(2)}) async-start(bf16[8,8,512]{2,1,0:T(8,128)(2,1)} %broadcast_in_dim.252), calls=%async_computation.15 | async-start | bytes 131072 | tf_op jit(solution)/shard_map/all_to_all | solution.py:43
  270.6 12.2 %all-to-all-start.16 = ((bf16[16,8,1024]{2,1,0:T(8,128)(2,1)}), bf16[16,8,1024]{2,1,0:T(8,128)(2,1)S(1)}, u32[]{:S(2)}, u32[]{:S(2)}) async-start(bf16[16,8,1024]{2,1,0:T(8,128)(2,1)} %broadcast_in_dim.253), calls=%async_computation.16 | async-start | bytes 524288 | tf_op jit(solution)/shard_map/all_to_all | solution.py:43
Sparse Core Ops, SparseCore 0:
  10.0 34.5 all-gather.11
  46.3 32.7 all-gather.15
  80.8 23.2 all-gather.9
  105.7 23.1 all-gather.13
  130.5 23.1 all-gather.17
  155.3 23.1 all-gather.19
  180.3 23.1 all-gather.21
  228.0 24.0 all-gather.23
  253.8 24.7 all-gather.25

commit v2 on v1

v2 whole, which is shorter than its diff:
```python
import functools

import jax
import jax.numpy as jnp
from jax import lax
from jax.experimental import pallas as pl
from jax.experimental.pallas import tpu as pltpu
from jax.sharding import PartitionSpec as P

PAGE = 128
LANES = 128

eps_norm = 1e-06
score_scale = 192.0 ** (-0.5)


def dot(a, b):
    return jnp.dot(a, b, preferred_element_type=jnp.float32)


def dot_t(a, b):
    return lax.dot_general(a, b, (((1,), (1,)), ((), ())), preferred_element_type=jnp.float32)


def square_columns(state):
    values = state.astype(jnp.float32)
    squares = jnp.sum(values * values, axis=1, keepdims=True)
    high = squares.astype(jnp.bfloat16)
    low = (squares - high.astype(jnp.float32)).astype(jnp.bfloat16)
    column = lax.broadcasted_iota(jnp.int32, (state.shape[0], LANES), 1)
    return jnp.where(column == 0, high, jnp.where(column == 1, low, jnp.zeros_like(low)))


def scatter_sum(parts, axis):
    size = lax.axis_size(axis)
    rows = parts.shape[0] // size
    sent = parts.reshape(size, rows, parts.shape[1])
    received = lax.all_to_all(sent, axis, 0, 0, tiled=True)
    return jnp.sum(received.astype(jnp.float32), axis=0)


def gathered(block, axis):
    size = lax.axis_size(axis)
    sent = jnp.broadcast_to(block[None], (size,) + block.shape)
    return lax.all_to_all(sent, axis, 0, 0, tiled=True)


def silu(latent):
    return jax.nn.silu(latent.astype(jnp.float32)).astype(jnp.bfloat16)


def core_swap(x):
    length = lax.axis_size("segment")
    return lax.ppermute(x, "segment", [(i, i ^ 1) for i in range(length)])


def along_x(x):
    length = lax.axis_size("segment")
    groups = [list(range(core, length, 2)) for core in range(2)]
    return lax.all_gather(x, "segment", axis=0, axis_index_groups=groups)


def decode_kernel(slots, q_ref, new_ref, limit_ref, first_ref, second_ref, *rest):
    out_ref = rest[-1]
    requests, _, heads, lat = q_ref.shape
    rows = requests * heads
    q = q_ref[...].reshape(rows, lat)
    row = lax.broadcasted_iota(jnp.int32, (rows, requests), 0)
    start = lax.broadcasted_iota(jnp.int32, (rows, requests), 1) * heads
    pick = jnp.where((row >= start) & (row < start + heads), 1.0, 0.0).astype(jnp.bfloat16)
    own = dot(pick, new_ref[...].reshape(requests, lat))
    keys = jnp.concatenate([first_ref[0], second_ref[0]], axis=0)
    scores = dot_t(q, keys) * score_scale
    place = lax.broadcasted_iota(jnp.int32, scores.shape, 1)
    scores = jnp.where(place < limit_ref[0], scores, -jnp.inf)
    own_score = jnp.sum(q.astype(jnp.float32) * own, axis=1, keepdims=True) * score_scale
    top = jnp.maximum(jnp.max(scores, axis=1, keepdims=True), own_score)
    weights = jnp.exp(scores - top)
    own_weight = jnp.exp(own_score - top)
    total = jnp.sum(weights, axis=1, keepdims=True) + own_weight
    numer = dot(weights.astype(jnp.bfloat16), keys) + own_weight * own
    out_ref[...] = (numer / total).astype(jnp.bfloat16).reshape(out_ref.shape)


def decode_pair(layer, slots, queries, new, limit, pages, carried, in_order):
    requests, _, heads, lat = queries.shape

    def page(which):
        if in_order:
            return pl.BlockSpec((1, PAGE, lat), lambda i, s: (which, 0, i))
        return pl.BlockSpec((1, PAGE, lat), lambda i, s: (s[2 * (layer + i) + which], 0, i))

    in_specs = [
        pl.BlockSpec((requests, 1, heads, lat), lambda i, s: (0, layer + i, 0, 0)),
        pl.BlockSpec((1, requests, lat), lambda i, s: (layer + i, 0, 0)),
        pl.BlockSpec((1, requests * heads, 1), lambda i, s: (layer + i, 0, 0)),
        page(0),
        page(1),
    ]
    operands = [slots, queries, new, limit, pages, pages]
    aliases = {}
    if carried is not None:
        in_specs.append(pl.BlockSpec(memory_space=pl.ANY))
        aliases = {len(operands): 0}
        operands.append(carried)
    return pl.pallas_call(
        decode_kernel,
        grid_spec=pltpu.PrefetchScalarGridSpec(
            num_scalar_prefetch=1,
            grid=(2,),
            in_specs=in_specs,
            out_specs=pl.BlockSpec((requests, 1, heads, lat), lambda i, s: (0, layer + i, 0, 0)),
        ),
        out_shape=jax.ShapeDtypeStruct(queries.shape, jnp.bfloat16),
        input_output_aliases=aliases,
        compiler_params=pltpu.CompilerParams(vmem_limit_bytes=16 * 1024 * 1024),
        cost_estimate=pl.CostEstimate(
            flops=2 * 4 * requests * heads * 2 * PAGE * lat,
            bytes_accessed=2 * 2 * (2 * requests * heads + 2 * PAGE) * lat,
            transcendentals=2 * requests * heads * 2 * PAGE,
        ),
    )(*operands)


def shards(
    prompt_states, norm_gain, w_latent, w_back, page_lists, queries, new_latent, context_lengths
):
    segments = lax.axis_size("segment")
    wide_size = lax.axis_size("wide")
    position = lax.axis_index("segment")
    core = position & 1
    batches, tok_rows, local_width = prompt_states.shape
    width = local_width * wide_size
    tokens = batches * tok_rows
    mine = tokens // segments
    layers = segments
    lat = w_latent.shape[2]

    gained = (
        w_latent[0].astype(jnp.float32) * norm_gain[0].astype(jnp.float32)[:, None]
    ).astype(jnp.bfloat16)
    back = w_back[0]

    first = along_x(jnp.where(core == 0, back, gained))
    second = along_x(jnp.where(core == 0, gained, back))
    first_swapped = core_swap(first)
    second_swapped = core_swap(second)

    def latent_weight(layer):
        a, b = (second, second_swapped) if layer % 2 == 0 else (first_swapped, first)
        return jnp.where(core == 0, a[layer // 2], b[layer // 2])

    def back_weight(layer):
        a, b = (first, first_swapped) if layer % 2 == 0 else (second_swapped, second)
        return jnp.where(core == 0, a[layer // 2], b[layer // 2])

    states = prompt_states.reshape(tokens, local_width)
    state = lax.dynamic_slice_in_dim(states, position * mine, mine, 0)
    lent = lax.ppermute(
        jnp.where(position == 0, gained, back),
        "segment",
        [(i, i + 1) for i in range(0, segments, 2)],
    )
    home_weight = jnp.where(position == 0, gained, lent)
    by_core = states.reshape(segments // 2, 2, mine, local_width)
    turn = lax.dynamic_index_in_dim(by_core, core, 1, keepdims=False)
    home = dot(turn.reshape(tokens // 2, local_width), home_weight).astype(jnp.bfloat16)
    home = home.reshape(segments // 2, mine, lat)
    product = jnp.where(position < 2, home[0], jnp.zeros_like(home[0]))
    for hop in range(1, segments // 2):
        product = product + lax.ppermute(
            home[hop], "segment", [(0, 2 * hop), (1, 2 * hop + 1)]
        )

    cross = jnp.where(core == 0, dot_t(back, back), dot(lent, gained)).astype(jnp.bfloat16)
    share = lat // wide_size // (mine // wide_size)
    cross = cross.reshape(wide_size, share, mine // wide_size, lat)
    cross = [cross[:, part].reshape(mine, lat) for part in range(share)]

    def normed(total, squares):
        return (total * lax.rsqrt(squares / width + eps_norm)).astype(jnp.bfloat16)

    summed = scatter_sum(jnp.concatenate([product, square_columns(state)] + cross, axis=1), "wide")
    squares = summed[:, lat : lat + 1] + summed[:, lat + 1 : lat + 2]
    latent = normed(summed[:, :lat], squares)
    block = jnp.concatenate([latent, summed[:, lat + LANES :].astype(jnp.bfloat16)], axis=1)
    got = gathered(block, "wide")
    whole0 = got[:, :, :lat].reshape(mine, lat)
    cross = got[:, :, lat:].reshape(wide_size, mine // wide_size, share, lat)
    cross = along_x(cross.transpose(0, 2, 1, 3).reshape(lat, lat))
    cross_swapped = core_swap(cross)
    state = (state.astype(jnp.float32) + dot(silu(whole0), back_weight(0))).astype(jnp.bfloat16)

    product = dot(state, latent_weight(1)).astype(jnp.bfloat16)
    summed = scatter_sum(jnp.concatenate([product, square_columns(state)], axis=1), "wide")
    squares = summed[:, lat : lat + 1] + summed[:, lat + 1 : lat + 2]
    latent = normed(summed[:, :lat], squares)
    whole1 = gathered(latent, "wide").reshape(mine, lat)
    state = (state.astype(jnp.float32) + dot(silu(whole1), back_weight(1))).astype(jnp.bfloat16)
    pages = [lax.all_gather(jnp.concatenate([whole0, whole1], axis=1), "segment", axis=0)]

    for pair in range(1, layers // 2):
        even, odd = 2 * pair, 2 * pair + 1
        back_even = back_weight(even)
        mixing = jnp.where(core == 0, cross_swapped[pair], cross[pair])
        gram = jnp.where(core == 0, cross[pair], cross_swapped[pair])
        parts = [
            dot(state, latent_weight(even)).astype(jnp.bfloat16),
            dot(state, latent_weight(odd)).astype(jnp.bfloat16),
            dot_t(state, back_even).astype(jnp.bfloat16),
            square_columns(state),
        ]
        summed = scatter_sum(jnp.concatenate(parts, axis=1), "wide")
        squares = summed[:, 3 * lat : 3 * lat + 1] + summed[:, 3 * lat + 1 : 3 * lat + 2]
        latent_even = normed(summed[:, :lat], squares)
        activated = silu(latent_even)
        values = activated.astype(jnp.float32)
        towards = 2.0 * summed[:, 2 * lat : 3 * lat] + dot(activated, gram)
        squares = squares + jnp.sum(values * towards, axis=1, keepdims=True)
        latent_odd = normed(summed[:, lat : 2 * lat] + dot(activated, mixing), squares)
        latent = jnp.concatenate([latent_even, latent_odd], axis=1)
        if odd < layers - 1:
            whole = gathered(latent, "wide").reshape(mine, 2 * lat)
            activated = silu(whole)
            update = dot(activated[:, :lat], back_even) + dot(activated[:, lat:], back_weight(odd))
            state = (state.astype(jnp.float32) + update).astype(jnp.bfloat16)
            pages.append(lax.all_gather(whole, "segment", axis=0))

    targets = page_lists[:, :, 0]
    owned = targets == position
    counts = jnp.sum(owned.astype(jnp.int32), axis=1)
    none = targets.shape[1]
    order = jnp.arange(none, dtype=jnp.int32)[None, :]
    slot0 = jnp.min(jnp.where(owned, order, none), axis=1)
    slot1 = jnp.min(jnp.where(owned & (order > slot0[:, None]), order, none), axis=1)
    slots = jnp.minimum(jnp.stack([slot0, slot1], axis=1), none - 1)
    limit = jnp.minimum(context_lengths, counts[None, :] * PAGE)
    limit = jnp.repeat(limit.T, queries.shape[2], axis=1)[:, :, None]
    new = new_latent.transpose(1, 0, 2)

    flat_slots = slots.reshape(-1)
    out = None
    for pair, held in enumerate(pages):
        out = decode_pair(2 * pair, flat_slots, queries, new, limit, held, out, False)

    spread = gathered(latent, "segment")
    chosen = [
        lax.dynamic_index_in_dim(spread, slots[layers - 2 + i, which], 0, keepdims=False)[
            :, i * lat : (i + 1) * lat
        ]
        for which in range(2)
        for i in range(2)
    ]
    ends = gathered(jnp.concatenate(chosen, axis=1), "wide").reshape(mine, 4 * lat)
    ends = jnp.stack([ends[:, : 2 * lat], ends[:, 2 * lat :]])
    return decode_pair(layers - 2, flat_slots, queries, new, limit, ends, out, True)


def solution(mesh):
    in_specs = (
        P(None, None, "wide"),
        P("segment", "wide"),
        P("segment", "wide", None),
        P("segment", None, "wide"),
        P(),
        P("segment", None, "wide", None),
        P("segment", None, None),
        P("segment", None),
    )
    out_specs = P("segment", None, "wide", None)
    return jax.shard_map(shards, mesh=mesh, in_specs=in_specs, out_specs=out_specs, check_vma=False)
```

time: 300 us -> 263 us (0.88)
  blocking collectives: 51.5 us -> 107 us
  waiting for transfers between devices: 89.2 us -> 45.4 us
  starting transfers between devices: 61.5 us -> 25.2 us
  between operations: 45.4 us -> 21.5 us
  matrix products: 21.4 us -> 34 us
  Pallas kernels: 0 us -> 9.41 us
  local copies, waits for them, and re-layouts: 15 us -> 10 us
  other arithmetic: 13.7 us -> 8.87 us
    all_to_all x1 -> x4, blocking collectives: 18.4 us -> 67 us  [scatter_sum(): received = lax.all_to_all(sent, axis, 0, 0, tiled=True)]
    all_to_all x7 -> x1, waiting for transfers between devices: 44.8 us -> 9.22 us  [scatter_sum(): received = lax.all_to_all(sent, axis, 0, 0, tiled=True)]
    all_to_all x7 -> x1, starting transfers between devices: 30 us -> 3.56 us  [scatter_sum(): received = lax.all_to_all(sent, axis, 0, 0, tiled=True)]
    all_to_all x6 -> x3, waiting for transfers between devices: 30.2 us -> 11.5 us  [gathered(): return lax.all_to_all(sent, axis, 0, 0, tiled=True)]
    all_to_all x6 -> x3, starting transfers between devices: 24.8 us -> 10.5 us  [gathered(): return lax.all_to_all(sent, axis, 0, 0, tiled=True)]
    all_gather x2 -> x4, waiting for transfers between devices: 6.23 us -> 16.2 us  [the longest x3 16.2 us: along_x(): return lax.all_gather(x, 'segment', axis=0, axis_index_groups=groups)]
    dot_general x15 -> x21, matrix products: 19.4 us -> 29.3 us  [dot(): return jnp.dot(a, b, preferred_element_type=jnp.float32)]
    pallas_call x0 -> x4, Pallas kernels: none -> 9.41 us  [decode_pair(): pl.pallas_call(decode_kernel, grid_spec=pltpu.PrefetchScalarGridSpec(num_...]
  transfers between devices with their start and end apart: 26 -> 17, of which waited for: 15 -> 6; matrix products, arithmetic and copies ran while one was open for 14% -> 17% of each run, Pallas kernels for 0% -> 2%
where the time goes in v2:
time: 263 us; the launch traced here: 261 us
  blocking collectives  107 us (41%)
  waiting for transfers between devices  45.4 us (17%)
  matrix products  34 us (13%)
  starting transfers between devices  25.2 us (10%)
  between operations  21.5 us (8%)
  local copies, waits for them, and re-layouts  10 us (4%)
  Pallas kernels  9.41 us (4%)
  other arithmetic  8.87 us (3%)
    all_to_all x4, blocking collectives, scatter_sum(): received = lax.all_to_all(sent, axis, 0, 0, tiled=True)  67 us
    all_to_all x3, blocking collectives, gathered(): return lax.all_to_all(sent, axis, 0, 0, tiled=True)  39.8 us
    dot_general x21, matrix products, dot(): return jnp.dot(a, b, preferred_element_type=jnp.float32)  29.3 us
    all_gather x3, waiting for transfers between devices, along_x(): return lax.all_gather(x, 'segment', axis=0, axis_index_groups=groups)  16.2 us
    all_to_all x3, waiting for transfers between devices, gathered(): return lax.all_to_all(sent, axis, 0, 0, tiled=True)  11.5 us
    all_to_all x3, starting transfers between devices, gathered(): return lax.all_to_all(sent, axis, 0, 0, tiled=True)  10.5 us
    pallas_call x4, Pallas kernels, decode_pair(): pl.pallas_call(decode_kernel, grid_spec=pltpu.PrefetchScalarGridSpec(num_...  9.41 us
    all_to_all x1, waiting for transfers between devices, scatter_sum(): received = lax.all_to_all(sent, axis, 0, 0, tiled=True)  9.22 us
  transfers between devices with their start and end apart: 17, of which 6 were waited for; matrix products, arithmetic and copies ran while one was open for 17% of the time, Pallas kernels for 2%

profile of v2, /device:TPU:0, one launch (start us, length us, event | category | flops | bytes accessed | tf_op | source)
XLA Modules:
  0.0 261.3 jit_solution(15722894650983571319)
XLA Ops:
  6.5 0.8 convert_element_type.416
  7.3 2.5 broadcast_select_fusion.3
  10.0 0.2 bitcast_select_fusion
  10.2 2.1 collective-permute-start
  12.7 0.5 fusion.58
  13.2 0.6 convolution_convert_fusion
  13.8 6.2 %collective-permute-start.3 = (bf16[128,512]{1,0:T(8,128)(2,1)S(1)}, bf16[128,512]{1,0:T(8,128)(2,1)S(1)}, u32[]{:S(2)}, u32[]{:S(2)}) collective-permute-start(bf16[128,512]{1,0:T(8,128)(2,1)S(1)} %get-tuple-element.16), channel_id=1, source_target_pairs={{0,96},{16,112},{1,97},{17,113},{2,98},{18,114},{3,99},{19,115},{4... | collective-permute-start | bytes 393224 | tf_op jit(solution)/shard_map/ppermute | solution.py:171
  20.0 1.3 collective-permute-start.2
  21.3 1.3 collective-permute-start.1
  22.6 1.6 fusion
  24.3 3.3 %collective-permute-done.2 = bf16[128,512]{1,0:T(8,128)(2,1)S(1)} collective-permute-done((bf16[128,512]{1,0:T(8,128)(2,1)S(1)}, bf16[128,512]{1,0:T(8,128)(2,1)S(1)}, u32[]{:S(2)}, u32[]{:S(2)}) %collective-permute-start.2) | collective-permute-done | bytes 131104 | tf_op jit(solution)/shard_map/ppermute | solution.py:171
  27.6 5.1 %collective-permute-done.1 = bf16[128,512]{1,0:T(8,128)(2,1)S(1)} collective-permute-done((bf16[128,512]{1,0:T(8,128)(2,1)S(1)}, bf16[128,512]{1,0:T(8,128)(2,1)S(1)}, u32[]{:S(2)}, u32[]{:S(2)}) %collective-permute-start.1) | collective-permute-done | bytes 131104 | tf_op jit(solution)/shard_map/ppermute | solution.py:171
  33.0 21.5 %all_to_all.55 = bf16[16,8,2688]{2,1,0:T(8,128)(2,1)S(1)} all-to-all(bf16[16,8,2688]{2,1,0:T(8,128)(2,1)S(1)} %fusion.148), channel_id=1, replica_groups=mesh['segment'=8,'wide'=16] {'wide'}, dimensions={0} | all-to-all | bytes 1376256 | tf_op jit(solution)/shard_map/all_to_all | solution.py:38
  55.0 16.6 %all_to_all.56 = bf16[16,8,2560]{2,1,0:T(8,128)(2,1)S(1)} all-to-all(bf16[16,8,2560]{2,1,0:T(8,128)(2,1)S(1)} %broadcast_in_dim.167), channel_id=1, replica_groups=mesh['segment'=8,'wide'=16] {'wide'}, dimensions={0} | all-to-all | bytes 1310720 | tf_op jit(solution)/shard_map/all_to_all | solution.py:45
  71.6 0.8 slice.323
  72.5 6.4 %all-gather.10.cloned.1.call-done = bf16[4,512,512]{2,1,0:T(8,128)(2,1)} async-done(((bf16[1,512,512]{2,1,0:T(8,128)(2,1)}), bf16[4,512,512]{2,1,0:T(8,128)(2,1)}) %all-gather.10.cloned.1.call-update) | async-done | bytes 2097168 | tf_op jit(solution)/shard_map/all_gather | solution.py:60
  78.8 1.6 fusion.133
  80.5 1.4 convolution_convert_fusion.10
  82.0 15.1 %all_to_all.57 = bf16[16,8,640]{2,1,0:T(8,128)(2,1)S(1)} all-to-all(bf16[16,8,640]{2,1,0:T(8,128)(2,1)S(1)} %maximum_bitcast_fusion.3), channel_id=1, replica_groups=mesh['segment'=8,'wide'=16] {'wide'}, dimensions={0} | all-to-all | bytes 327680 | tf_op jit(solution)/shard_map/all_to_all | solution.py:38
  97.4 0.7 broadcast_in_dim.171
  98.0 3.5 %all-to-all-start.3 = ((bf16[16,8,512]{2,1,0:T(8,128)(2,1)}), bf16[16,8,512]{2,1,0:T(8,128)(2,1)S(1)}, u32[]{:S(2)}, u32[]{:S(2)}) async-start(bf16[16,8,512]{2,1,0:T(8,128)(2,1)} %broadcast_in_dim.171), calls=%async_computation.3 | async-start | bytes 262144 | tf_op jit(solution)/shard_map/all_to_all | solution.py:45
  101.6 9.8 %all-gather.12.cloned.1.call-done = bf16[4,512,512]{2,1,0:T(8,128)(2,1)} async-done(((bf16[1,512,512]{2,1,0:T(8,128)(2,1)}), bf16[4,512,512]{2,1,0:T(8,128)(2,1)}) %all-gather.12.cloned.1.call-update) | async-done | bytes 2097168 | tf_op jit(solution)/shard_map/all_gather | solution.py:60
  111.4 1.6 fusion.138
  113.0 0.7 pad_maximum_fusion.1
  113.8 1.5 convolution_convert_fusion.7
  115.4 1.3 convolution_convert_fusion.8
  116.7 1.4 convolution_convert_fusion.9
  118.2 17.9 %all_to_all.58 = bf16[16,8,1664]{2,1,0:T(8,128)(2,1)S(1)} all-to-all(bf16[16,8,1664]{2,1,0:T(8,128)(2,1)S(1)} %maximum_bitcast_fusion), channel_id=1, replica_groups=mesh['segment'=8,'wide'=16] {'wide'}, dimensions={0} | all-to-all | bytes 851968 | tf_op jit(solution)/shard_map/all_to_all | solution.py:38
  136.5 1.5 fusion.16
  138.3 1.4 fusion.13
  139.7 11.6 %all_to_all.59 = bf16[16,8,1024]{2,1,0:T(8,128)(2,1)S(1)} all-to-all(bf16[16,8,1024]{2,1,0:T(8,128)(2,1)S(1)} %broadcast_in_dim.175), channel_id=1, replica_groups=mesh['segment'=8,'wide'=16] {'wide'}, dimensions={0} | all-to-all | bytes 524288 | tf_op jit(solution)/shard_map/all_to_all | solution.py:45
  151.4 1.4 fusion.48
  152.8 1.4 fusion.139
  154.3 1.4 convolution_convert_fusion.4
  155.8 1.3 convolution_convert_fusion.5
  157.1 1.4 convolution_convert_fusion.6
  158.6 12.5 %all_to_all.60 = bf16[16,8,1664]{2,1,0:T(8,128)(2,1)S(1)} all-to-all(bf16[16,8,1664]{2,1,0:T(8,128)(2,1)S(1)} %maximum_bitcast_fusion.1), channel_id=1, replica_groups=mesh['segment'=8,'wide'=16] {'wide'}, dimensions={0} | all-to-all | bytes 851968 | tf_op jit(solution)/shard_map/all_to_all | solution.py:38
  171.4 1.5 fusion.17
  173.2 1.4 fusion.14
  174.7 11.6 %all_to_all.61 = bf16[16,8,1024]{2,1,0:T(8,128)(2,1)S(1)} all-to-all(bf16[16,8,1024]{2,1,0:T(8,128)(2,1)S(1)} %broadcast_in_dim.179), channel_id=1, replica_groups=mesh['segment'=8,'wide'=16] {'wide'}, dimensions={0} | all-to-all | bytes 524288 | tf_op jit(solution)/shard_map/all_to_all | solution.py:45
  186.4 1.4 fusion.40
  187.9 1.4 multiply_reduce_fusion
  189.3 1.4 convolution_convert_fusion.1
  190.7 1.3 convolution_convert_fusion.2
  192.1 1.4 convolution_convert_fusion.3
  193.6 0.8 maximum_bitcast_fusion.2
  194.4 3.6 %all-to-all-start.8 = ((bf16[16,8,1664]{2,1,0:T(8,128)(2,1)}), bf16[16,8,1664]{2,1,0:T(8,128)(2,1)S(1)}, u32[]{:S(2)}, u32[]{:S(2)}) async-start(bf16[16,8,1664]{2,1,0:T(8,128)(2,1)} %maximum_bitcast_fusion.2), calls=%async_computation.8 | async-start | bytes 851968 | tf_op jit(solution)/shard_map/all_to_all | solution.py:38
  198.2 9.2 %all-to-all-done.8 = bf16[16,8,1664]{2,1,0:T(8,128)(2,1)S(1)} async-done(((bf16[16,8,1664]{2,1,0:T(8,128)(2,1)}), bf16[16,8,1664]{2,1,0:T(8,128)(2,1)S(1)}, u32[]{:S(2)}, u32[]{:S(2)}) %all-to-all-start.8) | async-done | bytes 426016 | tf_op jit(solution)/shard_map/all_to_all | solution.py:38
  207.8 1.5 fusion.18
  209.6 1.4 fusion.15
  211.0 0.7 broadcast_in_dim.183
  211.7 3.4 %all-to-all-start.9 = ((bf16[8,8,1024]{2,1,0:T(8,128)(2,1)}), bf16[8,8,1024]{2,1,0:T(8,128)(2,1)S(1)}, u32[]{:S(2)}, u32[]{:S(2)}) async-start(bf16[8,8,1024]{2,1,0:T(8,128)(2,1)} %broadcast_in_dim.183), calls=%async_computation.9 | async-start | bytes 262144 | tf_op jit(solution)/shard_map/all_to_all | solution.py:45
  215.1 0.7 fusion.197
  223.3 0.8 broadcast_in_dim.184
  224.1 3.6 %all-to-all-start.10 = ((bf16[16,8,2048]{2,1,0:T(8,128)(2,1)}), bf16[16,8,2048]{2,1,0:T(8,128)(2,1)S(1)}, u32[]{:S(2)}, u32[]{:S(2)}) async-start(bf16[16,8,2048]{2,1,0:T(8,128)(2,1)} %broadcast_in_dim.184), calls=%async_computation.10 | async-start | bytes 1048576 | tf_op jit(solution)/shard_map/all_to_all | solution.py:45
  228.1 0.5 copy.51.limit_ref
  228.6 11.5 %all-to-all-done.10 = bf16[16,8,2048]{2,1,0:T(8,128)(2,1)S(1)} async-done(((bf16[16,8,2048]{2,1,0:T(8,128)(2,1)}), bf16[16,8,2048]{2,1,0:T(8,128)(2,1)S(1)}, u32[]{:S(2)}, u32[]{:S(2)}) %all-to-all-start.10) | async-done | bytes 524320 | tf_op jit(solution)/shard_map/all_to_all | solution.py:45
  240.2 1.6 copy-done
  241.8 2.4 shard_map.82.rest_0_
  244.2 1.6 copy-done.1
  245.8 2.4 shard_map.83.rest_0_
  248.1 1.6 copy-done.2
  249.7 2.4 shard_map.84.rest_0_
  252.1 2.3 shard_map.85
  (122 shorter events, 5.3 us)
Async XLA Ops:
  6.5 3.4 %copy-start.6 = (bf16[1,512,512]{2,1,0:T(8,128)(2,1)S(1)}, bf16[1,512,512]{2,1,0:T(8,128)(2,1)}, u32[]{:S(2)}) copy-start(bf16[1,512,512]{2,1,0:T(8,128)(2,1)} %param.11) | copy-start | bytes 1572868
  6.5 3.4 %copy-start.7 = (bf16[1,512,512]{2,1,0:T(8,128)(2,1)S(1)}, bf16[1,512,512]{2,1,0:T(8,128)(2,1)}, u32[]{:S(2)}) copy-start(bf16[1,512,512]{2,1,0:T(8,128)(2,1)} %param.10) | copy-start | bytes 1572868
  6.5 48.3 %all-gather.8.cloned.1.call-start = ((), (), s32[]{:S(2)}) async-start(), calls=%async_computation.11 | async-start | bytes 2621440 | tf_op jit(solution)/shard_map/all_gather | solution.py:60
  7.3 5.1 %copy-start.8 = (bf16[4,256,512]{2,1,0:T(8,128)(2,1)S(1)}, bf16[4,256,512]{2,1,0:T(8,128)(2,1)}, u32[]{:S(2)}) copy-start(bf16[4,256,512]{2,1,0:T(8,128)(2,1)} %param.8) | copy-start | bytes 3145732
  9.9 69.0 %all-gather.10.cloned.1.call-start = ((), (), s32[]{:S(2)}) async-start(), calls=%async_computation.12 | async-start | bytes 2621440 | tf_op jit(solution)/shard_map/all_gather | solution.py:60
  10.2 3.0 %collective-permute-start = (bf16[512,512]{1,0:T(8,128)(2,1)S(1)}, bf16[512,512]{1,0:T(8,128)(2,1)}, u32[]{:S(2)}, u32[]{:S(2)}) collective-permute-start(bf16[512,512]{1,0:T(8,128)(2,1)S(1)} %bitcast_select_fusion), channel_id=1, source_target_pairs={{0,16},{32,48},{64,80},{96,112},{1,17},{33,49},{65,81},{97,113},{2... | collective-permute-start | bytes 1572872 | tf_op jit(solution)/shard_map/ppermute | solution.py:159
  12.3 99.1 %all-gather.12.cloned.1.call-start = ((), (), s32[]{:S(2)}) async-start(), calls=%async_computation.13 | async-start | bytes 2621440 | tf_op jit(solution)/shard_map/all_gather | solution.py:60
  13.8 10.5 %collective-permute-start.3 = (bf16[128,512]{1,0:T(8,128)(2,1)S(1)}, bf16[128,512]{1,0:T(8,128)(2,1)S(1)}, u32[]{:S(2)}, u32[]{:S(2)}) collective-permute-start(bf16[128,512]{1,0:T(8,128)(2,1)S(1)} %get-tuple-element.16), channel_id=1, source_target_pairs={{0,96},{16,112},{1,97},{17,113},{2,98},{18,114},{3,99},{19,115},{4... | collective-permute-start | bytes 393224 | tf_op jit(solution)/shard_map/ppermute | solution.py:171
  20.0 7.6 %collective-permute-start.2 = (bf16[128,512]{1,0:T(8,128)(2,1)S(1)}, bf16[128,512]{1,0:T(8,128)(2,1)S(1)}, u32[]{:S(2)}, u32[]{:S(2)}) collective-permute-start(bf16[128,512]{1,0:T(8,128)(2,1)S(1)} %get-tuple-element.17), channel_id=1, source_target_pairs={{0,64},{16,80},{1,65},{17,81},{2,66},{18,82},{3,67},{19,83},{4,68}... | collective-permute-start | bytes 393224 | tf_op jit(solution)/shard_map/ppermute | solution.py:171
  21.3 11.3 %collective-permute-start.1 = (bf16[128,512]{1,0:T(8,128)(2,1)S(1)}, bf16[128,512]{1,0:T(8,128)(2,1)S(1)}, u32[]{:S(2)}, u32[]{:S(2)}) collective-permute-start(bf16[128,512]{1,0:T(8,128)(2,1)S(1)} %get-tuple-element.15), channel_id=1, source_target_pairs={{0,32},{16,48},{1,33},{17,49},{2,34},{18,50},{3,35},{19,51},{4,36}... | collective-permute-start | bytes 393224 | tf_op jit(solution)/shard_map/ppermute | solution.py:171
  54.8 24.0 %collective-permute-start.4 = (bf16[4,512,512]{2,1,0:T(8,128)(2,1)}, bf16[4,512,512]{2,1,0:T(8,128)(2,1)}, u32[]{:S(2)}, u32[]{:S(2)}) collective-permute-start(bf16[4,512,512]{2,1,0:T(8,128)(2,1)} %all-gather.8.cloned.1.call-done), channel_id=1, source_target_pairs={{0,16},{16,0},{32,48},{48,32},{64,80},{80,64},{96,112},{112,96},{1... | collective-permute-start | bytes 6291464 | tf_op jit(solution)/shard_map/ppermute | solution.py:54
  78.8 32.6 %collective-permute-start.5 = (bf16[4,512,512]{2,1,0:T(8,128)(2,1)}, bf16[4,512,512]{2,1,0:T(8,128)(2,1)}, u32[]{:S(2)}, u32[]{:S(2)}) collective-permute-start(bf16[4,512,512]{2,1,0:T(8,128)(2,1)} %all-gather.10.cloned.1.call-done), channel_id=1, source_target_pairs={{0,16},{16,0},{32,48},{48,32},{64,80},{80,64},{96,112},{112,96},{1... | collective-permute-start | bytes 6291464 | tf_op jit(solution)/shard_map/ppermute | solution.py:54
  98.0 13.4 %all-to-all-start.3 = ((bf16[16,8,512]{2,1,0:T(8,128)(2,1)}), bf16[16,8,512]{2,1,0:T(8,128)(2,1)S(1)}, u32[]{:S(2)}, u32[]{:S(2)}) async-start(bf16[16,8,512]{2,1,0:T(8,128)(2,1)} %broadcast_in_dim.171), calls=%async_computation.3 | async-start | bytes 262144 | tf_op jit(solution)/shard_map/all_to_all | solution.py:45
  101.5 138.7 %all-gather.18.cloned.1.call-start = ((), (), s32[]{:S(2)}) async-start(), calls=%async_computation.16 | async-start | bytes 2359296 | tf_op jit(solution)/shard_map/all_gather | solution.py:200
  111.4 25.1 %collective-permute-start.6 = (bf16[4,512,512]{2,1,0:T(8,128)(2,1)}, bf16[4,512,512]{2,1,0:T(8,128)(2,1)}, u32[]{:S(2)}, u32[]{:S(2)}) collective-permute-start(bf16[4,512,512]{2,1,0:T(8,128)(2,1)} %all-gather.12.cloned.1.call-done), channel_id=1, source_target_pairs={{0,16},{16,0},{32,48},{48,32},{64,80},{80,64},{96,112},{112,96},{1... | collective-permute-start | bytes 6291464 | tf_op jit(solution)/shard_map/ppermute | solution.py:54
  113.0 2.4 copy-start.12
  113.7 130.4 %all-gather.16.cloned.1.call-start = ((), (), s32[]{:S(2)}) async-start(), calls=%async_computation.15 | async-start | bytes 2359296 | tf_op jit(solution)/shard_map/all_gather | solution.py:227
  151.2 3.0 %copy-start.4 = (bf16[16,8,1024]{2,1,0:T(8,128)(2,1)}, bf16[16,8,1024]{2,1,0:T(8,128)(2,1)S(1)}, u32[]{:S(2)}) copy-start(bf16[16,8,1024]{2,1,0:T(8,128)(2,1)S(1)} %all_to_all.59) | copy-start | bytes 786436
  154.3 93.8 %all-gather.14.cloned.1.call-start = ((), (), s32[]{:S(2)}) async-start(), calls=%async_computation.14 | async-start | bytes 2359296 | tf_op jit(solution)/shard_map/all_gather | solution.py:227
  186.3 3.0 %copy-start.5 = (bf16[16,8,1024]{2,1,0:T(8,128)(2,1)}, bf16[16,8,1024]{2,1,0:T(8,128)(2,1)S(1)}, u32[]{:S(2)}) copy-start(bf16[16,8,1024]{2,1,0:T(8,128)(2,1)S(1)} %all_to_all.61) | copy-start | bytes 786436
  192.0 5.9 %copy-start.10 = (s32[8,8,1]{1,2,0:T(1,128)S(1)}, s32[8,8,1]{1,2,0:T(1,128)}, u32[]{:S(2)}) copy-start(s32[8,8,1]{1,2,0:T(1,128)} %param.12) | copy-start | bytes 772
  194.4 13.1 %all-to-all-start.8 = ((bf16[16,8,1664]{2,1,0:T(8,128)(2,1)}), bf16[16,8,1664]{2,1,0:T(8,128)(2,1)S(1)}, u32[]{:S(2)}, u32[]{:S(2)}) async-start(bf16[16,8,1664]{2,1,0:T(8,128)(2,1)} %maximum_bitcast_fusion.2), calls=%async_computation.8 | async-start | bytes 851968 | tf_op jit(solution)/shard_map/all_to_all | solution.py:38
  209.3 18.6 %copy-start.9 = (bf16[16,8,512]{2,1,0:T(8,128)(2,1)S(1)}, bf16[16,8,512]{2,1,0:T(8,128)(2,1)}, u32[]{:S(2)}) copy-start(bf16[16,8,512]{2,1,0:T(8,128)(2,1)} %param.14) | copy-start | bytes 393220
  209.6 18.3 %copy-start.11 = (s32[16,8]{0,1:T(8,128)S(1)}, s32[16,8]{0,1:T(8,128)}, u32[]{:S(2)}) copy-start(s32[16,8]{0,1:T(8,128)} %param.15) | copy-start | bytes 1540
  211.7 11.5 %all-to-all-start.9 = ((bf16[8,8,1024]{2,1,0:T(8,128)(2,1)}), bf16[8,8,1024]{2,1,0:T(8,128)(2,1)S(1)}, u32[]{:S(2)}, u32[]{:S(2)}) async-start(bf16[8,8,1024]{2,1,0:T(8,128)(2,1)} %broadcast_in_dim.183), calls=%async_computation.9 | async-start | bytes 262144 | tf_op jit(solution)/shard_map/all_to_all | solution.py:45
  223.3 16.9 %copy-start.3 = (bf16[16,8,4,512]{3,2,1,0:T(4,128)(2,1)S(1)}, bf16[16,8,4,512]{3,2,1,0:T(4,128)(2,1)}, u32[]{:S(2)}) copy-start(bf16[16,8,4,512]{3,2,1,0:T(4,128)(2,1)} %q_ref.7) | copy-start | bytes 1572868
  224.1 16.0 %all-to-all-start.10 = ((bf16[16,8,2048]{2,1,0:T(8,128)(2,1)}), bf16[16,8,2048]{2,1,0:T(8,128)(2,1)S(1)}, u32[]{:S(2)}, u32[]{:S(2)}) async-start(bf16[16,8,2048]{2,1,0:T(8,128)(2,1)} %broadcast_in_dim.184), calls=%async_computation.10 | async-start | bytes 1048576 | tf_op jit(solution)/shard_map/all_to_all | solution.py:45
  240.2 1.6 copy-start
  244.2 1.6 copy-start.1
  248.1 1.6 copy-start.2
Sparse Core Ops, SparseCore 0:
  10.0 34.3 all-gather.7
  46.1 32.7 all-gather.9
  80.5 30.8 all-gather.11
  113.9 25.4 all-gather.17
  154.4 21.2 all-gather.15
  189.4 21.2 all-gather.13

commit v3 on v2

v3 whole, which is shorter than its diff:
```python
import functools

import jax
import jax.numpy as jnp
from jax import lax
from jax.experimental import pallas as pl
from jax.experimental.pallas import tpu as pltpu
from jax.sharding import PartitionSpec as P

PAGE = 128
LANES = 128

eps_norm = 1e-06
score_scale = 192.0 ** (-0.5)

params = pltpu.CompilerParams(vmem_limit_bytes=24 * 1024 * 1024)
anywhere = pl.BlockSpec(memory_space=pl.ANY)
bf16 = jnp.bfloat16
f32 = jnp.float32


def dot(a, b):
    return jnp.dot(a, b, preferred_element_type=jnp.float32)


def dot_t(a, b):
    return lax.dot_general(a, b, (((1,), (1,)), ((), ())), preferred_element_type=jnp.float32)


def square_columns(values):
    squares = jnp.sum(values * values, axis=1, keepdims=True)
    high = squares.astype(bf16).astype(f32)
    column = lax.broadcasted_iota(jnp.int32, (values.shape[0], LANES), 1)
    return jnp.where(column == 0, high, jnp.where(column == 1, squares - high, 0.0))


def silu(latent):
    values = latent.astype(f32)
    return (values / (1.0 + jnp.exp(-values))).astype(bf16)


def exchanged(sent, axis):
    return lax.all_to_all(sent, axis, 0, 0, tiled=True)


def whole(shape):
    return pl.BlockSpec(shape, lambda i, *s: (0,) * len(shape))


def call(body, in_specs, out_specs, out_shape, operands, scalars=(), scratch=(), flops=0):
    moved = sum(o.size * 2 for o in out_shape)
    return pl.pallas_call(
        body,
        grid_spec=pltpu.PrefetchScalarGridSpec(
            num_scalar_prefetch=len(scalars),
            grid=(1,),
            in_specs=in_specs,
            out_specs=out_specs,
            scratch_shapes=scratch,
        ),
        out_shape=out_shape,
        compiler_params=params,
        cost_estimate=pl.CostEstimate(flops=flops, bytes_accessed=2 * moved, transcendentals=0),
    )(*scalars, *operands)


def weights_kernel(where, latent_ref, gain_ref, back_ref, both_ref, lent_ref):
    size = latent_ref.shape[1]
    row = lax.broadcasted_iota(jnp.int32, (size, size), 0)
    column = lax.broadcasted_iota(jnp.int32, (size, size), 1)
    gains = jnp.where(row == column, gain_ref[...].astype(f32), 0.0).astype(bf16)
    gained = dot(gains, latent_ref[0]).astype(bf16)
    both_ref[0] = gained
    both_ref[1] = back_ref[0]

    @pl.when(where[0] == 0)
    def _():
        lent_ref[...] = gained

    @pl.when(where[0] != 0)
    def _():
        lent_ref[...] = back_ref[0]


def home_kernel(where, states_ref, both_ref, lent_ref, out_ref, weight, cross):
    groups, _, rows, width = states_ref.shape
    lat = both_ref.shape[2]
    wide = out_ref.shape[0]

    @pl.when(where[0] == 0)
    def _():
        weight[...] = both_ref[0]

    @pl.when(where[0] != 0)
    def _():
        weight[...] = lent_ref[...]

    @pl.when(where[1] == 0)
    def _():
        cross[...] = dot_t(both_ref[1], both_ref[1])

    @pl.when(where[1] != 0)
    def _():
        cross[...] = dot(lent_ref[...], both_ref[0])

    share = rows // wide
    for group in range(groups):
        tokens = states_ref[group, 0]
        at = slice(group * share, (group + 1) * share)
        out_ref[:, at, :lat] = dot(tokens, weight[...]).reshape(wide, share, lat).astype(bf16)
        squares = square_columns(tokens.astype(f32))
        out_ref[:, at, lat : lat + LANES] = squares.reshape(wide, share, LANES).astype(bf16)
    out_ref[:, :, lat + LANES :] = cross[...].reshape(wide, lat // wide, lat).astype(bf16)


def home_sum_kernel(width, got_ref, latent_ref, cross_ref):
    lat = cross_ref.shape[1]
    summed = jnp.sum(got_ref[...].astype(f32), axis=0)
    squares = summed[:, lat : lat + 1] + summed[:, lat + 1 : lat + 2]
    latent = summed[:, :lat] * lax.rsqrt(squares / width + eps_norm)
    latent_ref[...] = latent.reshape(latent_ref.shape).astype(bf16)
    cross_ref[...] = summed[:, lat + LANES :].astype(bf16)


def home_send_kernel(where, mine_ref, a_ref, b_ref, c_ref, cross_ref, out_ref):
    wide = out_ref.shape[0]
    high = cross_ref.shape[0]
    taken = a_ref[...].astype(f32) + b_ref[...].astype(f32) + c_ref[...].astype(f32)
    latent = jnp.where(where[0] < 2, mine_ref[0].astype(f32), taken).astype(bf16)
    block = cross_ref[...]
    for place in range(wide):
        out_ref[place, :high] = block
        out_ref[place, high:] = latent


def advance_kernel(before, layers, first, where, got_ref, *refs):
    if first:
        states_ref, both_ref, out_ref, state_ref, held_ref, weights, sems = refs
    elif len(before) < len(layers):
        earlier_ref, states_ref, both_ref, out_ref, state_ref, held_ref, weights, sems = refs
    else:
        states_ref, both_ref, out_ref, state_ref, weights, sems = refs
    needed = [(layer, 1) for layer in before] + [(layer, 0) for layer in layers]
    if len(layers) == 2:
        needed.append((layers[0], 1))
    copies = [
        pltpu.make_async_copy(both_ref.at[layer, kind], weights.at[i], sems.at[i])
        for i, (layer, kind) in enumerate(needed)
    ]
    for copy in copies:
        copy.start()
    wide = out_ref.shape[0]
    share = out_ref.shape[1]
    rows = wide * share
    lat = weights.shape[2]
    got = got_ref[...]
    if first:
        held_ref[...] = got[:, : got.shape[1] - share]
        got = got[:, got.shape[1] - share :]
    latents = got.astype(f32).reshape(rows, got.shape[2])
    if not first and len(before) < len(layers):
        earlier = earlier_ref[:, earlier_ref.shape[1] - share :]
        held_ref[:, :lat] = earlier.astype(f32).reshape(rows, lat).astype(bf16)
        held_ref[:, lat:] = latents.astype(bf16)
    activated = silu(latents)
    state = states_ref[...].reshape(rows, lat).astype(f32)
    for i in range(len(before)):
        copies[i].wait()
        state = state + dot(activated[:, i * lat : (i + 1) * lat], weights[i])
    state = state.astype(bf16)
    state_ref[...] = state
    squares = square_columns(state.astype(f32))
    out_ref[:, :, :LANES] = squares.reshape(wide, share, LANES).astype(bf16)
    for i in range(len(before), len(needed)):
        copies[i].wait()
        product = (dot_t if needed[i][1] else dot)(state, weights[i])
        at = LANES + (i - len(before)) * lat
        out_ref[:, :, at : at + lat] = product.reshape(wide, share, lat).astype(bf16)


def single_kernel(width, got_ref, out_ref):
    summed = jnp.sum(got_ref[...].astype(f32), axis=0)
    squares = summed[:, 0:1] + summed[:, 1:2]
    latent = (summed[:, LANES:] * lax.rsqrt(squares / width + eps_norm)).astype(bf16)
    for place in range(out_ref.shape[0]):
        out_ref[place] = latent


def pair_kernel(width, even, got_ref, cross_ref, out_ref, crosses, sems):
    copies = [
        pltpu.make_async_copy(cross_ref.at[even + i], crosses.at[i], sems.at[i]) for i in range(2)
    ]
    for copy in copies:
        copy.start()
    lat = crosses.shape[2]
    summed = jnp.sum(got_ref[...].astype(f32), axis=0)
    squares = summed[:, 0:1] + summed[:, 1:2]
    at = [LANES + i * lat for i in range(4)]
    first = (summed[:, at[0] : at[1]] * lax.rsqrt(squares / width + eps_norm)).astype(bf16)
    activated = silu(first)
    copies[0].wait()
    towards = 2.0 * summed[:, at[2] : at[3]] + dot(activated, crosses[0])
    squares = squares + jnp.sum(activated.astype(f32) * towards, axis=1, keepdims=True)
    copies[1].wait()
    second = summed[:, at[1] : at[2]] + dot(activated, crosses[1])
    second = (second * lax.rsqrt(squares / width + eps_norm)).astype(bf16)
    for place in range(out_ref.shape[0]):
        out_ref[place, :, :lat] = first
        out_ref[place, :, lat:] = second


def choose_kernel(layer, slots, got_ref, out_ref):
    lat = got_ref.shape[2] // 2
    parts = []
    for i in range(2):
        for which in range(2):
            shard = got_ref[slots[2 * (layer + i) + which]]
            parts.append(shard[:, i * lat : (i + 1) * lat])
    for place in range(out_ref.shape[0]):
        for i, part in enumerate(parts):
            out_ref[place, :, i * lat : (i + 1) * lat] = part


def decode_kernel(slots, q_ref, new_ref, limit_ref, first_ref, second_ref, *rest):
    out_ref = rest[-1]
    requests, _, heads, lat = q_ref.shape
    rows = requests * heads
    q = q_ref[...].reshape(rows, lat)
    row = lax.broadcasted_iota(jnp.int32, (rows, requests), 0)
    start = lax.broadcasted_iota(jnp.int32, (rows, requests), 1) * heads
    pick = jnp.where((row >= start) & (row < start + heads), 1.0, 0.0).astype(bf16)
    own = dot(pick, new_ref[...].reshape(requests, lat))
    pages = [ref[...].astype(f32).reshape(PAGE, lat) for ref in (first_ref, second_ref)]
    keys = jnp.concatenate(pages, axis=0).astype(bf16)
    scores = dot_t(q, keys) * score_scale
    place = lax.broadcasted_iota(jnp.int32, scores.shape, 1)
    scores = jnp.where(place < limit_ref[0], scores, -jnp.inf)
    own_score = jnp.sum(q.astype(f32) * own, axis=1, keepdims=True) * score_scale
    top = jnp.maximum(jnp.max(scores, axis=1, keepdims=True), own_score)
    weights = jnp.exp(scores - top)
    own_weight = jnp.exp(own_score - top)
    total = jnp.sum(weights, axis=1, keepdims=True) + own_weight
    numer = dot(weights.astype(bf16), keys) + own_weight * own
    out_ref[...] = (numer / total).astype(bf16).reshape(out_ref.shape)


def decode_pair(layer, slots, queries, new, limit, pages, carried):
    requests, _, heads, lat = queries.shape

    def page(which):
        if pages.shape[0] * pages.shape[1] == PAGE:
            return pl.BlockSpec(pages.shape[:2] + (lat,), lambda i, s: (0, 0, 2 * i + which))
        return pl.BlockSpec((1, PAGE, lat), lambda i, s: (s[2 * (layer + i) + which], 0, i))

    in_specs = [
        pl.BlockSpec((requests, 1, heads, lat), lambda i, s: (0, layer + i, 0, 0)),
        pl.BlockSpec((1, requests, lat), lambda i, s: (layer + i, 0, 0)),
        pl.BlockSpec((1, requests * heads, 1), lambda i, s: (layer + i, 0, 0)),
        page(0),
        page(1),
    ]
    operands = [slots, queries, new, limit, pages, pages]
    aliases = {}
    if carried is not None:
        in_specs.append(anywhere)
        aliases = {len(operands): 0}
        operands.append(carried)
    return pl.pallas_call(
        decode_kernel,
        grid_spec=pltpu.PrefetchScalarGridSpec(
            num_scalar_prefetch=1,
            grid=(2,),
            in_specs=in_specs,
            out_specs=pl.BlockSpec((requests, 1, heads, lat), lambda i, s: (0, layer + i, 0, 0)),
        ),
        out_shape=jax.ShapeDtypeStruct(queries.shape, bf16),
        input_output_aliases=aliases,
        compiler_params=params,
        cost_estimate=pl.CostEstimate(
            flops=2 * 4 * requests * heads * 2 * PAGE * lat,
            bytes_accessed=2 * 2 * (2 * requests * heads + 2 * PAGE) * lat,
            transcendentals=2 * requests * heads * 2 * PAGE,
        ),
    )(*operands)


def shards(
    prompt_states, norm_gain, w_latent, w_back, page_lists, queries, new_latent, context_lengths
):
    segments = lax.axis_size("segment")
    wide = lax.axis_size("wide")
    position = lax.axis_index("segment")
    core = position & 1
    batches, tok_rows, local_width = prompt_states.shape
    width = local_width * wide
    tokens = batches * tok_rows
    mine = tokens // segments
    share = mine // wide
    layers = segments
    lat = w_latent.shape[2]
    where = jnp.stack([position, core]).astype(jnp.int32)

    def array(*shape):
        return jax.ShapeDtypeStruct(shape, bf16)

    both, lent = call(
        weights_kernel,
        [whole(w_latent.shape), whole(norm_gain.shape), whole(w_back.shape)],
        [whole((2, local_width, lat)), whole((local_width, lat))],
        [array(2, local_width, lat), array(local_width, lat)],
        [w_latent, norm_gain, w_back],
        [where],
        flops=2 * local_width**3,
    )
    every = lax.all_gather(both, "segment", axis=0)
    lent = lax.ppermute(lent, "segment", [(i, i + 1) for i in range(0, segments, 2)])

    states = prompt_states.reshape(segments // 2, 2, mine, local_width)
    high = lat // wide
    columns = 2 * lat + LANES
    (sent,) = call(
        home_kernel,
        [
            pl.BlockSpec((segments // 2, 1, mine, local_width), lambda i, s: (0, s[1], 0, 0)),
            whole(both.shape),
            whole(lent.shape),
        ],
        [whole((wide, high, columns))],
        [array(wide, high, columns)],
        [states, both, lent],
        [where],
        [pltpu.VMEM((local_width, lat), bf16), pltpu.VMEM((lat, lat), f32)],
        flops=2 * 2 * local_width**3,
    )
    got = exchanged(sent, "wide")
    latent, cross = call(
        functools.partial(home_sum_kernel, width),
        [whole(got.shape)],
        [whole((segments // 2, share, lat)), whole((high, lat))],
        [array(segments // 2, share, lat), array(high, lat)],
        [got],
    )
    taken = [
        lax.ppermute(latent[hop], "segment", [(0, 2 * hop), (1, 2 * hop + 1)])
        for hop in range(1, segments // 2)
    ]
    (sent,) = call(
        home_send_kernel,
        [whole((1, share, lat))] + [whole((share, lat))] * 3 + [whole((high, lat))],
        [whole((wide, high + share, lat))],
        [array(wide, high + share, lat)],
        [latent] + taken + [cross],
        [where],
    )
    got = exchanged(sent, "wide")

    def advance(before, following, got, state, extra=None):
        first = before == (0,)
        in_specs, operands = [whole(got.shape)], [got]
        if extra is not None:
            in_specs.append(whole(extra.shape))
            operands.append(extra)
        if first:
            in_specs.append(
                pl.BlockSpec((1, 1, mine, local_width), lambda i, s: (s[0] >> 1, s[1], 0, 0))
            )
        else:
            in_specs.append(whole(state.shape))
        operands += [state, every]
        in_specs.append(anywhere)
        count = len(following) + (len(following) == 2)
        shapes = [array(wide, share, LANES + count * lat), array(mine, local_width)]
        if first:
            shapes.append(array(wide, high, lat))
        elif extra is not None:
            shapes.append(array(mine, 2 * lat))
        needed = len(before) + count
        return call(
            functools.partial(advance_kernel, before, following, first),
            in_specs,
            [whole(s.shape) for s in shapes],
            shapes,
            operands,
            [where],
            [pltpu.VMEM((needed, local_width, lat), bf16), pltpu.SemaphoreType.DMA((needed,))],
            flops=2 * needed * mine * lat * local_width,
        )

    sent, state, cross = advance((0,), (1,), got, states)
    crosses = lax.all_gather(cross.reshape(lat, lat), "segment", axis=0)
    earlier = got
    got = exchanged(sent, "wide")
    (sent,) = call(
        functools.partial(single_kernel, width),
        [whole(got.shape)],
        [whole((wide, share, lat))],
        [array(wide, share, lat)],
        [got],
    )
    got = exchanged(sent, "wide")

    def pair_step(even, got):
        (sent,) = call(
            functools.partial(pair_kernel, width, even),
            [whole(got.shape), anywhere],
            [whole((wide, share, 2 * lat))],
            [array(wide, share, 2 * lat)],
            [got, crosses],
            [],
            [pltpu.VMEM((2, lat, lat), bf16), pltpu.SemaphoreType.DMA((2,))],
            flops=2 * 2 * share * lat * lat,
        )
        return sent

    targets = page_lists[:, :, 0]
    owned = targets == position
    counts = jnp.sum(owned.astype(jnp.int32), axis=1)
    none = targets.shape[1]
    order = jnp.arange(none, dtype=jnp.int32)[None, :]
    slot0 = jnp.min(jnp.where(owned, order, none), axis=1)
    slot1 = jnp.min(jnp.where(owned & (order > slot0[:, None]), order, none), axis=1)
    slots = jnp.minimum(jnp.stack([slot0, slot1], axis=1), none - 1).reshape(-1)
    limit = jnp.minimum(context_lengths, counts[None, :] * PAGE)
    limit = jnp.repeat(limit.T, queries.shape[2], axis=1)[:, :, None]
    new = new_latent.transpose(1, 0, 2)

    def decode(layer, pages, carried):
        return decode_pair(layer, slots, queries, new, limit, pages, carried)

    sent, state, held = advance((1,), (2, 3), got, state, earlier)
    pages01 = lax.all_gather(held, "segment", axis=0)
    got = exchanged(sent, "wide")
    sent = pair_step(2, got)
    got = exchanged(sent, "wide")

    pages23 = lax.all_gather(got.reshape(mine, 2 * lat), "segment", axis=0)
    sent, state = advance((2, 3), (4, 5), got, state)
    got = exchanged(sent, "wide")
    sent = pair_step(4, got)
    got = exchanged(sent, "wide")

    pages45 = lax.all_gather(got.reshape(mine, 2 * lat), "segment", axis=0)
    sent, state = advance((4, 5), (6, 7), got, state)
    got = exchanged(sent, "wide")
    out = decode(0, pages01, None)
    got, out = lax.optimization_barrier((got, out))
    sent = pair_step(6, got)

    got = exchanged(sent[:segments], "segment")
    out = decode(2, pages23, out)
    got, out = lax.optimization_barrier((got, out))
    (sent,) = call(
        functools.partial(choose_kernel, layers - 2),
        [whole(got.shape)],
        [whole((wide, share, 4 * lat))],
        [array(wide, share, 4 * lat)],
        [got],
        [slots],
    )
    got = exchanged(sent, "wide")
    out = decode(4, pages45, out)
    got, out = lax.optimization_barrier((got, out))
    return decode(layers - 2, got, out)


def solution(mesh):
    in_specs = (
        P(None, None, "wide"),
        P("segment", "wide"),
        P("segment", "wide", None),
        P("segment", None, "wide"),
        P(),
        P("segment", None, "wide", None),
        P("segment", None, None),
        P("segment", None),
    )
    out_specs = P("segment", None, "wide", None)
    return jax.shard_map(shards, mesh=mesh, in_specs=in_specs, out_specs=out_specs, check_vma=False)
```

time: 263 us -> 224 us (0.85)
  matrix products: 34 us -> 0 us
  waiting for transfers between devices: 45.4 us -> 17.6 us
  local copies, waits for them, and re-layouts: 10 us -> 29.3 us
  Pallas kernels: 9.41 us -> 27.9 us
  other arithmetic: 8.87 us -> 0.46 us
  between operations: 21.5 us -> 13.4 us
  blocking collectives: 107 us -> 114 us
  starting transfers between devices: 25.2 us -> 20.4 us
    dot_general x25 -> x0, matrix products: 34 us -> none  [the longest x21 29.3 us: dot(): return jnp.dot(a, b, preferred_element_type=jnp.float32)]
    unnamed x30 -> x41, local copies, waits for them, and re-layouts: 4.89 us -> 27.9 us
    pallas_call x0 -> x13, Pallas kernels: none -> 18.5 us  [call(): pl.pallas_call(body, grid_spec=pltpu.PrefetchScalarGridSpec(num_scalar_pr...]
    all_gather x6 -> x5, waiting for transfers between devices: 16.2 us -> 0.06 us  [the longest x1 0.02 us: shards(): pages45 = lax.all_gather(got.reshape(mine, 2 * lat), 'segment', axis=0)]
    all_to_all x7 -> x8, blocking collectives: 107 us -> 114 us  [exchanged(): return lax.all_to_all(sent, axis, 0, 0, tiled=True)]
    all_to_all x4 -> x3, waiting for transfers between devices: 20.7 us -> 14.6 us  [exchanged(): return lax.all_to_all(sent, axis, 0, 0, tiled=True)]
    ppermute x7 -> x4, waiting for transfers between devices: 8.41 us -> 2.83 us  [the longest x1 1.49 us: shards(): lax.ppermute(lent, 'segment', [(i, i + 1) for i in range(0, segments, 2)])]
    select_n x6 -> x0, other arithmetic: 3.18 us -> none  [the longest x1 2.54 us: shards(): first = along_x(jnp.where(core == 0, back, gained))]
  transfers between devices with their start and end apart: 17 -> 12, of which waited for: 6 -> 5; matrix products, arithmetic and copies ran while one was open for 17% -> 1% of each run, Pallas kernels for 2% -> 10%
where the time goes in v3:
time: 224 us; the launch traced here: 223 us
  blocking collectives  114 us (51%)
  local copies, waits for them, and re-layouts  29.3 us (13%)
  Pallas kernels  27.9 us (12%)
  starting transfers between devices  20.4 us (9%)
  waiting for transfers between devices  17.6 us (8%)
  between operations  13.4 us (6%)
    all_to_all x8, blocking collectives, exchanged(): return lax.all_to_all(sent, axis, 0, 0, tiled=True)  114 us
    unnamed x41, local copies, waits for them, and re-layouts  27.9 us
    pallas_call x13, Pallas kernels, call(): pl.pallas_call(body, grid_spec=pltpu.PrefetchScalarGridSpec(num_scalar_pr...  18.5 us
    all_to_all x3, waiting for transfers between devices, exchanged(): return lax.all_to_all(sent, axis, 0, 0, tiled=True)  14.6 us
    all_to_all x3, starting transfers between devices, exchanged(): return lax.all_to_all(sent, axis, 0, 0, tiled=True)  12 us
    pallas_call x4, Pallas kernels, decode_pair(): pl.pallas_call(decode_kernel, grid_spec=pltpu.PrefetchScalarGridSpec(num_...  9.42 us
    ppermute x3, starting transfers between devices, shards(): lax.ppermute(latent[hop], 'segment', [(0, 2 * hop), (1, 2 * hop + 1)])  6.88 us
  transfers between devices with their start and end apart: 12, of which 5 were waited for; matrix products, arithmetic and copies ran while one was open for 1% of the time, Pallas kernels for 10%

profile of v3, /device:TPU:0, one launch (start us, length us, event | category | flops | bytes accessed | tf_op | source)
XLA Modules:
  0.0 222.6 jit_solution(14574003024934341430)
XLA Ops:
  6.5 0.1 pad_add_fusion.where
  6.6 1.1 copy-done.14
  7.7 1.0 copy-done.15
  8.8 0.7 copy-done.16
  9.5 2.0 shard_map.82
  11.5 0.0 all-gather.8.cloned.1.call-start
  11.5 1.3 collective-permute-start
  12.9 1.5 collective-permute-done.lent_ref
  14.3 2.7 %shard_map.83 = bf16[16,32,1152]{2,1,0:T(8,128)(2,1)S(1)} custom-call(s32[2]{0:T(128)S(1)} %pad_add_fusion.where, bf16[4,2,128,512]{3,2,1,0:T(8,128)(2,1)S(1)} %bitcast.33, bf16[2,512,512]{2,1,0:T(8,128)(2,1)} %get-tuple-element.24.both_ref, bf16[512,512]{1,0:T(8,128)(2,1)S(1)} %collective-permute-done.lent_ref), custom_call_target="tpu_custom_call" | custom-call | flops 536870912 | bytes 2359296 | tf_op jit(solution)/shard_map/pallas_call | solution.py:52
  17.1 27.4 %all_to_all.55.got_ref = bf16[16,32,1152]{2,1,0:T(8,128)(2,1)S(1)} all-to-all(bf16[16,32,1152]{2,1,0:T(8,128)(2,1)S(1)} %shard_map.83), channel_id=1, replica_groups=mesh['segment'=8,'wide'=16] {'wide'}, dimensions={0} | all-to-all | bytes 2359296 | tf_op jit(solution)/shard_map/all_to_all | solution.py:43
  44.5 0.2 shard_map.84
  44.8 3.4 %collective-permute-start.1 = (bf16[8,512]{1,0:T(8,128)(2,1)S(1)}, bf16[8,512]{1,0:T(8,128)(2,1)S(1)}, u32[]{:S(2)}, u32[]{:S(2)}) collective-permute-start(bf16[8,512]{1,0:T(8,128)(2,1)S(1)} %get-tuple-element.49), channel_id=1, source_target_pairs={{0,32},{16,48},{1,33},{17,49},{2,34},{18,50},{3,35},{19,51},{4,36}... | collective-permute-start | bytes 24584 | tf_op jit(solution)/shard_map/ppermute | solution.py:344
  48.2 2.2 collective-permute-start.2
  50.4 1.3 collective-permute-start.3
  51.7 1.3 collective-permute-done.3.c_ref
  53.0 0.6 shard_map.85
  53.6 14.8 %all_to_all.56.got_ref.refs_0_ = bf16[16,40,512]{2,1,0:T(8,128)(2,1)S(1)} all-to-all(bf16[16,40,512]{2,1,0:T(8,128)(2,1)S(1)} %shard_map.85), channel_id=1, replica_groups=mesh['segment'=8,'wide'=16] {'wide'}, dimensions={0} | all-to-all | bytes 1310720 | tf_op jit(solution)/shard_map/all_to_all | solution.py:43
  68.4 3.4 %copy-done = bf16[16,512,512]{2,1,0:T(8,128)(2,1)S(1)} copy-done((bf16[16,512,512]{2,1,0:T(8,128)(2,1)S(1)}, bf16[16,512,512]{2,1,0:T(8,128)(2,1)}, u32[]{:S(2)}) %copy-start) | copy-done | bytes 8388632
  71.8 1.9 shard_map.86
  73.7 0.0 all-gather.16.cloned.1.call-start
  73.8 11.2 %all_to_all.57.got_ref = bf16[16,8,640]{2,1,0:T(8,128)(2,1)S(1)} all-to-all(bf16[16,8,640]{2,1,0:T(8,128)(2,1)S(1)} %get-tuple-element.28), channel_id=1, replica_groups=mesh['segment'=8,'wide'=16] {'wide'}, dimensions={0} | all-to-all | bytes 327680 | tf_op jit(solution)/shard_map/all_to_all | solution.py:43
  85.0 0.2 shard_map.87
  85.2 11.0 %all_to_all.58.got_ref = bf16[16,8,512]{2,1,0:T(8,128)(2,1)S(1)} all-to-all(bf16[16,8,512]{2,1,0:T(8,128)(2,1)S(1)} %shard_map.87), channel_id=1, replica_groups=mesh['segment'=8,'wide'=16] {'wide'}, dimensions={0} | all-to-all | bytes 262144 | tf_op jit(solution)/shard_map/all_to_all | solution.py:43
  96.2 3.6 %copy-done.1 = bf16[16,512,512]{2,1,0:T(8,128)(2,1)S(1)} copy-done((bf16[16,512,512]{2,1,0:T(8,128)(2,1)S(1)}, bf16[16,512,512]{2,1,0:T(8,128)(2,1)}, u32[]{:S(2)}) %copy-start.1) | copy-done | bytes 8388632
  99.8 2.3 %shard_map.88 = (bf16[16,8,1664]{2,1,0:T(8,128)(2,1)S(1)}, bf16[128,512]{1,0:T(8,128)(2,1)S(1)}, bf16[128,1024]{1,0:T(8,128)(2,1)}) custom-call(s32[2]{0:T(128)S(1)} %pad_add_fusion.where, bf16[16,8,512]{2,1,0:T(8,128)(2,1)S(1)} %all_to_all.58.got_ref, bf16[16,40,512]{2,1,0:T(8,128)(2,1)S(1)} %all_to_all.56.got_ref.refs_0_, ...), custom_call_target="tpu_custom_call" | custom-call | flops 268435456 | bytes 1638400 | tf_op jit(solution)/shard_map/pallas_call | solution.py:52
  102.1 0.0 all-gather.10.cloned.1.call-start
  102.2 12.6 %all_to_all.59.got_ref = bf16[16,8,1664]{2,1,0:T(8,128)(2,1)S(1)} all-to-all(bf16[16,8,1664]{2,1,0:T(8,128)(2,1)S(1)} %get-tuple-element.30), channel_id=1, replica_groups=mesh['segment'=8,'wide'=16] {'wide'}, dimensions={0} | all-to-all | bytes 851968 | tf_op jit(solution)/shard_map/all_to_all | solution.py:43
  114.8 2.4 %copy-done.4 = bf16[8,512,512]{2,1,0:T(8,128)(2,1)S(1)} copy-done((bf16[8,512,512]{2,1,0:T(8,128)(2,1)S(1)}, bf16[8,512,512]{2,1,0:T(8,128)(2,1)}, u32[]{:S(2)}) %copy-start.4) | copy-done | bytes 4194328
  117.2 0.7 shard_map.89
  118.0 12.0 %all_to_all.60.got_ref = bf16[16,8,1024]{2,1,0:T(8,128)(2,1)} all-to-all(bf16[16,8,1024]{2,1,0:T(8,128)(2,1)S(1)} %shard_map.89), channel_id=1, replica_groups=mesh['segment'=8,'wide'=16] {'wide'}, dimensions={0} | all-to-all | bytes 524288 | tf_op jit(solution)/shard_map/all_to_all | solution.py:43
  129.9 0.0 all-gather.12.cloned.1.call-start
  130.0 3.4 %copy-done.2 = bf16[16,512,512]{2,1,0:T(8,128)(2,1)S(1)} copy-done((bf16[16,512,512]{2,1,0:T(8,128)(2,1)S(1)}, bf16[16,512,512]{2,1,0:T(8,128)(2,1)}, u32[]{:S(2)}) %copy-start.2) | copy-done | bytes 8388632
  133.4 0.9 copy-done.12
  134.3 2.1 shard_map.90
  136.5 12.5 %all_to_all.61.got_ref = bf16[16,8,1664]{2,1,0:T(8,128)(2,1)S(1)} all-to-all(bf16[16,8,1664]{2,1,0:T(8,128)(2,1)S(1)} %get-tuple-element.33), channel_id=1, replica_groups=mesh['segment'=8,'wide'=16] {'wide'}, dimensions={0} | all-to-all | bytes 851968 | tf_op jit(solution)/shard_map/all_to_all | solution.py:43
  149.0 0.7 shard_map.91
  149.8 12.0 %all_to_all.62.got_ref = bf16[16,8,1024]{2,1,0:T(8,128)(2,1)} all-to-all(bf16[16,8,1024]{2,1,0:T(8,128)(2,1)S(1)} %shard_map.91), channel_id=1, replica_groups=mesh['segment'=8,'wide'=16] {'wide'}, dimensions={0} | all-to-all | bytes 524288 | tf_op jit(solution)/shard_map/all_to_all | solution.py:43
  161.8 0.1 select_reduce_fusion.1
  161.9 0.2 convert_reduce_fusion
  162.1 0.1 copy.24
  162.2 0.1 min.16.slots
  162.2 3.4 %copy-done.3 = bf16[16,512,512]{2,1,0:T(8,128)(2,1)S(1)} copy-done((bf16[16,512,512]{2,1,0:T(8,128)(2,1)S(1)}, bf16[16,512,512]{2,1,0:T(8,128)(2,1)}, u32[]{:S(2)}) %copy-start.3) | copy-done | bytes 8388632
  165.6 0.9 copy-done.13
  166.6 2.9 %shard_map.92 = (bf16[16,8,1664]{2,1,0:T(8,128)(2,1)}, bf16[128,512]{1,0:T(8,128)(2,1)}) custom-call(s32[2]{0:T(128)S(1)} %pad_add_fusion.where, bf16[16,8,1024]{2,1,0:T(8,128)(2,1)S(1)} %copy-done.13, bf16[128,512]{1,0:T(8,128)(2,1)S(1)} %get-tuple-element.34.refs_0_, bf16[8,2,512,512]{3,2,1,0:T(8,128)(2,1)S(1)} %bitcast.30), custom_call_target="tpu_custom_call" | custom-call | flops 335544320 | bytes 1114112 | tf_op jit(solution)/shard_map/pallas_call | solution.py:52
  169.5 3.6 %all-to-all-start.8 = ((bf16[16,8,1664]{2,1,0:T(8,128)(2,1)}), bf16[16,8,1664]{2,1,0:T(8,128)(2,1)S(1)}, u32[]{:S(2)}, u32[]{:S(2)}) async-start(bf16[16,8,1664]{2,1,0:T(8,128)(2,1)} %get-tuple-element.35), calls=%async_computation.8 | async-start | bytes 851968 | tf_op jit(solution)/shard_map/all_to_all | solution.py:43
  173.1 0.1 minimum_bitcast_fusion
  173.2 0.1 copy.26
  173.3 0.5 copy.30.limit_ref
  173.8 1.6 copy-done.8
  175.4 2.4 %shard_map.93.rest_0_ = bf16[16,8,4,512]{3,2,1,0:T(4,128)(2,1)} custom-call(s32[16]{0:T(128)S(1)} %min.16.slots, bf16[16,8,4,512]{3,2,1,0:T(4,128)(2,1)S(1)} %copy-done.10, bf16[8,16,512]{2,1,0:T(8,128)(2,1)S(1)} %bitcast.35, s32[8,64,1]{2,1,0:T(8,128)S(1)} %copy.30.limit_ref, bf16[8,128,1024]{2,1,0:T(8,128)(2,1)S(1)} %bitcast.31, ...), custom_call_target="tpu_custom_call" | custom-call | flops 67108864 | bytes 786432 | tf_op jit(solution)/shard_map/pallas_call | solution.py:268
  177.8 4.8 %all-to-all-done.8.got_ref = bf16[16,8,1664]{2,1,0:T(8,128)(2,1)S(1)} async-done(((bf16[16,8,1664]{2,1,0:T(8,128)(2,1)}), bf16[16,8,1664]{2,1,0:T(8,128)(2,1)S(1)}, u32[]{:S(2)}, u32[]{:S(2)}) %all-to-all-start.8) | async-done | bytes 426016 | tf_op jit(solution)/shard_map/all_to_all | solution.py:43
  182.6 2.2 %copy-done.6 = bf16[8,512,512]{2,1,0:T(8,128)(2,1)S(1)} copy-done((bf16[8,512,512]{2,1,0:T(8,128)(2,1)S(1)}, bf16[8,512,512]{2,1,0:T(8,128)(2,1)}, u32[]{:S(2)}) %copy-start.6) | copy-done | bytes 4194328
  184.8 0.7 shard_map.94
  185.6 0.7 slice.16
  186.2 4.9 %all-to-all-start.9 = ((bf16[8,8,1024]{2,1,0:T(8,128)(2,1)}), bf16[8,8,1024]{2,1,0:T(8,128)(2,1)S(1)}, u32[]{:S(2)}, u32[]{:S(2)}) async-start(bf16[8,8,1024]{2,1,0:T(8,128)(2,1)} %slice.16), calls=%async_computation.9 | async-start | bytes 262144 | tf_op jit(solution)/shard_map/all_to_all | solution.py:43
  191.1 1.6 copy-done.7
  192.7 2.4 %shard_map.95.rest_0_ = bf16[16,8,4,512]{3,2,1,0:T(4,128)(2,1)} custom-call(s32[16]{0:T(128)S(1)} %min.16.slots, bf16[16,8,4,512]{3,2,1,0:T(4,128)(2,1)S(1)} %copy-done.10, bf16[8,16,512]{2,1,0:T(8,128)(2,1)S(1)} %bitcast.36, s32[8,64,1]{2,1,0:T(8,128)S(1)} %copy.30.limit_ref, bf16[8,128,1024]{2,1,0:T(8,128)(2,1)S(1)} %copy-done.7, ...), custom_call_target="tpu_custom_call", output_to_operand_aliasing={{}: (6, {})} | custom-call | flops 67108864 | bytes 786432 | tf_op jit(solution)/shard_map/pallas_call | solution.py:268
  195.1 2.2 all-to-all-done.9.got_ref
  197.2 1.4 shard_map.96
  198.6 3.6 %all-to-all-start.10 = ((bf16[16,8,2048]{2,1,0:T(8,128)(2,1)}), bf16[16,8,2048]{2,1,0:T(8,128)(2,1)S(1)}, u32[]{:S(2)}, u32[]{:S(2)}) async-start(bf16[16,8,2048]{2,1,0:T(8,128)(2,1)} %shard_map.96), calls=%async_computation.10 | async-start | bytes 1048576 | tf_op jit(solution)/shard_map/all_to_all | solution.py:43
  202.2 1.6 copy-done.9
  203.8 2.4 %shard_map.97.rest_0_ = bf16[16,8,4,512]{3,2,1,0:T(4,128)(2,1)} custom-call(s32[16]{0:T(128)S(1)} %min.16.slots, bf16[16,8,4,512]{3,2,1,0:T(4,128)(2,1)S(1)} %copy-done.10, bf16[8,16,512]{2,1,0:T(8,128)(2,1)S(1)} %bitcast.37, s32[8,64,1]{2,1,0:T(8,128)S(1)} %copy.30.limit_ref, bf16[8,128,1024]{2,1,0:T(8,128)(2,1)S(1)} %copy-done.9, ...), custom_call_target="tpu_custom_call", output_to_operand_aliasing={{}: (6, {})} | custom-call | flops 67108864 | bytes 786432 | tf_op jit(solution)/shard_map/pallas_call | solution.py:268
  206.2 7.6 %all-to-all-done.10.first_ref.second_ref = bf16[16,8,2048]{2,1,0:T(8,128)(2,1)S(1)} async-done(((bf16[16,8,2048]{2,1,0:T(8,128)(2,1)}), bf16[16,8,2048]{2,1,0:T(8,128)(2,1)S(1)}, u32[]{:S(2)}, u32[]{:S(2)}) %all-to-all-start.10) | async-done | bytes 524320 | tf_op jit(solution)/shard_map/all_to_all | solution.py:43
  213.8 2.3 %shard_map.98 = bf16[16,8,4,512]{3,2,1,0:T(4,128)(2,1)} custom-call(s32[16]{0:T(128)S(1)} %min.16.slots, bf16[16,8,4,512]{3,2,1,0:T(4,128)(2,1)S(1)} %copy-done.10, bf16[8,16,512]{2,1,0:T(8,128)(2,1)S(1)} %bitcast.38, s32[8,64,1]{2,1,0:T(8,128)S(1)} %copy.30.limit_ref, ...), custom_call_target="tpu_custom_call", output_to_operand_aliasing={{}: (6, {})} | custom-call | flops 67108864 | bytes 786432 | tf_op jit(solution)/shard_map/pallas_call | solution.py:268
  (44 shorter events, 0.3 us)
Async XLA Ops:
  6.5 7.8 %copy-start.11 = (bf16[4,256,512]{2,1,0:T(8,128)(2,1)S(1)}, bf16[4,256,512]{2,1,0:T(8,128)(2,1)}, u32[]{:S(2)}) copy-start(bf16[4,256,512]{2,1,0:T(8,128)(2,1)} %param.8) | copy-start | bytes 3145732
  6.5 61.9 %all-gather.14.cloned.1.call-start = ((), (), s32[]{:S(2)}) async-start(), calls=%async_computation.14 | async-start | bytes 9437184 | tf_op jit(solution)/shard_map/all_gather | solution.py:315
  6.6 1.1 copy-start.14
  7.7 1.0 copy-start.15
  8.8 0.7 copy-start.16
  11.5 103.3 %all-gather.8.cloned.1.call-start = ((), (), s32[]{:S(2)}) async-start(), calls=%async_computation.11 | async-start | bytes 4718592 | tf_op jit(solution)/shard_map/all_gather | solution.py:390
  11.5 2.8 %collective-permute-start = (bf16[512,512]{1,0:T(8,128)(2,1)S(1)}, bf16[512,512]{1,0:T(8,128)(2,1)S(1)}, u32[]{:S(2)}, u32[]{:S(2)}) collective-permute-start(bf16[512,512]{1,0:T(8,128)(2,1)S(1)} %get-tuple-element.25), channel_id=1, source_target_pairs={{0,16},{32,48},{64,80},{96,112},{1,17},{33,49},{65,81},{97,113},{2... | collective-permute-start | bytes 1572872 | tf_op jit(solution)/shard_map/ppermute | solution.py:316
  44.8 6.9 %collective-permute-start.1 = (bf16[8,512]{1,0:T(8,128)(2,1)S(1)}, bf16[8,512]{1,0:T(8,128)(2,1)S(1)}, u32[]{:S(2)}, u32[]{:S(2)}) collective-permute-start(bf16[8,512]{1,0:T(8,128)(2,1)S(1)} %get-tuple-element.49), channel_id=1, source_target_pairs={{0,32},{16,48},{1,33},{17,49},{2,34},{18,50},{3,35},{19,51},{4,36}... | collective-permute-start | bytes 24584 | tf_op jit(solution)/shard_map/ppermute | solution.py:344
  48.2 3.6 %collective-permute-start.2 = (bf16[8,512]{1,0:T(8,128)(2,1)S(1)}, bf16[8,512]{1,0:T(8,128)(2,1)S(1)}, u32[]{:S(2)}, u32[]{:S(2)}) collective-permute-start(bf16[8,512]{1,0:T(8,128)(2,1)S(1)} %get-tuple-element.48), channel_id=1, source_target_pairs={{0,64},{16,80},{1,65},{17,81},{2,66},{18,82},{3,67},{19,83},{4,68}... | collective-permute-start | bytes 24584 | tf_op jit(solution)/shard_map/ppermute | solution.py:344
  50.4 2.6 %collective-permute-start.3 = (bf16[8,512]{1,0:T(8,128)(2,1)S(1)}, bf16[8,512]{1,0:T(8,128)(2,1)S(1)}, u32[]{:S(2)}, u32[]{:S(2)}) collective-permute-start(bf16[8,512]{1,0:T(8,128)(2,1)S(1)} %get-tuple-element.47), channel_id=1, source_target_pairs={{0,96},{16,112},{1,97},{17,113},{2,98},{18,114},{3,99},{19,115},{4... | collective-permute-start | bytes 24584 | tf_op jit(solution)/shard_map/ppermute | solution.py:344
  68.4 3.4 %copy-start = (bf16[16,512,512]{2,1,0:T(8,128)(2,1)S(1)}, bf16[16,512,512]{2,1,0:T(8,128)(2,1)}, u32[]{:S(2)}) copy-start(bf16[16,512,512]{2,1,0:T(8,128)(2,1)} %all-gather.14.cloned.1.call-done) | copy-start | bytes 25165828
  73.7 100.1 %all-gather.16.cloned.1.call-start = ((), (), s32[]{:S(2)}) async-start(), calls=%async_computation.15 | async-start | bytes 2359296 | tf_op jit(solution)/shard_map/all_gather | solution.py:431
  96.2 3.6 %copy-start.1 = (bf16[16,512,512]{2,1,0:T(8,128)(2,1)S(1)}, bf16[16,512,512]{2,1,0:T(8,128)(2,1)}, u32[]{:S(2)}) copy-start(bf16[16,512,512]{2,1,0:T(8,128)(2,1)} %all-gather.14.cloned.1.call-done) | copy-start | bytes 25165828
  102.1 89.0 %all-gather.10.cloned.1.call-start = ((), (), s32[]{:S(2)}) async-start(), calls=%async_computation.12 | async-start | bytes 2359296 | tf_op jit(solution)/shard_map/all_gather | solution.py:436
  114.8 2.4 %copy-start.4 = (bf16[8,512,512]{2,1,0:T(8,128)(2,1)S(1)}, bf16[8,512,512]{2,1,0:T(8,128)(2,1)}, u32[]{:S(2)}) copy-start(bf16[8,512,512]{2,1,0:T(8,128)(2,1)} %all-gather.8.cloned.1.call-done.cross_ref) | copy-start | bytes 12582916
  129.9 72.3 %all-gather.12.cloned.1.call-start = ((), (), s32[]{:S(2)}) async-start(), calls=%async_computation.13 | async-start | bytes 2359296 | tf_op jit(solution)/shard_map/all_gather | solution.py:442
  130.0 3.4 %copy-start.2 = (bf16[16,512,512]{2,1,0:T(8,128)(2,1)S(1)}, bf16[16,512,512]{2,1,0:T(8,128)(2,1)}, u32[]{:S(2)}) copy-start(bf16[16,512,512]{2,1,0:T(8,128)(2,1)} %all-gather.14.cloned.1.call-done) | copy-start | bytes 25165828
  133.4 0.9 copy-start.12
  134.3 14.7 %copy-start.5 = (bf16[8,512,512]{2,1,0:T(8,128)(2,1)S(1)}, bf16[8,512,512]{2,1,0:T(8,128)(2,1)}, u32[]{:S(2)}) copy-start(bf16[8,512,512]{2,1,0:T(8,128)(2,1)} %all-gather.8.cloned.1.call-done.cross_ref) | copy-start | bytes 12582916
  149.0 12.7 %copy-start.18 = (s32[8,8,1]{1,2,0:T(1,128)S(1)}, s32[8,8,1]{1,2,0:T(1,128)}, u32[]{:S(2)}) copy-start(s32[8,8,1]{1,2,0:T(1,128)} %param.12) | copy-start | bytes 772
  162.2 3.4 %copy-start.3 = (bf16[16,512,512]{2,1,0:T(8,128)(2,1)S(1)}, bf16[16,512,512]{2,1,0:T(8,128)(2,1)}, u32[]{:S(2)}) copy-start(bf16[16,512,512]{2,1,0:T(8,128)(2,1)} %all-gather.14.cloned.1.call-done) | copy-start | bytes 25165828
  165.6 0.9 copy-start.13
  166.6 6.5 %copy-start.19 = (s32[16,8]{0,1:T(8,128)S(1)}, s32[16,8]{0,1:T(8,128)}, u32[]{:S(2)}) copy-start(s32[16,8]{0,1:T(8,128)} %param.15) | copy-start | bytes 1540
  166.6 7.1 %copy-start.17 = (bf16[16,8,512]{2,1,0:T(8,128)(2,1)S(1)}, bf16[16,8,512]{2,1,0:T(8,128)(2,1)}, u32[]{:S(2)}) copy-start(bf16[16,8,512]{2,1,0:T(8,128)(2,1)} %param.14) | copy-start | bytes 393220
  166.6 7.2 %copy-start.10 = (bf16[16,8,4,512]{3,2,1,0:T(4,128)(2,1)S(1)}, bf16[16,8,4,512]{3,2,1,0:T(4,128)(2,1)}, u32[]{:S(2)}) copy-start(bf16[16,8,4,512]{3,2,1,0:T(4,128)(2,1)} %q_ref.7) | copy-start | bytes 1572868
  169.5 13.1 %all-to-all-start.8 = ((bf16[16,8,1664]{2,1,0:T(8,128)(2,1)}), bf16[16,8,1664]{2,1,0:T(8,128)(2,1)S(1)}, u32[]{:S(2)}, u32[]{:S(2)}) async-start(bf16[16,8,1664]{2,1,0:T(8,128)(2,1)} %get-tuple-element.35), calls=%async_computation.8 | async-start | bytes 851968 | tf_op jit(solution)/shard_map/all_to_all | solution.py:43
  173.8 1.6 copy-start.8
  182.6 2.2 %copy-start.6 = (bf16[8,512,512]{2,1,0:T(8,128)(2,1)S(1)}, bf16[8,512,512]{2,1,0:T(8,128)(2,1)}, u32[]{:S(2)}) copy-start(bf16[8,512,512]{2,1,0:T(8,128)(2,1)} %all-gather.8.cloned.1.call-done.cross_ref) | copy-start | bytes 12582916
  186.2 11.0 %all-to-all-start.9 = ((bf16[8,8,1024]{2,1,0:T(8,128)(2,1)}), bf16[8,8,1024]{2,1,0:T(8,128)(2,1)S(1)}, u32[]{:S(2)}, u32[]{:S(2)}) async-start(bf16[8,8,1024]{2,1,0:T(8,128)(2,1)} %slice.16), calls=%async_computation.9 | async-start | bytes 262144 | tf_op jit(solution)/shard_map/all_to_all | solution.py:43
  191.1 1.6 copy-start.7
  198.6 15.2 %all-to-all-start.10 = ((bf16[16,8,2048]{2,1,0:T(8,128)(2,1)}), bf16[16,8,2048]{2,1,0:T(8,128)(2,1)S(1)}, u32[]{:S(2)}, u32[]{:S(2)}) async-start(bf16[16,8,2048]{2,1,0:T(8,128)(2,1)} %shard_map.96), calls=%async_computation.10 | async-start | bytes 1048576 | tf_op jit(solution)/shard_map/all_to_all | solution.py:43
  202.2 1.6 copy-start.9
Sparse Core Ops, SparseCore 0:
  11.6 52.1 all-gather.13
  73.8 30.3 all-gather.7
  106.0 25.0 all-gather.15
  132.7 25.4 all-gather.9
  161.9 23.4 all-gather.11

commit v4 on v3

v4 whole, which is shorter than its diff:
```python
import functools

import jax
import jax.numpy as jnp
from jax import lax
from jax.experimental import pallas as pl
from jax.experimental.pallas import tpu as pltpu
from jax.sharding import PartitionSpec as P

PAGE = 128
LANES = 128

eps_norm = 1e-06
score_scale = 192.0 ** (-0.5)

params = pltpu.CompilerParams(vmem_limit_bytes=24 * 1024 * 1024)
in_hbm = pl.BlockSpec(memory_space=pltpu.HBM)
bf16 = jnp.bfloat16
f32 = jnp.float32


def dot(a, b):
    return jnp.dot(a, b, preferred_element_type=jnp.float32)


def dot_t(a, b):
    return lax.dot_general(a, b, (((1,), (1,)), ((), ())), preferred_element_type=jnp.float32)


def square_columns(values):
    squares = jnp.sum(values * values, axis=1, keepdims=True)
    high = squares.astype(bf16).astype(f32)
    column = lax.broadcasted_iota(jnp.int32, (values.shape[0], LANES), 1)
    return jnp.where(column == 0, high, jnp.where(column == 1, squares - high, 0.0))


def silu(latent):
    values = latent.astype(f32)
    return (values / (1.0 + jnp.exp(-values))).astype(bf16)


def exchanged(sent, axis):
    return lax.all_to_all(sent, axis, 0, 0, tiled=True)


def core_swap(x):
    length = lax.axis_size("segment")
    return lax.ppermute(x, "segment", [(i, i ^ 1) for i in range(length)])


def whole(shape):
    return pl.BlockSpec(shape, lambda i, *s: (0,) * len(shape))


def call(body, in_specs, out_specs, out_shape, operands, scalars=(), scratch=(), flops=0):
    moved = sum(o.size * 2 for o in out_shape)
    return pl.pallas_call(
        body,
        grid_spec=pltpu.PrefetchScalarGridSpec(
            num_scalar_prefetch=len(scalars),
            grid=(1,),
            in_specs=in_specs,
            out_specs=out_specs,
            scratch_shapes=scratch,
        ),
        out_shape=out_shape,
        compiler_params=params,
        cost_estimate=pl.CostEstimate(flops=flops, bytes_accessed=2 * moved, transcendentals=0),
    )(*scalars, *operands)


def weights_kernel(latent_ref, gain_ref, back_ref, both_ref, latent, sems):
    copies = [
        pltpu.make_async_copy(latent_ref.at[0], latent, sems.at[0]),
        pltpu.make_async_copy(back_ref.at[0], both_ref.at[1], sems.at[1]),
    ]
    for copy in copies:
        copy.start()
    size = latent.shape[0]
    row = lax.broadcasted_iota(jnp.int32, (size, size), 0)
    column = lax.broadcasted_iota(jnp.int32, (size, size), 1)
    gains = jnp.where(row == column, gain_ref[...].astype(f32), 0.0).astype(bf16)
    copies[0].wait()
    both_ref[0] = dot(gains, latent[...]).astype(bf16)
    copies[1].wait()


def home_kernel(where, states_ref, both_ref, other_ref, out_ref):
    groups, _, rows, width = states_ref.shape
    lat = both_ref.shape[2]
    wide = out_ref.shape[0]
    share = rows // wide
    tokens = states_ref[...].reshape(groups * rows, width)

    def put(product, at):
        for group in range(groups):
            part = product[group * rows : (group + 1) * rows]
            part = part.reshape(wide, share, part.shape[1]).astype(bf16)
            out_ref[:, group * share : (group + 1) * share, at : at + part.shape[2]] = part

    def partials(even_ref, odd_ref):
        put(dot(tokens, even_ref[0]), LANES)
        put(dot(tokens, odd_ref[0]), LANES + lat)
        put(dot_t(tokens, even_ref[1]), LANES + 2 * lat)

    def put_cross(cross):
        cross = cross.reshape(wide, lat // wide, lat).astype(bf16)
        out_ref[:, :, LANES + 3 * lat :] = cross

    put(square_columns(tokens.astype(f32)), 0)

    @pl.when(where[1] == 0)
    def _():
        put_cross(dot_t(both_ref[1], both_ref[1]))
        partials(both_ref, other_ref)

    @pl.when(where[1] != 0)
    def _():
        put_cross(dot(other_ref[1], both_ref[0]))
        partials(other_ref, both_ref)


def home_sum_kernel(got_ref, sums_ref, cross_ref):
    summed = jnp.sum(got_ref[...].astype(f32), axis=0)
    sums_ref[...] = summed[:, : sums_ref.shape[1]]
    cross = summed[:, sums_ref.shape[1] :].astype(bf16)
    for place in range(cross_ref.shape[0]):
        cross_ref[place] = cross


def chain(width, summed, gram, mixing):
    lat = gram().shape[1]
    squares = summed[:, 0:1] + summed[:, 1:2]
    at = [LANES + i * lat for i in range(4)]
    first = (summed[:, at[0] : at[1]] * lax.rsqrt(squares / width + eps_norm)).astype(bf16)
    activated = silu(first)
    towards = 2.0 * summed[:, at[2] : at[3]] + dot(activated, gram())
    squares = squares + jnp.sum(activated.astype(f32) * towards, axis=1, keepdims=True)
    second = summed[:, at[1] : at[2]] + dot(activated, mixing())
    second = (second * lax.rsqrt(squares / width + eps_norm)).astype(bf16)
    return first, second


def home_pair_kernel(width, where, sums_ref, mine_ref, other_ref, out_ref):
    def run(gram_ref, mixing_ref):
        parts = chain(width, sums_ref[...], lambda: gram_ref[...], lambda: mixing_ref[...])
        lat = parts[0].shape[1]
        for i, part in enumerate(parts):
            part = part.astype(f32).reshape(out_ref.shape[:2] + (lat,)).astype(bf16)
            out_ref[:, :, i * lat : (i + 1) * lat] = part

    @pl.when(where[1] == 0)
    def _():
        run(mine_ref, other_ref)

    @pl.when(where[1] != 0)
    def _():
        run(other_ref, mine_ref)


def home_send_kernel(where, mine_ref, a_ref, b_ref, c_ref, out_ref):
    taken = a_ref[...].astype(f32) + b_ref[...].astype(f32) + c_ref[...].astype(f32)
    latent = jnp.where(where[0] < 2, mine_ref[0].astype(f32), taken).astype(bf16)
    for place in range(out_ref.shape[0]):
        out_ref[place] = latent


def advance_kernel(before, layers, where, got_ref, states_ref, both_ref, out_ref, state_ref, *rest):
    got, weights, sems = rest
    needed = [(layer, 1) for layer in before] + [(layer, 0) for layer in layers] + [(layers[0], 1)]
    taking = pltpu.make_async_copy(got_ref, got, sems.at[len(needed)])
    taking.start()
    copies = [
        pltpu.make_async_copy(both_ref.at[layer, kind], weights.at[i], sems.at[i])
        for i, (layer, kind) in enumerate(needed)
    ]
    for copy in copies:
        copy.start()
    wide, share, _ = out_ref.shape
    rows = wide * share
    lat = weights.shape[2]
    state = states_ref[...].reshape(rows, weights.shape[1]).astype(f32)
    taking.wait()
    activated = silu(got[...].astype(f32).reshape(rows, got.shape[2]))
    for i in range(len(before)):
        copies[i].wait()
        state = state + dot(activated[:, i * lat : (i + 1) * lat], weights[i])
    state = state.astype(bf16)
    state_ref[...] = state
    squares = square_columns(state.astype(f32))
    out_ref[:, :, :LANES] = squares.reshape(wide, share, LANES).astype(bf16)
    for i in range(len(before), len(needed)):
        copies[i].wait()
        product = (dot_t if needed[i][1] else dot)(state, weights[i])
        at = LANES + (i - len(before)) * lat
        out_ref[:, :, at : at + lat] = product.reshape(wide, share, lat).astype(bf16)


def pair_kernel(width, even, got_ref, cross_ref, out_ref, crosses, sems):
    copies = [
        pltpu.make_async_copy(cross_ref.at[even + i], crosses.at[i], sems.at[i]) for i in range(2)
    ]
    for copy in copies:
        copy.start()

    def fetched(i):
        def read():
            return crosses[i]

        return read

    summed = jnp.sum(got_ref[...].astype(f32), axis=0)
    for copy in copies:
        copy.wait()
    first, second = chain(width, summed, fetched(0), fetched(1))
    lat = first.shape[1]
    for place in range(out_ref.shape[0]):
        out_ref[place, :, :lat] = first
        out_ref[place, :, lat:] = second


def choose_kernel(layer, slots, got_ref, out_ref):
    lat = got_ref.shape[2] // 2
    parts = []
    for i in range(2):
        for which in range(2):
            shard = got_ref[slots[2 * (layer + i) + which]]
            parts.append(shard[:, i * lat : (i + 1) * lat])
    for place in range(out_ref.shape[0]):
        for i, part in enumerate(parts):
            out_ref[place, :, i * lat : (i + 1) * lat] = part


def attend(q, new, keys, limit, heads):
    rows = q.shape[0]
    requests = new.shape[0]
    row = lax.broadcasted_iota(jnp.int32, (rows, requests), 0)
    start = lax.broadcasted_iota(jnp.int32, (rows, requests), 1) * heads
    pick = jnp.where((row >= start) & (row < start + heads), 1.0, 0.0).astype(bf16)
    own = dot(pick, new)
    scores = dot_t(q, keys) * score_scale
    place = lax.broadcasted_iota(jnp.int32, scores.shape, 1)
    scores = jnp.where(place < limit, scores, -jnp.inf)
    own_score = jnp.sum(q.astype(f32) * own, axis=1, keepdims=True) * score_scale
    top = jnp.maximum(jnp.max(scores, axis=1, keepdims=True), own_score)
    weights = jnp.exp(scores - top)
    own_weight = jnp.exp(own_score - top)
    total = jnp.sum(weights, axis=1, keepdims=True) + own_weight
    numer = dot(weights.astype(bf16), keys) + own_weight * own
    return (numer / total).astype(bf16)


def decode_kernel(layer, slots, q_ref, new_ref, limit_ref, pages_ref, *rest):
    out_ref, keys, sems = rest[-3:]
    requests, count, heads, lat = q_ref.shape
    copies = []
    for i in range(count):
        for which in range(2):
            page = pages_ref.at[slots[2 * (layer + i) + which], :, pl.ds(i * lat, lat)]
            at = keys.at[i, pl.ds(which * PAGE, PAGE)]
            copies.append(pltpu.make_async_copy(page, at, sems.at[2 * i + which]))
    for copy in copies:
        copy.start()
    for i in range(count):
        q = q_ref[:, i].reshape(requests * heads, lat)
        copies[2 * i].wait()
        copies[2 * i + 1].wait()
        result = attend(q, new_ref[i], keys[i], limit_ref[i], heads)
        out_ref[:, i] = result.reshape(requests, heads, lat)


def last_decode_kernel(q_ref, new_ref, limit_ref, pages_ref, carried_ref, out_ref):
    requests, count, heads, lat = q_ref.shape
    for i in range(count):
        q = q_ref[:, i].reshape(requests * heads, lat)
        at = 2 * i * lat
        pages = pages_ref[:, :, at : at + 2 * lat].astype(f32).reshape(PAGE, 2 * lat)
        keys = jnp.concatenate([pages[:, :lat], pages[:, lat:]], axis=0).astype(bf16)
        result = attend(q, new_ref[i], keys, limit_ref[i], heads)
        out_ref[:, i] = result.reshape(requests, heads, lat)


def decode_pair(layer, slots, queries, new, limit, pages, carried, last=False):
    requests, _, heads, lat = queries.shape
    half = layer // 2
    in_specs = [
        pl.BlockSpec((requests, 2, heads, lat), lambda i, *s: (0, half, 0, 0)),
        pl.BlockSpec((2, requests, lat), lambda i, *s: (half, 0, 0)),
        pl.BlockSpec((2, requests * heads, 1), lambda i, *s: (half, 0, 0)),
        whole(pages.shape) if last else in_hbm,
    ]
    scalars = [] if last else [slots]
    operands = scalars + [queries, new, limit, pages]
    aliases = {}
    if carried is not None:
        in_specs.append(in_hbm)
        aliases = {len(operands): 0}
        operands.append(carried)
    scratch = [pltpu.VMEM((2, 2 * PAGE, lat), bf16), pltpu.SemaphoreType.DMA((4,))]
    return pl.pallas_call(
        last_decode_kernel if last else functools.partial(decode_kernel, layer),
        grid_spec=pltpu.PrefetchScalarGridSpec(
            num_scalar_prefetch=len(scalars),
            grid=(1,),
            in_specs=in_specs,
            out_specs=pl.BlockSpec((requests, 2, heads, lat), lambda i, *s: (0, half, 0, 0)),
            scratch_shapes=[] if last else scratch,
        ),
        out_shape=jax.ShapeDtypeStruct(queries.shape, bf16),
        input_output_aliases=aliases,
        compiler_params=params,
        cost_estimate=pl.CostEstimate(
            flops=2 * 4 * requests * heads * 2 * PAGE * lat,
            bytes_accessed=2 * 2 * (2 * requests * heads + 2 * PAGE) * lat,
            transcendentals=2 * requests * heads * 2 * PAGE,
        ),
    )(*operands)


def shards(
    prompt_states, norm_gain, w_latent, w_back, page_lists, queries, new_latent, context_lengths
):
    segments = lax.axis_size("segment")
    wide = lax.axis_size("wide")
    position = lax.axis_index("segment")
    core = position & 1
    batches, tok_rows, local_width = prompt_states.shape
    width = local_width * wide
    tokens = batches * tok_rows
    mine = tokens // segments
    share = mine // wide
    layers = segments
    lat = w_latent.shape[2]
    where = jnp.stack([position, core]).astype(jnp.int32)

    def array(*shape):
        return jax.ShapeDtypeStruct(shape, bf16)

    size = (2, local_width, lat)
    (both,) = call(
        weights_kernel,
        [in_hbm, whole(norm_gain.shape), in_hbm],
        [whole(size)],
        [array(*size)],
        [w_latent, norm_gain, w_back],
        scratch=[pltpu.VMEM(size[1:], bf16), pltpu.SemaphoreType.DMA((2,))],
        flops=2 * local_width**3,
    )
    every = lax.all_gather(both, "segment", axis=0)
    other = core_swap(both)

    states = prompt_states.reshape(segments // 2, 2, mine, local_width)
    high = lat // wide
    partial_columns = LANES + 3 * lat
    columns = partial_columns + lat
    (sent,) = call(
        home_kernel,
        [
            pl.BlockSpec((segments // 2, 1, mine, local_width), lambda i, s: (0, s[1], 0, 0)),
            whole(size),
            whole(size),
        ],
        [whole((wide, high, columns))],
        [array(wide, high, columns)],
        [states, both, other],
        [where],
        flops=4 * 2 * local_width**3,
    )
    got = exchanged(sent, "wide")
    sums, sent = call(
        home_sum_kernel,
        [whole(got.shape)],
        [whole((high, partial_columns)), whole((wide, high, lat))],
        [jax.ShapeDtypeStruct((high, partial_columns), f32), array(wide, high, lat)],
        [got],
    )
    cross = exchanged(sent, "wide").reshape(lat, lat)
    crosses = lax.all_gather(cross, "segment", axis=0)
    (latent,) = call(
        functools.partial(home_pair_kernel, width),
        [whole(sums.shape), whole(cross.shape), whole(cross.shape)],
        [whole((segments // 2, share, 2 * lat))],
        [array(segments // 2, share, 2 * lat)],
        [sums, cross, core_swap(cross)],
        [where],
        flops=2 * 2 * high * lat * lat,
    )
    taken = [
        lax.ppermute(latent[hop], "segment", [(0, 2 * hop), (1, 2 * hop + 1)])
        for hop in range(1, segments // 2)
    ]
    (sent,) = call(
        home_send_kernel,
        [whole((1, share, 2 * lat))] + [whole((share, 2 * lat))] * 3,
        [whole((wide, share, 2 * lat))],
        [array(wide, share, 2 * lat)],
        [latent] + taken,
        [where],
    )
    got = exchanged(sent, "wide")

    def advance(before, following, got, state):
        if state.ndim == 4:
            spec = pl.BlockSpec((1, 1, mine, local_width), lambda i, s: (s[0] >> 1, s[1], 0, 0))
        else:
            spec = whole(state.shape)
        shapes = [array(wide, share, partial_columns), array(mine, local_width)]
        return call(
            functools.partial(advance_kernel, before, following),
            [in_hbm, spec, in_hbm],
            [whole(s.shape) for s in shapes],
            shapes,
            [got, state, every],
            [where],
            [
                pltpu.VMEM(got.shape, bf16),
                pltpu.VMEM((5, local_width, lat), bf16),
                pltpu.SemaphoreType.DMA((6,)),
            ],
            flops=2 * 5 * mine * lat * local_width,
        )

    def pair_step(even, got, copies):
        (sent,) = call(
            functools.partial(pair_kernel, width, even),
            [whole(got.shape), in_hbm],
            [whole((copies, share, 2 * lat))],
            [array(copies, share, 2 * lat)],
            [got, crosses],
            [],
            [pltpu.VMEM((2, lat, lat), bf16), pltpu.SemaphoreType.DMA((2,))],
            flops=2 * 2 * share * lat * lat,
        )
        return sent

    targets = page_lists[:, :, 0]
    owned = targets == position
    counts = jnp.sum(owned.astype(jnp.int32), axis=1)
    none = targets.shape[1]
    order = jnp.arange(none, dtype=jnp.int32)[None, :]
    slot0 = jnp.min(jnp.where(owned, order, none), axis=1)
    slot1 = jnp.min(jnp.where(owned & (order > slot0[:, None]), order, none), axis=1)
    slots = jnp.minimum(jnp.stack([slot0, slot1], axis=1), none - 1).reshape(-1)
    limit = jnp.minimum(context_lengths, counts[None, :] * PAGE)
    limit = jnp.repeat(limit.T, queries.shape[2], axis=1)[:, :, None]
    new = new_latent.transpose(1, 0, 2)

    def decode(layer, pages, carried, last=False):
        return decode_pair(layer, slots, queries, new, limit, pages, carried, last)

    pages = []
    state = states
    for even in range(2, layers, 2):
        pages.append(lax.all_gather(got.reshape(mine, 2 * lat), "segment", axis=0))
        sent, state = advance((even - 2, even - 1), (even, even + 1), got, state)
        got = exchanged(sent, "wide")
        if even < layers - 2:
            got = exchanged(pair_step(even, got, wide), "wide")
    out = decode(0, pages[0], None)
    got, out = lax.optimization_barrier((got, out))

    got = exchanged(pair_step(layers - 2, got, segments), "segment")
    out = decode(2, pages[1], out)
    got, out = lax.optimization_barrier((got, out))
    (sent,) = call(
        functools.partial(choose_kernel, layers - 2),
        [whole(got.shape)],
        [whole((wide, share, 4 * lat))],
        [array(wide, share, 4 * lat)],
        [got],
        [slots],
    )
    got = exchanged(sent, "wide")
    out = decode(4, pages[2], out)
    got, out = lax.optimization_barrier((got, out))
    return decode(layers - 2, got, out, True)


def solution(mesh):
    in_specs = (
        P(None, None, "wide"),
        P("segment", "wide"),
        P("segment", "wide", None),
        P("segment", None, "wide"),
        P(),
        P("segment", None, "wide", None),
        P("segment", None, None),
        P("segment", None),
    )
    out_specs = P("segment", None, "wide", None)
    return jax.shard_map(shards, mesh=mesh, in_specs=in_specs, out_specs=out_specs, check_vma=False)
```

time: 224 us -> 224 us (level)
  blocking collectives: 114 us -> 101 us
  waiting for transfers between devices: 17.6 us -> 30.6 us
  local copies, waits for them, and re-layouts: 29.3 us -> 27 us
    all_to_all x8 -> x6, blocking collectives: 114 us -> 101 us  [exchanged(): return lax.all_to_all(sent, axis, 0, 0, tiled=True)]
    all_to_all x3 -> x4, waiting for transfers between devices: 14.6 us -> 24 us  [exchanged(): return lax.all_to_all(sent, axis, 0, 0, tiled=True)]
    all_to_all x3 -> x4, starting transfers between devices: 12 us -> 15.5 us  [exchanged(): return lax.all_to_all(sent, axis, 0, 0, tiled=True)]
    ppermute x1 -> x2, waiting for transfers between devices: 1.49 us -> 4.88 us  [core_swap(): return lax.ppermute(x, 'segment', [(i, i ^ 1) for i in range(length)])]
    unnamed x41 -> x43, local copies, waits for them, and re-layouts: 27.9 us -> 26.3 us
    pallas_call x13 -> x12, Pallas kernels: 18.5 us -> 18.7 us  [call(): pl.pallas_call(body, grid_spec=pltpu.PrefetchScalarGridSpec(num_scalar_pr...]
  transfers between devices with their start and end apart: 12 -> 14, of which waited for: 5 -> 8; matrix products, arithmetic and copies ran while one was open for 1% -> 1% of each run, Pallas kernels for 10% -> 11%
where the time goes in v4:
time: 224 us; the launch traced here: 222 us
  blocking collectives  101 us (45%)
  waiting for transfers between devices  30.6 us (14%)
  Pallas kernels  27.4 us (12%)
  local copies, waits for them, and re-layouts  27 us (12%)
  starting transfers between devices  22.6 us (10%)
  between operations  13.5 us (6%)
    all_to_all x6, blocking collectives, exchanged(): return lax.all_to_all(sent, axis, 0, 0, tiled=True)  101 us
    unnamed x43, local copies, waits for them, and re-layouts  26.3 us
    all_to_all x4, waiting for transfers between devices, exchanged(): return lax.all_to_all(sent, axis, 0, 0, tiled=True)  24 us
    pallas_call x12, Pallas kernels, call(): pl.pallas_call(body, grid_spec=pltpu.PrefetchScalarGridSpec(num_scalar_pr...  18.7 us
    all_to_all x4, starting transfers between devices, exchanged(): return lax.all_to_all(sent, axis, 0, 0, tiled=True)  15.5 us
    pallas_call x4, Pallas kernels, decode_pair(): pl.pallas_call(last_decode_kernel if last else functools.partial(decode_k...  8.74 us
    ppermute x3, starting transfers between devices, shards(): lax.ppermute(latent[hop], 'segment', [(0, 2 * hop), (1, 2 * hop + 1)])  6.74 us
    ppermute x2, waiting for transfers between devices, core_swap(): return lax.ppermute(x, 'segment', [(i, i ^ 1) for i in range(length)])  4.88 us
  transfers between devices with their start and end apart: 14, of which 8 were waited for; matrix products, arithmetic and copies ran while one was open for 1% of the time, Pallas kernels for 11%

profile of v4, /device:TPU:0, one launch (start us, length us, event | category | flops | bytes accessed | tf_op | source)
XLA Modules:
  0.0 222.3 jit_solution(13557259795280168159)
XLA Ops:
  6.5 1.1 copy-done.15
  7.7 1.0 copy-done.16
  8.7 0.7 copy-done.17
  9.4 1.5 shard_map.82.both_ref
  11.0 0.1 collective-permute-start
  11.1 0.1 pad_add_fusion.where
  11.2 2.8 %collective-permute-done.other_ref = bf16[2,512,512]{2,1,0:T(8,128)(2,1)S(1)} collective-permute-done((bf16[2,512,512]{2,1,0:T(8,128)(2,1)}, bf16[2,512,512]{2,1,0:T(8,128)(2,1)S(1)}, u32[]{:S(2)}, u32[]{:S(2)}) %collective-permute-start) | collective-permute-done | bytes 1048608 | tf_op jit(solution)/shard_map/ppermute | solution.py:48
  14.0 3.2 %shard_map.83 = bf16[16,32,2176]{2,1,0:T(8,128)(2,1)S(1)} custom-call(s32[2]{0:T(128)S(1)} %pad_add_fusion.where, bf16[4,2,128,512]{3,2,1,0:T(8,128)(2,1)S(1)} %bitcast.34, bf16[2,512,512]{2,1,0:T(8,128)(2,1)} %shard_map.82.both_ref, bf16[2,512,512]{2,1,0:T(8,128)(2,1)S(1)} %collective-permute-done.other_ref), custom_call_target="tpu_custom_call" | custom-call | flops 1073741824 | bytes 4456448 | tf_op jit(solution)/shard_map/pallas_call | solution.py:57
  17.2 38.0 %all_to_all.50.got_ref = bf16[16,32,2176]{2,1,0:T(8,128)(2,1)S(1)} all-to-all(bf16[16,32,2176]{2,1,0:T(8,128)(2,1)S(1)} %shard_map.83), channel_id=1, replica_groups=mesh['segment'=8,'wide'=16] {'wide'}, dimensions={0} | all-to-all | bytes 4456448 | tf_op jit(solution)/shard_map/all_to_all | solution.py:43
  55.2 0.3 shard_map.84
  55.5 14.4 %all_to_all.51 = bf16[16,32,512]{2,1,0:T(8,128)(2,1)} all-to-all(bf16[16,32,512]{2,1,0:T(8,128)(2,1)S(1)} %get-tuple-element.19), channel_id=1, replica_groups=mesh['segment'=8,'wide'=16] {'wide'}, dimensions={0} | all-to-all | bytes 1048576 | tf_op jit(solution)/shard_map/all_to_all | solution.py:43
  70.0 0.1 collective-permute-start.1
  70.1 2.1 collective-permute-done.1.other_ref
  72.2 1.0 copy-done.7
  73.2 1.1 shard_map.85.mine_ref
  74.3 3.3 %collective-permute-start.2 = (bf16[8,1024]{1,0:T(8,128)(2,1)S(1)}, bf16[8,1024]{1,0:T(8,128)(2,1)S(1)}, u32[]{:S(2)}, u32[]{:S(2)}) collective-permute-start(bf16[8,1024]{1,0:T(8,128)(2,1)S(1)} %get-tuple-element.37), channel_id=1, source_target_pairs={{0,32},{16,48},{1,33},{17,49},{2,34},{18,50},{3,35},{19,51},{4,36}... | collective-permute-start | bytes 49160 | tf_op jit(solution)/shard_map/ppermute | solution.py:389
  77.6 2.2 collective-permute-start.3
  79.8 1.3 collective-permute-start.4
  81.1 0.2 collective-permute-done.3.b_ref
  81.3 1.3 collective-permute-done.4.c_ref
  82.6 0.6 shard_map.86
  83.2 12.0 %all_to_all.52.got_ref = bf16[16,8,1024]{2,1,0:T(8,128)(2,1)} all-to-all(bf16[16,8,1024]{2,1,0:T(8,128)(2,1)S(1)} %shard_map.86), channel_id=1, replica_groups=mesh['segment'=8,'wide'=16] {'wide'}, dimensions={0} | all-to-all | bytes 524288 | tf_op jit(solution)/shard_map/all_to_all | solution.py:43
  95.2 3.5 %copy-done = bf16[16,512,512]{2,1,0:T(8,128)(2,1)S(1)} copy-done((bf16[16,512,512]{2,1,0:T(8,128)(2,1)S(1)}, bf16[16,512,512]{2,1,0:T(8,128)(2,1)}, u32[]{:S(2)}) %copy-start) | copy-done | bytes 8388632
  98.7 0.9 copy-done.9
  99.6 2.9 %shard_map.87 = (bf16[16,8,1664]{2,1,0:T(8,128)(2,1)}, bf16[128,512]{1,0:T(8,128)(2,1)S(1)}) custom-call(s32[2]{0:T(128)S(1)} %pad_add_fusion.where, bf16[16,8,1024]{2,1,0:T(8,128)(2,1)S(1)} %copy-done.9, bf16[4,2,128,512]{3,2,1,0:T(8,128)(2,1)S(1)} %bitcast.35, bf16[8,2,512,512]{3,2,1,0:T(8,128)(2,1)S(1)} %bitcast.28), custom_call_target="tpu_custom_call" | custom-call | flops 335544320 | bytes 1114112 | tf_op jit(solution)/shard_map/pallas_call | solution.py:57
  102.6 3.6 %all-to-all-start.3 = ((bf16[16,8,1664]{2,1,0:T(8,128)(2,1)}), bf16[16,8,1664]{2,1,0:T(8,128)(2,1)S(1)}, u32[]{:S(2)}, u32[]{:S(2)}) async-start(bf16[16,8,1664]{2,1,0:T(8,128)(2,1)} %get-tuple-element.20), calls=%async_computation.3 | async-start | bytes 851968 | tf_op jit(solution)/shard_map/all_to_all | solution.py:43
  106.2 0.0 all-gather.11.cloned.1.call-start
  106.2 9.5 %all-to-all-done.3.got_ref = bf16[16,8,1664]{2,1,0:T(8,128)(2,1)S(1)} async-done(((bf16[16,8,1664]{2,1,0:T(8,128)(2,1)}), bf16[16,8,1664]{2,1,0:T(8,128)(2,1)S(1)}, u32[]{:S(2)}, u32[]{:S(2)}) %all-to-all-start.3) | async-done | bytes 426016 | tf_op jit(solution)/shard_map/all_to_all | solution.py:43
  115.7 2.3 %copy-done.3 = bf16[8,512,512]{2,1,0:T(8,128)(2,1)S(1)} copy-done((bf16[8,512,512]{2,1,0:T(8,128)(2,1)S(1)}, bf16[8,512,512]{2,1,0:T(8,128)(2,1)}, u32[]{:S(2)}) %copy-start.3) | copy-done | bytes 4194328
  118.0 0.6 shard_map.88
  118.6 12.0 %all_to_all.53.got_ref = bf16[16,8,1024]{2,1,0:T(8,128)(2,1)} all-to-all(bf16[16,8,1024]{2,1,0:T(8,128)(2,1)S(1)} %shard_map.88), channel_id=1, replica_groups=mesh['segment'=8,'wide'=16] {'wide'}, dimensions={0} | all-to-all | bytes 524288 | tf_op jit(solution)/shard_map/all_to_all | solution.py:43
  130.6 0.0 all-gather.13.cloned.1.call-start
  130.7 3.4 %copy-done.1 = bf16[16,512,512]{2,1,0:T(8,128)(2,1)S(1)} copy-done((bf16[16,512,512]{2,1,0:T(8,128)(2,1)S(1)}, bf16[16,512,512]{2,1,0:T(8,128)(2,1)}, u32[]{:S(2)}) %copy-start.1) | copy-done | bytes 8388632
  134.0 0.9 copy-done.10
  135.0 2.2 shard_map.89
  137.2 12.5 %all_to_all.54.got_ref = bf16[16,8,1664]{2,1,0:T(8,128)(2,1)S(1)} all-to-all(bf16[16,8,1664]{2,1,0:T(8,128)(2,1)S(1)} %get-tuple-element.22), channel_id=1, replica_groups=mesh['segment'=8,'wide'=16] {'wide'}, dimensions={0} | all-to-all | bytes 851968 | tf_op jit(solution)/shard_map/all_to_all | solution.py:43
  149.7 0.6 shard_map.90
  150.3 12.0 %all_to_all.55.got_ref = bf16[16,8,1024]{2,1,0:T(8,128)(2,1)} all-to-all(bf16[16,8,1024]{2,1,0:T(8,128)(2,1)S(1)} %shard_map.90), channel_id=1, replica_groups=mesh['segment'=8,'wide'=16] {'wide'}, dimensions={0} | all-to-all | bytes 524288 | tf_op jit(solution)/shard_map/all_to_all | solution.py:43
  162.3 0.1 select_reduce_fusion.1
  162.4 0.2 select_reduce_fusion
  162.6 0.1 copy.26
  162.7 0.1 min.18.slots
  162.8 3.4 %copy-done.2 = bf16[16,512,512]{2,1,0:T(8,128)(2,1)S(1)} copy-done((bf16[16,512,512]{2,1,0:T(8,128)(2,1)S(1)}, bf16[16,512,512]{2,1,0:T(8,128)(2,1)}, u32[]{:S(2)}) %copy-start.2) | copy-done | bytes 8388632
  166.2 0.9 copy-done.11
  167.1 2.9 %shard_map.91 = (bf16[16,8,1664]{2,1,0:T(8,128)(2,1)}, bf16[128,512]{1,0:T(8,128)(2,1)}) custom-call(s32[2]{0:T(128)S(1)} %pad_add_fusion.where, bf16[16,8,1024]{2,1,0:T(8,128)(2,1)S(1)} %copy-done.11, bf16[128,512]{1,0:T(8,128)(2,1)S(1)} %get-tuple-element.23.states_ref, bf16[8,2,512,512]{3,2,1,0:T(8,128)(2,1)S(1)} %bitcast.30), custom_call_target="tpu_custom_call" | custom-call | flops 335544320 | bytes 1114112 | tf_op jit(solution)/shard_map/pallas_call | solution.py:57
  170.1 3.6 %all-to-all-start.7 = ((bf16[16,8,1664]{2,1,0:T(8,128)(2,1)}), bf16[16,8,1664]{2,1,0:T(8,128)(2,1)S(1)}, u32[]{:S(2)}, u32[]{:S(2)}) async-start(bf16[16,8,1664]{2,1,0:T(8,128)(2,1)} %get-tuple-element.24), calls=%async_computation.7 | async-start | bytes 851968 | tf_op jit(solution)/shard_map/all_to_all | solution.py:43
  173.7 0.1 minimum_bitcast_fusion
  173.7 0.1 copy.25
  173.8 0.5 copy.30.limit_ref
  174.4 1.6 copy-done.12
  176.0 2.4 %shard_map.92.rest_0_ = bf16[16,8,4,512]{3,2,1,0:T(4,128)(2,1)} custom-call(s32[16]{0:T(128)S(1)} %min.18.slots, bf16[16,8,4,512]{3,2,1,0:T(4,128)(2,1)S(1)} %copy-done.6, bf16[8,16,512]{2,1,0:T(8,128)(2,1)S(1)} %bitcast.36, s32[8,64,1]{2,1,0:T(8,128)S(1)} %copy.30.limit_ref, bf16[8,128,1024]{2,1,0:T(8,128)(2,1)S(1)} %copy-done.12), custom_call_target="tpu_custom_call" | custom-call | flops 67108864 | bytes 786432 | tf_op jit(solution)/shard_map/pallas_call | solution.py:300
  178.4 4.8 %all-to-all-done.7.got_ref = bf16[16,8,1664]{2,1,0:T(8,128)(2,1)S(1)} async-done(((bf16[16,8,1664]{2,1,0:T(8,128)(2,1)}), bf16[16,8,1664]{2,1,0:T(8,128)(2,1)S(1)}, u32[]{:S(2)}, u32[]{:S(2)}) %all-to-all-start.7) | async-done | bytes 426016 | tf_op jit(solution)/shard_map/all_to_all | solution.py:43
  183.2 2.3 %copy-done.5 = bf16[8,512,512]{2,1,0:T(8,128)(2,1)S(1)} copy-done((bf16[8,512,512]{2,1,0:T(8,128)(2,1)S(1)}, bf16[8,512,512]{2,1,0:T(8,128)(2,1)}, u32[]{:S(2)}) %copy-start.5) | copy-done | bytes 4194328
  185.4 1.3 shard_map.93
  186.7 4.8 %all-to-all-start.8 = ((bf16[8,8,1024]{2,1,0:T(8,128)(2,1)}), bf16[8,8,1024]{2,1,0:T(8,128)(2,1)S(1)}, u32[]{:S(2)}, u32[]{:S(2)}) async-start(bf16[8,8,1024]{2,1,0:T(8,128)(2,1)} %shard_map.93), calls=%async_computation.8 | async-start | bytes 262144 | tf_op jit(solution)/shard_map/all_to_all | solution.py:43
  191.6 1.6 copy-done.13
  193.1 2.4 %shard_map.94.rest_0_ = bf16[16,8,4,512]{3,2,1,0:T(4,128)(2,1)} custom-call(s32[16]{0:T(128)S(1)} %min.18.slots, bf16[16,8,4,512]{3,2,1,0:T(4,128)(2,1)S(1)} %copy-done.6, bf16[8,16,512]{2,1,0:T(8,128)(2,1)S(1)} %bitcast.37, s32[8,64,1]{2,1,0:T(8,128)S(1)} %copy.30.limit_ref, bf16[8,128,1024]{2,1,0:T(8,128)(2,1)S(1)} %copy-done.13, ...), custom_call_target="tpu_custom_call", output_to_operand_aliasing={{}: (5, {})} | custom-call | flops 67108864 | bytes 786432 | tf_op jit(solution)/shard_map/pallas_call | solution.py:300
  195.5 2.1 all-to-all-done.8.got_ref
  197.7 1.4 shard_map.95
  199.1 3.6 %all-to-all-start.9 = ((bf16[16,8,2048]{2,1,0:T(8,128)(2,1)}), bf16[16,8,2048]{2,1,0:T(8,128)(2,1)S(1)}, u32[]{:S(2)}, u32[]{:S(2)}) async-start(bf16[16,8,2048]{2,1,0:T(8,128)(2,1)} %shard_map.95), calls=%async_computation.9 | async-start | bytes 1048576 | tf_op jit(solution)/shard_map/all_to_all | solution.py:43
  202.7 1.6 copy-done.14
  204.3 2.4 %shard_map.96.carried_ref = bf16[16,8,4,512]{3,2,1,0:T(4,128)(2,1)} custom-call(s32[16]{0:T(128)S(1)} %min.18.slots, bf16[16,8,4,512]{3,2,1,0:T(4,128)(2,1)S(1)} %copy-done.6, bf16[8,16,512]{2,1,0:T(8,128)(2,1)S(1)} %bitcast.38, s32[8,64,1]{2,1,0:T(8,128)S(1)} %copy.30.limit_ref, ...), custom_call_target="tpu_custom_call", output_to_operand_aliasing={{}: (5, {})} | custom-call | flops 67108864 | bytes 786432 | tf_op jit(solution)/shard_map/pallas_call | solution.py:300
  206.7 7.6 %all-to-all-done.9.pages_ref = bf16[16,8,2048]{2,1,0:T(8,128)(2,1)S(1)} async-done(((bf16[16,8,2048]{2,1,0:T(8,128)(2,1)}), bf16[16,8,2048]{2,1,0:T(8,128)(2,1)S(1)}, u32[]{:S(2)}, u32[]{:S(2)}) %all-to-all-start.9) | async-done | bytes 524320 | tf_op jit(solution)/shard_map/all_to_all | solution.py:43
  214.2 1.6 shard_map.97
  (46 shorter events, 0.4 us)
Async XLA Ops:
  6.5 7.4 %copy-start.8 = (bf16[4,256,512]{2,1,0:T(8,128)(2,1)S(1)}, bf16[4,256,512]{2,1,0:T(8,128)(2,1)}, u32[]{:S(2)}) copy-start(bf16[4,256,512]{2,1,0:T(8,128)(2,1)} %param.8) | copy-start | bytes 3145732
  6.5 88.7 %all-gather.15.cloned.1.call-start = ((), (), s32[]{:S(2)}) async-start(), calls=%async_computation.14 | async-start | bytes 9437184 | tf_op jit(solution)/shard_map/all_gather | solution.py:349
  6.5 1.1 copy-start.15
  7.7 1.0 copy-start.16
  8.7 0.7 copy-start.17
  11.0 95.3 %all-gather.7.cloned.1.call-start = ((), (), s32[]{:S(2)}) async-start(), calls=%async_computation.10 | async-start | bytes 4718592 | tf_op jit(solution)/shard_map/all_gather | solution.py:378
  11.0 3.0 %collective-permute-start = (bf16[2,512,512]{2,1,0:T(8,128)(2,1)}, bf16[2,512,512]{2,1,0:T(8,128)(2,1)S(1)}, u32[]{:S(2)}, u32[]{:S(2)}) collective-permute-start(bf16[2,512,512]{2,1,0:T(8,128)(2,1)} %shard_map.82.both_ref), channel_id=1, source_target_pairs={{0,16},{16,0},{32,48},{48,32},{64,80},{80,64},{96,112},{112,96},{1... | collective-permute-start | bytes 3145736 | tf_op jit(solution)/shard_map/ppermute | solution.py:48
  70.0 104.4 %all-gather.9.cloned.1.call-start = ((), (), s32[]{:S(2)}) async-start(), calls=%async_computation.11 | async-start | bytes 2359296 | tf_op jit(solution)/shard_map/all_gather | solution.py:454
  70.0 2.2 collective-permute-start.1
  72.2 1.0 copy-start.7
  74.3 6.8 %collective-permute-start.2 = (bf16[8,1024]{1,0:T(8,128)(2,1)S(1)}, bf16[8,1024]{1,0:T(8,128)(2,1)S(1)}, u32[]{:S(2)}, u32[]{:S(2)}) collective-permute-start(bf16[8,1024]{1,0:T(8,128)(2,1)S(1)} %get-tuple-element.37), channel_id=1, source_target_pairs={{0,32},{16,48},{1,33},{17,49},{2,34},{18,50},{3,35},{19,51},{4,36}... | collective-permute-start | bytes 49160 | tf_op jit(solution)/shard_map/ppermute | solution.py:389
  77.6 3.8 %collective-permute-start.3 = (bf16[8,1024]{1,0:T(8,128)(2,1)S(1)}, bf16[8,1024]{1,0:T(8,128)(2,1)S(1)}, u32[]{:S(2)}, u32[]{:S(2)}) collective-permute-start(bf16[8,1024]{1,0:T(8,128)(2,1)S(1)} %get-tuple-element.36), channel_id=1, source_target_pairs={{0,64},{16,80},{1,65},{17,81},{2,66},{18,82},{3,67},{19,83},{4,68}... | collective-permute-start | bytes 49160 | tf_op jit(solution)/shard_map/ppermute | solution.py:389
  79.8 2.9 %collective-permute-start.4 = (bf16[8,1024]{1,0:T(8,128)(2,1)S(1)}, bf16[8,1024]{1,0:T(8,128)(2,1)S(1)}, u32[]{:S(2)}, u32[]{:S(2)}) collective-permute-start(bf16[8,1024]{1,0:T(8,128)(2,1)S(1)} %get-tuple-element.35), channel_id=1, source_target_pairs={{0,96},{16,112},{1,97},{17,113},{2,98},{18,114},{3,99},{19,115},{4... | collective-permute-start | bytes 49160 | tf_op jit(solution)/shard_map/ppermute | solution.py:389
  95.2 3.5 %copy-start = (bf16[16,512,512]{2,1,0:T(8,128)(2,1)S(1)}, bf16[16,512,512]{2,1,0:T(8,128)(2,1)}, u32[]{:S(2)}) copy-start(bf16[16,512,512]{2,1,0:T(8,128)(2,1)} %all-gather.15.cloned.1.call-done) | copy-start | bytes 25165828
  98.7 0.9 copy-start.9
  102.6 13.1 %all-to-all-start.3 = ((bf16[16,8,1664]{2,1,0:T(8,128)(2,1)}), bf16[16,8,1664]{2,1,0:T(8,128)(2,1)S(1)}, u32[]{:S(2)}, u32[]{:S(2)}) async-start(bf16[16,8,1664]{2,1,0:T(8,128)(2,1)} %get-tuple-element.20), calls=%async_computation.3 | async-start | bytes 851968 | tf_op jit(solution)/shard_map/all_to_all | solution.py:43
  106.2 85.4 %all-gather.11.cloned.1.call-start = ((), (), s32[]{:S(2)}) async-start(), calls=%async_computation.12 | async-start | bytes 2359296 | tf_op jit(solution)/shard_map/all_gather | solution.py:454
  115.7 2.3 %copy-start.3 = (bf16[8,512,512]{2,1,0:T(8,128)(2,1)S(1)}, bf16[8,512,512]{2,1,0:T(8,128)(2,1)}, u32[]{:S(2)}) copy-start(bf16[8,512,512]{2,1,0:T(8,128)(2,1)} %all-gather.7.cloned.1.call-done.cross_ref) | copy-start | bytes 12582916
  130.6 72.0 %all-gather.13.cloned.1.call-start = ((), (), s32[]{:S(2)}) async-start(), calls=%async_computation.13 | async-start | bytes 2359296 | tf_op jit(solution)/shard_map/all_gather | solution.py:454
  130.7 3.4 %copy-start.1 = (bf16[16,512,512]{2,1,0:T(8,128)(2,1)S(1)}, bf16[16,512,512]{2,1,0:T(8,128)(2,1)}, u32[]{:S(2)}) copy-start(bf16[16,512,512]{2,1,0:T(8,128)(2,1)} %all-gather.15.cloned.1.call-done) | copy-start | bytes 25165828
  134.0 0.9 copy-start.10
  135.0 14.7 %copy-start.4 = (bf16[8,512,512]{2,1,0:T(8,128)(2,1)S(1)}, bf16[8,512,512]{2,1,0:T(8,128)(2,1)}, u32[]{:S(2)}) copy-start(bf16[8,512,512]{2,1,0:T(8,128)(2,1)} %all-gather.7.cloned.1.call-done.cross_ref) | copy-start | bytes 12582916
  149.7 12.6 %copy-start.19 = (s32[8,8,1]{1,2,0:T(1,128)S(1)}, s32[8,8,1]{1,2,0:T(1,128)}, u32[]{:S(2)}) copy-start(s32[8,8,1]{1,2,0:T(1,128)} %param.12) | copy-start | bytes 772
  162.8 3.4 %copy-start.2 = (bf16[16,512,512]{2,1,0:T(8,128)(2,1)S(1)}, bf16[16,512,512]{2,1,0:T(8,128)(2,1)}, u32[]{:S(2)}) copy-start(bf16[16,512,512]{2,1,0:T(8,128)(2,1)} %all-gather.15.cloned.1.call-done) | copy-start | bytes 25165828
  166.2 0.9 copy-start.11
  167.1 6.5 %copy-start.20 = (s32[16,8]{0,1:T(8,128)S(1)}, s32[16,8]{0,1:T(8,128)}, u32[]{:S(2)}) copy-start(s32[16,8]{0,1:T(8,128)} %param.15) | copy-start | bytes 1540
  167.1 7.1 %copy-start.18 = (bf16[16,8,512]{2,1,0:T(8,128)(2,1)S(1)}, bf16[16,8,512]{2,1,0:T(8,128)(2,1)}, u32[]{:S(2)}) copy-start(bf16[16,8,512]{2,1,0:T(8,128)(2,1)} %param.14) | copy-start | bytes 393220
  167.1 7.2 %copy-start.6 = (bf16[16,8,4,512]{3,2,1,0:T(4,128)(2,1)S(1)}, bf16[16,8,4,512]{3,2,1,0:T(4,128)(2,1)}, u32[]{:S(2)}) copy-start(bf16[16,8,4,512]{3,2,1,0:T(4,128)(2,1)} %q_ref.7) | copy-start | bytes 1572868
  170.1 13.1 %all-to-all-start.7 = ((bf16[16,8,1664]{2,1,0:T(8,128)(2,1)}), bf16[16,8,1664]{2,1,0:T(8,128)(2,1)S(1)}, u32[]{:S(2)}, u32[]{:S(2)}) async-start(bf16[16,8,1664]{2,1,0:T(8,128)(2,1)} %get-tuple-element.24), calls=%async_computation.7 | async-start | bytes 851968 | tf_op jit(solution)/shard_map/all_to_all | solution.py:43
  174.4 1.6 copy-start.12
  183.2 2.3 %copy-start.5 = (bf16[8,512,512]{2,1,0:T(8,128)(2,1)S(1)}, bf16[8,512,512]{2,1,0:T(8,128)(2,1)}, u32[]{:S(2)}) copy-start(bf16[8,512,512]{2,1,0:T(8,128)(2,1)} %all-gather.7.cloned.1.call-done.cross_ref) | copy-start | bytes 12582916
  186.7 10.9 %all-to-all-start.8 = ((bf16[8,8,1024]{2,1,0:T(8,128)(2,1)}), bf16[8,8,1024]{2,1,0:T(8,128)(2,1)S(1)}, u32[]{:S(2)}, u32[]{:S(2)}) async-start(bf16[8,8,1024]{2,1,0:T(8,128)(2,1)} %shard_map.93), calls=%async_computation.8 | async-start | bytes 262144 | tf_op jit(solution)/shard_map/all_to_all | solution.py:43
  191.5 1.6 copy-start.13
  199.1 15.2 %all-to-all-start.9 = ((bf16[16,8,2048]{2,1,0:T(8,128)(2,1)}), bf16[16,8,2048]{2,1,0:T(8,128)(2,1)S(1)}, u32[]{:S(2)}, u32[]{:S(2)}) async-start(bf16[16,8,2048]{2,1,0:T(8,128)(2,1)} %shard_map.95), calls=%async_computation.9 | async-start | bytes 1048576 | tf_op jit(solution)/shard_map/all_to_all | solution.py:43
  202.7 1.6 copy-start.14
Sparse Core Ops, SparseCore 0:
  11.1 52.1 all-gather.14
  70.1 29.4 all-gather.6
  101.3 25.1 all-gather.8
  130.7 23.1 all-gather.10
  162.4 23.1 all-gather.12

commit v5 on v4

--- a/solution.py
+++ b/solution.py
@@ -46,6 +46,10 @@
 def core_swap(x):
     length = lax.axis_size("segment")
     return lax.ppermute(x, "segment", [(i, i ^ 1) for i in range(length)])
+
+
+def held_in_hbm(x):
+    return pltpu.with_memory_space_constraint(x, pltpu.HBM)
 
 
 def whole(shape):
@@ -69,7 +73,7 @@
     )(*scalars, *operands)
 
 
-def weights_kernel(latent_ref, gain_ref, back_ref, both_ref, latent, sems):
+def weights_kernel(where, latent_ref, gain_ref, back_ref, both_ref, lent_ref, latent, sems):
     copies = [
         pltpu.make_async_copy(latent_ref.at[0], latent, sems.at[0]),
         pltpu.make_async_copy(back_ref.at[0], both_ref.at[1], sems.at[1]),
@@ -84,48 +88,73 @@
     both_ref[0] = dot(gains, latent[...]).astype(bf16)
     copies[1].wait()
 
-
-def home_kernel(where, states_ref, both_ref, other_ref, out_ref):
+    @pl.when(where[0] == 0)
+    def _():
+        lent_ref[...] = both_ref[0]
+
+    @pl.when(where[0] != 0)
+    def _():
+        lent_ref[...] = both_ref[1]
+
+
+def home_kernel(where, states_ref, both_ref, lent_ref, *out_refs):
     groups, _, rows, width = states_ref.shape
-    lat = both_ref.shape[2]
-    wide = out_ref.shape[0]
-    share = rows // wide
     tokens = states_ref[...].reshape(groups * rows, width)
 
-    def put(product, at):
+    def products(weight):
+        product = dot(tokens, weight).astype(bf16)
         for group in range(groups):
-            part = product[group * rows : (group + 1) * rows]
-            part = part.reshape(wide, share, part.shape[1]).astype(bf16)
-            out_ref[:, group * share : (group + 1) * share, at : at + part.shape[2]] = part
-
-    def partials(even_ref, odd_ref):
-        put(dot(tokens, even_ref[0]), LANES)
-        put(dot(tokens, odd_ref[0]), LANES + lat)
-        put(dot_t(tokens, even_ref[1]), LANES + 2 * lat)
-
-    def put_cross(cross):
-        cross = cross.reshape(wide, lat // wide, lat).astype(bf16)
-        out_ref[:, :, LANES + 3 * lat :] = cross
-
-    put(square_columns(tokens.astype(f32)), 0)
+            out_refs[group][...] = product[group * rows : (group + 1) * rows]
+
+    @pl.when(where[0] == 0)
+    def _():
+        products(both_ref[0])
+
+    @pl.when(where[0] != 0)
+    def _():
+        products(lent_ref[...])
 
     @pl.when(where[1] == 0)
     def _():
-        put_cross(dot_t(both_ref[1], both_ref[1]))
-        partials(both_ref, other_ref)
+        out_refs[groups][...] = dot_t(both_ref[1], both_ref[1]).astype(bf16)
 
     @pl.when(where[1] != 0)
     def _():
-        put_cross(dot(other_ref[1], both_ref[0]))
-        partials(other_ref, both_ref)
-
-
-def home_sum_kernel(got_ref, sums_ref, cross_ref):
+        out_refs[groups][...] = dot(lent_ref[...], both_ref[0]).astype(bf16)
+
+
+def home_send_kernel(where, home_ref, a_ref, b_ref, c_ref, cross_ref, states_ref, out_ref):
+    wide, share, _ = out_ref.shape
+    rows, lat = home_ref.shape
+    taken = a_ref[...].astype(f32) + b_ref[...].astype(f32) + c_ref[...].astype(f32)
+    product = jnp.where(where[0] < 2, home_ref[...].astype(f32), taken)
+    squares = square_columns(states_ref[...].reshape(rows, states_ref.shape[3]).astype(f32))
+    out_ref[:, :, :LANES] = squares.reshape(wide, share, LANES).astype(bf16)
+    out_ref[:, :, LANES : LANES + lat] = product.reshape(wide, share, lat).astype(bf16)
+    parts = cross_ref.shape[0] // rows
+    cross = cross_ref[...].astype(f32).reshape(wide, parts, share, lat)
+    for part in range(parts):
+        at = LANES + (1 + part) * lat
+        out_ref[:, :, at : at + lat] = cross[:, part].astype(bf16)
+
+
+def home_sum_kernel(width, got_ref, out_ref):
+    wide, high, lat = out_ref.shape
     summed = jnp.sum(got_ref[...].astype(f32), axis=0)
-    sums_ref[...] = summed[:, : sums_ref.shape[1]]
-    cross = summed[:, sums_ref.shape[1] :].astype(bf16)
-    for place in range(cross_ref.shape[0]):
-        cross_ref[place] = cross
+    squares = summed[:, 0:1] + summed[:, 1:2]
+    latent = summed[:, LANES : LANES + lat] * lax.rsqrt(squares / width + eps_norm)
+    parts = [summed[:, at : at + lat] for at in range(LANES + lat, summed.shape[1], lat)]
+    block = jnp.concatenate(parts + [latent], axis=0).astype(bf16)
+    for place in range(wide):
+        out_ref[place] = block
+
+
+def single_kernel(width, got_ref, out_ref):
+    summed = jnp.sum(got_ref[...].astype(f32), axis=0)
+    squares = summed[:, 0:1] + summed[:, 1:2]
+    latent = (summed[:, LANES:] * lax.rsqrt(squares / width + eps_norm)).astype(bf16)
+    for place in range(out_ref.shape[0]):
+        out_ref[place] = latent
 
 
 def chain(width, summed, gram, mixing):
@@ -141,33 +170,12 @@
     return first, second
 
 
-def home_pair_kernel(width, where, sums_ref, mine_ref, other_ref, out_ref):
-    def run(gram_ref, mixing_ref):
-        parts = chain(width, sums_ref[...], lambda: gram_ref[...], lambda: mixing_ref[...])
-        lat = parts[0].shape[1]
-        for i, part in enumerate(parts):
-            part = part.astype(f32).reshape(out_ref.shape[:2] + (lat,)).astype(bf16)
-            out_ref[:, :, i * lat : (i + 1) * lat] = part
-
-    @pl.when(where[1] == 0)
-    def _():
-        run(mine_ref, other_ref)
-
-    @pl.when(where[1] != 0)
-    def _():
-        run(other_ref, mine_ref)
-
-
-def home_send_kernel(where, mine_ref, a_ref, b_ref, c_ref, out_ref):
-    taken = a_ref[...].astype(f32) + b_ref[...].astype(f32) + c_ref[...].astype(f32)
-    latent = jnp.where(where[0] < 2, mine_ref[0].astype(f32), taken).astype(bf16)
-    for place in range(out_ref.shape[0]):
-        out_ref[place] = latent
-
-
-def advance_kernel(before, layers, where, got_ref, states_ref, both_ref, out_ref, state_ref, *rest):
-    got, weights, sems = rest
-    needed = [(layer, 1) for layer in before] + [(layer, 0) for layer in layers] + [(layers[0], 1)]
+def advance_kernel(before, layers, held, where, got_ref, states_ref, both_ref, *rest):
+    got, weights, sems = rest[-3:]
+    out_ref, state_ref = rest[held : held + 2]
+    needed = [(layer, 1) for layer in before] + [(layer, 0) for layer in layers]
+    if len(layers) == 2:
+        needed.append((layers[0], 1))
     taking = pltpu.make_async_copy(got_ref, got, sems.at[len(needed)])
     taking.start()
     copies = [
@@ -181,7 +189,12 @@
     lat = weights.shape[2]
     state = states_ref[...].reshape(rows, weights.shape[1]).astype(f32)
     taking.wait()
-    activated = silu(got[...].astype(f32).reshape(rows, got.shape[2]))
+    latents = got[...].astype(f32).reshape(rows, got.shape[2])
+    if held:
+        earlier_ref, held_ref = rest[0], rest[3]
+        held_ref[:, :lat] = earlier_ref[...].astype(f32).reshape(rows, lat).astype(bf16)
+        held_ref[:, lat:] = latents.astype(bf16)
+    activated = silu(latents)
     for i in range(len(before)):
         copies[i].wait()
         state = state + dot(activated[:, i * lat : (i + 1) * lat], weights[i])
@@ -290,7 +303,7 @@
         whole(pages.shape) if last else in_hbm,
     ]
     scalars = [] if last else [slots]
-    operands = scalars + [queries, new, limit, pages]
+    operands = scalars + [queries, new, limit, pages if last else held_in_hbm(pages)]
     aliases = {}
     if carried is not None:
         in_specs.append(in_hbm)
@@ -337,88 +350,99 @@
         return jax.ShapeDtypeStruct(shape, bf16)
 
     size = (2, local_width, lat)
-    (both,) = call(
+    both, lent = call(
         weights_kernel,
         [in_hbm, whole(norm_gain.shape), in_hbm],
-        [whole(size)],
-        [array(*size)],
-        [w_latent, norm_gain, w_back],
-        scratch=[pltpu.VMEM(size[1:], bf16), pltpu.SemaphoreType.DMA((2,))],
+        [whole(size), whole(size[1:])],
+        [array(*size), array(*size[1:])],
+        [held_in_hbm(w_latent), norm_gain, held_in_hbm(w_back)],
+        [where],
+        [pltpu.VMEM(size[1:], bf16), pltpu.SemaphoreType.DMA((2,))],
         flops=2 * local_width**3,
     )
-    every = lax.all_gather(both, "segment", axis=0)
-    other = core_swap(both)
+    every = held_in_hbm(lax.all_gather(both, "segment", axis=0))
+    lent = lax.ppermute(lent, "segment", [(i, i + 1) for i in range(0, segments, 2)])
 
     states = prompt_states.reshape(segments // 2, 2, mine, local_width)
-    high = lat // wide
-    partial_columns = LANES + 3 * lat
-    columns = partial_columns + lat
-    (sent,) = call(
+    groups = segments // 2
+    own_states = pl.BlockSpec((1, 1, mine, local_width), lambda i, s: (s[0] >> 1, s[1], 0, 0))
+    *home, cross = call(
         home_kernel,
         [
-            pl.BlockSpec((segments // 2, 1, mine, local_width), lambda i, s: (0, s[1], 0, 0)),
+            pl.BlockSpec((groups, 1, mine, local_width), lambda i, s: (0, s[1], 0, 0)),
             whole(size),
-            whole(size),
+            whole(size[1:]),
         ],
-        [whole((wide, high, columns))],
-        [array(wide, high, columns)],
-        [states, both, other],
+        [whole((mine, lat))] * groups + [whole((lat, lat))],
+        [array(mine, lat)] * groups + [array(lat, lat)],
+        [states, both, lent],
         [where],
-        flops=4 * 2 * local_width**3,
-    )
-    got = exchanged(sent, "wide")
-    sums, sent = call(
-        home_sum_kernel,
-        [whole(got.shape)],
-        [whole((high, partial_columns)), whole((wide, high, lat))],
-        [jax.ShapeDtypeStruct((high, partial_columns), f32), array(wide, high, lat)],
-        [got],
-    )
-    cross = exchanged(sent, "wide").reshape(lat, lat)
-    crosses = lax.all_gather(cross, "segment", axis=0)
-    (latent,) = call(
-        functools.partial(home_pair_kernel, width),
-        [whole(sums.shape), whole(cross.shape), whole(cross.shape)],
-        [whole((segments // 2, share, 2 * lat))],
-        [array(segments // 2, share, 2 * lat)],
-        [sums, cross, core_swap(cross)],
-        [where],
-        flops=2 * 2 * high * lat * lat,
+        flops=2 * 2 * local_width**3,
     )
     taken = [
-        lax.ppermute(latent[hop], "segment", [(0, 2 * hop), (1, 2 * hop + 1)])
-        for hop in range(1, segments // 2)
+        lax.ppermute(home[hop], "segment", [(0, 2 * hop), (1, 2 * hop + 1)])
+        for hop in range(1, groups)
     ]
+    high = lat // wide
+    columns = LANES + lat + high // share * lat
     (sent,) = call(
         home_send_kernel,
-        [whole((1, share, 2 * lat))] + [whole((share, 2 * lat))] * 3,
-        [whole((wide, share, 2 * lat))],
-        [array(wide, share, 2 * lat)],
-        [latent] + taken,
+        [whole((mine, lat))] * groups + [whole((lat, lat)), own_states],
+        [whole((wide, share, columns))],
+        [array(wide, share, columns)],
+        [home[0]] + taken + [cross, states],
         [where],
     )
     got = exchanged(sent, "wide")
-
-    def advance(before, following, got, state):
-        if state.ndim == 4:
-            spec = pl.BlockSpec((1, 1, mine, local_width), lambda i, s: (s[0] >> 1, s[1], 0, 0))
-        else:
-            spec = whole(state.shape)
-        shapes = [array(wide, share, partial_columns), array(mine, local_width)]
+    (sent,) = call(
+        functools.partial(home_sum_kernel, width),
+        [whole(got.shape)],
+        [whole((wide, high + share, lat))],
+        [array(wide, high + share, lat)],
+        [got],
+    )
+    got = exchanged(sent, "wide")
+    crosses = lax.all_gather(got[:, :high].reshape(lat, lat), "segment", axis=0)
+    crosses = held_in_hbm(crosses)
+    got = got[:, high:]
+
+    def advance(before, following, got, state, earlier=None):
+        held = earlier is not None
+        count = len(following) + (len(following) == 2)
+        shapes = [array(wide, share, LANES + count * lat), array(mine, local_width)]
+        in_specs = [in_hbm, own_states if state.ndim == 4 else whole(state.shape), in_hbm]
+        operands = [held_in_hbm(got), state, every]
+        if held:
+            shapes.append(array(mine, 2 * lat))
+            in_specs.append(whole(earlier.shape))
+            operands.append(earlier)
+        needed = len(before) + count
         return call(
-            functools.partial(advance_kernel, before, following),
-            [in_hbm, spec, in_hbm],
+            functools.partial(advance_kernel, before, following, held),
+            in_specs,
             [whole(s.shape) for s in shapes],
             shapes,
-            [got, state, every],
+            operands,
             [where],
             [
                 pltpu.VMEM(got.shape, bf16),
-                pltpu.VMEM((5, local_width, lat), bf16),
-                pltpu.SemaphoreType.DMA((6,)),
+                pltpu.VMEM((needed, local_width, lat), bf16),
+                pltpu.SemaphoreType.DMA((needed + 1,)),
             ],
-            flops=2 * 5 * mine * lat * local_width,
+            flops=2 * needed * mine * lat * local_width,
         )
+
+    earlier = got
+    sent, state = advance((0,), (1,), got, states)
+    got = exchanged(sent, "wide")
+    (sent,) = call(
+        functools.partial(single_kernel, width),
+        [whole(got.shape)],
+        [whole((wide, share, lat))],
+        [array(wide, share, lat)],
+        [got],
+    )
+    got = exchanged(sent, "wide")
 
     def pair_step(even, got, copies):
         (sent,) = call(
@@ -449,10 +473,13 @@
         return decode_pair(layer, slots, queries, new, limit, pages, carried, last)
 
     pages = []
-    state = states
     for even in range(2, layers, 2):
-        pages.append(lax.all_gather(got.reshape(mine, 2 * lat), "segment", axis=0))
-        sent, state = advance((even - 2, even - 1), (even, even + 1), got, state)
+        if even == 2:
+            sent, state, held = advance((1,), (2, 3), got, state, earlier)
+        else:
+            held = got.reshape(mine, 2 * lat)
+            sent, state = advance((even - 2, even - 1), (even, even + 1), got, state)
+        pages.append(lax.all_gather(held, "segment", axis=0))
         got = exchanged(sent, "wide")
         if even < layers - 2:
             got = exchanged(pair_step(even, got, wide), "wide")

time: 224 us -> 209 us (0.933)
  local copies, waits for them, and re-layouts: 27 us -> 3.04 us
  Pallas kernels: 27.4 us -> 38 us
  blocking collectives: 101 us -> 94.6 us
  waiting for transfers between devices: 30.6 us -> 33.7 us
  starting transfers between devices: 22.6 us -> 24.9 us
    unnamed x43 -> x15, local copies, waits for them, and re-layouts: 26.3 us -> 0.82 us
    pallas_call x12 -> x13, Pallas kernels: 18.7 us -> 26.6 us  [call(): pl.pallas_call(body, grid_spec=pltpu.PrefetchScalarGridSpec(num_scalar_pr...]
    all_to_all x6 -> x7, blocking collectives: 101 us -> 94.6 us  [exchanged(): return lax.all_to_all(sent, axis, 0, 0, tiled=True)]
    pallas_call x4, Pallas kernels: 8.74 us -> 11.4 us  [decode_pair(): pl.pallas_call(last_decode_kernel if last else functools.partial(decode_k...]
    ppermute x5 -> x4, starting transfers between devices: 6.91 us -> 8.75 us  [the longest x3 7.42 us: shards(): lax.ppermute(home[hop], 'segment', [(0, 2 * hop), (1, 2 * hop + 1)])]
    ppermute x5 -> x4, waiting for transfers between devices: 6.44 us -> 7.49 us  [the longest x3 6 us: shards(): lax.ppermute(home[hop], 'segment', [(0, 2 * hop), (1, 2 * hop + 1)])]
  transfers between devices with their start and end apart: 14 -> 13, of which waited for: 8 -> 8; matrix products, arithmetic and copies ran while one was open for 1% -> 1% of each run, Pallas kernels for 11% -> 16%
where the time goes in v5:
time: 209 us; the launch traced here: 208 us
  blocking collectives  94.6 us (45%)
  Pallas kernels  38 us (18%)
  waiting for transfers between devices  33.7 us (16%)
  starting transfers between devices  24.9 us (12%)
  between operations  13.4 us (6%)
  local copies, waits for them, and re-layouts  3.04 us (1%)
    all_to_all x7, blocking collectives, exchanged(): return lax.all_to_all(sent, axis, 0, 0, tiled=True)  94.6 us
    pallas_call x13, Pallas kernels, call(): pl.pallas_call(body, grid_spec=pltpu.PrefetchScalarGridSpec(num_scalar_pr...  26.6 us
    all_to_all x4, waiting for transfers between devices, exchanged(): return lax.all_to_all(sent, axis, 0, 0, tiled=True)  26.1 us
    all_to_all x4, starting transfers between devices, exchanged(): return lax.all_to_all(sent, axis, 0, 0, tiled=True)  16 us
    pallas_call x4, Pallas kernels, decode_pair(): pl.pallas_call(last_decode_kernel if last else functools.partial(decode_k...  11.4 us
    ppermute x3, starting transfers between devices, shards(): lax.ppermute(home[hop], 'segment', [(0, 2 * hop), (1, 2 * hop + 1)])  7.42 us
    ppermute x3, waiting for transfers between devices, shards(): lax.ppermute(home[hop], 'segment', [(0, 2 * hop), (1, 2 * hop + 1)])  6 us
  transfers between devices with their start and end apart: 13, of which 8 were waited for; matrix products, arithmetic and copies ran while one was open for 1% of the time, Pallas kernels for 16%

profile of v5, /device:TPU:0, one launch (start us, length us, event | category | flops | bytes accessed | tf_op | source)
XLA Modules:
  0.0 208.2 jit_solution(7814005799986633888)
XLA Ops:
  6.5 0.1 pad_add_fusion.where
  6.6 0.8 copy-done.3
  7.4 3.1 %shard_map.82 = (bf16[2,512,512]{2,1,0:T(8,128)(2,1)}, bf16[512,512]{1,0:T(8,128)(2,1)S(1)}) custom-call(s32[2]{0:T(128)S(1)} %pad_add_fusion.where, bf16[1,512,512]{2,1,0:T(8,128)(2,1)} %latent_ref.1, bf16[1,512]{1,0:T(2,128)(2,1)S(1)} %copy-done.3, bf16[1,512,512]{2,1,0:T(8,128)(2,1)} %back_ref.1), custom_call_target="tpu_custom_call" | custom-call | flops 268435456 | bytes 3145728 | tf_op jit(solution)/shard_map/pallas_call | solution.py:61
  10.4 0.0 all-gather.14.cloned.1.call-update
  10.5 0.0 all-gather.8.cloned.1.call-start
  10.5 1.3 collective-permute-start
  11.8 1.5 collective-permute-done.lent_ref
  13.3 2.7 %shard_map.83 = (bf16[128,512]{1,0:T(8,128)(2,1)S(1)}, bf16[128,512]{1,0:T(8,128)(2,1)S(1)}, bf16[128,512]{1,0:T(8,128)(2,1)S(1)}, bf16[128,512]{1,0:T(8,128)(2,1)S(1)}, bf16[512,512]{1,0:T(8,128)(2,1)S(1)}) custom-call(s32[2]{0:T(128)S(1)} %pad_add_fusion.where, bf16[4,2,128,512]{3,2,1,0:T(8,128)(2,1)S(1)} %bitcast.21, ...), custom_call_target="tpu_custom_call" | custom-call | flops 536870912 | bytes 2097152 | tf_op jit(solution)/shard_map/pallas_call | solution.py:61
  16.0 3.9 %collective-permute-start.1 = (bf16[128,512]{1,0:T(8,128)(2,1)S(1)}, bf16[128,512]{1,0:T(8,128)(2,1)S(1)}, u32[]{:S(2)}, u32[]{:S(2)}) collective-permute-start(bf16[128,512]{1,0:T(8,128)(2,1)S(1)} %get-tuple-element.29), channel_id=1, source_target_pairs={{0,32},{16,48},{1,33},{17,49},{2,34},{18,50},{3,35},{19,51},{4,36}... | collective-permute-start | bytes 393224 | tf_op jit(solution)/shard_map/ppermute | solution.py:383
  20.0 2.2 %collective-permute-start.2 = (bf16[128,512]{1,0:T(8,128)(2,1)S(1)}, bf16[128,512]{1,0:T(8,128)(2,1)S(1)}, u32[]{:S(2)}, u32[]{:S(2)}) collective-permute-start(bf16[128,512]{1,0:T(8,128)(2,1)S(1)} %get-tuple-element.30), channel_id=1, source_target_pairs={{0,64},{16,80},{1,65},{17,81},{2,66},{18,82},{3,67},{19,83},{4,68}... | collective-permute-start | bytes 393224 | tf_op jit(solution)/shard_map/ppermute | solution.py:383
  22.2 1.3 collective-permute-start.3
  23.5 0.3 collective-permute-done.1.a_ref
  23.8 4.9 %collective-permute-done.2.b_ref = bf16[128,512]{1,0:T(8,128)(2,1)S(1)} collective-permute-done((bf16[128,512]{1,0:T(8,128)(2,1)S(1)}, bf16[128,512]{1,0:T(8,128)(2,1)S(1)}, u32[]{:S(2)}, u32[]{:S(2)}) %collective-permute-start.2) | collective-permute-done | bytes 131104 | tf_op jit(solution)/shard_map/ppermute | solution.py:383
  28.6 0.9 collective-permute-done.3.c_ref
  29.5 0.7 shard_map.84
  30.2 21.1 %all_to_all.55.got_ref = bf16[16,8,2688]{2,1,0:T(8,128)(2,1)S(1)} all-to-all(bf16[16,8,2688]{2,1,0:T(8,128)(2,1)S(1)} %shard_map.84), channel_id=1, replica_groups=mesh['segment'=8,'wide'=16] {'wide'}, dimensions={0} | all-to-all | bytes 1376256 | tf_op jit(solution)/shard_map/all_to_all | solution.py:43
  51.3 0.2 shard_map.85
  51.5 14.6 %all_to_all.56 = bf16[16,40,512]{2,1,0:T(8,128)(2,1)S(1)} all-to-all(bf16[16,40,512]{2,1,0:T(8,128)(2,1)S(1)} %shard_map.85), channel_id=1, replica_groups=mesh['segment'=8,'wide'=16] {'wide'}, dimensions={0} | all-to-all | bytes 1310720 | tf_op jit(solution)/shard_map/all_to_all | solution.py:43
  66.0 0.8 slice.9
  66.9 0.0 all-gather.8.cloned.1.call-update
  66.9 0.0 all-gather.16.cloned.1.call-start
  67.0 0.7 slice.8.got_ref.rest_0_
  67.6 2.2 %shard_map.86 = (bf16[16,8,640]{2,1,0:T(8,128)(2,1)S(1)}, bf16[128,512]{1,0:T(8,128)(2,1)S(1)}) custom-call(s32[2]{0:T(128)S(1)} %pad_add_fusion.where, bf16[16,8,512]{2,1,0:T(8,128)(2,1)} %slice.8.got_ref.rest_0_, bf16[4,2,128,512]{3,2,1,0:T(8,128)(2,1)S(1)} %bitcast.23, bf16[8,2,512,512]{3,2,1,0:T(8,128)(2,1)} %bitcast.28), custom_call_target="tpu_custom_call" | custom-call | flops 134217728 | bytes 589824 | tf_op jit(solution)/shard_map/pallas_call | solution.py:61
  69.9 11.2 %all_to_all.57.got_ref = bf16[16,8,640]{2,1,0:T(8,128)(2,1)S(1)} all-to-all(bf16[16,8,640]{2,1,0:T(8,128)(2,1)S(1)} %get-tuple-element.33), channel_id=1, replica_groups=mesh['segment'=8,'wide'=16] {'wide'}, dimensions={0} | all-to-all | bytes 327680 | tf_op jit(solution)/shard_map/all_to_all | solution.py:43
  81.1 0.2 shard_map.87
  81.3 11.3 %all_to_all.58.got_ref = bf16[16,8,512]{2,1,0:T(8,128)(2,1)} all-to-all(bf16[16,8,512]{2,1,0:T(8,128)(2,1)S(1)} %shard_map.87), channel_id=1, replica_groups=mesh['segment'=8,'wide'=16] {'wide'}, dimensions={0} | all-to-all | bytes 262144 | tf_op jit(solution)/shard_map/all_to_all | solution.py:43
  92.6 3.6 %shard_map.88 = (bf16[16,8,1664]{2,1,0:T(8,128)(2,1)}, bf16[128,512]{1,0:T(8,128)(2,1)S(1)}, bf16[128,1024]{1,0:T(8,128)(2,1)}) custom-call(s32[2]{0:T(128)S(1)} %pad_add_fusion.where, bf16[16,8,512]{2,1,0:T(8,128)(2,1)} %all_to_all.58.got_ref, bf16[128,512]{1,0:T(8,128)(2,1)S(1)} %get-tuple-element.34.states_ref, bf16[8,2,512,512]{3,2,1,0:T(8,128)(2,1)} %bitcast.29, ...), custom_call_target="tpu_custom_call" | custom-call | flops 268435456 | bytes 1638400 | tf_op jit(solution)/shard_map/pallas_call | solution.py:61
  96.2 0.0 all-gather.16.cloned.1.call-update
  96.2 3.6 %all-to-all-start.4 = ((bf16[16,8,1664]{2,1,0:T(8,128)(2,1)}), bf16[16,8,1664]{2,1,0:T(8,128)(2,1)S(1)}, u32[]{:S(2)}, u32[]{:S(2)}) async-start(bf16[16,8,1664]{2,1,0:T(8,128)(2,1)} %get-tuple-element.35), calls=%async_computation.4 | async-start | bytes 851968 | tf_op jit(solution)/shard_map/all_to_all | solution.py:43
  99.8 0.0 all-gather.10.cloned.1.call-start
  99.8 0.0 all-gather.8.cloned.1.call-done.cross_ref
  99.9 9.5 %all-to-all-done.4.got_ref = bf16[16,8,1664]{2,1,0:T(8,128)(2,1)S(1)} async-done(((bf16[16,8,1664]{2,1,0:T(8,128)(2,1)}), bf16[16,8,1664]{2,1,0:T(8,128)(2,1)S(1)}, u32[]{:S(2)}, u32[]{:S(2)}) %all-to-all-start.4) | async-done | bytes 426016 | tf_op jit(solution)/shard_map/all_to_all | solution.py:43
  109.3 1.7 shard_map.89
  111.1 12.0 %all_to_all.59.got_ref = bf16[16,8,1024]{2,1,0:T(8,128)(2,1)} all-to-all(bf16[16,8,1024]{2,1,0:T(8,128)(2,1)S(1)} %shard_map.89), channel_id=1, replica_groups=mesh['segment'=8,'wide'=16] {'wide'}, dimensions={0} | all-to-all | bytes 524288 | tf_op jit(solution)/shard_map/all_to_all | solution.py:43
  123.0 0.0 all-gather.10.cloned.1.call-update
  123.0 0.0 all-gather.12.cloned.1.call-start
  123.1 3.0 %shard_map.90 = (bf16[16,8,1664]{2,1,0:T(8,128)(2,1)S(1)}, bf16[128,512]{1,0:T(8,128)(2,1)S(1)}) custom-call(s32[2]{0:T(128)S(1)} %pad_add_fusion.where, bf16[16,8,1024]{2,1,0:T(8,128)(2,1)} %all_to_all.59.got_ref, bf16[128,512]{1,0:T(8,128)(2,1)S(1)} %get-tuple-element.36.states_ref, bf16[8,2,512,512]{3,2,1,0:T(8,128)(2,1)} %bitcast.30), custom_call_target="tpu_custom_call" | custom-call | flops 335544320 | bytes 1114112 | tf_op jit(solution)/shard_map/pallas_call | solution.py:61
  126.1 12.5 %all_to_all.60.got_ref = bf16[16,8,1664]{2,1,0:T(8,128)(2,1)S(1)} all-to-all(bf16[16,8,1664]{2,1,0:T(8,128)(2,1)S(1)} %get-tuple-element.37), channel_id=1, replica_groups=mesh['segment'=8,'wide'=16] {'wide'}, dimensions={0} | all-to-all | bytes 851968 | tf_op jit(solution)/shard_map/all_to_all | solution.py:43
  138.6 1.7 shard_map.91
  140.3 12.0 %all_to_all.61.got_ref = bf16[16,8,1024]{2,1,0:T(8,128)(2,1)} all-to-all(bf16[16,8,1024]{2,1,0:T(8,128)(2,1)S(1)} %shard_map.91), channel_id=1, replica_groups=mesh['segment'=8,'wide'=16] {'wide'}, dimensions={0} | all-to-all | bytes 524288 | tf_op jit(solution)/shard_map/all_to_all | solution.py:43
  152.3 0.0 all-gather.12.cloned.1.call-update
  152.3 0.1 select_reduce_fusion.1
  152.4 0.2 select_reduce_fusion
  152.6 0.1 copy.26
  152.7 0.1 min.18.slots
  152.8 3.8 %shard_map.92 = (bf16[16,8,1664]{2,1,0:T(8,128)(2,1)}, bf16[128,512]{1,0:T(8,128)(2,1)}) custom-call(s32[2]{0:T(128)S(1)} %pad_add_fusion.where, bf16[16,8,1024]{2,1,0:T(8,128)(2,1)} %all_to_all.61.got_ref, bf16[128,512]{1,0:T(8,128)(2,1)S(1)} %get-tuple-element.38.states_ref, bf16[8,2,512,512]{3,2,1,0:T(8,128)(2,1)} %bitcast.31), custom_call_target="tpu_custom_call" | custom-call | flops 335544320 | bytes 1114112 | tf_op jit(solution)/shard_map/pallas_call | solution.py:61
  156.6 3.6 %all-to-all-start.8 = ((bf16[16,8,1664]{2,1,0:T(8,128)(2,1)}), bf16[16,8,1664]{2,1,0:T(8,128)(2,1)S(1)}, u32[]{:S(2)}, u32[]{:S(2)}) async-start(bf16[16,8,1664]{2,1,0:T(8,128)(2,1)} %get-tuple-element.39), calls=%async_computation.8 | async-start | bytes 851968 | tf_op jit(solution)/shard_map/all_to_all | solution.py:43
  160.2 0.1 minimum_bitcast_fusion
  160.3 0.1 copy.25
  160.3 0.5 copy.30.limit_ref
  160.9 0.0 all-gather.16.cloned.1.call-done
  160.9 3.3 %shard_map.93.rest_0_ = bf16[16,8,4,512]{3,2,1,0:T(4,128)(2,1)} custom-call(s32[16]{0:T(128)S(1)} %min.18.slots, bf16[16,8,4,512]{3,2,1,0:T(4,128)(2,1)S(1)} %copy-done.1, bf16[8,16,512]{2,1,0:T(8,128)(2,1)S(1)} %bitcast.24, s32[8,64,1]{2,1,0:T(8,128)S(1)} %copy.30.limit_ref, bf16[8,128,1024]{2,1,0:T(8,128)(2,1)} %bitcast.34), custom_call_target="tpu_custom_call" | custom-call | flops 67108864 | bytes 786432 | tf_op jit(solution)/shard_map/pallas_call | solution.py:313
  164.2 5.5 %all-to-all-done.8.got_ref = bf16[16,8,1664]{2,1,0:T(8,128)(2,1)S(1)} async-done(((bf16[16,8,1664]{2,1,0:T(8,128)(2,1)}), bf16[16,8,1664]{2,1,0:T(8,128)(2,1)S(1)}, u32[]{:S(2)}, u32[]{:S(2)}) %all-to-all-start.8) | async-done | bytes 426016 | tf_op jit(solution)/shard_map/all_to_all | solution.py:43
  169.7 2.3 %shard_map.94 = bf16[8,8,1024]{2,1,0:T(8,128)(2,1)} custom-call(bf16[16,8,1664]{2,1,0:T(8,128)(2,1)S(1)} %all-to-all-done.8.got_ref, bf16[8,512,512]{2,1,0:T(8,128)(2,1)} %all-gather.8.cloned.1.call-done.cross_ref), custom_call_target="tpu_custom_call" | custom-call | flops 8388608 | bytes 262144 | tf_op jit(solution)/shard_map/pallas_call | solution.py:61
  172.1 5.3 %all-to-all-start.9 = ((bf16[8,8,1024]{2,1,0:T(8,128)(2,1)}), bf16[8,8,1024]{2,1,0:T(8,128)(2,1)S(1)}, u32[]{:S(2)}, u32[]{:S(2)}) async-start(bf16[8,8,1024]{2,1,0:T(8,128)(2,1)} %shard_map.94), calls=%async_computation.9 | async-start | bytes 262144 | tf_op jit(solution)/shard_map/all_to_all | solution.py:43
  177.4 0.0 all-gather.10.cloned.1.call-done.pages_ref
  177.4 3.3 %shard_map.95.rest_0_ = bf16[16,8,4,512]{3,2,1,0:T(4,128)(2,1)} custom-call(s32[16]{0:T(128)S(1)} %min.18.slots, bf16[16,8,4,512]{3,2,1,0:T(4,128)(2,1)S(1)} %copy-done.1, bf16[8,16,512]{2,1,0:T(8,128)(2,1)S(1)} %bitcast.25, s32[8,64,1]{2,1,0:T(8,128)S(1)} %copy.30.limit_ref, ...), custom_call_target="tpu_custom_call", output_to_operand_aliasing={{}: (5, {})} | custom-call | flops 67108864 | bytes 786432 | tf_op jit(solution)/shard_map/pallas_call | solution.py:313
  180.7 2.8 %all-to-all-done.9.got_ref = bf16[8,8,1024]{2,1,0:T(8,128)(2,1)S(1)} async-done(((bf16[8,8,1024]{2,1,0:T(8,128)(2,1)}), bf16[8,8,1024]{2,1,0:T(8,128)(2,1)S(1)}, u32[]{:S(2)}, u32[]{:S(2)}) %all-to-all-start.9) | async-done | bytes 131104 | tf_op jit(solution)/shard_map/all_to_all | solution.py:43
  183.5 1.4 shard_map.96
  184.9 3.6 %all-to-all-start.10 = ((bf16[16,8,2048]{2,1,0:T(8,128)(2,1)}), bf16[16,8,2048]{2,1,0:T(8,128)(2,1)S(1)}, u32[]{:S(2)}, u32[]{:S(2)}) async-start(bf16[16,8,2048]{2,1,0:T(8,128)(2,1)} %shard_map.96), calls=%async_computation.10 | async-start | bytes 1048576 | tf_op jit(solution)/shard_map/all_to_all | solution.py:43
  188.5 0.0 all-gather.12.cloned.1.call-done.pages_ref
  188.5 3.3 %shard_map.97.carried_ref = bf16[16,8,4,512]{3,2,1,0:T(4,128)(2,1)} custom-call(s32[16]{0:T(128)S(1)} %min.18.slots, bf16[16,8,4,512]{3,2,1,0:T(4,128)(2,1)S(1)} %copy-done.1, bf16[8,16,512]{2,1,0:T(8,128)(2,1)S(1)} %bitcast.26, s32[8,64,1]{2,1,0:T(8,128)S(1)} %copy.30.limit_ref, ...), custom_call_target="tpu_custom_call", output_to_operand_aliasing={{}: (5, {})} | custom-call | flops 67108864 | bytes 786432 | tf_op jit(solution)/shard_map/pallas_call | solution.py:313
  191.8 8.3 %all-to-all-done.10.pages_ref = bf16[16,8,2048]{2,1,0:T(8,128)(2,1)S(1)} async-done(((bf16[16,8,2048]{2,1,0:T(8,128)(2,1)}), bf16[16,8,2048]{2,1,0:T(8,128)(2,1)S(1)}, u32[]{:S(2)}, u32[]{:S(2)}) %all-to-all-start.10) | async-done | bytes 524320 | tf_op jit(solution)/shard_map/all_to_all | solution.py:43
  200.1 1.6 shard_map.98
  (19 shorter events, 0.1 us)
Async XLA Ops:
  6.5 6.8 %copy-start = (bf16[4,256,512]{2,1,0:T(8,128)(2,1)S(1)}, bf16[4,256,512]{2,1,0:T(8,128)(2,1)}, u32[]{:S(2)}) copy-start(bf16[4,256,512]{2,1,0:T(8,128)(2,1)} %param.8) | copy-start | bytes 3145732
  6.5 61.1 %all-gather.14.cloned.1.call-start = ((), (), s32[]{:S(2)}) async-start(), calls=%async_computation.14 | async-start | bytes 9437184 | tf_op jit(solution)/shard_map/all_gather | solution.py:363
  6.6 0.8 copy-start.3
  10.5 89.4 %all-gather.8.cloned.1.call-start = ((), (), s32[]{:S(2)}) async-start(), calls=%async_computation.11 | async-start | bytes 4718592 | tf_op jit(solution)/shard_map/all_gather | solution.py:405
  10.5 2.8 %collective-permute-start = (bf16[512,512]{1,0:T(8,128)(2,1)S(1)}, bf16[512,512]{1,0:T(8,128)(2,1)S(1)}, u32[]{:S(2)}, u32[]{:S(2)}) collective-permute-start(bf16[512,512]{1,0:T(8,128)(2,1)S(1)} %get-tuple-element.27), channel_id=1, source_target_pairs={{0,16},{32,48},{64,80},{96,112},{1,17},{33,49},{65,81},{97,113},{2... | collective-permute-start | bytes 1572872 | tf_op jit(solution)/shard_map/ppermute | solution.py:364
  16.0 7.7 %collective-permute-start.1 = (bf16[128,512]{1,0:T(8,128)(2,1)S(1)}, bf16[128,512]{1,0:T(8,128)(2,1)S(1)}, u32[]{:S(2)}, u32[]{:S(2)}) collective-permute-start(bf16[128,512]{1,0:T(8,128)(2,1)S(1)} %get-tuple-element.29), channel_id=1, source_target_pairs={{0,32},{16,48},{1,33},{17,49},{2,34},{18,50},{3,35},{19,51},{4,36}... | collective-permute-start | bytes 393224 | tf_op jit(solution)/shard_map/ppermute | solution.py:383
  20.0 8.7 %collective-permute-start.2 = (bf16[128,512]{1,0:T(8,128)(2,1)S(1)}, bf16[128,512]{1,0:T(8,128)(2,1)S(1)}, u32[]{:S(2)}, u32[]{:S(2)}) collective-permute-start(bf16[128,512]{1,0:T(8,128)(2,1)S(1)} %get-tuple-element.30), channel_id=1, source_target_pairs={{0,64},{16,80},{1,65},{17,81},{2,66},{18,82},{3,67},{19,83},{4,68}... | collective-permute-start | bytes 393224 | tf_op jit(solution)/shard_map/ppermute | solution.py:383
  22.2 7.3 %collective-permute-start.3 = (bf16[128,512]{1,0:T(8,128)(2,1)S(1)}, bf16[128,512]{1,0:T(8,128)(2,1)S(1)}, u32[]{:S(2)}, u32[]{:S(2)}) collective-permute-start(bf16[128,512]{1,0:T(8,128)(2,1)S(1)} %get-tuple-element.31), channel_id=1, source_target_pairs={{0,96},{16,112},{1,97},{17,113},{2,98},{18,114},{3,99},{19,115},{4... | collective-permute-start | bytes 393224 | tf_op jit(solution)/shard_map/ppermute | solution.py:383
  66.9 94.0 %all-gather.16.cloned.1.call-start = ((), (), s32[]{:S(2)}) async-start(), calls=%async_computation.15 | async-start | bytes 2359296 | tf_op jit(solution)/shard_map/all_gather | solution.py:482
  67.6 24.9 %copy-start.2 = (bf16[16,8,512]{2,1,0:T(8,128)(2,1)S(1)}, bf16[16,8,512]{2,1,0:T(8,128)(2,1)}, u32[]{:S(2)}) copy-start(bf16[16,8,512]{2,1,0:T(8,128)(2,1)} %slice.8.got_ref.rest_0_) | copy-start | bytes 393220
  96.2 13.1 %all-to-all-start.4 = ((bf16[16,8,1664]{2,1,0:T(8,128)(2,1)}), bf16[16,8,1664]{2,1,0:T(8,128)(2,1)S(1)}, u32[]{:S(2)}, u32[]{:S(2)}) async-start(bf16[16,8,1664]{2,1,0:T(8,128)(2,1)} %get-tuple-element.35), calls=%async_computation.4 | async-start | bytes 851968 | tf_op jit(solution)/shard_map/all_to_all | solution.py:43
  99.8 77.6 %all-gather.10.cloned.1.call-start = ((), (), s32[]{:S(2)}) async-start(), calls=%async_computation.12 | async-start | bytes 2359296 | tf_op jit(solution)/shard_map/all_gather | solution.py:482
  123.0 65.4 %all-gather.12.cloned.1.call-start = ((), (), s32[]{:S(2)}) async-start(), calls=%async_computation.13 | async-start | bytes 2359296 | tf_op jit(solution)/shard_map/all_gather | solution.py:482
  138.6 13.7 %copy-start.5 = (s32[8,8,1]{1,2,0:T(1,128)S(1)}, s32[8,8,1]{1,2,0:T(1,128)}, u32[]{:S(2)}) copy-start(s32[8,8,1]{1,2,0:T(1,128)} %param.12) | copy-start | bytes 772
  152.8 7.4 %copy-start.6 = (s32[16,8]{0,1:T(8,128)S(1)}, s32[16,8]{0,1:T(8,128)}, u32[]{:S(2)}) copy-start(s32[16,8]{0,1:T(8,128)} %param.15) | copy-start | bytes 1540
  152.8 8.0 %copy-start.4 = (bf16[16,8,512]{2,1,0:T(8,128)(2,1)S(1)}, bf16[16,8,512]{2,1,0:T(8,128)(2,1)}, u32[]{:S(2)}) copy-start(bf16[16,8,512]{2,1,0:T(8,128)(2,1)} %param.14) | copy-start | bytes 393220
  152.8 8.1 %copy-start.1 = (bf16[16,8,4,512]{3,2,1,0:T(4,128)(2,1)S(1)}, bf16[16,8,4,512]{3,2,1,0:T(4,128)(2,1)}, u32[]{:S(2)}) copy-start(bf16[16,8,4,512]{3,2,1,0:T(4,128)(2,1)} %q_ref.7) | copy-start | bytes 1572868
  156.6 13.1 %all-to-all-start.8 = ((bf16[16,8,1664]{2,1,0:T(8,128)(2,1)}), bf16[16,8,1664]{2,1,0:T(8,128)(2,1)S(1)}, u32[]{:S(2)}, u32[]{:S(2)}) async-start(bf16[16,8,1664]{2,1,0:T(8,128)(2,1)} %get-tuple-element.39), calls=%async_computation.8 | async-start | bytes 851968 | tf_op jit(solution)/shard_map/all_to_all | solution.py:43
  172.1 11.4 %all-to-all-start.9 = ((bf16[8,8,1024]{2,1,0:T(8,128)(2,1)}), bf16[8,8,1024]{2,1,0:T(8,128)(2,1)S(1)}, u32[]{:S(2)}, u32[]{:S(2)}) async-start(bf16[8,8,1024]{2,1,0:T(8,128)(2,1)} %shard_map.94), calls=%async_computation.9 | async-start | bytes 262144 | tf_op jit(solution)/shard_map/all_to_all | solution.py:43
  184.9 15.2 %all-to-all-start.10 = ((bf16[16,8,2048]{2,1,0:T(8,128)(2,1)}), bf16[16,8,2048]{2,1,0:T(8,128)(2,1)S(1)}, u32[]{:S(2)}, u32[]{:S(2)}) async-start(bf16[16,8,2048]{2,1,0:T(8,128)(2,1)} %shard_map.96), calls=%async_computation.10 | async-start | bytes 1048576 | tf_op jit(solution)/shard_map/all_to_all | solution.py:43
Sparse Core Ops, SparseCore 0:
  10.6 52.1 all-gather.13
  67.0 31.6 all-gather.7
  100.4 25.1 all-gather.15
  127.1 25.4 all-gather.9
  154.2 25.4 all-gather.11

commit v6 on v5

--- a/solution.py
+++ b/solution.py
@@ -1,4 +1,5 @@
 import functools
+import math
 
 import jax
 import jax.numpy as jnp
@@ -52,12 +53,16 @@
     return pltpu.with_memory_space_constraint(x, pltpu.HBM)
 
 
+def in_vmem(x):
+    return pltpu.with_memory_space_constraint(x, pltpu.VMEM)
+
+
 def whole(shape):
     return pl.BlockSpec(shape, lambda i, *s: (0,) * len(shape))
 
 
 def call(body, in_specs, out_specs, out_shape, operands, scalars=(), scratch=(), flops=0):
-    moved = sum(o.size * 2 for o in out_shape)
+    moved = sum(2 * math.prod(o.shape) for o in out_shape)
     return pl.pallas_call(
         body,
         grid_spec=pltpu.PrefetchScalarGridSpec(
@@ -73,54 +78,73 @@
     )(*scalars, *operands)
 
 
-def weights_kernel(where, latent_ref, gain_ref, back_ref, both_ref, lent_ref, latent, sems):
+def weights_kernel(where, latent_ref, gain_ref, back_ref, both_ref, lent_ref, *scratch):
+    latent, gain, pair, sems = scratch
     copies = [
         pltpu.make_async_copy(latent_ref.at[0], latent, sems.at[0]),
-        pltpu.make_async_copy(back_ref.at[0], both_ref.at[1], sems.at[1]),
+        pltpu.make_async_copy(gain_ref, gain, sems.at[1]),
+        pltpu.make_async_copy(back_ref.at[0], pair.at[1], sems.at[2]),
     ]
     for copy in copies:
         copy.start()
     size = latent.shape[0]
     row = lax.broadcasted_iota(jnp.int32, (size, size), 0)
     column = lax.broadcasted_iota(jnp.int32, (size, size), 1)
-    gains = jnp.where(row == column, gain_ref[...].astype(f32), 0.0).astype(bf16)
+    copies[1].wait()
+    gains = jnp.where(row == column, gain[...].astype(f32), 0.0).astype(bf16)
+    copies[2].wait()
+    sending = [pltpu.make_async_copy(pair.at[i], both_ref.at[i], sems.at[3 + i]) for i in range(2)]
+    sending[1].start()
+
+    @pl.when(where[0] != 0)
+    def _():
+        pltpu.make_async_copy(pair.at[1], lent_ref, sems.at[5]).start()
+
     copies[0].wait()
-    both_ref[0] = dot(gains, latent[...]).astype(bf16)
-    copies[1].wait()
+    pair[0] = dot(gains, latent[...]).astype(bf16)
+    sending[0].start()
 
     @pl.when(where[0] == 0)
     def _():
-        lent_ref[...] = both_ref[0]
+        pltpu.make_async_copy(pair.at[0], lent_ref, sems.at[5]).start()
+
+    pltpu.make_async_copy(pair.at[0], lent_ref, sems.at[5]).wait()
+    for copy in sending:
+        copy.wait()
+
+
+def home_kernel(where, states_ref, both_ref, lent_ref, *rest):
+    out_refs, (tokens, weight, sems) = rest[:-3], rest[-3:]
+    groups, rows, width = tokens.shape
+    loading = pltpu.make_async_copy(states_ref.at[:, where[1]], tokens, sems.at[0])
+    loading.start()
+
+    def products(weight_ref):
+        loading.wait()
+        product = dot(tokens[...].reshape(groups * rows, width), weight_ref[...]).astype(bf16)
+        for group in range(groups):
+            out_refs[group][...] = product[group * rows : (group + 1) * rows]
+
+    @pl.when(where[0] == 0)
+    def _():
+        fetching = pltpu.make_async_copy(both_ref.at[0], weight, sems.at[1])
+        fetching.start()
+        fetching.wait()
+        products(weight)
 
     @pl.when(where[0] != 0)
     def _():
-        lent_ref[...] = both_ref[1]
-
-
-def home_kernel(where, states_ref, both_ref, lent_ref, *out_refs):
-    groups, _, rows, width = states_ref.shape
-    tokens = states_ref[...].reshape(groups * rows, width)
-
-    def products(weight):
-        product = dot(tokens, weight).astype(bf16)
-        for group in range(groups):
-            out_refs[group][...] = product[group * rows : (group + 1) * rows]
-
-    @pl.when(where[0] == 0)
+        products(lent_ref)
+
+
+def cross_kernel(where, both_ref, lent_ref, out_ref):
+    @pl.when(where[0] & 1 == 0)
     def _():
-        products(both_ref[0])
-
-    @pl.when(where[0] != 0)
+        out_ref[...] = dot_t(both_ref[1], both_ref[1]).astype(bf16)
+
+    @pl.when(where[0] & 1 != 0)
     def _():
-        products(lent_ref[...])
-
-    @pl.when(where[1] == 0)
-    def _():
-        out_refs[groups][...] = dot_t(both_ref[1], both_ref[1]).astype(bf16)
-
-    @pl.when(where[1] != 0)
-    def _():
-        out_refs[groups][...] = dot(lent_ref[...], both_ref[0]).astype(bf16)
+        out_ref[...] = dot(lent_ref[...], both_ref[0]).astype(bf16)
 
 
 def home_send_kernel(where, home_ref, a_ref, b_ref, c_ref, cross_ref, states_ref, out_ref):
@@ -158,7 +182,7 @@
 
 
 def chain(width, summed, gram, mixing):
-    lat = gram().shape[1]
+    lat = (summed.shape[1] - LANES) // 3
     squares = summed[:, 0:1] + summed[:, 1:2]
     at = [LANES + i * lat for i in range(4)]
     first = (summed[:, at[0] : at[1]] * lax.rsqrt(squares / width + eps_norm)).astype(bf16)
@@ -170,62 +194,61 @@
     return first, second
 
 
-def advance_kernel(before, layers, held, where, got_ref, states_ref, both_ref, *rest):
-    got, weights, sems = rest[-3:]
-    out_ref, state_ref = rest[held : held + 2]
-    needed = [(layer, 1) for layer in before] + [(layer, 0) for layer in layers]
-    if len(layers) == 2:
-        needed.append((layers[0], 1))
-    taking = pltpu.make_async_copy(got_ref, got, sems.at[len(needed)])
-    taking.start()
-    copies = [
-        pltpu.make_async_copy(both_ref.at[layer, kind], weights.at[i], sems.at[i])
-        for i, (layer, kind) in enumerate(needed)
-    ]
+def reside_kernel(lists, source_ref, *rest):
+    out_refs, sems = rest[:-1], rest[-1]
+    copies = []
+    for out_ref, slots in zip(out_refs, lists):
+        for i, slot in enumerate(slots):
+            sem = sems.at[len(copies)]
+            copies.append(pltpu.make_async_copy(source_ref.at[slot], out_ref.at[i], sem))
     for copy in copies:
         copy.start()
+    for copy in copies:
+        copy.wait()
+
+
+def advance_kernel(before, layers, mode, where, got_ref, states_ref, *rest):
+    refs = rest[: 1 + len(layers)]
+    back_ref, latent_ref = refs[:2]
+    outs = rest[len(refs) :]
+    if mode == "later":
+        earlier_ref, outs = outs[0], outs[1:]
+    out_ref, state_ref, held_ref = outs[:3]
     wide, share, _ = out_ref.shape
     rows = wide * share
-    lat = weights.shape[2]
-    state = states_ref[...].reshape(rows, weights.shape[1]).astype(f32)
-    taking.wait()
-    latents = got[...].astype(f32).reshape(rows, got.shape[2])
-    if held:
-        earlier_ref, held_ref = rest[0], rest[3]
-        held_ref[:, :lat] = earlier_ref[...].astype(f32).reshape(rows, lat).astype(bf16)
-        held_ref[:, lat:] = latents.astype(bf16)
+    lat = back_ref.shape[2]
+
+    def latents_of(ref):
+        block = ref[:, ref.shape[1] - share :]
+        return block.astype(f32).reshape(rows, ref.shape[2])
+
+    latents = latents_of(got_ref)
     activated = silu(latents)
+    state = states_ref[...].reshape(rows, states_ref.shape[-1]).astype(f32)
     for i in range(len(before)):
-        copies[i].wait()
-        state = state + dot(activated[:, i * lat : (i + 1) * lat], weights[i])
+        state = state + dot(activated[:, i * lat : (i + 1) * lat], back_ref[i])
     state = state.astype(bf16)
     state_ref[...] = state
     squares = square_columns(state.astype(f32))
     out_ref[:, :, :LANES] = squares.reshape(wide, share, LANES).astype(bf16)
-    for i in range(len(before), len(needed)):
-        copies[i].wait()
-        product = (dot_t if needed[i][1] else dot)(state, weights[i])
-        at = LANES + (i - len(before)) * lat
+    products = [dot(state, latent_ref[i]) for i in range(len(layers))]
+    if len(layers) == 2:
+        products.append(dot_t(state, refs[2][0]))
+    for i, product in enumerate(products):
+        at = LANES + i * lat
         out_ref[:, :, at : at + lat] = product.reshape(wide, share, lat).astype(bf16)
-
-
-def pair_kernel(width, even, got_ref, cross_ref, out_ref, crosses, sems):
-    copies = [
-        pltpu.make_async_copy(cross_ref.at[even + i], crosses.at[i], sems.at[i]) for i in range(2)
-    ]
-    for copy in copies:
-        copy.start()
-
-    def fetched(i):
-        def read():
-            return crosses[i]
-
-        return read
-
+    if mode == "first":
+        held_ref[...] = got_ref[:, : got_ref.shape[1] - share]
+    elif mode == "later":
+        held_ref[:, :lat] = latents_of(earlier_ref).astype(bf16)
+        held_ref[:, lat:] = latents.astype(bf16)
+    else:
+        held_ref[...] = latents.astype(bf16)
+
+
+def pair_kernel(width, got_ref, cross_ref, out_ref):
     summed = jnp.sum(got_ref[...].astype(f32), axis=0)
-    for copy in copies:
-        copy.wait()
-    first, second = chain(width, summed, fetched(0), fetched(1))
+    first, second = chain(width, summed, lambda: cross_ref[0], lambda: cross_ref[1])
     lat = first.shape[1]
     for place in range(out_ref.shape[0]):
         out_ref[place, :, :lat] = first
@@ -349,35 +372,56 @@
     def array(*shape):
         return jax.ShapeDtypeStruct(shape, bf16)
 
+    def near(*shape):
+        return pltpu.VMEM(shape, bf16)
+
+    def far(*shape):
+        return pltpu.HBM(shape, bf16)
+
     size = (2, local_width, lat)
     both, lent = call(
         weights_kernel,
-        [in_hbm, whole(norm_gain.shape), in_hbm],
-        [whole(size), whole(size[1:])],
-        [array(*size), array(*size[1:])],
-        [held_in_hbm(w_latent), norm_gain, held_in_hbm(w_back)],
+        [in_hbm] * 3,
+        [in_hbm] * 2,
+        [far(*size), far(*size[1:])],
+        [held_in_hbm(w_latent), held_in_hbm(norm_gain), held_in_hbm(w_back)],
         [where],
-        [pltpu.VMEM(size[1:], bf16), pltpu.SemaphoreType.DMA((2,))],
+        [
+            pltpu.VMEM(size[1:], bf16),
+            pltpu.VMEM(norm_gain.shape, bf16),
+            pltpu.VMEM(size, bf16),
+            pltpu.SemaphoreType.DMA((6,)),
+        ],
         flops=2 * local_width**3,
     )
-    every = held_in_hbm(lax.all_gather(both, "segment", axis=0))
+    every = lax.all_gather(both, "segment", axis=0)
     lent = lax.ppermute(lent, "segment", [(i, i + 1) for i in range(0, segments, 2)])
 
     states = prompt_states.reshape(segments // 2, 2, mine, local_width)
     groups = segments // 2
     own_states = pl.BlockSpec((1, 1, mine, local_width), lambda i, s: (s[0] >> 1, s[1], 0, 0))
-    *home, cross = call(
+    home = call(
         home_kernel,
+        [in_hbm, in_hbm, whole(size[1:])],
+        [whole((mine, lat))] * groups,
+        [near(mine, lat)] * groups,
+        [held_in_hbm(states), held_in_hbm(both), lent],
+        [where],
         [
-            pl.BlockSpec((groups, 1, mine, local_width), lambda i, s: (0, s[1], 0, 0)),
-            whole(size),
-            whole(size[1:]),
+            pltpu.VMEM((groups, mine, local_width), bf16),
+            pltpu.VMEM((local_width, lat), bf16),
+            pltpu.SemaphoreType.DMA((2,)),
         ],
-        [whole((mine, lat))] * groups + [whole((lat, lat))],
-        [array(mine, lat)] * groups + [array(lat, lat)],
-        [states, both, lent],
+        flops=2 * local_width**3,
+    )
+    (cross,) = call(
+        cross_kernel,
+        [whole(size), whole(size[1:])],
+        [whole((lat, lat))],
+        [near(lat, lat)],
+        [both, lent],
         [where],
-        flops=2 * 2 * local_width**3,
+        flops=2 * local_width**3,
     )
     taken = [
         lax.ppermute(home[hop], "segment", [(0, 2 * hop), (1, 2 * hop + 1)])
@@ -401,39 +445,71 @@
         [array(wide, high + share, lat)],
         [got],
     )
-    got = exchanged(sent, "wide")
-    crosses = lax.all_gather(got[:, :high].reshape(lat, lat), "segment", axis=0)
-    crosses = held_in_hbm(crosses)
-    got = got[:, high:]
-
-    def advance(before, following, got, state, earlier=None):
-        held = earlier is not None
+    def resident(source, *lists):
+        parts = source.reshape((-1,) + source.shape[-2:])
+        count = sum(len(slots) for slots in lists)
+        return pl.pallas_call(
+            functools.partial(reside_kernel, lists),
+            in_specs=[in_hbm],
+            out_specs=[pl.BlockSpec(memory_space=pltpu.VMEM)] * len(lists),
+            out_shape=[pltpu.VMEM((len(slots),) + parts.shape[1:], bf16) for slots in lists],
+            scratch_shapes=[pltpu.SemaphoreType.DMA((count,))],
+            compiler_params=params,
+            cost_estimate=pl.CostEstimate(
+                flops=0, bytes_accessed=2 * count * parts.shape[1] * lat, transcendentals=0
+            ),
+        )(held_in_hbm(parts))
+
+    def resident_weights(before, following):
+        backs = [2 * layer + 1 for layer in before]
+        latents = [2 * layer for layer in following]
+        if len(following) == 1:
+            return resident(every, backs, latents)
+        return resident(every, backs, latents, [2 * following[0] + 1])
+
+    def tied(*values):
+        return lax.optimization_barrier(values)
+
+    def advance(before, following, got, state, weights, earlier=None):
+        mode = "first" if before == (0,) else "later" if earlier is not None else "pair"
         count = len(following) + (len(following) == 2)
-        shapes = [array(wide, share, LANES + count * lat), array(mine, local_width)]
-        in_specs = [in_hbm, own_states if state.ndim == 4 else whole(state.shape), in_hbm]
-        operands = [held_in_hbm(got), state, every]
-        if held:
-            shapes.append(array(mine, 2 * lat))
+        shapes = [
+            array(wide, share, LANES + count * lat),
+            near(mine, local_width),
+            far(wide, high, lat) if mode == "first" else far(mine, 2 * lat),
+        ]
+        operands = [got, state] + [in_vmem(weight) for weight in weights]
+        in_specs = [whole(got.shape), own_states if mode == "first" else whole(state.shape)]
+        in_specs += [whole(weight.shape) for weight in weights]
+        if mode == "later":
             in_specs.append(whole(earlier.shape))
             operands.append(earlier)
-        needed = len(before) + count
         return call(
-            functools.partial(advance_kernel, before, following, held),
+            functools.partial(advance_kernel, before, following, mode),
             in_specs,
             [whole(s.shape) for s in shapes],
             shapes,
             operands,
             [where],
-            [
-                pltpu.VMEM(got.shape, bf16),
-                pltpu.VMEM((needed, local_width, lat), bf16),
-                pltpu.SemaphoreType.DMA((needed + 1,)),
-            ],
-            flops=2 * needed * mine * lat * local_width,
+            flops=2 * (len(before) + count) * mine * lat * local_width,
         )
 
+    def pair_step(got, crosses, copies):
+        (sent,) = call(
+            functools.partial(pair_kernel, width),
+            [whole(got.shape), whole(crosses[0].shape)],
+            [whole((copies, share, 2 * lat))],
+            [array(copies, share, 2 * lat)],
+            [got, in_vmem(crosses[0])],
+            flops=2 * 2 * share * lat * lat,
+        )
+        return sent
+
+    got, weights = tied(exchanged(sent, "wide"), resident_weights((0,), (1,)))
+
     earlier = got
-    sent, state = advance((0,), (1,), got, states)
+    sent, state, cross = advance((0,), (1,), got, states, weights)
+    crosses = lax.all_gather(cross.reshape(lat, lat), "segment", axis=0)
     got = exchanged(sent, "wide")
     (sent,) = call(
         functools.partial(single_kernel, width),
@@ -442,20 +518,20 @@
         [array(wide, share, lat)],
         [got],
     )
-    got = exchanged(sent, "wide")
-
-    def pair_step(even, got, copies):
-        (sent,) = call(
-            functools.partial(pair_kernel, width, even),
-            [whole(got.shape), in_hbm],
-            [whole((copies, share, 2 * lat))],
-            [array(copies, share, 2 * lat)],
-            [got, crosses],
-            [],
-            [pltpu.VMEM((2, lat, lat), bf16), pltpu.SemaphoreType.DMA((2,))],
-            flops=2 * 2 * share * lat * lat,
-        )
-        return sent
+    got, weights = tied(exchanged(sent, "wide"), resident_weights((1,), (2, 3)))
+
+    pages = []
+    for even in range(2, layers, 2):
+        odd = even + 1
+        before = (1,) if even == 2 else (even - 2, even - 1)
+        extra = earlier if even == 2 else None
+        sent, state, held = advance(before, (even, odd), got, state, weights, extra)
+        pages.append(lax.all_gather(held, "segment", axis=0))
+        got, mixing = tied(exchanged(sent, "wide"), resident(crosses, [even, odd]))
+        if odd < layers - 1:
+            sent = pair_step(got, mixing, wide)
+            following = resident_weights((even, odd), (even + 2, even + 3))
+            got, weights = tied(exchanged(sent, "wide"), following)
 
     targets = page_lists[:, :, 0]
     owned = targets == position
@@ -472,21 +548,10 @@
     def decode(layer, pages, carried, last=False):
         return decode_pair(layer, slots, queries, new, limit, pages, carried, last)
 
-    pages = []
-    for even in range(2, layers, 2):
-        if even == 2:
-            sent, state, held = advance((1,), (2, 3), got, state, earlier)
-        else:
-            held = got.reshape(mine, 2 * lat)
-            sent, state = advance((even - 2, even - 1), (even, even + 1), got, state)
-        pages.append(lax.all_gather(held, "segment", axis=0))
-        got = exchanged(sent, "wide")
-        if even < layers - 2:
-            got = exchanged(pair_step(even, got, wide), "wide")
     out = decode(0, pages[0], None)
     got, out = lax.optimization_barrier((got, out))
 
-    got = exchanged(pair_step(layers - 2, got, segments), "segment")
+    got = exchanged(pair_step(got, mixing, segments), "segment")
     out = decode(2, pages[1], out)
     got, out = lax.optimization_barrier((got, out))
     (sent,) = call(

time: 209 us -> 205 us (0.981)
  blocking collectives: 94.6 us -> 32.7 us
  waiting for transfers between devices: 33.7 us -> 68.8 us
  starting transfers between devices: 24.9 us -> 43.1 us
  Pallas kernels: 38 us -> 42.8 us
    all_to_all x7 -> x2, blocking collectives: 94.6 us -> 32.7 us  [exchanged(): return lax.all_to_all(sent, axis, 0, 0, tiled=True)]
    all_to_all x4 -> x9, waiting for transfers between devices: 26.1 us -> 53.7 us  [exchanged(): return lax.all_to_all(sent, axis, 0, 0, tiled=True)]
    all_to_all x4 -> x9, starting transfers between devices: 16 us -> 34.3 us  [exchanged(): return lax.all_to_all(sent, axis, 0, 0, tiled=True)]
    pallas_call x0 -> x7, Pallas kernels: none -> 9.94 us  [resident(): pl.pallas_call(functools.partial(reside_kernel, lists), in_specs=[in_hbm]...]
    all_gather x2, waiting for transfers between devices: 0.02 us -> 8.57 us  [the longest x1 6.99 us: shards(): every = lax.all_gather(both, 'segment', axis=0)]
    pallas_call x13 -> x14, Pallas kernels: 26.6 us -> 21.4 us  [call(): pl.pallas_call(body, grid_spec=pltpu.PrefetchScalarGridSpec(num_scalar_pr...]
  transfers between devices with their start and end apart: 13 -> 18, of which waited for: 8 -> 14; matrix products, arithmetic and copies ran while one was open for 1% -> 1% of each run, Pallas kernels for 16% -> 18%
where the time goes in v6:
time: 205 us; the launch traced here: 204 us
  waiting for transfers between devices  68.8 us (34%)
  starting transfers between devices  43.1 us (21%)
  Pallas kernels  42.8 us (21%)
  blocking collectives  32.7 us (16%)
  between operations  13.5 us (7%)
  local copies, waits for them, and re-layouts  2.45 us (1%)
    all_to_all x9, waiting for transfers between devices, exchanged(): return lax.all_to_all(sent, axis, 0, 0, tiled=True)  53.7 us
    all_to_all x9, starting transfers between devices, exchanged(): return lax.all_to_all(sent, axis, 0, 0, tiled=True)  34.3 us
    all_to_all x2, blocking collectives, exchanged(): return lax.all_to_all(sent, axis, 0, 0, tiled=True)  32.7 us
    pallas_call x14, Pallas kernels, call(): pl.pallas_call(body, grid_spec=pltpu.PrefetchScalarGridSpec(num_scalar_pr...  21.4 us
    pallas_call x4, Pallas kernels, decode_pair(): pl.pallas_call(last_decode_kernel if last else functools.partial(decode_k...  11.4 us
    pallas_call x7, Pallas kernels, resident(): pl.pallas_call(functools.partial(reside_kernel, lists), in_specs=[in_hbm]...  9.94 us
    ppermute x3, starting transfers between devices, shards(): lax.ppermute(home[hop], 'segment', [(0, 2 * hop), (1, 2 * hop + 1)])  7.15 us
    all_gather x1, waiting for transfers between devices, shards(): every = lax.all_gather(both, 'segment', axis=0)  6.99 us
  transfers between devices with their start and end apart: 18, of which 14 were waited for; matrix products, arithmetic and copies ran while one was open for 1% of the time, Pallas kernels for 18%

profile of v6, /device:TPU:0, one launch (start us, length us, event | category | flops | bytes accessed | tf_op | source)
XLA Modules:
  0.0 203.7 jit_solution(8313968096208342759)
XLA Ops:
  6.5 0.1 pad_add_fusion.where
  6.6 3.2 %shard_map.82 = (bf16[2,512,512]{2,1,0:T(8,128)(2,1)}, bf16[512,512]{1,0:T(8,128)(2,1)}) custom-call(s32[2]{0:T(128)S(1)} %pad_add_fusion.where, bf16[1,512,512]{2,1,0:T(8,128)(2,1)} %latent_ref.1, bf16[1,512]{1,0:T(2,128)(2,1)} %gain_ref.1, bf16[1,512,512]{2,1,0:T(8,128)(2,1)} %back_ref.1), custom_call_target="tpu_custom_call" | custom-call | flops 268435456 | bytes 3145728 | tf_op jit(solution)/shard_map/pallas_call | solution.py:66
  9.9 1.5 collective-permute-start
  11.3 1.7 collective-permute-done.lent_ref
  13.0 2.2 %shard_map.83 = (bf16[128,512]{1,0:T(8,128)(2,1)S(1)}, bf16[128,512]{1,0:T(8,128)(2,1)S(1)}, bf16[128,512]{1,0:T(8,128)(2,1)S(1)}, bf16[128,512]{1,0:T(8,128)(2,1)S(1)}) custom-call(s32[2]{0:T(128)S(1)} %pad_add_fusion.where, bf16[4,2,128,512]{3,2,1,0:T(8,128)(2,1)} %bitcast.20, bf16[2,512,512]{2,1,0:T(8,128)(2,1)} %get-tuple-element.60.both_ref, ...), custom_call_target="tpu_custom_call" | custom-call | flops 268435456 | bytes 1048576 | tf_op jit(solution)/shard_map/pallas_call | solution.py:66
  15.2 3.7 %collective-permute-start.1 = (bf16[128,512]{1,0:T(8,128)(2,1)S(1)}, bf16[128,512]{1,0:T(8,128)(2,1)S(1)}, u32[]{:S(2)}, u32[]{:S(2)}) collective-permute-start(bf16[128,512]{1,0:T(8,128)(2,1)S(1)} %get-tuple-element.63), channel_id=1, source_target_pairs={{0,32},{16,48},{1,33},{17,49},{2,34},{18,50},{3,35},{19,51},{4,36}... | collective-permute-start | bytes 393224 | tf_op jit(solution)/shard_map/ppermute | solution.py:427
  18.9 2.2 %collective-permute-start.2 = (bf16[128,512]{1,0:T(8,128)(2,1)S(1)}, bf16[128,512]{1,0:T(8,128)(2,1)S(1)}, u32[]{:S(2)}, u32[]{:S(2)}) collective-permute-start(bf16[128,512]{1,0:T(8,128)(2,1)S(1)} %get-tuple-element.64), channel_id=1, source_target_pairs={{0,64},{16,80},{1,65},{17,81},{2,66},{18,82},{3,67},{19,83},{4,68}... | collective-permute-start | bytes 393224 | tf_op jit(solution)/shard_map/ppermute | solution.py:427
  21.1 1.3 collective-permute-start.3
  22.4 1.0 shard_map.84.cross_ref
  23.5 3.8 %collective-permute-done.2.b_ref = bf16[128,512]{1,0:T(8,128)(2,1)S(1)} collective-permute-done((bf16[128,512]{1,0:T(8,128)(2,1)S(1)}, bf16[128,512]{1,0:T(8,128)(2,1)S(1)}, u32[]{:S(2)}, u32[]{:S(2)}) %collective-permute-start.2) | collective-permute-done | bytes 131104 | tf_op jit(solution)/shard_map/ppermute | solution.py:427
  27.2 0.9 collective-permute-done.3.c_ref
  28.2 0.7 shard_map.85
  28.9 21.5 %all_to_all.55.got_ref = bf16[16,8,2688]{2,1,0:T(8,128)(2,1)S(1)} all-to-all(bf16[16,8,2688]{2,1,0:T(8,128)(2,1)S(1)} %shard_map.85), channel_id=1, replica_groups=mesh['segment'=8,'wide'=16] {'wide'}, dimensions={0} | all-to-all | bytes 1376256 | tf_op jit(solution)/shard_map/all_to_all | solution.py:44
  50.3 1.1 shard_map.86
  51.4 3.6 %all-to-all-start.1 = ((bf16[16,40,512]{2,1,0:T(8,128)(2,1)}), bf16[16,40,512]{2,1,0:T(8,128)(2,1)S(1)}, u32[]{:S(2)}, u32[]{:S(2)}) async-start(bf16[16,40,512]{2,1,0:T(8,128)(2,1)} %shard_map.86), calls=%async_computation.1 | async-start | bytes 1310720 | tf_op jit(solution)/shard_map/all_to_all | solution.py:44
  55.0 7.0 %all-gather.12.cloned.1.call-done.source_ref = bf16[16,512,512]{2,1,0:T(8,128)(2,1)} async-done(((bf16[2,512,512]{2,1,0:T(8,128)(2,1)}), bf16[16,512,512]{2,1,0:T(8,128)(2,1)}) %all-gather.12.cloned.1.call-update) | async-done | bytes 8388624 | tf_op jit(solution)/shard_map/all_gather | solution.py:397
  62.0 1.2 shard_map.87
  63.3 3.8 %all-to-all-done.1.got_ref.rest_3_ = bf16[16,40,512]{2,1,0:T(8,128)(2,1)S(1)} async-done(((bf16[16,40,512]{2,1,0:T(8,128)(2,1)}), bf16[16,40,512]{2,1,0:T(8,128)(2,1)S(1)}, u32[]{:S(2)}, u32[]{:S(2)}) %all-to-all-start.1) | async-done | bytes 655392 | tf_op jit(solution)/shard_map/all_to_all | solution.py:44
  67.1 1.7 shard_map.88
  68.8 11.2 %all_to_all.56.got_ref = bf16[16,8,640]{2,1,0:T(8,128)(2,1)S(1)} all-to-all(bf16[16,8,640]{2,1,0:T(8,128)(2,1)S(1)} %get-tuple-element.71), channel_id=1, replica_groups=mesh['segment'=8,'wide'=16] {'wide'}, dimensions={0} | all-to-all | bytes 327680 | tf_op jit(solution)/shard_map/all_to_all | solution.py:44
  80.0 0.8 shard_map.89
  80.9 3.5 %all-to-all-start.3 = ((bf16[16,8,512]{2,1,0:T(8,128)(2,1)}), bf16[16,8,512]{2,1,0:T(8,128)(2,1)S(1)}, u32[]{:S(2)}, u32[]{:S(2)}) async-start(bf16[16,8,512]{2,1,0:T(8,128)(2,1)} %shard_map.89), calls=%async_computation.3 | async-start | bytes 262144 | tf_op jit(solution)/shard_map/all_to_all | solution.py:44
  84.4 1.6 shard_map.90
  86.1 6.3 %all-to-all-done.3.got_ref = bf16[16,8,512]{2,1,0:T(8,128)(2,1)S(1)} async-done(((bf16[16,8,512]{2,1,0:T(8,128)(2,1)}), bf16[16,8,512]{2,1,0:T(8,128)(2,1)S(1)}, u32[]{:S(2)}, u32[]{:S(2)}) %all-to-all-start.3) | async-done | bytes 131104 | tf_op jit(solution)/shard_map/all_to_all | solution.py:44
  92.3 2.0 shard_map.91
  94.3 3.6 %all-to-all-start.4 = ((bf16[16,8,1664]{2,1,0:T(8,128)(2,1)}), bf16[16,8,1664]{2,1,0:T(8,128)(2,1)S(1)}, u32[]{:S(2)}, u32[]{:S(2)}) async-start(bf16[16,8,1664]{2,1,0:T(8,128)(2,1)} %get-tuple-element.80), calls=%async_computation.4 | async-start | bytes 851968 | tf_op jit(solution)/shard_map/all_to_all | solution.py:44
  97.9 1.6 all-gather.10.cloned.1.call-done.source_ref
  99.5 1.2 shard_map.92.cross_ref
  100.7 6.7 %all-to-all-done.4.got_ref = bf16[16,8,1664]{2,1,0:T(8,128)(2,1)S(1)} async-done(((bf16[16,8,1664]{2,1,0:T(8,128)(2,1)}), bf16[16,8,1664]{2,1,0:T(8,128)(2,1)S(1)}, u32[]{:S(2)}, u32[]{:S(2)}) %all-to-all-start.4) | async-done | bytes 426016 | tf_op jit(solution)/shard_map/all_to_all | solution.py:44
  107.5 1.2 shard_map.93
  108.7 3.5 %all-to-all-start.5 = ((bf16[16,8,1024]{2,1,0:T(8,128)(2,1)}), bf16[16,8,1024]{2,1,0:T(8,128)(2,1)S(1)}, u32[]{:S(2)}, u32[]{:S(2)}) async-start(bf16[16,8,1024]{2,1,0:T(8,128)(2,1)} %shard_map.93), calls=%async_computation.5 | async-start | bytes 524288 | tf_op jit(solution)/shard_map/all_to_all | solution.py:44
  112.2 1.7 shard_map.94
  114.0 6.9 %all-to-all-done.5.got_ref = bf16[16,8,1024]{2,1,0:T(8,128)(2,1)S(1)} async-done(((bf16[16,8,1024]{2,1,0:T(8,128)(2,1)}), bf16[16,8,1024]{2,1,0:T(8,128)(2,1)S(1)}, u32[]{:S(2)}, u32[]{:S(2)}) %all-to-all-start.5) | async-done | bytes 262176 | tf_op jit(solution)/shard_map/all_to_all | solution.py:44
  120.8 2.0 shard_map.95
  122.9 3.6 %all-to-all-start.6 = ((bf16[16,8,1664]{2,1,0:T(8,128)(2,1)}), bf16[16,8,1664]{2,1,0:T(8,128)(2,1)S(1)}, u32[]{:S(2)}, u32[]{:S(2)}) async-start(bf16[16,8,1664]{2,1,0:T(8,128)(2,1)} %get-tuple-element.92), calls=%async_computation.6 | async-start | bytes 851968 | tf_op jit(solution)/shard_map/all_to_all | solution.py:44
  126.5 1.2 shard_map.96.cross_ref
  127.7 8.3 %all-to-all-done.6.got_ref = bf16[16,8,1664]{2,1,0:T(8,128)(2,1)S(1)} async-done(((bf16[16,8,1664]{2,1,0:T(8,128)(2,1)}), bf16[16,8,1664]{2,1,0:T(8,128)(2,1)S(1)}, u32[]{:S(2)}, u32[]{:S(2)}) %all-to-all-start.6) | async-done | bytes 426016 | tf_op jit(solution)/shard_map/all_to_all | solution.py:44
  136.0 1.2 shard_map.97
  137.2 3.5 %all-to-all-start.7 = ((bf16[16,8,1024]{2,1,0:T(8,128)(2,1)}), bf16[16,8,1024]{2,1,0:T(8,128)(2,1)S(1)}, u32[]{:S(2)}, u32[]{:S(2)}) async-start(bf16[16,8,1024]{2,1,0:T(8,128)(2,1)} %shard_map.97), calls=%async_computation.7 | async-start | bytes 524288 | tf_op jit(solution)/shard_map/all_to_all | solution.py:44
  140.8 1.7 shard_map.98
  142.6 6.9 %all-to-all-done.7.got_ref = bf16[16,8,1024]{2,1,0:T(8,128)(2,1)S(1)} async-done(((bf16[16,8,1024]{2,1,0:T(8,128)(2,1)}), bf16[16,8,1024]{2,1,0:T(8,128)(2,1)S(1)}, u32[]{:S(2)}, u32[]{:S(2)}) %all-to-all-start.7) | async-done | bytes 262176 | tf_op jit(solution)/shard_map/all_to_all | solution.py:44
  149.4 1.8 shard_map.99
  151.2 0.8 copy-done.3
  152.0 0.1 select_reduce_fusion.1
  152.1 0.2 select_reduce_fusion
  152.3 0.1 copy.26
  152.4 0.1 min.18.slots
  152.5 3.6 %all-to-all-start.8 = ((bf16[16,8,1664]{2,1,0:T(8,128)(2,1)}), bf16[16,8,1664]{2,1,0:T(8,128)(2,1)S(1)}, u32[]{:S(2)}, u32[]{:S(2)}) async-start(bf16[16,8,1664]{2,1,0:T(8,128)(2,1)} %copy-done.3), calls=%async_computation.8 | async-start | bytes 851968 | tf_op jit(solution)/shard_map/all_to_all | solution.py:44
  156.1 0.1 minimum_bitcast_fusion
  156.1 0.1 copy.25
  156.2 0.5 copy.30.limit_ref
  156.7 1.0 copy.32
  157.7 3.3 %shard_map.101.rest_0_ = bf16[16,8,4,512]{3,2,1,0:T(4,128)(2,1)} custom-call(s32[16]{0:T(128)S(1)} %min.18.slots, bf16[16,8,4,512]{3,2,1,0:T(4,128)(2,1)S(1)} %copy-done.2, bf16[8,16,512]{2,1,0:T(8,128)(2,1)S(1)} %bitcast.23, s32[8,64,1]{2,1,0:T(8,128)S(1)} %copy.30.limit_ref, bf16[8,128,1024]{2,1,0:T(8,128)(2,1)} %bitcast.27), custom_call_target="tpu_custom_call" | custom-call | flops 67108864 | bytes 786432 | tf_op jit(solution)/shard_map/pallas_call | solution.py:336
  160.9 1.2 shard_map.100.cross_ref
  162.2 3.4 %all-to-all-done.8.got_ref = bf16[16,8,1664]{2,1,0:T(8,128)(2,1)S(1)} async-done(((bf16[16,8,1664]{2,1,0:T(8,128)(2,1)}), bf16[16,8,1664]{2,1,0:T(8,128)(2,1)S(1)}, u32[]{:S(2)}, u32[]{:S(2)}) %all-to-all-start.8) | async-done | bytes 426016 | tf_op jit(solution)/shard_map/all_to_all | solution.py:44
  165.6 1.1 shard_map.102
  166.7 5.2 %all-to-all-start.9 = ((bf16[8,8,1024]{2,1,0:T(8,128)(2,1)}), bf16[8,8,1024]{2,1,0:T(8,128)(2,1)S(1)}, u32[]{:S(2)}, u32[]{:S(2)}) async-start(bf16[8,8,1024]{2,1,0:T(8,128)(2,1)} %shard_map.102), calls=%async_computation.9 | async-start | bytes 262144 | tf_op jit(solution)/shard_map/all_to_all | solution.py:44
  171.9 3.3 %shard_map.103.rest_0_ = bf16[16,8,4,512]{3,2,1,0:T(4,128)(2,1)} custom-call(s32[16]{0:T(128)S(1)} %min.18.slots, bf16[16,8,4,512]{3,2,1,0:T(4,128)(2,1)S(1)} %copy-done.2, bf16[8,16,512]{2,1,0:T(8,128)(2,1)S(1)} %bitcast.24, s32[8,64,1]{2,1,0:T(8,128)S(1)} %copy.30.limit_ref, bf16[8,128,1024]{2,1,0:T(8,128)(2,1)} %bitcast.28, ...), custom_call_target="tpu_custom_call", output_to_operand_aliasing={{}: (5, {})} | custom-call | flops 67108864 | bytes 786432 | tf_op jit(solution)/shard_map/pallas_call | solution.py:336
  175.2 3.7 %all-to-all-done.9.got_ref = bf16[8,8,1024]{2,1,0:T(8,128)(2,1)S(1)} async-done(((bf16[8,8,1024]{2,1,0:T(8,128)(2,1)}), bf16[8,8,1024]{2,1,0:T(8,128)(2,1)S(1)}, u32[]{:S(2)}, u32[]{:S(2)}) %all-to-all-start.9) | async-done | bytes 131104 | tf_op jit(solution)/shard_map/all_to_all | solution.py:44
  178.9 1.4 shard_map.104
  180.3 4.3 %all-to-all-start.10 = ((bf16[16,8,2048]{2,1,0:T(8,128)(2,1)}), bf16[16,8,2048]{2,1,0:T(8,128)(2,1)S(1)}, u32[]{:S(2)}, u32[]{:S(2)}) async-start(bf16[16,8,2048]{2,1,0:T(8,128)(2,1)} %shard_map.104), calls=%async_computation.10 | async-start | bytes 1048576 | tf_op jit(solution)/shard_map/all_to_all | solution.py:44
  184.6 3.3 %shard_map.105.carried_ref = bf16[16,8,4,512]{3,2,1,0:T(4,128)(2,1)} custom-call(s32[16]{0:T(128)S(1)} %min.18.slots, bf16[16,8,4,512]{3,2,1,0:T(4,128)(2,1)S(1)} %copy-done.2, bf16[8,16,512]{2,1,0:T(8,128)(2,1)S(1)} %bitcast.25, s32[8,64,1]{2,1,0:T(8,128)S(1)} %copy.30.limit_ref, bf16[8,128,1024]{2,1,0:T(8,128)(2,1)} %bitcast.29, ...), custom_call_target="tpu_custom_call", output_to_operand_aliasing={{}: (5, {})} | custom-call | flops 67108864 | bytes 786432 | tf_op jit(solution)/shard_map/pallas_call | solution.py:336
  187.9 7.7 %all-to-all-done.10.pages_ref = bf16[16,8,2048]{2,1,0:T(8,128)(2,1)S(1)} async-done(((bf16[16,8,2048]{2,1,0:T(8,128)(2,1)}), bf16[16,8,2048]{2,1,0:T(8,128)(2,1)S(1)}, u32[]{:S(2)}, u32[]{:S(2)}) %all-to-all-start.10) | async-done | bytes 524320 | tf_op jit(solution)/shard_map/all_to_all | solution.py:44
  195.6 1.6 shard_map.106
  (28 shorter events, 0.4 us)
Async XLA Ops:
  6.5 55.5 %all-gather.12.cloned.1.call-start = ((), (), s32[]{:S(2)}) async-start(), calls=%async_computation.12 | async-start | bytes 9437184 | tf_op jit(solution)/shard_map/all_gather | solution.py:397
  9.8 12.6 %copy-start = (bf16[2,512,512]{2,1,0:T(8,128)(2,1)S(1)}, bf16[2,512,512]{2,1,0:T(8,128)(2,1)}, u32[]{:S(2)}) copy-start(bf16[2,512,512]{2,1,0:T(8,128)(2,1)} %get-tuple-element.60.both_ref) | copy-start | bytes 3145732
  9.9 3.2 %collective-permute-start = (bf16[512,512]{1,0:T(8,128)(2,1)}, bf16[512,512]{1,0:T(8,128)(2,1)S(1)}, u32[]{:S(2)}, u32[]{:S(2)}) collective-permute-start(bf16[512,512]{1,0:T(8,128)(2,1)} %get-tuple-element.61), channel_id=1, source_target_pairs={{0,16},{32,48},{64,80},{96,112},{1,17},{33,49},{65,81},{97,113},{2... | collective-permute-start | bytes 1572872 | tf_op jit(solution)/shard_map/ppermute | solution.py:398
  13.0 15.1 %copy-start.1 = (bf16[4,256,512]{2,1,0:T(8,128)(2,1)S(1)}, bf16[4,256,512]{2,1,0:T(8,128)(2,1)}, u32[]{:S(2)}) copy-start(bf16[4,256,512]{2,1,0:T(8,128)(2,1)} %param.8) | copy-start | bytes 3145732
  15.2 8.2 %collective-permute-start.1 = (bf16[128,512]{1,0:T(8,128)(2,1)S(1)}, bf16[128,512]{1,0:T(8,128)(2,1)S(1)}, u32[]{:S(2)}, u32[]{:S(2)}) collective-permute-start(bf16[128,512]{1,0:T(8,128)(2,1)S(1)} %get-tuple-element.63), channel_id=1, source_target_pairs={{0,32},{16,48},{1,33},{17,49},{2,34},{18,50},{3,35},{19,51},{4,36}... | collective-permute-start | bytes 393224 | tf_op jit(solution)/shard_map/ppermute | solution.py:427
  18.9 8.3 %collective-permute-start.2 = (bf16[128,512]{1,0:T(8,128)(2,1)S(1)}, bf16[128,512]{1,0:T(8,128)(2,1)S(1)}, u32[]{:S(2)}, u32[]{:S(2)}) collective-permute-start(bf16[128,512]{1,0:T(8,128)(2,1)S(1)} %get-tuple-element.64), channel_id=1, source_target_pairs={{0,64},{16,80},{1,65},{17,81},{2,66},{18,82},{3,67},{19,83},{4,68}... | collective-permute-start | bytes 393224 | tf_op jit(solution)/shard_map/ppermute | solution.py:427
  21.1 7.1 %collective-permute-start.3 = (bf16[128,512]{1,0:T(8,128)(2,1)S(1)}, bf16[128,512]{1,0:T(8,128)(2,1)S(1)}, u32[]{:S(2)}, u32[]{:S(2)}) collective-permute-start(bf16[128,512]{1,0:T(8,128)(2,1)S(1)} %get-tuple-element.65), channel_id=1, source_target_pairs={{0,96},{16,112},{1,97},{17,113},{2,98},{18,114},{3,99},{19,115},{4... | collective-permute-start | bytes 393224 | tf_op jit(solution)/shard_map/ppermute | solution.py:427
  51.4 15.7 %all-to-all-start.1 = ((bf16[16,40,512]{2,1,0:T(8,128)(2,1)}), bf16[16,40,512]{2,1,0:T(8,128)(2,1)S(1)}, u32[]{:S(2)}, u32[]{:S(2)}) async-start(bf16[16,40,512]{2,1,0:T(8,128)(2,1)} %shard_map.86), calls=%async_computation.1 | async-start | bytes 1310720 | tf_op jit(solution)/shard_map/all_to_all | solution.py:44
  55.0 44.5 %all-gather.10.cloned.1.call-start = ((), (), s32[]{:S(2)}) async-start(), calls=%async_computation.11 | async-start | bytes 4718592 | tf_op jit(solution)/shard_map/all_gather | solution.py:512
  80.9 11.5 %all-to-all-start.3 = ((bf16[16,8,512]{2,1,0:T(8,128)(2,1)}), bf16[16,8,512]{2,1,0:T(8,128)(2,1)S(1)}, u32[]{:S(2)}, u32[]{:S(2)}) async-start(bf16[16,8,512]{2,1,0:T(8,128)(2,1)} %shard_map.89), calls=%async_computation.3 | async-start | bytes 262144 | tf_op jit(solution)/shard_map/all_to_all | solution.py:44
  84.4 73.3 %all-gather.14.cloned.1.call-start = ((), (), s32[]{:S(2)}) async-start(), calls=%async_computation.13 | async-start | bytes 2359296 | tf_op jit(solution)/shard_map/all_gather | solution.py:529
  94.3 13.1 %all-to-all-start.4 = ((bf16[16,8,1664]{2,1,0:T(8,128)(2,1)}), bf16[16,8,1664]{2,1,0:T(8,128)(2,1)S(1)}, u32[]{:S(2)}, u32[]{:S(2)}) async-start(bf16[16,8,1664]{2,1,0:T(8,128)(2,1)} %get-tuple-element.80), calls=%async_computation.4 | async-start | bytes 851968 | tf_op jit(solution)/shard_map/all_to_all | solution.py:44
  108.7 12.2 %all-to-all-start.5 = ((bf16[16,8,1024]{2,1,0:T(8,128)(2,1)}), bf16[16,8,1024]{2,1,0:T(8,128)(2,1)S(1)}, u32[]{:S(2)}, u32[]{:S(2)}) async-start(bf16[16,8,1024]{2,1,0:T(8,128)(2,1)} %shard_map.93), calls=%async_computation.5 | async-start | bytes 524288 | tf_op jit(solution)/shard_map/all_to_all | solution.py:44
  112.2 59.7 %all-gather.16.cloned.1.call-start = ((), (), s32[]{:S(2)}) async-start(), calls=%async_computation.14 | async-start | bytes 2359296 | tf_op jit(solution)/shard_map/all_gather | solution.py:529
  122.9 13.1 %all-to-all-start.6 = ((bf16[16,8,1664]{2,1,0:T(8,128)(2,1)}), bf16[16,8,1664]{2,1,0:T(8,128)(2,1)S(1)}, u32[]{:S(2)}, u32[]{:S(2)}) async-start(bf16[16,8,1664]{2,1,0:T(8,128)(2,1)} %get-tuple-element.92), calls=%async_computation.6 | async-start | bytes 851968 | tf_op jit(solution)/shard_map/all_to_all | solution.py:44
  137.2 12.2 %all-to-all-start.7 = ((bf16[16,8,1024]{2,1,0:T(8,128)(2,1)}), bf16[16,8,1024]{2,1,0:T(8,128)(2,1)S(1)}, u32[]{:S(2)}, u32[]{:S(2)}) async-start(bf16[16,8,1024]{2,1,0:T(8,128)(2,1)} %shard_map.97), calls=%async_computation.7 | async-start | bytes 524288 | tf_op jit(solution)/shard_map/all_to_all | solution.py:44
  140.8 43.8 %all-gather.18.cloned.1.call-start = ((), (), s32[]{:S(2)}) async-start(), calls=%async_computation.15 | async-start | bytes 2359296 | tf_op jit(solution)/shard_map/all_gather | solution.py:529
  142.5 9.4 %copy-start.4 = (s32[8,8,1]{1,2,0:T(1,128)S(1)}, s32[8,8,1]{1,2,0:T(1,128)}, u32[]{:S(2)}) copy-start(s32[8,8,1]{1,2,0:T(1,128)} %param.12) | copy-start | bytes 772
  142.5 13.5 %copy-start.5 = (s32[16,8]{0,1:T(8,128)S(1)}, s32[16,8]{0,1:T(8,128)}, u32[]{:S(2)}) copy-start(s32[16,8]{0,1:T(8,128)} %param.15) | copy-start | bytes 1540
  149.4 8.2 %copy-start.2 = (bf16[16,8,4,512]{3,2,1,0:T(4,128)(2,1)S(1)}, bf16[16,8,4,512]{3,2,1,0:T(4,128)(2,1)}, u32[]{:S(2)}) copy-start(bf16[16,8,4,512]{3,2,1,0:T(4,128)(2,1)} %q_ref.7) | copy-start | bytes 1572868
  151.2 0.8 copy-start.3
  152.5 13.1 %all-to-all-start.8 = ((bf16[16,8,1664]{2,1,0:T(8,128)(2,1)}), bf16[16,8,1664]{2,1,0:T(8,128)(2,1)S(1)}, u32[]{:S(2)}, u32[]{:S(2)}) async-start(bf16[16,8,1664]{2,1,0:T(8,128)(2,1)} %copy-done.3), calls=%async_computation.8 | async-start | bytes 851968 | tf_op jit(solution)/shard_map/all_to_all | solution.py:44
  166.7 12.2 %all-to-all-start.9 = ((bf16[8,8,1024]{2,1,0:T(8,128)(2,1)}), bf16[8,8,1024]{2,1,0:T(8,128)(2,1)S(1)}, u32[]{:S(2)}, u32[]{:S(2)}) async-start(bf16[8,8,1024]{2,1,0:T(8,128)(2,1)} %shard_map.102), calls=%async_computation.9 | async-start | bytes 262144 | tf_op jit(solution)/shard_map/all_to_all | solution.py:44
  180.3 15.3 %all-to-all-start.10 = ((bf16[16,8,2048]{2,1,0:T(8,128)(2,1)}), bf16[16,8,2048]{2,1,0:T(8,128)(2,1)S(1)}, u32[]{:S(2)}, u32[]{:S(2)}) async-start(bf16[16,8,2048]{2,1,0:T(8,128)(2,1)} %shard_map.104), calls=%async_computation.10 | async-start | bytes 1048576 | tf_op jit(solution)/shard_map/all_to_all | solution.py:44
Sparse Core Ops, SparseCore 0:
  10.0 51.9 all-gather.11
  68.9 30.5 all-gather.9
  101.2 25.0 all-gather.13
  127.9 25.4 all-gather.15
  155.0 26.0 all-gather.17

commit v7 on v6

--- a/solution.py
+++ b/solution.py
@@ -474,7 +474,7 @@
         mode = "first" if before == (0,) else "later" if earlier is not None else "pair"
         count = len(following) + (len(following) == 2)
         shapes = [
-            array(wide, share, LANES + count * lat),
+            (array if mode == "first" else far)(wide, share, LANES + count * lat),
             near(mine, local_width),
             far(wide, high, lat) if mode == "first" else far(mine, 2 * lat),
         ]
@@ -527,11 +527,13 @@
         extra = earlier if even == 2 else None
         sent, state, held = advance(before, (even, odd), got, state, weights, extra)
         pages.append(lax.all_gather(held, "segment", axis=0))
-        got, mixing = tied(exchanged(sent, "wide"), resident(crosses, [even, odd]))
         if odd < layers - 1:
-            sent = pair_step(got, mixing, wide)
             following = resident_weights((even, odd), (even + 2, even + 3))
-            got, weights = tied(exchanged(sent, "wide"), following)
+            mixing = resident(crosses, [even, odd])
+            got, mixing, weights = tied(exchanged(sent, "wide"), mixing, following)
+            got = exchanged(pair_step(got, mixing, wide), "wide")
+        else:
+            got, mixing = tied(exchanged(sent, "wide"), resident(crosses, [even, odd]))
 
     targets = page_lists[:, :, 0]
     owned = targets == position

time: 205 us -> 202 us (0.985)
  blocking collectives: 32.7 us -> 55.9 us
  waiting for transfers between devices: 68.8 us -> 51.5 us
  starting transfers between devices: 43.1 us -> 35.3 us
    all_to_all x2 -> x4, blocking collectives: 32.7 us -> 55.9 us  [exchanged(): return lax.all_to_all(sent, axis, 0, 0, tiled=True)]
    all_to_all x9 -> x7, waiting for transfers between devices: 53.7 us -> 37.9 us  [exchanged(): return lax.all_to_all(sent, axis, 0, 0, tiled=True)]
    all_to_all x9 -> x7, starting transfers between devices: 34.3 us -> 26.6 us  [exchanged(): return lax.all_to_all(sent, axis, 0, 0, tiled=True)]
  transfers between devices with their start and end apart: 18 -> 16, of which waited for: 14 -> 11; matrix products, arithmetic and copies ran while one was open for 1% -> 1% of each run, Pallas kernels for 18% -> 18%
where the time goes in v7:
time: 202 us; the launch traced here: 201 us
  blocking collectives  55.9 us (28%)
  waiting for transfers between devices  51.5 us (25%)
  Pallas kernels  41.7 us (21%)
  starting transfers between devices  35.3 us (17%)
  between operations  13.5 us (7%)
  local copies, waits for them, and re-layouts  2.79 us (1%)
    all_to_all x4, blocking collectives, exchanged(): return lax.all_to_all(sent, axis, 0, 0, tiled=True)  55.9 us
    all_to_all x7, waiting for transfers between devices, exchanged(): return lax.all_to_all(sent, axis, 0, 0, tiled=True)  37.9 us
    all_to_all x7, starting transfers between devices, exchanged(): return lax.all_to_all(sent, axis, 0, 0, tiled=True)  26.6 us
    pallas_call x14, Pallas kernels, call(): pl.pallas_call(body, grid_spec=pltpu.PrefetchScalarGridSpec(num_scalar_pr...  20.3 us
    pallas_call x4, Pallas kernels, decode_pair(): pl.pallas_call(last_decode_kernel if last else functools.partial(decode_k...  11.4 us
    pallas_call x7, Pallas kernels, resident(): pl.pallas_call(functools.partial(reside_kernel, lists), in_specs=[in_hbm]...  9.99 us
    ppermute x3, starting transfers between devices, shards(): lax.ppermute(home[hop], 'segment', [(0, 2 * hop), (1, 2 * hop + 1)])  7.15 us
    all_gather x1, waiting for transfers between devices, shards(): every = lax.all_gather(both, 'segment', axis=0)  6.99 us
  transfers between devices with their start and end apart: 16, of which 11 were waited for; matrix products, arithmetic and copies ran while one was open for 1% of the time, Pallas kernels for 18%

profile of v7, /device:TPU:0, one launch (start us, length us, event | category | flops | bytes accessed | tf_op | source)
XLA Modules:
  0.0 201.1 jit_solution(6409950664141524959)
XLA Ops:
  6.5 0.1 pad_add_fusion.where
  6.6 3.2 %shard_map.82 = (bf16[2,512,512]{2,1,0:T(8,128)(2,1)}, bf16[512,512]{1,0:T(8,128)(2,1)}) custom-call(s32[2]{0:T(128)S(1)} %pad_add_fusion.where, bf16[1,512,512]{2,1,0:T(8,128)(2,1)} %latent_ref.1, bf16[1,512]{1,0:T(2,128)(2,1)} %gain_ref.1, bf16[1,512,512]{2,1,0:T(8,128)(2,1)} %back_ref.1), custom_call_target="tpu_custom_call" | custom-call | flops 268435456 | bytes 3145728 | tf_op jit(solution)/shard_map/pallas_call | solution.py:66
  9.9 1.5 collective-permute-start
  11.3 1.7 collective-permute-done.lent_ref
  13.0 2.2 %shard_map.83 = (bf16[128,512]{1,0:T(8,128)(2,1)S(1)}, bf16[128,512]{1,0:T(8,128)(2,1)S(1)}, bf16[128,512]{1,0:T(8,128)(2,1)S(1)}, bf16[128,512]{1,0:T(8,128)(2,1)S(1)}) custom-call(s32[2]{0:T(128)S(1)} %pad_add_fusion.where, bf16[4,2,128,512]{3,2,1,0:T(8,128)(2,1)} %bitcast.20, bf16[2,512,512]{2,1,0:T(8,128)(2,1)} %get-tuple-element.58.both_ref, ...), custom_call_target="tpu_custom_call" | custom-call | flops 268435456 | bytes 1048576 | tf_op jit(solution)/shard_map/pallas_call | solution.py:66
  15.2 3.7 %collective-permute-start.1 = (bf16[128,512]{1,0:T(8,128)(2,1)S(1)}, bf16[128,512]{1,0:T(8,128)(2,1)S(1)}, u32[]{:S(2)}, u32[]{:S(2)}) collective-permute-start(bf16[128,512]{1,0:T(8,128)(2,1)S(1)} %get-tuple-element.61), channel_id=1, source_target_pairs={{0,32},{16,48},{1,33},{17,49},{2,34},{18,50},{3,35},{19,51},{4,36}... | collective-permute-start | bytes 393224 | tf_op jit(solution)/shard_map/ppermute | solution.py:427
  18.9 2.2 %collective-permute-start.2 = (bf16[128,512]{1,0:T(8,128)(2,1)S(1)}, bf16[128,512]{1,0:T(8,128)(2,1)S(1)}, u32[]{:S(2)}, u32[]{:S(2)}) collective-permute-start(bf16[128,512]{1,0:T(8,128)(2,1)S(1)} %get-tuple-element.62), channel_id=1, source_target_pairs={{0,64},{16,80},{1,65},{17,81},{2,66},{18,82},{3,67},{19,83},{4,68}... | collective-permute-start | bytes 393224 | tf_op jit(solution)/shard_map/ppermute | solution.py:427
  21.1 1.3 collective-permute-start.3
  22.4 1.0 shard_map.84.cross_ref
  23.5 3.8 %collective-permute-done.2.b_ref = bf16[128,512]{1,0:T(8,128)(2,1)S(1)} collective-permute-done((bf16[128,512]{1,0:T(8,128)(2,1)S(1)}, bf16[128,512]{1,0:T(8,128)(2,1)S(1)}, u32[]{:S(2)}, u32[]{:S(2)}) %collective-permute-start.2) | collective-permute-done | bytes 131104 | tf_op jit(solution)/shard_map/ppermute | solution.py:427
  27.2 0.9 collective-permute-done.3.c_ref
  28.2 0.7 shard_map.85
  28.9 21.5 %all_to_all.55.got_ref = bf16[16,8,2688]{2,1,0:T(8,128)(2,1)S(1)} all-to-all(bf16[16,8,2688]{2,1,0:T(8,128)(2,1)S(1)} %shard_map.85), channel_id=1, replica_groups=mesh['segment'=8,'wide'=16] {'wide'}, dimensions={0} | all-to-all | bytes 1376256 | tf_op jit(solution)/shard_map/all_to_all | solution.py:44
  50.3 1.1 shard_map.86
  51.4 3.6 %all-to-all-start.1 = ((bf16[16,40,512]{2,1,0:T(8,128)(2,1)}), bf16[16,40,512]{2,1,0:T(8,128)(2,1)S(1)}, u32[]{:S(2)}, u32[]{:S(2)}) async-start(bf16[16,40,512]{2,1,0:T(8,128)(2,1)} %shard_map.86), calls=%async_computation.1 | async-start | bytes 1310720 | tf_op jit(solution)/shard_map/all_to_all | solution.py:44
  55.0 0.0 all-gather.10.cloned.1.call-start
  55.0 7.0 %all-gather.12.cloned.1.call-done.source_ref = bf16[16,512,512]{2,1,0:T(8,128)(2,1)} async-done(((bf16[2,512,512]{2,1,0:T(8,128)(2,1)}), bf16[16,512,512]{2,1,0:T(8,128)(2,1)}) %all-gather.12.cloned.1.call-update) | async-done | bytes 8388624 | tf_op jit(solution)/shard_map/all_gather | solution.py:397
  62.0 1.2 shard_map.87
  63.3 3.8 %all-to-all-done.1.got_ref.rest_3_ = bf16[16,40,512]{2,1,0:T(8,128)(2,1)S(1)} async-done(((bf16[16,40,512]{2,1,0:T(8,128)(2,1)}), bf16[16,40,512]{2,1,0:T(8,128)(2,1)S(1)}, u32[]{:S(2)}, u32[]{:S(2)}) %all-to-all-start.1) | async-done | bytes 655392 | tf_op jit(solution)/shard_map/all_to_all | solution.py:44
  67.1 1.7 shard_map.88
  68.8 11.2 %all_to_all.56.got_ref = bf16[16,8,640]{2,1,0:T(8,128)(2,1)S(1)} all-to-all(bf16[16,8,640]{2,1,0:T(8,128)(2,1)S(1)} %get-tuple-element.69), channel_id=1, replica_groups=mesh['segment'=8,'wide'=16] {'wide'}, dimensions={0} | all-to-all | bytes 327680 | tf_op jit(solution)/shard_map/all_to_all | solution.py:44
  80.0 0.8 shard_map.89
  80.9 3.5 %all-to-all-start.3 = ((bf16[16,8,512]{2,1,0:T(8,128)(2,1)}), bf16[16,8,512]{2,1,0:T(8,128)(2,1)S(1)}, u32[]{:S(2)}, u32[]{:S(2)}) async-start(bf16[16,8,512]{2,1,0:T(8,128)(2,1)} %shard_map.89), calls=%async_computation.3 | async-start | bytes 262144 | tf_op jit(solution)/shard_map/all_to_all | solution.py:44
  84.4 1.6 shard_map.90
  86.1 6.3 %all-to-all-done.3.got_ref = bf16[16,8,512]{2,1,0:T(8,128)(2,1)S(1)} async-done(((bf16[16,8,512]{2,1,0:T(8,128)(2,1)}), bf16[16,8,512]{2,1,0:T(8,128)(2,1)S(1)}, u32[]{:S(2)}, u32[]{:S(2)}) %all-to-all-start.3) | async-done | bytes 131104 | tf_op jit(solution)/shard_map/all_to_all | solution.py:44
  92.3 2.0 shard_map.91
  94.3 3.6 %all-to-all-start.4 = ((bf16[16,8,1664]{2,1,0:T(8,128)(2,1)}), bf16[16,8,1664]{2,1,0:T(8,128)(2,1)S(1)}, u32[]{:S(2)}, u32[]{:S(2)}) async-start(bf16[16,8,1664]{2,1,0:T(8,128)(2,1)} %get-tuple-element.78), calls=%async_computation.4 | async-start | bytes 851968 | tf_op jit(solution)/shard_map/all_to_all | solution.py:44
  97.9 0.0 all-gather.16.cloned.1.call-start
  98.0 1.8 shard_map.93
  99.7 1.0 copy-done.3
  100.7 1.2 shard_map.92.cross_ref
  102.0 5.5 %all-to-all-done.4.got_ref = bf16[16,8,1664]{2,1,0:T(8,128)(2,1)S(1)} async-done(((bf16[16,8,1664]{2,1,0:T(8,128)(2,1)}), bf16[16,8,1664]{2,1,0:T(8,128)(2,1)S(1)}, u32[]{:S(2)}, u32[]{:S(2)}) %all-to-all-start.4) | async-done | bytes 426016 | tf_op jit(solution)/shard_map/all_to_all | solution.py:44
  107.4 0.5 shard_map.94
  107.9 11.6 %all_to_all.57.got_ref = bf16[16,8,1024]{2,1,0:T(8,128)(2,1)S(1)} all-to-all(bf16[16,8,1024]{2,1,0:T(8,128)(2,1)S(1)} %shard_map.94), channel_id=1, replica_groups=mesh['segment'=8,'wide'=16] {'wide'}, dimensions={0} | all-to-all | bytes 524288 | tf_op jit(solution)/shard_map/all_to_all | solution.py:44
  119.6 2.0 %shard_map.95 = (bf16[16,8,1664]{2,1,0:T(8,128)(2,1)}, bf16[128,512]{1,0:T(8,128)(2,1)S(1)}, bf16[128,1024]{1,0:T(8,128)(2,1)}) custom-call(s32[2]{0:T(128)S(1)} %pad_add_fusion.where, bf16[16,8,1024]{2,1,0:T(8,128)(2,1)S(1)} %all_to_all.57.got_ref, bf16[128,512]{1,0:T(8,128)(2,1)S(1)} %get-tuple-element.85.states_ref, ...), custom_call_target="tpu_custom_call" | custom-call | flops 335544320 | bytes 1638400 | tf_op jit(solution)/shard_map/pallas_call | solution.py:66
  121.6 3.6 %all-to-all-start.6 = ((bf16[16,8,1664]{2,1,0:T(8,128)(2,1)}), bf16[16,8,1664]{2,1,0:T(8,128)(2,1)S(1)}, u32[]{:S(2)}, u32[]{:S(2)}) async-start(bf16[16,8,1664]{2,1,0:T(8,128)(2,1)} %get-tuple-element.89), calls=%async_computation.6 | async-start | bytes 851968 | tf_op jit(solution)/shard_map/all_to_all | solution.py:44
  125.2 0.0 all-gather.18.cloned.1.call-start
  125.2 1.7 shard_map.97
  127.0 1.0 copy-done.5
  128.0 1.2 shard_map.96.cross_ref
  129.2 5.5 %all-to-all-done.6.got_ref = bf16[16,8,1664]{2,1,0:T(8,128)(2,1)S(1)} async-done(((bf16[16,8,1664]{2,1,0:T(8,128)(2,1)}), bf16[16,8,1664]{2,1,0:T(8,128)(2,1)S(1)}, u32[]{:S(2)}, u32[]{:S(2)}) %all-to-all-start.6) | async-done | bytes 426016 | tf_op jit(solution)/shard_map/all_to_all | solution.py:44
  134.7 0.5 shard_map.98
  135.2 11.6 %all_to_all.58.got_ref = bf16[16,8,1024]{2,1,0:T(8,128)(2,1)S(1)} all-to-all(bf16[16,8,1024]{2,1,0:T(8,128)(2,1)S(1)} %shard_map.98), channel_id=1, replica_groups=mesh['segment'=8,'wide'=16] {'wide'}, dimensions={0} | all-to-all | bytes 524288 | tf_op jit(solution)/shard_map/all_to_all | solution.py:44
  146.9 2.0 %shard_map.99 = (bf16[16,8,1664]{2,1,0:T(8,128)(2,1)}, bf16[128,512]{1,0:T(8,128)(2,1)}, bf16[128,1024]{1,0:T(8,128)(2,1)}) custom-call(s32[2]{0:T(128)S(1)} %pad_add_fusion.where, bf16[16,8,1024]{2,1,0:T(8,128)(2,1)S(1)} %all_to_all.58.got_ref, bf16[128,512]{1,0:T(8,128)(2,1)S(1)} %get-tuple-element.95.states_ref, ...), custom_call_target="tpu_custom_call" | custom-call | flops 335544320 | bytes 1638400 | tf_op jit(solution)/shard_map/pallas_call | solution.py:66
  148.9 0.1 select_reduce_fusion.1
  149.1 0.2 select_reduce_fusion
  149.3 0.1 copy.26
  149.4 0.1 min.18.slots
  149.4 3.6 %all-to-all-start.8 = ((bf16[16,8,1664]{2,1,0:T(8,128)(2,1)}), bf16[16,8,1664]{2,1,0:T(8,128)(2,1)S(1)}, u32[]{:S(2)}, u32[]{:S(2)}) async-start(bf16[16,8,1664]{2,1,0:T(8,128)(2,1)} %get-tuple-element.99), calls=%async_computation.8 | async-start | bytes 851968 | tf_op jit(solution)/shard_map/all_to_all | solution.py:44
  153.0 0.1 minimum_bitcast_fusion
  153.1 0.1 copy.25
  153.2 0.5 copy.30.limit_ref
  153.7 3.3 %shard_map.101.rest_0_ = bf16[16,8,4,512]{3,2,1,0:T(4,128)(2,1)} custom-call(s32[16]{0:T(128)S(1)} %min.18.slots, bf16[16,8,4,512]{3,2,1,0:T(4,128)(2,1)S(1)} %copy-done.2, bf16[8,16,512]{2,1,0:T(8,128)(2,1)S(1)} %bitcast.23, s32[8,64,1]{2,1,0:T(8,128)S(1)} %copy.30.limit_ref, bf16[8,128,1024]{2,1,0:T(8,128)(2,1)} %bitcast.27), custom_call_target="tpu_custom_call" | custom-call | flops 67108864 | bytes 786432 | tf_op jit(solution)/shard_map/pallas_call | solution.py:336
  157.0 1.2 shard_map.100.cross_ref
  158.2 4.3 %all-to-all-done.8.got_ref = bf16[16,8,1664]{2,1,0:T(8,128)(2,1)S(1)} async-done(((bf16[16,8,1664]{2,1,0:T(8,128)(2,1)}), bf16[16,8,1664]{2,1,0:T(8,128)(2,1)S(1)}, u32[]{:S(2)}, u32[]{:S(2)}) %all-to-all-start.8) | async-done | bytes 426016 | tf_op jit(solution)/shard_map/all_to_all | solution.py:44
  162.5 1.1 shard_map.102
  163.7 5.2 %all-to-all-start.9 = ((bf16[8,8,1024]{2,1,0:T(8,128)(2,1)}), bf16[8,8,1024]{2,1,0:T(8,128)(2,1)S(1)}, u32[]{:S(2)}, u32[]{:S(2)}) async-start(bf16[8,8,1024]{2,1,0:T(8,128)(2,1)} %shard_map.102), calls=%async_computation.9 | async-start | bytes 262144 | tf_op jit(solution)/shard_map/all_to_all | solution.py:44
  168.9 3.3 %shard_map.103.rest_0_ = bf16[16,8,4,512]{3,2,1,0:T(4,128)(2,1)} custom-call(s32[16]{0:T(128)S(1)} %min.18.slots, bf16[16,8,4,512]{3,2,1,0:T(4,128)(2,1)S(1)} %copy-done.2, bf16[8,16,512]{2,1,0:T(8,128)(2,1)S(1)} %bitcast.24, s32[8,64,1]{2,1,0:T(8,128)S(1)} %copy.30.limit_ref, bf16[8,128,1024]{2,1,0:T(8,128)(2,1)} %bitcast.28, ...), custom_call_target="tpu_custom_call", output_to_operand_aliasing={{}: (5, {})} | custom-call | flops 67108864 | bytes 786432 | tf_op jit(solution)/shard_map/pallas_call | solution.py:336
  172.2 4.2 %all-to-all-done.9.got_ref = bf16[8,8,1024]{2,1,0:T(8,128)(2,1)S(1)} async-done(((bf16[8,8,1024]{2,1,0:T(8,128)(2,1)}), bf16[8,8,1024]{2,1,0:T(8,128)(2,1)S(1)}, u32[]{:S(2)}, u32[]{:S(2)}) %all-to-all-start.9) | async-done | bytes 131104 | tf_op jit(solution)/shard_map/all_to_all | solution.py:44
  176.4 1.4 shard_map.104
  177.8 3.6 %all-to-all-start.10 = ((bf16[16,8,2048]{2,1,0:T(8,128)(2,1)}), bf16[16,8,2048]{2,1,0:T(8,128)(2,1)S(1)}, u32[]{:S(2)}, u32[]{:S(2)}) async-start(bf16[16,8,2048]{2,1,0:T(8,128)(2,1)} %shard_map.104), calls=%async_computation.10 | async-start | bytes 1048576 | tf_op jit(solution)/shard_map/all_to_all | solution.py:44
  181.4 3.3 %shard_map.105.carried_ref = bf16[16,8,4,512]{3,2,1,0:T(4,128)(2,1)} custom-call(s32[16]{0:T(128)S(1)} %min.18.slots, bf16[16,8,4,512]{3,2,1,0:T(4,128)(2,1)S(1)} %copy-done.2, bf16[8,16,512]{2,1,0:T(8,128)(2,1)S(1)} %bitcast.25, s32[8,64,1]{2,1,0:T(8,128)S(1)} %copy.30.limit_ref, bf16[8,128,1024]{2,1,0:T(8,128)(2,1)} %bitcast.29, ...), custom_call_target="tpu_custom_call", output_to_operand_aliasing={{}: (5, {})} | custom-call | flops 67108864 | bytes 786432 | tf_op jit(solution)/shard_map/pallas_call | solution.py:336
  184.7 8.4 %all-to-all-done.10.pages_ref = bf16[16,8,2048]{2,1,0:T(8,128)(2,1)S(1)} async-done(((bf16[16,8,2048]{2,1,0:T(8,128)(2,1)}), bf16[16,8,2048]{2,1,0:T(8,128)(2,1)S(1)}, u32[]{:S(2)}, u32[]{:S(2)}) %all-to-all-start.10) | async-done | bytes 524320 | tf_op jit(solution)/shard_map/all_to_all | solution.py:44
  193.0 1.6 shard_map.106
  (34 shorter events, 0.3 us)
Async XLA Ops:
  6.5 55.5 %all-gather.12.cloned.1.call-start = ((), (), s32[]{:S(2)}) async-start(), calls=%async_computation.12 | async-start | bytes 9437184 | tf_op jit(solution)/shard_map/all_gather | solution.py:397
  9.8 12.6 %copy-start = (bf16[2,512,512]{2,1,0:T(8,128)(2,1)S(1)}, bf16[2,512,512]{2,1,0:T(8,128)(2,1)}, u32[]{:S(2)}) copy-start(bf16[2,512,512]{2,1,0:T(8,128)(2,1)} %get-tuple-element.58.both_ref) | copy-start | bytes 3145732
  9.9 3.2 %collective-permute-start = (bf16[512,512]{1,0:T(8,128)(2,1)}, bf16[512,512]{1,0:T(8,128)(2,1)S(1)}, u32[]{:S(2)}, u32[]{:S(2)}) collective-permute-start(bf16[512,512]{1,0:T(8,128)(2,1)} %get-tuple-element.59), channel_id=1, source_target_pairs={{0,16},{32,48},{64,80},{96,112},{1,17},{33,49},{65,81},{97,113},{2... | collective-permute-start | bytes 1572872 | tf_op jit(solution)/shard_map/ppermute | solution.py:398
  13.0 15.1 %copy-start.1 = (bf16[4,256,512]{2,1,0:T(8,128)(2,1)S(1)}, bf16[4,256,512]{2,1,0:T(8,128)(2,1)}, u32[]{:S(2)}) copy-start(bf16[4,256,512]{2,1,0:T(8,128)(2,1)} %param.8) | copy-start | bytes 3145732
  15.2 8.2 %collective-permute-start.1 = (bf16[128,512]{1,0:T(8,128)(2,1)S(1)}, bf16[128,512]{1,0:T(8,128)(2,1)S(1)}, u32[]{:S(2)}, u32[]{:S(2)}) collective-permute-start(bf16[128,512]{1,0:T(8,128)(2,1)S(1)} %get-tuple-element.61), channel_id=1, source_target_pairs={{0,32},{16,48},{1,33},{17,49},{2,34},{18,50},{3,35},{19,51},{4,36}... | collective-permute-start | bytes 393224 | tf_op jit(solution)/shard_map/ppermute | solution.py:427
  18.9 8.3 %collective-permute-start.2 = (bf16[128,512]{1,0:T(8,128)(2,1)S(1)}, bf16[128,512]{1,0:T(8,128)(2,1)S(1)}, u32[]{:S(2)}, u32[]{:S(2)}) collective-permute-start(bf16[128,512]{1,0:T(8,128)(2,1)S(1)} %get-tuple-element.62), channel_id=1, source_target_pairs={{0,64},{16,80},{1,65},{17,81},{2,66},{18,82},{3,67},{19,83},{4,68}... | collective-permute-start | bytes 393224 | tf_op jit(solution)/shard_map/ppermute | solution.py:427
  21.1 7.1 %collective-permute-start.3 = (bf16[128,512]{1,0:T(8,128)(2,1)S(1)}, bf16[128,512]{1,0:T(8,128)(2,1)S(1)}, u32[]{:S(2)}, u32[]{:S(2)}) collective-permute-start(bf16[128,512]{1,0:T(8,128)(2,1)S(1)} %get-tuple-element.63), channel_id=1, source_target_pairs={{0,96},{16,112},{1,97},{17,113},{2,98},{18,114},{3,99},{19,115},{4... | collective-permute-start | bytes 393224 | tf_op jit(solution)/shard_map/ppermute | solution.py:427
  51.4 15.7 %all-to-all-start.1 = ((bf16[16,40,512]{2,1,0:T(8,128)(2,1)}), bf16[16,40,512]{2,1,0:T(8,128)(2,1)S(1)}, u32[]{:S(2)}, u32[]{:S(2)}) async-start(bf16[16,40,512]{2,1,0:T(8,128)(2,1)} %shard_map.86), calls=%async_computation.1 | async-start | bytes 1310720 | tf_op jit(solution)/shard_map/all_to_all | solution.py:44
  55.0 45.8 %all-gather.10.cloned.1.call-start = ((), (), s32[]{:S(2)}) async-start(), calls=%async_computation.11 | async-start | bytes 4718592 | tf_op jit(solution)/shard_map/all_gather | solution.py:512
  80.9 11.5 %all-to-all-start.3 = ((bf16[16,8,512]{2,1,0:T(8,128)(2,1)}), bf16[16,8,512]{2,1,0:T(8,128)(2,1)S(1)}, u32[]{:S(2)}, u32[]{:S(2)}) async-start(bf16[16,8,512]{2,1,0:T(8,128)(2,1)} %shard_map.89), calls=%async_computation.3 | async-start | bytes 262144 | tf_op jit(solution)/shard_map/all_to_all | solution.py:44
  84.4 69.3 %all-gather.14.cloned.1.call-start = ((), (), s32[]{:S(2)}) async-start(), calls=%async_computation.13 | async-start | bytes 2359296 | tf_op jit(solution)/shard_map/all_gather | solution.py:529
  94.3 13.1 %all-to-all-start.4 = ((bf16[16,8,1664]{2,1,0:T(8,128)(2,1)}), bf16[16,8,1664]{2,1,0:T(8,128)(2,1)S(1)}, u32[]{:S(2)}, u32[]{:S(2)}) async-start(bf16[16,8,1664]{2,1,0:T(8,128)(2,1)} %get-tuple-element.78), calls=%async_computation.4 | async-start | bytes 851968 | tf_op jit(solution)/shard_map/all_to_all | solution.py:44
  97.9 71.0 %all-gather.16.cloned.1.call-start = ((), (), s32[]{:S(2)}) async-start(), calls=%async_computation.14 | async-start | bytes 2359296 | tf_op jit(solution)/shard_map/all_gather | solution.py:529
  99.7 1.0 copy-start.3
  107.4 12.1 %copy-start.4 = (bf16[2,512,512]{2,1,0:T(8,128)(2,1)S(1)}, bf16[2,512,512]{2,1,0:T(8,128)(2,1)}, u32[]{:S(2)}) copy-start(bf16[2,512,512]{2,1,0:T(8,128)(2,1)} %copy-done.3) | copy-start | bytes 3145732
  121.6 13.1 %all-to-all-start.6 = ((bf16[16,8,1664]{2,1,0:T(8,128)(2,1)}), bf16[16,8,1664]{2,1,0:T(8,128)(2,1)S(1)}, u32[]{:S(2)}, u32[]{:S(2)}) async-start(bf16[16,8,1664]{2,1,0:T(8,128)(2,1)} %get-tuple-element.89), calls=%async_computation.6 | async-start | bytes 851968 | tf_op jit(solution)/shard_map/all_to_all | solution.py:44
  125.2 56.2 %all-gather.18.cloned.1.call-start = ((), (), s32[]{:S(2)}) async-start(), calls=%async_computation.15 | async-start | bytes 2359296 | tf_op jit(solution)/shard_map/all_gather | solution.py:529
  127.0 1.0 copy-start.5
  134.7 12.1 %copy-start.6 = (bf16[2,512,512]{2,1,0:T(8,128)(2,1)S(1)}, bf16[2,512,512]{2,1,0:T(8,128)(2,1)}, u32[]{:S(2)}) copy-start(bf16[2,512,512]{2,1,0:T(8,128)(2,1)} %copy-done.5) | copy-start | bytes 3145732
  135.2 13.7 %copy-start.8 = (s32[8,8,1]{1,2,0:T(1,128)S(1)}, s32[8,8,1]{1,2,0:T(1,128)}, u32[]{:S(2)}) copy-start(s32[8,8,1]{1,2,0:T(1,128)} %param.12) | copy-start | bytes 772
  146.8 6.2 %copy-start.9 = (s32[16,8]{0,1:T(8,128)S(1)}, s32[16,8]{0,1:T(8,128)}, u32[]{:S(2)}) copy-start(s32[16,8]{0,1:T(8,128)} %param.15) | copy-start | bytes 1540
  146.9 6.8 %copy-start.7 = (bf16[16,8,512]{2,1,0:T(8,128)(2,1)S(1)}, bf16[16,8,512]{2,1,0:T(8,128)(2,1)}, u32[]{:S(2)}) copy-start(bf16[16,8,512]{2,1,0:T(8,128)(2,1)} %param.14) | copy-start | bytes 393220
  146.9 6.9 %copy-start.2 = (bf16[16,8,4,512]{3,2,1,0:T(4,128)(2,1)S(1)}, bf16[16,8,4,512]{3,2,1,0:T(4,128)(2,1)}, u32[]{:S(2)}) copy-start(bf16[16,8,4,512]{3,2,1,0:T(4,128)(2,1)} %q_ref.7) | copy-start | bytes 1572868
  149.4 13.1 %all-to-all-start.8 = ((bf16[16,8,1664]{2,1,0:T(8,128)(2,1)}), bf16[16,8,1664]{2,1,0:T(8,128)(2,1)S(1)}, u32[]{:S(2)}, u32[]{:S(2)}) async-start(bf16[16,8,1664]{2,1,0:T(8,128)(2,1)} %get-tuple-element.99), calls=%async_computation.8 | async-start | bytes 851968 | tf_op jit(solution)/shard_map/all_to_all | solution.py:44
  163.7 12.7 %all-to-all-start.9 = ((bf16[8,8,1024]{2,1,0:T(8,128)(2,1)}), bf16[8,8,1024]{2,1,0:T(8,128)(2,1)S(1)}, u32[]{:S(2)}, u32[]{:S(2)}) async-start(bf16[8,8,1024]{2,1,0:T(8,128)(2,1)} %shard_map.102), calls=%async_computation.9 | async-start | bytes 262144 | tf_op jit(solution)/shard_map/all_to_all | solution.py:44
  177.8 15.2 %all-to-all-start.10 = ((bf16[16,8,2048]{2,1,0:T(8,128)(2,1)}), bf16[16,8,2048]{2,1,0:T(8,128)(2,1)S(1)}, u32[]{:S(2)}, u32[]{:S(2)}) async-start(bf16[16,8,2048]{2,1,0:T(8,128)(2,1)} %shard_map.104), calls=%async_computation.10 | async-start | bytes 1048576 | tf_op jit(solution)/shard_map/all_to_all | solution.py:44
Sparse Core Ops, SparseCore 0:
  10.0 51.9 all-gather.11
  68.9 30.5 all-gather.9
  101.2 25.0 all-gather.13
  127.9 25.4 all-gather.15
  155.0 26.1 all-gather.17

commit v8 on v7

--- a/solution.py
+++ b/solution.py
@@ -80,57 +80,55 @@
 
 def weights_kernel(where, latent_ref, gain_ref, back_ref, both_ref, lent_ref, *scratch):
     latent, gain, pair, sems = scratch
+    size = latent.shape[0]
+    half = size // 2
+    halves = [pl.ds(i * half, half) for i in range(2)]
     copies = [
-        pltpu.make_async_copy(latent_ref.at[0], latent, sems.at[0]),
-        pltpu.make_async_copy(gain_ref, gain, sems.at[1]),
-        pltpu.make_async_copy(back_ref.at[0], pair.at[1], sems.at[2]),
+        pltpu.make_async_copy(gain_ref, gain, sems.at[0]),
+        pltpu.make_async_copy(latent_ref.at[0, halves[0]], latent.at[halves[0]], sems.at[1]),
+        pltpu.make_async_copy(latent_ref.at[0, halves[1]], latent.at[halves[1]], sems.at[2]),
+        pltpu.make_async_copy(back_ref.at[0], pair.at[1], sems.at[3]),
     ]
     for copy in copies:
         copy.start()
-    size = latent.shape[0]
-    row = lax.broadcasted_iota(jnp.int32, (size, size), 0)
-    column = lax.broadcasted_iota(jnp.int32, (size, size), 1)
-    copies[1].wait()
-    gains = jnp.where(row == column, gain[...].astype(f32), 0.0).astype(bf16)
-    copies[2].wait()
-    sending = [pltpu.make_async_copy(pair.at[i], both_ref.at[i], sems.at[3 + i]) for i in range(2)]
-    sending[1].start()
+    copies[0].wait()
+    gains = jnp.broadcast_to(gain[...].astype(f32), (8, size)).T[:, :1]
+    sending = []
+    for i, rows in enumerate(halves):
+        copies[1 + i].wait()
+        scaled = latent[rows].astype(f32) * gains[i * half : (i + 1) * half]
+        pair[0, rows] = scaled.astype(bf16)
+        to = both_ref.at[0, rows]
+        sending.append(pltpu.make_async_copy(pair.at[0, rows], to, sems.at[4 + i]))
+        sending[i].start()
+    copies[3].wait()
+    sending.append(pltpu.make_async_copy(pair.at[1], both_ref.at[1], sems.at[6]))
+    sending[2].start()
+
+    @pl.when(where[0] == 0)
+    def _():
+        lent_ref[...] = pair[0]
 
     @pl.when(where[0] != 0)
     def _():
-        pltpu.make_async_copy(pair.at[1], lent_ref, sems.at[5]).start()
-
-    copies[0].wait()
-    pair[0] = dot(gains, latent[...]).astype(bf16)
-    sending[0].start()
+        lent_ref[...] = pair[1]
+
+    for copy in sending:
+        copy.wait()
+
+
+def home_kernel(where, states_ref, mine_ref, lent_ref, *out_refs):
+    groups, _, rows, width = states_ref.shape
+
+    def products(weight_ref):
+        tokens = states_ref[:, where[1]].reshape(groups * rows, width)
+        product = dot(tokens, weight_ref[...]).astype(bf16)
+        for group in range(groups):
+            out_refs[group][...] = product[group * rows : (group + 1) * rows]
 
     @pl.when(where[0] == 0)
     def _():
-        pltpu.make_async_copy(pair.at[0], lent_ref, sems.at[5]).start()
-
-    pltpu.make_async_copy(pair.at[0], lent_ref, sems.at[5]).wait()
-    for copy in sending:
-        copy.wait()
-
-
-def home_kernel(where, states_ref, both_ref, lent_ref, *rest):
-    out_refs, (tokens, weight, sems) = rest[:-3], rest[-3:]
-    groups, rows, width = tokens.shape
-    loading = pltpu.make_async_copy(states_ref.at[:, where[1]], tokens, sems.at[0])
-    loading.start()
-
-    def products(weight_ref):
-        loading.wait()
-        product = dot(tokens[...].reshape(groups * rows, width), weight_ref[...]).astype(bf16)
-        for group in range(groups):
-            out_refs[group][...] = product[group * rows : (group + 1) * rows]
-
-    @pl.when(where[0] == 0)
-    def _():
-        fetching = pltpu.make_async_copy(both_ref.at[0], weight, sems.at[1])
-        fetching.start()
-        fetching.wait()
-        products(weight)
+        products(mine_ref)
 
     @pl.when(where[0] != 0)
     def _():
@@ -379,39 +377,33 @@
         return pltpu.HBM(shape, bf16)
 
     size = (2, local_width, lat)
-    both, lent = call(
+    both, mine_lent = call(
         weights_kernel,
         [in_hbm] * 3,
-        [in_hbm] * 2,
-        [far(*size), far(*size[1:])],
+        [in_hbm, whole(size[1:])],
+        [far(*size), near(*size[1:])],
         [held_in_hbm(w_latent), held_in_hbm(norm_gain), held_in_hbm(w_back)],
         [where],
         [
             pltpu.VMEM(size[1:], bf16),
             pltpu.VMEM(norm_gain.shape, bf16),
             pltpu.VMEM(size, bf16),
-            pltpu.SemaphoreType.DMA((6,)),
+            pltpu.SemaphoreType.DMA((7,)),
         ],
-        flops=2 * local_width**3,
     )
     every = lax.all_gather(both, "segment", axis=0)
-    lent = lax.ppermute(lent, "segment", [(i, i + 1) for i in range(0, segments, 2)])
+    lent = lax.ppermute(mine_lent, "segment", [(i, i + 1) for i in range(0, segments, 2)])
 
     states = prompt_states.reshape(segments // 2, 2, mine, local_width)
     groups = segments // 2
     own_states = pl.BlockSpec((1, 1, mine, local_width), lambda i, s: (s[0] >> 1, s[1], 0, 0))
     home = call(
         home_kernel,
-        [in_hbm, in_hbm, whole(size[1:])],
+        [whole(states.shape), whole(size[1:]), whole(size[1:])],
         [whole((mine, lat))] * groups,
         [near(mine, lat)] * groups,
-        [held_in_hbm(states), held_in_hbm(both), lent],
+        [in_vmem(states), in_vmem(mine_lent), lent],
         [where],
-        [
-            pltpu.VMEM((groups, mine, local_width), bf16),
-            pltpu.VMEM((local_width, lat), bf16),
-            pltpu.SemaphoreType.DMA((2,)),
-        ],
         flops=2 * local_width**3,
     )
     (cross,) = call(
@@ -554,8 +546,6 @@
     got, out = lax.optimization_barrier((got, out))
 
     got = exchanged(pair_step(got, mixing, segments), "segment")
-    out = decode(2, pages[1], out)
-    got, out = lax.optimization_barrier((got, out))
     (sent,) = call(
         functools.partial(choose_kernel, layers - 2),
         [whole(got.shape)],
@@ -565,7 +555,7 @@
         [slots],
     )
     got = exchanged(sent, "wide")
-    out = decode(4, pages[2], out)
+    out = decode(4, pages[2], decode(2, pages[1], out))
     got, out = lax.optimization_barrier((got, out))
     return decode(layers - 2, got, out, True)
 

time: 202 us -> 200 us (0.990)
  blocking collectives: 55.9 us -> 70.2 us
  waiting for transfers between devices: 51.5 us -> 41.9 us
  starting transfers between devices: 35.3 us -> 30.4 us
  Pallas kernels: 41.7 us -> 39.3 us
    all_to_all x4 -> x5, blocking collectives: 55.9 us -> 70.2 us  [exchanged(): return lax.all_to_all(sent, axis, 0, 0, tiled=True)]
    all_to_all x7 -> x6, waiting for transfers between devices: 37.9 us -> 26.8 us  [exchanged(): return lax.all_to_all(sent, axis, 0, 0, tiled=True)]
    all_to_all x7 -> x6, starting transfers between devices: 26.6 us -> 21.4 us  [exchanged(): return lax.all_to_all(sent, axis, 0, 0, tiled=True)]
    all_gather x1, waiting for transfers between devices: 6.99 us -> 10.2 us  [shards(): every = lax.all_gather(both, 'segment', axis=0)]
    pallas_call x14, Pallas kernels: 20.3 us -> 17.9 us  [call(): pl.pallas_call(body, grid_spec=pltpu.PrefetchScalarGridSpec(num_scalar_pr...]
  transfers between devices with their start and end apart: 16 -> 15, of which waited for: 11 -> 9; matrix products, arithmetic and copies ran while one was open for 1% -> 1% of each run, Pallas kernels for 18% -> 17%
where the time goes in v8:
time: 200 us; the launch traced here: 199 us
  blocking collectives  70.2 us (35%)
  waiting for transfers between devices  41.9 us (21%)
  Pallas kernels  39.3 us (20%)
  starting transfers between devices  30.4 us (15%)
  between operations  13.5 us (7%)
  local copies, waits for them, and re-layouts  2.77 us (1%)
    all_to_all x5, blocking collectives, exchanged(): return lax.all_to_all(sent, axis, 0, 0, tiled=True)  70.2 us
    all_to_all x6, waiting for transfers between devices, exchanged(): return lax.all_to_all(sent, axis, 0, 0, tiled=True)  26.8 us
    all_to_all x6, starting transfers between devices, exchanged(): return lax.all_to_all(sent, axis, 0, 0, tiled=True)  21.4 us
    pallas_call x14, Pallas kernels, call(): pl.pallas_call(body, grid_spec=pltpu.PrefetchScalarGridSpec(num_scalar_pr...  17.9 us
    pallas_call x4, Pallas kernels, decode_pair(): pl.pallas_call(last_decode_kernel if last else functools.partial(decode_k...  11.4 us
    all_gather x1, waiting for transfers between devices, shards(): every = lax.all_gather(both, 'segment', axis=0)  10.2 us
    pallas_call x7, Pallas kernels, resident(): pl.pallas_call(functools.partial(reside_kernel, lists), in_specs=[in_hbm]...  9.94 us
    ppermute x3, starting transfers between devices, shards(): lax.ppermute(home[hop], 'segment', [(0, 2 * hop), (1, 2 * hop + 1)])  7.45 us
  transfers between devices with their start and end apart: 15, of which 9 were waited for; matrix products, arithmetic and copies ran while one was open for 1% of the time, Pallas kernels for 17%

profile of v8, /device:TPU:0, one launch (start us, length us, event | category | flops | bytes accessed | tf_op | source)
XLA Modules:
  0.0 198.6 jit_solution(308919456293113303)
XLA Ops:
  6.5 0.1 pad_add_fusion.where
  6.6 2.7 %shard_map.82 = (bf16[2,512,512]{2,1,0:T(8,128)(2,1)}, bf16[512,512]{1,0:T(8,128)(2,1)S(1)}) custom-call(s32[2]{0:T(128)S(1)} %pad_add_fusion.where, bf16[1,512,512]{2,1,0:T(8,128)(2,1)} %latent_ref.1, bf16[1,512]{1,0:T(2,128)(2,1)} %gain_ref.1, bf16[1,512,512]{2,1,0:T(8,128)(2,1)} %back_ref.1), custom_call_target="tpu_custom_call" | custom-call | bytes 3145728 | tf_op jit(solution)/shard_map/pallas_call | solution.py:66
  9.3 1.5 collective-permute-start
  10.8 1.5 collective-permute-done.lent_ref
  12.3 1.0 shard_map.83
  13.3 3.9 %collective-permute-start.1 = (bf16[128,512]{1,0:T(8,128)(2,1)S(1)}, bf16[128,512]{1,0:T(8,128)(2,1)S(1)}, u32[]{:S(2)}, u32[]{:S(2)}) collective-permute-start(bf16[128,512]{1,0:T(8,128)(2,1)S(1)} %get-tuple-element.58), channel_id=1, source_target_pairs={{0,32},{16,48},{1,33},{17,49},{2,34},{18,50},{3,35},{19,51},{4,36}... | collective-permute-start | bytes 393224 | tf_op jit(solution)/shard_map/ppermute | solution.py:419
  17.2 2.2 %collective-permute-start.2 = (bf16[128,512]{1,0:T(8,128)(2,1)S(1)}, bf16[128,512]{1,0:T(8,128)(2,1)S(1)}, u32[]{:S(2)}, u32[]{:S(2)}) collective-permute-start(bf16[128,512]{1,0:T(8,128)(2,1)S(1)} %get-tuple-element.59), channel_id=1, source_target_pairs={{0,64},{16,80},{1,65},{17,81},{2,66},{18,82},{3,67},{19,83},{4,68}... | collective-permute-start | bytes 393224 | tf_op jit(solution)/shard_map/ppermute | solution.py:419
  19.4 1.3 collective-permute-start.3
  20.8 1.0 shard_map.84.cross_ref
  21.8 2.5 %collective-permute-done.2.b_ref = bf16[128,512]{1,0:T(8,128)(2,1)S(1)} collective-permute-done((bf16[128,512]{1,0:T(8,128)(2,1)S(1)}, bf16[128,512]{1,0:T(8,128)(2,1)S(1)}, u32[]{:S(2)}, u32[]{:S(2)}) %collective-permute-start.2) | collective-permute-done | bytes 131104 | tf_op jit(solution)/shard_map/ppermute | solution.py:419
  24.3 0.8 collective-permute-done.3.c_ref
  25.1 0.7 shard_map.85
  25.8 21.0 %all_to_all.55.got_ref = bf16[16,8,2688]{2,1,0:T(8,128)(2,1)S(1)} all-to-all(bf16[16,8,2688]{2,1,0:T(8,128)(2,1)S(1)} %shard_map.85), channel_id=1, replica_groups=mesh['segment'=8,'wide'=16] {'wide'}, dimensions={0} | all-to-all | bytes 1376256 | tf_op jit(solution)/shard_map/all_to_all | solution.py:44
  46.8 1.1 shard_map.86
  47.8 3.6 %all-to-all-start.1 = ((bf16[16,40,512]{2,1,0:T(8,128)(2,1)}), bf16[16,40,512]{2,1,0:T(8,128)(2,1)S(1)}, u32[]{:S(2)}, u32[]{:S(2)}) async-start(bf16[16,40,512]{2,1,0:T(8,128)(2,1)} %shard_map.86), calls=%async_computation.1 | async-start | bytes 1310720 | tf_op jit(solution)/shard_map/all_to_all | solution.py:44
  51.4 0.0 all-gather.10.cloned.1.call-start
  51.5 10.2 %all-gather.12.cloned.1.call-done.source_ref = bf16[16,512,512]{2,1,0:T(8,128)(2,1)} async-done(((bf16[2,512,512]{2,1,0:T(8,128)(2,1)}), bf16[16,512,512]{2,1,0:T(8,128)(2,1)}) %all-gather.12.cloned.1.call-update) | async-done | bytes 8388624 | tf_op jit(solution)/shard_map/all_gather | solution.py:394
  61.6 1.2 shard_map.87
  62.9 1.7 shard_map.88
  64.6 14.9 %all_to_all.56.got_ref = bf16[16,8,640]{2,1,0:T(8,128)(2,1)S(1)} all-to-all(bf16[16,8,640]{2,1,0:T(8,128)(2,1)S(1)} %get-tuple-element.67), channel_id=1, replica_groups=mesh['segment'=8,'wide'=16] {'wide'}, dimensions={0} | all-to-all | bytes 327680 | tf_op jit(solution)/shard_map/all_to_all | solution.py:44
  79.5 0.8 shard_map.89
  80.4 3.5 %all-to-all-start.3 = ((bf16[16,8,512]{2,1,0:T(8,128)(2,1)}), bf16[16,8,512]{2,1,0:T(8,128)(2,1)S(1)}, u32[]{:S(2)}, u32[]{:S(2)}) async-start(bf16[16,8,512]{2,1,0:T(8,128)(2,1)} %shard_map.89), calls=%async_computation.3 | async-start | bytes 262144 | tf_op jit(solution)/shard_map/all_to_all | solution.py:44
  83.9 0.0 all-gather.14.cloned.1.call-start
  83.9 1.6 shard_map.90
  85.6 6.3 %all-to-all-done.3.got_ref = bf16[16,8,512]{2,1,0:T(8,128)(2,1)S(1)} async-done(((bf16[16,8,512]{2,1,0:T(8,128)(2,1)}), bf16[16,8,512]{2,1,0:T(8,128)(2,1)S(1)}, u32[]{:S(2)}, u32[]{:S(2)}) %all-to-all-start.3) | async-done | bytes 131104 | tf_op jit(solution)/shard_map/all_to_all | solution.py:44
  91.8 2.0 %shard_map.91 = (bf16[16,8,1664]{2,1,0:T(8,128)(2,1)}, bf16[128,512]{1,0:T(8,128)(2,1)S(1)}, bf16[128,1024]{1,0:T(8,128)(2,1)}) custom-call(s32[2]{0:T(128)S(1)} %pad_add_fusion.where, bf16[16,8,512]{2,1,0:T(8,128)(2,1)S(1)} %all-to-all-done.3.got_ref, bf16[128,512]{1,0:T(8,128)(2,1)S(1)} %get-tuple-element.72.states_ref, ...), custom_call_target="tpu_custom_call" | custom-call | flops 268435456 | bytes 1638400 | tf_op jit(solution)/shard_map/pallas_call | solution.py:66
  93.9 3.6 %all-to-all-start.4 = ((bf16[16,8,1664]{2,1,0:T(8,128)(2,1)}), bf16[16,8,1664]{2,1,0:T(8,128)(2,1)S(1)}, u32[]{:S(2)}, u32[]{:S(2)}) async-start(bf16[16,8,1664]{2,1,0:T(8,128)(2,1)} %get-tuple-element.76), calls=%async_computation.4 | async-start | bytes 851968 | tf_op jit(solution)/shard_map/all_to_all | solution.py:44
  97.4 0.0 all-gather.18.cloned.1.call-start
  97.5 1.7 shard_map.93
  99.2 1.0 copy-done.3
  100.2 1.2 shard_map.92.cross_ref
  101.5 5.5 %all-to-all-done.4.got_ref = bf16[16,8,1664]{2,1,0:T(8,128)(2,1)S(1)} async-done(((bf16[16,8,1664]{2,1,0:T(8,128)(2,1)}), bf16[16,8,1664]{2,1,0:T(8,128)(2,1)S(1)}, u32[]{:S(2)}, u32[]{:S(2)}) %all-to-all-start.4) | async-done | bytes 426016 | tf_op jit(solution)/shard_map/all_to_all | solution.py:44
  107.0 0.5 shard_map.94
  107.5 11.6 %all_to_all.57.got_ref = bf16[16,8,1024]{2,1,0:T(8,128)(2,1)S(1)} all-to-all(bf16[16,8,1024]{2,1,0:T(8,128)(2,1)S(1)} %shard_map.94), channel_id=1, replica_groups=mesh['segment'=8,'wide'=16] {'wide'}, dimensions={0} | all-to-all | bytes 524288 | tf_op jit(solution)/shard_map/all_to_all | solution.py:44
  119.1 2.0 %shard_map.95 = (bf16[16,8,1664]{2,1,0:T(8,128)(2,1)}, bf16[128,512]{1,0:T(8,128)(2,1)S(1)}, bf16[128,1024]{1,0:T(8,128)(2,1)}) custom-call(s32[2]{0:T(128)S(1)} %pad_add_fusion.where, bf16[16,8,1024]{2,1,0:T(8,128)(2,1)S(1)} %all_to_all.57.got_ref, bf16[128,512]{1,0:T(8,128)(2,1)S(1)} %get-tuple-element.83.states_ref, ...), custom_call_target="tpu_custom_call" | custom-call | flops 335544320 | bytes 1638400 | tf_op jit(solution)/shard_map/pallas_call | solution.py:66
  121.1 3.6 %all-to-all-start.6 = ((bf16[16,8,1664]{2,1,0:T(8,128)(2,1)}), bf16[16,8,1664]{2,1,0:T(8,128)(2,1)S(1)}, u32[]{:S(2)}, u32[]{:S(2)}) async-start(bf16[16,8,1664]{2,1,0:T(8,128)(2,1)} %get-tuple-element.87), calls=%async_computation.6 | async-start | bytes 851968 | tf_op jit(solution)/shard_map/all_to_all | solution.py:44
  124.7 0.0 all-gather.16.cloned.1.call-start
  124.8 1.7 shard_map.97
  126.5 1.0 copy-done.5
  127.5 1.2 shard_map.96.cross_ref
  128.7 5.5 %all-to-all-done.6.got_ref = bf16[16,8,1664]{2,1,0:T(8,128)(2,1)S(1)} async-done(((bf16[16,8,1664]{2,1,0:T(8,128)(2,1)}), bf16[16,8,1664]{2,1,0:T(8,128)(2,1)S(1)}, u32[]{:S(2)}, u32[]{:S(2)}) %all-to-all-start.6) | async-done | bytes 426016 | tf_op jit(solution)/shard_map/all_to_all | solution.py:44
  134.2 0.5 shard_map.98
  134.8 11.6 %all_to_all.58.got_ref = bf16[16,8,1024]{2,1,0:T(8,128)(2,1)S(1)} all-to-all(bf16[16,8,1024]{2,1,0:T(8,128)(2,1)S(1)} %shard_map.98), channel_id=1, replica_groups=mesh['segment'=8,'wide'=16] {'wide'}, dimensions={0} | all-to-all | bytes 524288 | tf_op jit(solution)/shard_map/all_to_all | solution.py:44
  146.4 2.1 %shard_map.99 = (bf16[16,8,1664]{2,1,0:T(8,128)(2,1)}, bf16[128,512]{1,0:T(8,128)(2,1)}, bf16[128,1024]{1,0:T(8,128)(2,1)}) custom-call(s32[2]{0:T(128)S(1)} %pad_add_fusion.where, bf16[16,8,1024]{2,1,0:T(8,128)(2,1)S(1)} %all_to_all.58.got_ref, bf16[128,512]{1,0:T(8,128)(2,1)S(1)} %get-tuple-element.93.states_ref, ...), custom_call_target="tpu_custom_call" | custom-call | flops 335544320 | bytes 1638400 | tf_op jit(solution)/shard_map/pallas_call | solution.py:66
  148.5 0.1 select_reduce_fusion.1
  148.6 0.2 select_reduce_fusion
  148.8 0.1 copy.26
  148.9 0.1 min.18.slots
  149.0 3.6 %all-to-all-start.8 = ((bf16[16,8,1664]{2,1,0:T(8,128)(2,1)}), bf16[16,8,1664]{2,1,0:T(8,128)(2,1)S(1)}, u32[]{:S(2)}, u32[]{:S(2)}) async-start(bf16[16,8,1664]{2,1,0:T(8,128)(2,1)} %get-tuple-element.97), calls=%async_computation.8 | async-start | bytes 851968 | tf_op jit(solution)/shard_map/all_to_all | solution.py:44
  152.6 0.1 minimum_bitcast_fusion
  152.6 0.1 copy.25
  152.7 0.5 copy.30.limit_ref
  153.3 3.3 %shard_map.101.rest_0_ = bf16[16,8,4,512]{3,2,1,0:T(4,128)(2,1)} custom-call(s32[16]{0:T(128)S(1)} %min.18.slots, bf16[16,8,4,512]{3,2,1,0:T(4,128)(2,1)S(1)} %copy-done.1, bf16[8,16,512]{2,1,0:T(8,128)(2,1)S(1)} %bitcast.23, s32[8,64,1]{2,1,0:T(8,128)S(1)} %copy.30.limit_ref, bf16[8,128,1024]{2,1,0:T(8,128)(2,1)} %bitcast.27), custom_call_target="tpu_custom_call" | custom-call | flops 67108864 | bytes 786432 | tf_op jit(solution)/shard_map/pallas_call | solution.py:334
  156.6 1.2 shard_map.100.cross_ref
  157.8 4.3 %all-to-all-done.8.got_ref = bf16[16,8,1664]{2,1,0:T(8,128)(2,1)S(1)} async-done(((bf16[16,8,1664]{2,1,0:T(8,128)(2,1)}), bf16[16,8,1664]{2,1,0:T(8,128)(2,1)S(1)}, u32[]{:S(2)}, u32[]{:S(2)}) %all-to-all-start.8) | async-done | bytes 426016 | tf_op jit(solution)/shard_map/all_to_all | solution.py:44
  162.1 0.5 shard_map.102
  162.6 11.1 %all_to_all.59.got_ref = bf16[8,8,1024]{2,1,0:T(8,128)(2,1)S(1)} all-to-all(bf16[8,8,1024]{2,1,0:T(8,128)(2,1)S(1)} %shard_map.102), channel_id=1, replica_groups=mesh['segment'=8,'wide'=16] {'segment'}, dimensions={0} | all-to-all | bytes 262144 | tf_op jit(solution)/shard_map/all_to_all | solution.py:44
  173.6 1.4 shard_map.103
  175.0 3.6 %all-to-all-start.10 = ((bf16[16,8,2048]{2,1,0:T(8,128)(2,1)}), bf16[16,8,2048]{2,1,0:T(8,128)(2,1)S(1)}, u32[]{:S(2)}, u32[]{:S(2)}) async-start(bf16[16,8,2048]{2,1,0:T(8,128)(2,1)} %shard_map.103), calls=%async_computation.10 | async-start | bytes 1048576 | tf_op jit(solution)/shard_map/all_to_all | solution.py:44
  178.6 0.0 all-gather.18.cloned.1.call-done
  178.6 3.3 %shard_map.104.rest_0_ = bf16[16,8,4,512]{3,2,1,0:T(4,128)(2,1)} custom-call(s32[16]{0:T(128)S(1)} %min.18.slots, bf16[16,8,4,512]{3,2,1,0:T(4,128)(2,1)S(1)} %copy-done.1, bf16[8,16,512]{2,1,0:T(8,128)(2,1)S(1)} %bitcast.24, s32[8,64,1]{2,1,0:T(8,128)S(1)} %copy.30.limit_ref, bf16[8,128,1024]{2,1,0:T(8,128)(2,1)} %bitcast.28, ...), custom_call_target="tpu_custom_call", output_to_operand_aliasing={{}: (5, {})} | custom-call | flops 67108864 | bytes 786432 | tf_op jit(solution)/shard_map/pallas_call | solution.py:334
  182.0 3.3 %shard_map.105.carried_ref = bf16[16,8,4,512]{3,2,1,0:T(4,128)(2,1)} custom-call(s32[16]{0:T(128)S(1)} %min.18.slots, bf16[16,8,4,512]{3,2,1,0:T(4,128)(2,1)S(1)} %copy-done.1, bf16[8,16,512]{2,1,0:T(8,128)(2,1)S(1)} %bitcast.25, s32[8,64,1]{2,1,0:T(8,128)S(1)} %copy.30.limit_ref, bf16[8,128,1024]{2,1,0:T(8,128)(2,1)} %bitcast.29, ...), custom_call_target="tpu_custom_call", output_to_operand_aliasing={{}: (5, {})} | custom-call | flops 67108864 | bytes 786432 | tf_op jit(solution)/shard_map/pallas_call | solution.py:334
  185.2 5.2 %all-to-all-done.10.pages_ref = bf16[16,8,2048]{2,1,0:T(8,128)(2,1)S(1)} async-done(((bf16[16,8,2048]{2,1,0:T(8,128)(2,1)}), bf16[16,8,2048]{2,1,0:T(8,128)(2,1)S(1)}, u32[]{:S(2)}, u32[]{:S(2)}) %all-to-all-start.10) | async-done | bytes 524320 | tf_op jit(solution)/shard_map/all_to_all | solution.py:44
  190.5 1.6 shard_map.106
  (33 shorter events, 0.2 us)
Async XLA Ops:
  6.5 5.7 %copy-start = (bf16[4,256,512]{2,1,0:T(8,128)(2,1)S(1)}, bf16[4,256,512]{2,1,0:T(8,128)(2,1)}, u32[]{:S(2)}) copy-start(bf16[4,256,512]{2,1,0:T(8,128)(2,1)} %param.8) | copy-start | bytes 3145732
  6.5 55.1 %all-gather.12.cloned.1.call-start = ((), (), s32[]{:S(2)}) async-start(), calls=%async_computation.12 | async-start | bytes 9437184 | tf_op jit(solution)/shard_map/all_gather | solution.py:394
  9.3 11.4 %copy-start.2 = (bf16[2,512,512]{2,1,0:T(8,128)(2,1)S(1)}, bf16[2,512,512]{2,1,0:T(8,128)(2,1)}, u32[]{:S(2)}) copy-start(bf16[2,512,512]{2,1,0:T(8,128)(2,1)} %get-tuple-element.61.both_ref) | copy-start | bytes 3145732
  9.3 2.9 %collective-permute-start = (bf16[512,512]{1,0:T(8,128)(2,1)S(1)}, bf16[512,512]{1,0:T(8,128)(2,1)S(1)}, u32[]{:S(2)}, u32[]{:S(2)}) collective-permute-start(bf16[512,512]{1,0:T(8,128)(2,1)S(1)} %get-tuple-element.56.mine_ref), channel_id=1, source_target_pairs={{0,16},{32,48},{64,80},{96,112},{1,17},{33,49},{65,81},{97,113},{2... | collective-permute-start | bytes 1572872 | tf_op jit(solution)/shard_map/ppermute | solution.py:395
  13.3 8.5 %collective-permute-start.1 = (bf16[128,512]{1,0:T(8,128)(2,1)S(1)}, bf16[128,512]{1,0:T(8,128)(2,1)S(1)}, u32[]{:S(2)}, u32[]{:S(2)}) collective-permute-start(bf16[128,512]{1,0:T(8,128)(2,1)S(1)} %get-tuple-element.58), channel_id=1, source_target_pairs={{0,32},{16,48},{1,33},{17,49},{2,34},{18,50},{3,35},{19,51},{4,36}... | collective-permute-start | bytes 393224 | tf_op jit(solution)/shard_map/ppermute | solution.py:419
  17.2 7.0 %collective-permute-start.2 = (bf16[128,512]{1,0:T(8,128)(2,1)S(1)}, bf16[128,512]{1,0:T(8,128)(2,1)S(1)}, u32[]{:S(2)}, u32[]{:S(2)}) collective-permute-start(bf16[128,512]{1,0:T(8,128)(2,1)S(1)} %get-tuple-element.59), channel_id=1, source_target_pairs={{0,64},{16,80},{1,65},{17,81},{2,66},{18,82},{3,67},{19,83},{4,68}... | collective-permute-start | bytes 393224 | tf_op jit(solution)/shard_map/ppermute | solution.py:419
  19.4 5.6 %collective-permute-start.3 = (bf16[128,512]{1,0:T(8,128)(2,1)S(1)}, bf16[128,512]{1,0:T(8,128)(2,1)S(1)}, u32[]{:S(2)}, u32[]{:S(2)}) collective-permute-start(bf16[128,512]{1,0:T(8,128)(2,1)S(1)} %get-tuple-element.60), channel_id=1, source_target_pairs={{0,96},{16,112},{1,97},{17,113},{2,98},{18,114},{3,99},{19,115},{4... | collective-permute-start | bytes 393224 | tf_op jit(solution)/shard_map/ppermute | solution.py:419
  47.8 15.0 %all-to-all-start.1 = ((bf16[16,40,512]{2,1,0:T(8,128)(2,1)}), bf16[16,40,512]{2,1,0:T(8,128)(2,1)S(1)}, u32[]{:S(2)}, u32[]{:S(2)}) async-start(bf16[16,40,512]{2,1,0:T(8,128)(2,1)} %shard_map.86), calls=%async_computation.1 | async-start | bytes 1310720 | tf_op jit(solution)/shard_map/all_to_all | solution.py:44
  51.4 48.8 %all-gather.10.cloned.1.call-start = ((), (), s32[]{:S(2)}) async-start(), calls=%async_computation.11 | async-start | bytes 4718592 | tf_op jit(solution)/shard_map/all_gather | solution.py:504
  80.4 11.5 %all-to-all-start.3 = ((bf16[16,8,512]{2,1,0:T(8,128)(2,1)}), bf16[16,8,512]{2,1,0:T(8,128)(2,1)S(1)}, u32[]{:S(2)}, u32[]{:S(2)}) async-start(bf16[16,8,512]{2,1,0:T(8,128)(2,1)} %shard_map.89), calls=%async_computation.3 | async-start | bytes 262144 | tf_op jit(solution)/shard_map/all_to_all | solution.py:44
  83.9 69.4 %all-gather.14.cloned.1.call-start = ((), (), s32[]{:S(2)}) async-start(), calls=%async_computation.13 | async-start | bytes 2359296 | tf_op jit(solution)/shard_map/all_gather | solution.py:521
  93.9 13.1 %all-to-all-start.4 = ((bf16[16,8,1664]{2,1,0:T(8,128)(2,1)}), bf16[16,8,1664]{2,1,0:T(8,128)(2,1)S(1)}, u32[]{:S(2)}, u32[]{:S(2)}) async-start(bf16[16,8,1664]{2,1,0:T(8,128)(2,1)} %get-tuple-element.76), calls=%async_computation.4 | async-start | bytes 851968 | tf_op jit(solution)/shard_map/all_to_all | solution.py:44
  97.4 81.2 %all-gather.18.cloned.1.call-start = ((), (), s32[]{:S(2)}) async-start(), calls=%async_computation.15 | async-start | bytes 2359296 | tf_op jit(solution)/shard_map/all_gather | solution.py:521
  99.2 1.0 copy-start.3
  107.0 12.1 %copy-start.4 = (bf16[2,512,512]{2,1,0:T(8,128)(2,1)S(1)}, bf16[2,512,512]{2,1,0:T(8,128)(2,1)}, u32[]{:S(2)}) copy-start(bf16[2,512,512]{2,1,0:T(8,128)(2,1)} %copy-done.3) | copy-start | bytes 3145732
  121.1 13.1 %all-to-all-start.6 = ((bf16[16,8,1664]{2,1,0:T(8,128)(2,1)}), bf16[16,8,1664]{2,1,0:T(8,128)(2,1)S(1)}, u32[]{:S(2)}, u32[]{:S(2)}) async-start(bf16[16,8,1664]{2,1,0:T(8,128)(2,1)} %get-tuple-element.87), calls=%async_computation.6 | async-start | bytes 851968 | tf_op jit(solution)/shard_map/all_to_all | solution.py:44
  124.7 57.2 %all-gather.16.cloned.1.call-start = ((), (), s32[]{:S(2)}) async-start(), calls=%async_computation.14 | async-start | bytes 2359296 | tf_op jit(solution)/shard_map/all_gather | solution.py:521
  126.5 1.0 copy-start.5
  134.2 12.1 %copy-start.6 = (bf16[2,512,512]{2,1,0:T(8,128)(2,1)S(1)}, bf16[2,512,512]{2,1,0:T(8,128)(2,1)}, u32[]{:S(2)}) copy-start(bf16[2,512,512]{2,1,0:T(8,128)(2,1)} %copy-done.5) | copy-start | bytes 3145732
  134.7 13.7 %copy-start.8 = (s32[8,8,1]{1,2,0:T(1,128)S(1)}, s32[8,8,1]{1,2,0:T(1,128)}, u32[]{:S(2)}) copy-start(s32[8,8,1]{1,2,0:T(1,128)} %param.12) | copy-start | bytes 772
  146.4 6.2 %copy-start.9 = (s32[16,8]{0,1:T(8,128)S(1)}, s32[16,8]{0,1:T(8,128)}, u32[]{:S(2)}) copy-start(s32[16,8]{0,1:T(8,128)} %param.15) | copy-start | bytes 1540
  146.4 6.8 %copy-start.7 = (bf16[16,8,512]{2,1,0:T(8,128)(2,1)S(1)}, bf16[16,8,512]{2,1,0:T(8,128)(2,1)}, u32[]{:S(2)}) copy-start(bf16[16,8,512]{2,1,0:T(8,128)(2,1)} %param.14) | copy-start | bytes 393220
  146.4 6.9 %copy-start.1 = (bf16[16,8,4,512]{3,2,1,0:T(4,128)(2,1)S(1)}, bf16[16,8,4,512]{3,2,1,0:T(4,128)(2,1)}, u32[]{:S(2)}) copy-start(bf16[16,8,4,512]{3,2,1,0:T(4,128)(2,1)} %q_ref.7) | copy-start | bytes 1572868
  149.0 13.1 %all-to-all-start.8 = ((bf16[16,8,1664]{2,1,0:T(8,128)(2,1)}), bf16[16,8,1664]{2,1,0:T(8,128)(2,1)S(1)}, u32[]{:S(2)}, u32[]{:S(2)}) async-start(bf16[16,8,1664]{2,1,0:T(8,128)(2,1)} %get-tuple-element.97), calls=%async_computation.8 | async-start | bytes 851968 | tf_op jit(solution)/shard_map/all_to_all | solution.py:44
  175.0 15.4 %all-to-all-start.10 = ((bf16[16,8,2048]{2,1,0:T(8,128)(2,1)}), bf16[16,8,2048]{2,1,0:T(8,128)(2,1)S(1)}, u32[]{:S(2)}, u32[]{:S(2)}) async-start(bf16[16,8,2048]{2,1,0:T(8,128)(2,1)} %shard_map.103), calls=%async_computation.10 | async-start | bytes 1048576 | tf_op jit(solution)/shard_map/all_to_all | solution.py:44
Sparse Core Ops, SparseCore 0:
  9.5 52.1 all-gather.11
  64.7 32.8 all-gather.9
  99.3 25.0 all-gather.13
  126.0 25.6 all-gather.17
  153.3 25.6 all-gather.15

commit v9 on v8

--- a/solution.py
+++ b/solution.py
@@ -145,12 +145,16 @@
         out_ref[...] = dot(lent_ref[...], both_ref[0]).astype(bf16)
 
 
-def home_send_kernel(where, home_ref, a_ref, b_ref, c_ref, cross_ref, states_ref, out_ref):
+def home_send_kernel(
+    where, home_ref, a_ref, b_ref, c_ref, cross_ref, states_ref, out_ref, state_ref
+):
     wide, share, _ = out_ref.shape
     rows, lat = home_ref.shape
     taken = a_ref[...].astype(f32) + b_ref[...].astype(f32) + c_ref[...].astype(f32)
     product = jnp.where(where[0] < 2, home_ref[...].astype(f32), taken)
-    squares = square_columns(states_ref[...].reshape(rows, states_ref.shape[3]).astype(f32))
+    state = states_ref[where[0] >> 1, where[1]]
+    state_ref[...] = state
+    squares = square_columns(state.astype(f32))
     out_ref[:, :, :LANES] = squares.reshape(wide, share, LANES).astype(bf16)
     out_ref[:, :, LANES : LANES + lat] = product.reshape(wide, share, lat).astype(bf16)
     parts = cross_ref.shape[0] // rows
@@ -187,6 +191,7 @@
     activated = silu(first)
     towards = 2.0 * summed[:, at[2] : at[3]] + dot(activated, gram())
     squares = squares + jnp.sum(activated.astype(f32) * towards, axis=1, keepdims=True)
+    squares = jnp.maximum(squares, 0.0)
     second = summed[:, at[1] : at[2]] + dot(activated, mixing())
     second = (second * lax.rsqrt(squares / width + eps_norm)).astype(bf16)
     return first, second
@@ -205,7 +210,7 @@
         copy.wait()
 
 
-def advance_kernel(before, layers, mode, where, got_ref, states_ref, *rest):
+def advance_kernel(before, layers, mode, got_ref, states_ref, *rest):
     refs = rest[: 1 + len(layers)]
     back_ref, latent_ref = refs[:2]
     outs = rest[len(refs) :]
@@ -222,7 +227,7 @@
 
     latents = latents_of(got_ref)
     activated = silu(latents)
-    state = states_ref[...].reshape(rows, states_ref.shape[-1]).astype(f32)
+    state = states_ref[...].astype(f32)
     for i in range(len(before)):
         state = state + dot(activated[:, i * lat : (i + 1) * lat], back_ref[i])
     state = state.astype(bf16)
@@ -253,13 +258,18 @@
         out_ref[place, :, lat:] = second
 
 
-def choose_kernel(layer, slots, got_ref, out_ref):
+def choose_kernel(got_ref, hot_ref, out_ref):
+    pages = got_ref.shape[0]
     lat = got_ref.shape[2] // 2
     parts = []
     for i in range(2):
         for which in range(2):
-            shard = got_ref[slots[2 * (layer + i) + which]]
-            parts.append(shard[:, i * lat : (i + 1) * lat])
+            at = (2 * i + which) * pages
+            part = jnp.zeros((got_ref.shape[1], lat), f32)
+            for page in range(pages):
+                shard = got_ref[page, :, i * lat : (i + 1) * lat].astype(f32)
+                part = jnp.where(hot_ref[at + page : at + page + 1, :1] > 0, shard, part)
+            parts.append(part.astype(bf16))
     for place in range(out_ref.shape[0]):
         for i, part in enumerate(parts):
             out_ref[place, :, i * lat : (i + 1) * lat] = part
@@ -303,14 +313,14 @@
         out_ref[:, i] = result.reshape(requests, heads, lat)
 
 
-def last_decode_kernel(q_ref, new_ref, limit_ref, pages_ref, carried_ref, out_ref):
-    requests, count, heads, lat = q_ref.shape
+def last_decode_kernel(layer, q_ref, new_ref, limit_ref, pages_ref, carried_ref, out_ref):
+    requests, count, heads, lat = out_ref.shape
     for i in range(count):
-        q = q_ref[:, i].reshape(requests * heads, lat)
+        q = q_ref[:, layer + i].reshape(requests * heads, lat)
         at = 2 * i * lat
         pages = pages_ref[:, :, at : at + 2 * lat].astype(f32).reshape(PAGE, 2 * lat)
         keys = jnp.concatenate([pages[:, :lat], pages[:, lat:]], axis=0).astype(bf16)
-        result = attend(q, new_ref[i], keys, limit_ref[i], heads)
+        result = attend(q, new_ref[layer + i], keys, limit_ref[layer + i], heads)
         out_ref[:, i] = result.reshape(requests, heads, lat)
 
 
@@ -325,6 +335,9 @@
     ]
     scalars = [] if last else [slots]
     operands = scalars + [queries, new, limit, pages if last else held_in_hbm(pages)]
+    if last:
+        in_specs[:3] = [whole(operand.shape) for operand in operands[:3]]
+        operands[:3] = [in_vmem(operand) for operand in operands[:3]]
     aliases = {}
     if carried is not None:
         in_specs.append(in_hbm)
@@ -332,7 +345,7 @@
         operands.append(carried)
     scratch = [pltpu.VMEM((2, 2 * PAGE, lat), bf16), pltpu.SemaphoreType.DMA((4,))]
     return pl.pallas_call(
-        last_decode_kernel if last else functools.partial(decode_kernel, layer),
+        functools.partial(last_decode_kernel if last else decode_kernel, layer),
         grid_spec=pltpu.PrefetchScalarGridSpec(
             num_scalar_prefetch=len(scalars),
             grid=(1,),
@@ -396,7 +409,6 @@
 
     states = prompt_states.reshape(segments // 2, 2, mine, local_width)
     groups = segments // 2
-    own_states = pl.BlockSpec((1, 1, mine, local_width), lambda i, s: (s[0] >> 1, s[1], 0, 0))
     home = call(
         home_kernel,
         [whole(states.shape), whole(size[1:]), whole(size[1:])],
@@ -421,12 +433,12 @@
     ]
     high = lat // wide
     columns = LANES + lat + high // share * lat
-    (sent,) = call(
+    sent, state = call(
         home_send_kernel,
-        [whole((mine, lat))] * groups + [whole((lat, lat)), own_states],
-        [whole((wide, share, columns))],
-        [array(wide, share, columns)],
-        [home[0]] + taken + [cross, states],
+        [whole((mine, lat))] * groups + [whole((lat, lat)), whole(states.shape)],
+        [whole((wide, share, columns)), whole((mine, local_width))],
+        [array(wide, share, columns), near(mine, local_width)],
+        [home[0]] + taken + [cross, in_vmem(states)],
         [where],
     )
     got = exchanged(sent, "wide")
@@ -471,7 +483,7 @@
             far(wide, high, lat) if mode == "first" else far(mine, 2 * lat),
         ]
         operands = [got, state] + [in_vmem(weight) for weight in weights]
-        in_specs = [whole(got.shape), own_states if mode == "first" else whole(state.shape)]
+        in_specs = [whole(got.shape), whole(state.shape)]
         in_specs += [whole(weight.shape) for weight in weights]
         if mode == "later":
             in_specs.append(whole(earlier.shape))
@@ -482,7 +494,6 @@
             [whole(s.shape) for s in shapes],
             shapes,
             operands,
-            [where],
             flops=2 * (len(before) + count) * mine * lat * local_width,
         )
 
@@ -500,7 +511,7 @@
     got, weights = tied(exchanged(sent, "wide"), resident_weights((0,), (1,)))
 
     earlier = got
-    sent, state, cross = advance((0,), (1,), got, states, weights)
+    sent, state, cross = advance((0,), (1,), got, state, weights)
     crosses = lax.all_gather(cross.reshape(lat, lat), "segment", axis=0)
     got = exchanged(sent, "wide")
     (sent,) = call(
@@ -538,21 +549,22 @@
     limit = jnp.minimum(context_lengths, counts[None, :] * PAGE)
     limit = jnp.repeat(limit.T, queries.shape[2], axis=1)[:, :, None]
     new = new_latent.transpose(1, 0, 2)
+    hot = slots[2 * layers - 4 :, None] == jnp.arange(none, dtype=jnp.int32)[None, :]
+    hot = jnp.broadcast_to(hot.astype(f32).reshape(4 * none, 1), (4 * none, LANES))
 
     def decode(layer, pages, carried, last=False):
         return decode_pair(layer, slots, queries, new, limit, pages, carried, last)
 
     out = decode(0, pages[0], None)
-    got, out = lax.optimization_barrier((got, out))
+    got, out, hot = lax.optimization_barrier((got, out, in_vmem(hot)))
 
     got = exchanged(pair_step(got, mixing, segments), "segment")
     (sent,) = call(
-        functools.partial(choose_kernel, layers - 2),
-        [whole(got.shape)],
+        choose_kernel,
+        [whole(got.shape), whole(hot.shape)],
         [whole((wide, share, 4 * lat))],
         [array(wide, share, 4 * lat)],
-        [got],
-        [slots],
+        [got, hot],
     )
     got = exchanged(sent, "wide")
     out = decode(4, pages[2], decode(2, pages[1], out))

time: 200 us -> 197 us (0.985)
  Pallas kernels: 39.3 us -> 36.6 us
    pallas_call x14, Pallas kernels: 17.9 us -> 15.3 us  [call(): pl.pallas_call(body, grid_spec=pltpu.PrefetchScalarGridSpec(num_scalar_pr...]
  transfers between devices with their start and end apart: 15 -> 15, of which waited for: 9 -> 9; matrix products, arithmetic and copies ran while one was open for 1% -> 1% of each run, Pallas kernels for 17% -> 16%
where the time goes in v9:
time: 197 us; the launch traced here: 196 us
  blocking collectives  70.6 us (36%)
  waiting for transfers between devices  40.9 us (21%)
  Pallas kernels  36.6 us (19%)
  starting transfers between devices  30.5 us (15%)
  between operations  13.5 us (7%)
  local copies, waits for them, and re-layouts  3.18 us (2%)
    all_to_all x5, blocking collectives, exchanged(): return lax.all_to_all(sent, axis, 0, 0, tiled=True)  70.6 us
    all_to_all x6, waiting for transfers between devices, exchanged(): return lax.all_to_all(sent, axis, 0, 0, tiled=True)  25.9 us
    all_to_all x6, starting transfers between devices, exchanged(): return lax.all_to_all(sent, axis, 0, 0, tiled=True)  21.4 us
    pallas_call x14, Pallas kernels, call(): pl.pallas_call(body, grid_spec=pltpu.PrefetchScalarGridSpec(num_scalar_pr...  15.3 us
    pallas_call x4, Pallas kernels, decode_pair(): pl.pallas_call(functools.partial(last_decode_kernel if last else decode_k...  11.4 us
    all_gather x1, waiting for transfers between devices, shards(): every = lax.all_gather(both, 'segment', axis=0)  10.1 us
    pallas_call x7, Pallas kernels, resident(): pl.pallas_call(functools.partial(reside_kernel, lists), in_specs=[in_hbm]...  9.94 us
    ppermute x3, starting transfers between devices, shards(): lax.ppermute(home[hop], 'segment', [(0, 2 * hop), (1, 2 * hop + 1)])  7.45 us
  transfers between devices with their start and end apart: 15, of which 9 were waited for; matrix products, arithmetic and copies ran while one was open for 1% of the time, Pallas kernels for 16%

profile of v9, /device:TPU:0, one launch (start us, length us, event | category | flops | bytes accessed | tf_op | source)
XLA Modules:
  0.0 195.8 jit_solution(16275328922565023102)
XLA Ops:
  6.5 0.1 pad_add_fusion.where
  6.6 2.7 %shard_map.82 = (bf16[2,512,512]{2,1,0:T(8,128)(2,1)}, bf16[512,512]{1,0:T(8,128)(2,1)S(1)}) custom-call(s32[2]{0:T(128)S(1)} %pad_add_fusion.where, bf16[1,512,512]{2,1,0:T(8,128)(2,1)} %latent_ref.1, bf16[1,512]{1,0:T(2,128)(2,1)} %gain_ref.1, bf16[1,512,512]{2,1,0:T(8,128)(2,1)} %back_ref.1), custom_call_target="tpu_custom_call" | custom-call | bytes 3145728 | tf_op jit(solution)/shard_map/pallas_call | solution.py:66
  9.3 1.5 collective-permute-start
  10.8 1.5 collective-permute-done.lent_ref
  12.3 1.0 shard_map.83
  13.3 3.9 %collective-permute-start.1 = (bf16[128,512]{1,0:T(8,128)(2,1)S(1)}, bf16[128,512]{1,0:T(8,128)(2,1)S(1)}, u32[]{:S(2)}, u32[]{:S(2)}) collective-permute-start(bf16[128,512]{1,0:T(8,128)(2,1)S(1)} %get-tuple-element.61), channel_id=1, source_target_pairs={{0,32},{16,48},{1,33},{17,49},{2,34},{18,50},{3,35},{19,51},{4,36}... | collective-permute-start | bytes 393224 | tf_op jit(solution)/shard_map/ppermute | solution.py:431
  17.2 2.2 %collective-permute-start.2 = (bf16[128,512]{1,0:T(8,128)(2,1)S(1)}, bf16[128,512]{1,0:T(8,128)(2,1)S(1)}, u32[]{:S(2)}, u32[]{:S(2)}) collective-permute-start(bf16[128,512]{1,0:T(8,128)(2,1)S(1)} %get-tuple-element.62), channel_id=1, source_target_pairs={{0,64},{16,80},{1,65},{17,81},{2,66},{18,82},{3,67},{19,83},{4,68}... | collective-permute-start | bytes 393224 | tf_op jit(solution)/shard_map/ppermute | solution.py:431
  19.4 1.3 collective-permute-start.3
  20.7 1.0 shard_map.84.cross_ref
  21.8 2.5 %collective-permute-done.2.b_ref = bf16[128,512]{1,0:T(8,128)(2,1)S(1)} collective-permute-done((bf16[128,512]{1,0:T(8,128)(2,1)S(1)}, bf16[128,512]{1,0:T(8,128)(2,1)S(1)}, u32[]{:S(2)}, u32[]{:S(2)}) %collective-permute-start.2) | collective-permute-done | bytes 131104 | tf_op jit(solution)/shard_map/ppermute | solution.py:431
  24.2 0.8 collective-permute-done.3.c_ref
  25.0 0.7 shard_map.85
  25.8 21.0 %all_to_all.55.got_ref = bf16[16,8,2688]{2,1,0:T(8,128)(2,1)S(1)} all-to-all(bf16[16,8,2688]{2,1,0:T(8,128)(2,1)S(1)} %get-tuple-element.65), channel_id=1, replica_groups=mesh['segment'=8,'wide'=16] {'wide'}, dimensions={0} | all-to-all | bytes 1376256 | tf_op jit(solution)/shard_map/all_to_all | solution.py:44
  46.8 1.1 shard_map.86
  47.8 3.6 %all-to-all-start.1 = ((bf16[16,40,512]{2,1,0:T(8,128)(2,1)}), bf16[16,40,512]{2,1,0:T(8,128)(2,1)S(1)}, u32[]{:S(2)}, u32[]{:S(2)}) async-start(bf16[16,40,512]{2,1,0:T(8,128)(2,1)} %shard_map.86), calls=%async_computation.1 | async-start | bytes 1310720 | tf_op jit(solution)/shard_map/all_to_all | solution.py:44
  51.5 10.1 %all-gather.12.cloned.1.call-done.source_ref = bf16[16,512,512]{2,1,0:T(8,128)(2,1)} async-done(((bf16[2,512,512]{2,1,0:T(8,128)(2,1)}), bf16[16,512,512]{2,1,0:T(8,128)(2,1)}) %all-gather.12.cloned.1.call-update) | async-done | bytes 8388624 | tf_op jit(solution)/shard_map/all_gather | solution.py:407
  61.6 1.2 shard_map.87
  62.9 1.2 shard_map.88
  64.1 14.9 %all_to_all.56.got_ref = bf16[16,8,640]{2,1,0:T(8,128)(2,1)S(1)} all-to-all(bf16[16,8,640]{2,1,0:T(8,128)(2,1)S(1)} %get-tuple-element.72), channel_id=1, replica_groups=mesh['segment'=8,'wide'=16] {'wide'}, dimensions={0} | all-to-all | bytes 327680 | tf_op jit(solution)/shard_map/all_to_all | solution.py:44
  79.0 0.8 shard_map.89
  79.8 3.5 %all-to-all-start.3 = ((bf16[16,8,512]{2,1,0:T(8,128)(2,1)}), bf16[16,8,512]{2,1,0:T(8,128)(2,1)S(1)}, u32[]{:S(2)}, u32[]{:S(2)}) async-start(bf16[16,8,512]{2,1,0:T(8,128)(2,1)} %shard_map.89), calls=%async_computation.3 | async-start | bytes 262144 | tf_op jit(solution)/shard_map/all_to_all | solution.py:44
  83.4 1.6 shard_map.90
  85.0 6.3 %all-to-all-done.3.got_ref = bf16[16,8,512]{2,1,0:T(8,128)(2,1)S(1)} async-done(((bf16[16,8,512]{2,1,0:T(8,128)(2,1)}), bf16[16,8,512]{2,1,0:T(8,128)(2,1)S(1)}, u32[]{:S(2)}, u32[]{:S(2)}) %all-to-all-start.3) | async-done | bytes 131104 | tf_op jit(solution)/shard_map/all_to_all | solution.py:44
  91.3 1.4 shard_map.91
  92.7 3.6 %all-to-all-start.4 = ((bf16[16,8,1664]{2,1,0:T(8,128)(2,1)}), bf16[16,8,1664]{2,1,0:T(8,128)(2,1)S(1)}, u32[]{:S(2)}, u32[]{:S(2)}) async-start(bf16[16,8,1664]{2,1,0:T(8,128)(2,1)} %get-tuple-element.81), calls=%async_computation.4 | async-start | bytes 851968 | tf_op jit(solution)/shard_map/all_to_all | solution.py:44
  96.4 1.7 shard_map.93
  98.1 1.0 copy-done.3
  99.1 1.2 shard_map.92.cross_ref
  100.4 5.5 %all-to-all-done.4.got_ref = bf16[16,8,1664]{2,1,0:T(8,128)(2,1)S(1)} async-done(((bf16[16,8,1664]{2,1,0:T(8,128)(2,1)}), bf16[16,8,1664]{2,1,0:T(8,128)(2,1)S(1)}, u32[]{:S(2)}, u32[]{:S(2)}) %all-to-all-start.4) | async-done | bytes 426016 | tf_op jit(solution)/shard_map/all_to_all | solution.py:44
  105.9 0.5 shard_map.94
  106.4 11.6 %all_to_all.57.got_ref = bf16[16,8,1024]{2,1,0:T(8,128)(2,1)S(1)} all-to-all(bf16[16,8,1024]{2,1,0:T(8,128)(2,1)S(1)} %shard_map.94), channel_id=1, replica_groups=mesh['segment'=8,'wide'=16] {'wide'}, dimensions={0} | all-to-all | bytes 524288 | tf_op jit(solution)/shard_map/all_to_all | solution.py:44
  118.0 1.5 shard_map.95
  119.5 3.6 %all-to-all-start.6 = ((bf16[16,8,1664]{2,1,0:T(8,128)(2,1)}), bf16[16,8,1664]{2,1,0:T(8,128)(2,1)S(1)}, u32[]{:S(2)}, u32[]{:S(2)}) async-start(bf16[16,8,1664]{2,1,0:T(8,128)(2,1)} %get-tuple-element.92), calls=%async_computation.6 | async-start | bytes 851968 | tf_op jit(solution)/shard_map/all_to_all | solution.py:44
  123.1 1.7 shard_map.97
  124.9 1.0 copy-done.5
  125.9 1.2 shard_map.96.cross_ref
  127.1 5.5 %all-to-all-done.6.got_ref = bf16[16,8,1664]{2,1,0:T(8,128)(2,1)S(1)} async-done(((bf16[16,8,1664]{2,1,0:T(8,128)(2,1)}), bf16[16,8,1664]{2,1,0:T(8,128)(2,1)S(1)}, u32[]{:S(2)}, u32[]{:S(2)}) %all-to-all-start.6) | async-done | bytes 426016 | tf_op jit(solution)/shard_map/all_to_all | solution.py:44
  132.6 0.5 shard_map.98
  133.1 11.6 %all_to_all.58.got_ref = bf16[16,8,1024]{2,1,0:T(8,128)(2,1)S(1)} all-to-all(bf16[16,8,1024]{2,1,0:T(8,128)(2,1)S(1)} %shard_map.98), channel_id=1, replica_groups=mesh['segment'=8,'wide'=16] {'wide'}, dimensions={0} | all-to-all | bytes 524288 | tf_op jit(solution)/shard_map/all_to_all | solution.py:44
  144.8 1.5 shard_map.99
  146.3 0.1 select_reduce_fusion.1
  146.4 0.2 select_reduce_fusion
  146.6 0.1 copy.28
  146.7 0.1 slice.4
  146.8 0.1 min.18.slots
  146.9 3.6 %all-to-all-start.8 = ((bf16[16,8,1664]{2,1,0:T(8,128)(2,1)}), bf16[16,8,1664]{2,1,0:T(8,128)(2,1)S(1)}, u32[]{:S(2)}, u32[]{:S(2)}) async-start(bf16[16,8,1664]{2,1,0:T(8,128)(2,1)} %get-tuple-element.102), calls=%async_computation.8 | async-start | bytes 851968 | tf_op jit(solution)/shard_map/all_to_all | solution.py:44
  150.4 0.1 minimum_bitcast_fusion
  150.5 0.1 copy.27
  150.6 0.5 copy.33.limit_ref
  151.1 0.1 copy.30
  151.2 0.1 eq.32
  151.3 0.1 fusion.1
  151.4 0.1 reshape.43
  151.5 3.3 %shard_map.101.rest_0_ = bf16[16,8,4,512]{3,2,1,0:T(4,128)(2,1)} custom-call(s32[16]{0:T(128)S(1)} %min.18.slots, bf16[16,8,4,512]{3,2,1,0:T(4,128)(2,1)S(1)} %copy-done, bf16[8,16,512]{2,1,0:T(8,128)(2,1)S(1)} %bitcast.22, s32[8,64,1]{2,1,0:T(8,128)S(1)} %copy.33.limit_ref, bf16[8,128,1024]{2,1,0:T(8,128)(2,1)} %bitcast.26), custom_call_target="tpu_custom_call" | custom-call | flops 67108864 | bytes 786432 | tf_op jit(solution)/shard_map/pallas_call | solution.py:347
  154.7 1.2 shard_map.100.cross_ref
  156.0 4.0 %all-to-all-done.8.got_ref = bf16[16,8,1664]{2,1,0:T(8,128)(2,1)S(1)} async-done(((bf16[16,8,1664]{2,1,0:T(8,128)(2,1)}), bf16[16,8,1664]{2,1,0:T(8,128)(2,1)S(1)}, u32[]{:S(2)}, u32[]{:S(2)}) %all-to-all-start.8) | async-done | bytes 426016 | tf_op jit(solution)/shard_map/all_to_all | solution.py:44
  160.0 0.5 shard_map.102
  160.5 11.4 %all_to_all.59.got_ref = bf16[8,8,1024]{2,1,0:T(8,128)(2,1)S(1)} all-to-all(bf16[8,8,1024]{2,1,0:T(8,128)(2,1)S(1)} %shard_map.102), channel_id=1, replica_groups=mesh['segment'=8,'wide'=16] {'segment'}, dimensions={0} | all-to-all | bytes 262144 | tf_op jit(solution)/shard_map/all_to_all | solution.py:44
  172.0 0.9 shard_map.103
  172.8 3.6 %all-to-all-start.10 = ((bf16[16,8,2048]{2,1,0:T(8,128)(2,1)}), bf16[16,8,2048]{2,1,0:T(8,128)(2,1)S(1)}, u32[]{:S(2)}, u32[]{:S(2)}) async-start(bf16[16,8,2048]{2,1,0:T(8,128)(2,1)} %shard_map.103), calls=%async_computation.10 | async-start | bytes 1048576 | tf_op jit(solution)/shard_map/all_to_all | solution.py:44
  176.5 3.3 %shard_map.104.rest_0_ = bf16[16,8,4,512]{3,2,1,0:T(4,128)(2,1)} custom-call(s32[16]{0:T(128)S(1)} %min.18.slots, bf16[16,8,4,512]{3,2,1,0:T(4,128)(2,1)S(1)} %copy-done, bf16[8,16,512]{2,1,0:T(8,128)(2,1)S(1)} %bitcast.23, s32[8,64,1]{2,1,0:T(8,128)S(1)} %copy.33.limit_ref, bf16[8,128,1024]{2,1,0:T(8,128)(2,1)} %bitcast.27, ...), custom_call_target="tpu_custom_call", output_to_operand_aliasing={{}: (5, {})} | custom-call | flops 67108864 | bytes 786432 | tf_op jit(solution)/shard_map/pallas_call | solution.py:347
  179.8 3.3 %shard_map.105.carried_ref = bf16[16,8,4,512]{3,2,1,0:T(4,128)(2,1)} custom-call(s32[16]{0:T(128)S(1)} %min.18.slots, bf16[16,8,4,512]{3,2,1,0:T(4,128)(2,1)S(1)} %copy-done, bf16[8,16,512]{2,1,0:T(8,128)(2,1)S(1)} %bitcast.24, s32[8,64,1]{2,1,0:T(8,128)S(1)} %copy.33.limit_ref, bf16[8,128,1024]{2,1,0:T(8,128)(2,1)} %bitcast.28, ...), custom_call_target="tpu_custom_call", output_to_operand_aliasing={{}: (5, {})} | custom-call | flops 67108864 | bytes 786432 | tf_op jit(solution)/shard_map/pallas_call | solution.py:347
  183.0 4.6 %all-to-all-done.10.pages_ref = bf16[16,8,2048]{2,1,0:T(8,128)(2,1)S(1)} async-done(((bf16[16,8,2048]{2,1,0:T(8,128)(2,1)}), bf16[16,8,2048]{2,1,0:T(8,128)(2,1)S(1)}, u32[]{:S(2)}, u32[]{:S(2)}) %all-to-all-start.10) | async-done | bytes 524320 | tf_op jit(solution)/shard_map/all_to_all | solution.py:44
  187.7 1.6 shard_map.106
  (39 shorter events, 0.5 us)
Async XLA Ops:
  6.5 5.7 %copy-start.1 = (bf16[4,256,512]{2,1,0:T(8,128)(2,1)S(1)}, bf16[4,256,512]{2,1,0:T(8,128)(2,1)}, u32[]{:S(2)}) copy-start(bf16[4,256,512]{2,1,0:T(8,128)(2,1)} %param.8) | copy-start | bytes 3145732
  6.5 55.1 %all-gather.12.cloned.1.call-start = ((), (), s32[]{:S(2)}) async-start(), calls=%async_computation.12 | async-start | bytes 9437184 | tf_op jit(solution)/shard_map/all_gather | solution.py:407
  9.3 11.4 %copy-start.2 = (bf16[2,512,512]{2,1,0:T(8,128)(2,1)S(1)}, bf16[2,512,512]{2,1,0:T(8,128)(2,1)}, u32[]{:S(2)}) copy-start(bf16[2,512,512]{2,1,0:T(8,128)(2,1)} %get-tuple-element.64.both_ref) | copy-start | bytes 3145732
  9.3 2.9 %collective-permute-start = (bf16[512,512]{1,0:T(8,128)(2,1)S(1)}, bf16[512,512]{1,0:T(8,128)(2,1)S(1)}, u32[]{:S(2)}, u32[]{:S(2)}) collective-permute-start(bf16[512,512]{1,0:T(8,128)(2,1)S(1)} %get-tuple-element.59.mine_ref), channel_id=1, source_target_pairs={{0,16},{32,48},{64,80},{96,112},{1,17},{33,49},{65,81},{97,113},{2... | collective-permute-start | bytes 1572872 | tf_op jit(solution)/shard_map/ppermute | solution.py:408
  13.3 8.5 %collective-permute-start.1 = (bf16[128,512]{1,0:T(8,128)(2,1)S(1)}, bf16[128,512]{1,0:T(8,128)(2,1)S(1)}, u32[]{:S(2)}, u32[]{:S(2)}) collective-permute-start(bf16[128,512]{1,0:T(8,128)(2,1)S(1)} %get-tuple-element.61), channel_id=1, source_target_pairs={{0,32},{16,48},{1,33},{17,49},{2,34},{18,50},{3,35},{19,51},{4,36}... | collective-permute-start | bytes 393224 | tf_op jit(solution)/shard_map/ppermute | solution.py:431
  17.2 7.0 %collective-permute-start.2 = (bf16[128,512]{1,0:T(8,128)(2,1)S(1)}, bf16[128,512]{1,0:T(8,128)(2,1)S(1)}, u32[]{:S(2)}, u32[]{:S(2)}) collective-permute-start(bf16[128,512]{1,0:T(8,128)(2,1)S(1)} %get-tuple-element.62), channel_id=1, source_target_pairs={{0,64},{16,80},{1,65},{17,81},{2,66},{18,82},{3,67},{19,83},{4,68}... | collective-permute-start | bytes 393224 | tf_op jit(solution)/shard_map/ppermute | solution.py:431
  19.4 5.6 %collective-permute-start.3 = (bf16[128,512]{1,0:T(8,128)(2,1)S(1)}, bf16[128,512]{1,0:T(8,128)(2,1)S(1)}, u32[]{:S(2)}, u32[]{:S(2)}) collective-permute-start(bf16[128,512]{1,0:T(8,128)(2,1)S(1)} %get-tuple-element.63), channel_id=1, source_target_pairs={{0,96},{16,112},{1,97},{17,113},{2,98},{18,114},{3,99},{19,115},{4... | collective-permute-start | bytes 393224 | tf_op jit(solution)/shard_map/ppermute | solution.py:431
  47.8 15.0 %all-to-all-start.1 = ((bf16[16,40,512]{2,1,0:T(8,128)(2,1)}), bf16[16,40,512]{2,1,0:T(8,128)(2,1)S(1)}, u32[]{:S(2)}, u32[]{:S(2)}) async-start(bf16[16,40,512]{2,1,0:T(8,128)(2,1)} %shard_map.86), calls=%async_computation.1 | async-start | bytes 1310720 | tf_op jit(solution)/shard_map/all_to_all | solution.py:44
  51.5 47.7 %all-gather.10.cloned.1.call-start = ((), (), s32[]{:S(2)}) async-start(), calls=%async_computation.11 | async-start | bytes 4718592 | tf_op jit(solution)/shard_map/all_gather | solution.py:515
  79.8 11.5 %all-to-all-start.3 = ((bf16[16,8,512]{2,1,0:T(8,128)(2,1)}), bf16[16,8,512]{2,1,0:T(8,128)(2,1)S(1)}, u32[]{:S(2)}, u32[]{:S(2)}) async-start(bf16[16,8,512]{2,1,0:T(8,128)(2,1)} %shard_map.89), calls=%async_computation.3 | async-start | bytes 262144 | tf_op jit(solution)/shard_map/all_to_all | solution.py:44
  83.3 68.1 %all-gather.14.cloned.1.call-start = ((), (), s32[]{:S(2)}) async-start(), calls=%async_computation.13 | async-start | bytes 2359296 | tf_op jit(solution)/shard_map/all_gather | solution.py:532
  92.7 13.1 %all-to-all-start.4 = ((bf16[16,8,1664]{2,1,0:T(8,128)(2,1)}), bf16[16,8,1664]{2,1,0:T(8,128)(2,1)S(1)}, u32[]{:S(2)}, u32[]{:S(2)}) async-start(bf16[16,8,1664]{2,1,0:T(8,128)(2,1)} %get-tuple-element.81), calls=%async_computation.4 | async-start | bytes 851968 | tf_op jit(solution)/shard_map/all_to_all | solution.py:44
  96.3 80.1 %all-gather.18.cloned.1.call-start = ((), (), s32[]{:S(2)}) async-start(), calls=%async_computation.15 | async-start | bytes 2359296 | tf_op jit(solution)/shard_map/all_gather | solution.py:532
  98.1 1.0 copy-start.3
  105.9 12.1 %copy-start.4 = (bf16[2,512,512]{2,1,0:T(8,128)(2,1)S(1)}, bf16[2,512,512]{2,1,0:T(8,128)(2,1)}, u32[]{:S(2)}) copy-start(bf16[2,512,512]{2,1,0:T(8,128)(2,1)} %copy-done.3) | copy-start | bytes 3145732
  119.5 13.1 %all-to-all-start.6 = ((bf16[16,8,1664]{2,1,0:T(8,128)(2,1)}), bf16[16,8,1664]{2,1,0:T(8,128)(2,1)S(1)}, u32[]{:S(2)}, u32[]{:S(2)}) async-start(bf16[16,8,1664]{2,1,0:T(8,128)(2,1)} %get-tuple-element.92), calls=%async_computation.6 | async-start | bytes 851968 | tf_op jit(solution)/shard_map/all_to_all | solution.py:44
  123.1 56.7 %all-gather.16.cloned.1.call-start = ((), (), s32[]{:S(2)}) async-start(), calls=%async_computation.14 | async-start | bytes 2359296 | tf_op jit(solution)/shard_map/all_gather | solution.py:532
  124.9 1.0 copy-start.5
  132.6 12.1 %copy-start.6 = (bf16[2,512,512]{2,1,0:T(8,128)(2,1)S(1)}, bf16[2,512,512]{2,1,0:T(8,128)(2,1)}, u32[]{:S(2)}) copy-start(bf16[2,512,512]{2,1,0:T(8,128)(2,1)} %copy-done.5) | copy-start | bytes 3145732
  133.1 13.2 %copy-start.8 = (s32[8,8,1]{1,2,0:T(1,128)S(1)}, s32[8,8,1]{1,2,0:T(1,128)}, u32[]{:S(2)}) copy-start(s32[8,8,1]{1,2,0:T(1,128)} %param.12) | copy-start | bytes 772
  144.7 5.7 %copy-start.9 = (s32[16,8]{0,1:T(8,128)S(1)}, s32[16,8]{0,1:T(8,128)}, u32[]{:S(2)}) copy-start(s32[16,8]{0,1:T(8,128)} %param.15) | copy-start | bytes 1540
  144.7 6.3 %copy-start.7 = (bf16[16,8,512]{2,1,0:T(8,128)(2,1)S(1)}, bf16[16,8,512]{2,1,0:T(8,128)(2,1)}, u32[]{:S(2)}) copy-start(bf16[16,8,512]{2,1,0:T(8,128)(2,1)} %param.14) | copy-start | bytes 393220
  144.7 6.7 %copy-start = (bf16[16,8,4,512]{3,2,1,0:T(4,128)(2,1)S(1)}, bf16[16,8,4,512]{3,2,1,0:T(4,128)(2,1)}, u32[]{:S(2)}) copy-start(bf16[16,8,4,512]{3,2,1,0:T(4,128)(2,1)} %q_ref.7) | copy-start | bytes 1572868
  146.9 13.1 %all-to-all-start.8 = ((bf16[16,8,1664]{2,1,0:T(8,128)(2,1)}), bf16[16,8,1664]{2,1,0:T(8,128)(2,1)S(1)}, u32[]{:S(2)}, u32[]{:S(2)}) async-start(bf16[16,8,1664]{2,1,0:T(8,128)(2,1)} %get-tuple-element.102), calls=%async_computation.8 | async-start | bytes 851968 | tf_op jit(solution)/shard_map/all_to_all | solution.py:44
  172.8 14.8 %all-to-all-start.10 = ((bf16[16,8,2048]{2,1,0:T(8,128)(2,1)}), bf16[16,8,2048]{2,1,0:T(8,128)(2,1)S(1)}, u32[]{:S(2)}, u32[]{:S(2)}) async-start(bf16[16,8,2048]{2,1,0:T(8,128)(2,1)} %shard_map.103), calls=%async_computation.10 | async-start | bytes 1048576 | tf_op jit(solution)/shard_map/all_to_all | solution.py:44
Sparse Core Ops, SparseCore 0:
  9.4 52.1 all-gather.11
  64.2 32.8 all-gather.9
  98.8 25.0 all-gather.13
  125.5 25.4 all-gather.17
  152.6 25.9 all-gather.15

commit v10 on v9

--- a/solution.py
+++ b/solution.py
@@ -513,7 +513,7 @@
     earlier = got
     sent, state, cross = advance((0,), (1,), got, state, weights)
     crosses = lax.all_gather(cross.reshape(lat, lat), "segment", axis=0)
-    got = exchanged(sent, "wide")
+    got, weights = tied(exchanged(sent, "wide"), resident_weights((1,), (2, 3)))
     (sent,) = call(
         functools.partial(single_kernel, width),
         [whole(got.shape)],
@@ -521,7 +521,7 @@
         [array(wide, share, lat)],
         [got],
     )
-    got, weights = tied(exchanged(sent, "wide"), resident_weights((1,), (2, 3)))
+    got = exchanged(sent, "wide")
 
     pages = []
     for even in range(2, layers, 2):

time: 197 us -> 196 us (level)
  blocking collectives: 70.6 us -> 66.6 us
  starting transfers between devices: 30.5 us -> 33.9 us
    all_to_all x5, blocking collectives: 70.6 us -> 66.6 us  [exchanged(): return lax.all_to_all(sent, axis, 0, 0, tiled=True)]
    all_to_all x6, starting transfers between devices: 21.4 us -> 24.9 us  [exchanged(): return lax.all_to_all(sent, axis, 0, 0, tiled=True)]
  transfers between devices with their start and end apart: 15 -> 15, of which waited for: 9 -> 10; matrix products, arithmetic and copies ran while one was open for 1% -> 1% of each run, Pallas kernels for 16% -> 16%
where the time goes in v10:
time: 196 us; the launch traced here: 195 us
  blocking collectives  66.6 us (34%)
  waiting for transfers between devices  41.2 us (21%)
  Pallas kernels  36 us (18%)
  starting transfers between devices  33.9 us (17%)
  between operations  13.5 us (7%)
  local copies, waits for them, and re-layouts  3.18 us (2%)
    all_to_all x5, blocking collectives, exchanged(): return lax.all_to_all(sent, axis, 0, 0, tiled=True)  66.6 us
    all_to_all x6, waiting for transfers between devices, exchanged(): return lax.all_to_all(sent, axis, 0, 0, tiled=True)  26 us
    all_to_all x6, starting transfers between devices, exchanged(): return lax.all_to_all(sent, axis, 0, 0, tiled=True)  24.9 us
    pallas_call x14, Pallas kernels, call(): pl.pallas_call(body, grid_spec=pltpu.PrefetchScalarGridSpec(num_scalar_pr...  14.7 us
    pallas_call x4, Pallas kernels, decode_pair(): pl.pallas_call(functools.partial(last_decode_kernel if last else decode_k...  11.4 us
    all_gather x1, waiting for transfers between devices, shards(): every = lax.all_gather(both, 'segment', axis=0)  10.1 us
    pallas_call x7, Pallas kernels, resident(): pl.pallas_call(functools.partial(reside_kernel, lists), in_specs=[in_hbm]...  9.92 us
    ppermute x3, starting transfers between devices, shards(): lax.ppermute(home[hop], 'segment', [(0, 2 * hop), (1, 2 * hop + 1)])  7.45 us
  transfers between devices with their start and end apart: 15, of which 10 were waited for; matrix products, arithmetic and copies ran while one was open for 1% of the time, Pallas kernels for 16%

profile of v10, /device:TPU:0, one launch (start us, length us, event | category | flops | bytes accessed | tf_op | source)
XLA Modules:
  0.0 194.9 jit_solution(9780341217681544763)
XLA Ops:
  6.5 0.1 pad_add_fusion.where
  6.6 2.7 %shard_map.82 = (bf16[2,512,512]{2,1,0:T(8,128)(2,1)}, bf16[512,512]{1,0:T(8,128)(2,1)S(1)}) custom-call(s32[2]{0:T(128)S(1)} %pad_add_fusion.where, bf16[1,512,512]{2,1,0:T(8,128)(2,1)} %latent_ref.1, bf16[1,512]{1,0:T(2,128)(2,1)} %gain_ref.1, bf16[1,512,512]{2,1,0:T(8,128)(2,1)} %back_ref.1), custom_call_target="tpu_custom_call" | custom-call | bytes 3145728 | tf_op jit(solution)/shard_map/pallas_call | solution.py:66
  9.3 1.5 collective-permute-start
  10.8 1.5 collective-permute-done.lent_ref
  12.3 1.0 shard_map.83
  13.3 3.9 %collective-permute-start.1 = (bf16[128,512]{1,0:T(8,128)(2,1)S(1)}, bf16[128,512]{1,0:T(8,128)(2,1)S(1)}, u32[]{:S(2)}, u32[]{:S(2)}) collective-permute-start(bf16[128,512]{1,0:T(8,128)(2,1)S(1)} %get-tuple-element.61), channel_id=1, source_target_pairs={{0,32},{16,48},{1,33},{17,49},{2,34},{18,50},{3,35},{19,51},{4,36}... | collective-permute-start | bytes 393224 | tf_op jit(solution)/shard_map/ppermute | solution.py:431
  17.2 2.2 %collective-permute-start.2 = (bf16[128,512]{1,0:T(8,128)(2,1)S(1)}, bf16[128,512]{1,0:T(8,128)(2,1)S(1)}, u32[]{:S(2)}, u32[]{:S(2)}) collective-permute-start(bf16[128,512]{1,0:T(8,128)(2,1)S(1)} %get-tuple-element.62), channel_id=1, source_target_pairs={{0,64},{16,80},{1,65},{17,81},{2,66},{18,82},{3,67},{19,83},{4,68}... | collective-permute-start | bytes 393224 | tf_op jit(solution)/shard_map/ppermute | solution.py:431
  19.4 1.3 collective-permute-start.3
  20.7 1.0 shard_map.84.cross_ref
  21.8 2.5 %collective-permute-done.2.b_ref = bf16[128,512]{1,0:T(8,128)(2,1)S(1)} collective-permute-done((bf16[128,512]{1,0:T(8,128)(2,1)S(1)}, bf16[128,512]{1,0:T(8,128)(2,1)S(1)}, u32[]{:S(2)}, u32[]{:S(2)}) %collective-permute-start.2) | collective-permute-done | bytes 131104 | tf_op jit(solution)/shard_map/ppermute | solution.py:431
  24.2 0.8 collective-permute-done.3.c_ref
  25.0 0.7 shard_map.85
  25.8 21.0 %all_to_all.55.got_ref = bf16[16,8,2688]{2,1,0:T(8,128)(2,1)S(1)} all-to-all(bf16[16,8,2688]{2,1,0:T(8,128)(2,1)S(1)} %get-tuple-element.65), channel_id=1, replica_groups=mesh['segment'=8,'wide'=16] {'wide'}, dimensions={0} | all-to-all | bytes 1376256 | tf_op jit(solution)/shard_map/all_to_all | solution.py:44
  46.8 1.1 shard_map.86
  47.8 3.6 %all-to-all-start.1 = ((bf16[16,40,512]{2,1,0:T(8,128)(2,1)}), bf16[16,40,512]{2,1,0:T(8,128)(2,1)S(1)}, u32[]{:S(2)}, u32[]{:S(2)}) async-start(bf16[16,40,512]{2,1,0:T(8,128)(2,1)} %shard_map.86), calls=%async_computation.1 | async-start | bytes 1310720 | tf_op jit(solution)/shard_map/all_to_all | solution.py:44
  51.5 10.1 %all-gather.12.cloned.1.call-done.source_ref = bf16[16,512,512]{2,1,0:T(8,128)(2,1)} async-done(((bf16[2,512,512]{2,1,0:T(8,128)(2,1)}), bf16[16,512,512]{2,1,0:T(8,128)(2,1)}) %all-gather.12.cloned.1.call-update) | async-done | bytes 8388624 | tf_op jit(solution)/shard_map/all_gather | solution.py:407
  61.6 1.2 shard_map.87
  62.9 1.2 shard_map.88
  64.1 7.0 %all-to-all-start.2 = ((bf16[16,8,640]{2,1,0:T(8,128)(2,1)}), bf16[16,8,640]{2,1,0:T(8,128)(2,1)S(1)}, u32[]{:S(2)}, u32[]{:S(2)}) async-start(bf16[16,8,640]{2,1,0:T(8,128)(2,1)} %get-tuple-element.72), calls=%async_computation.2 | async-start | bytes 327680 | tf_op jit(solution)/shard_map/all_to_all | solution.py:44
  71.1 1.6 shard_map.89
  72.7 6.6 %all-to-all-done.2.got_ref = bf16[16,8,640]{2,1,0:T(8,128)(2,1)S(1)} async-done(((bf16[16,8,640]{2,1,0:T(8,128)(2,1)}), bf16[16,8,640]{2,1,0:T(8,128)(2,1)S(1)}, u32[]{:S(2)}, u32[]{:S(2)}) %all-to-all-start.2) | async-done | bytes 163872 | tf_op jit(solution)/shard_map/all_to_all | solution.py:44
  79.3 0.2 shard_map.90
  79.4 11.0 %all_to_all.56.got_ref = bf16[16,8,512]{2,1,0:T(8,128)(2,1)S(1)} all-to-all(bf16[16,8,512]{2,1,0:T(8,128)(2,1)S(1)} %shard_map.90), channel_id=1, replica_groups=mesh['segment'=8,'wide'=16] {'wide'}, dimensions={0} | all-to-all | bytes 262144 | tf_op jit(solution)/shard_map/all_to_all | solution.py:44
  90.5 1.4 shard_map.91
  91.9 3.6 %all-to-all-start.4 = ((bf16[16,8,1664]{2,1,0:T(8,128)(2,1)}), bf16[16,8,1664]{2,1,0:T(8,128)(2,1)S(1)}, u32[]{:S(2)}, u32[]{:S(2)}) async-start(bf16[16,8,1664]{2,1,0:T(8,128)(2,1)} %get-tuple-element.81), calls=%async_computation.4 | async-start | bytes 851968 | tf_op jit(solution)/shard_map/all_to_all | solution.py:44
  95.5 1.8 shard_map.93
  97.3 1.0 copy-done.3
  98.3 1.2 shard_map.92.cross_ref
  99.6 5.5 %all-to-all-done.4.got_ref = bf16[16,8,1664]{2,1,0:T(8,128)(2,1)S(1)} async-done(((bf16[16,8,1664]{2,1,0:T(8,128)(2,1)}), bf16[16,8,1664]{2,1,0:T(8,128)(2,1)S(1)}, u32[]{:S(2)}, u32[]{:S(2)}) %all-to-all-start.4) | async-done | bytes 426016 | tf_op jit(solution)/shard_map/all_to_all | solution.py:44
  105.0 0.5 shard_map.94
  105.5 11.6 %all_to_all.57.got_ref = bf16[16,8,1024]{2,1,0:T(8,128)(2,1)S(1)} all-to-all(bf16[16,8,1024]{2,1,0:T(8,128)(2,1)S(1)} %shard_map.94), channel_id=1, replica_groups=mesh['segment'=8,'wide'=16] {'wide'}, dimensions={0} | all-to-all | bytes 524288 | tf_op jit(solution)/shard_map/all_to_all | solution.py:44
  117.1 1.5 shard_map.95
  118.7 3.6 %all-to-all-start.6 = ((bf16[16,8,1664]{2,1,0:T(8,128)(2,1)}), bf16[16,8,1664]{2,1,0:T(8,128)(2,1)S(1)}, u32[]{:S(2)}, u32[]{:S(2)}) async-start(bf16[16,8,1664]{2,1,0:T(8,128)(2,1)} %get-tuple-element.92), calls=%async_computation.6 | async-start | bytes 851968 | tf_op jit(solution)/shard_map/all_to_all | solution.py:44
  122.3 1.7 shard_map.97
  124.0 1.0 copy-done.5
  125.0 1.2 shard_map.96.cross_ref
  126.3 5.5 %all-to-all-done.6.got_ref = bf16[16,8,1664]{2,1,0:T(8,128)(2,1)S(1)} async-done(((bf16[16,8,1664]{2,1,0:T(8,128)(2,1)}), bf16[16,8,1664]{2,1,0:T(8,128)(2,1)S(1)}, u32[]{:S(2)}, u32[]{:S(2)}) %all-to-all-start.6) | async-done | bytes 426016 | tf_op jit(solution)/shard_map/all_to_all | solution.py:44
  131.8 0.5 shard_map.98
  132.3 11.6 %all_to_all.58.got_ref = bf16[16,8,1024]{2,1,0:T(8,128)(2,1)S(1)} all-to-all(bf16[16,8,1024]{2,1,0:T(8,128)(2,1)S(1)} %shard_map.98), channel_id=1, replica_groups=mesh['segment'=8,'wide'=16] {'wide'}, dimensions={0} | all-to-all | bytes 524288 | tf_op jit(solution)/shard_map/all_to_all | solution.py:44
  143.9 1.5 shard_map.99
  145.5 0.1 select_reduce_fusion.1
  145.6 0.2 select_reduce_fusion
  145.8 0.1 copy.28
  145.9 0.1 slice.4
  145.9 0.1 min.18.slots
  146.0 3.6 %all-to-all-start.8 = ((bf16[16,8,1664]{2,1,0:T(8,128)(2,1)}), bf16[16,8,1664]{2,1,0:T(8,128)(2,1)S(1)}, u32[]{:S(2)}, u32[]{:S(2)}) async-start(bf16[16,8,1664]{2,1,0:T(8,128)(2,1)} %get-tuple-element.102), calls=%async_computation.8 | async-start | bytes 851968 | tf_op jit(solution)/shard_map/all_to_all | solution.py:44
  149.7 0.1 copy.27
  149.8 0.5 copy.33.limit_ref
  150.3 0.1 copy.30
  150.4 0.1 eq.32
  150.4 0.1 fusion.1
  150.5 0.1 reshape.43
  150.6 3.3 %shard_map.101.rest_0_ = bf16[16,8,4,512]{3,2,1,0:T(4,128)(2,1)} custom-call(s32[16]{0:T(128)S(1)} %min.18.slots, bf16[16,8,4,512]{3,2,1,0:T(4,128)(2,1)S(1)} %copy-done, bf16[8,16,512]{2,1,0:T(8,128)(2,1)S(1)} %bitcast.22, s32[8,64,1]{2,1,0:T(8,128)S(1)} %copy.33.limit_ref, bf16[8,128,1024]{2,1,0:T(8,128)(2,1)} %bitcast.26), custom_call_target="tpu_custom_call" | custom-call | flops 67108864 | bytes 786432 | tf_op jit(solution)/shard_map/pallas_call | solution.py:347
  153.9 1.2 shard_map.100.cross_ref
  155.1 4.0 %all-to-all-done.8.got_ref = bf16[16,8,1664]{2,1,0:T(8,128)(2,1)S(1)} async-done(((bf16[16,8,1664]{2,1,0:T(8,128)(2,1)}), bf16[16,8,1664]{2,1,0:T(8,128)(2,1)S(1)}, u32[]{:S(2)}, u32[]{:S(2)}) %all-to-all-start.8) | async-done | bytes 426016 | tf_op jit(solution)/shard_map/all_to_all | solution.py:44
  159.2 0.5 shard_map.102
  159.7 11.3 %all_to_all.59.got_ref = bf16[8,8,1024]{2,1,0:T(8,128)(2,1)S(1)} all-to-all(bf16[8,8,1024]{2,1,0:T(8,128)(2,1)S(1)} %shard_map.102), channel_id=1, replica_groups=mesh['segment'=8,'wide'=16] {'segment'}, dimensions={0} | all-to-all | bytes 262144 | tf_op jit(solution)/shard_map/all_to_all | solution.py:44
  171.0 0.9 shard_map.103
  171.9 3.6 %all-to-all-start.10 = ((bf16[16,8,2048]{2,1,0:T(8,128)(2,1)}), bf16[16,8,2048]{2,1,0:T(8,128)(2,1)S(1)}, u32[]{:S(2)}, u32[]{:S(2)}) async-start(bf16[16,8,2048]{2,1,0:T(8,128)(2,1)} %shard_map.103), calls=%async_computation.10 | async-start | bytes 1048576 | tf_op jit(solution)/shard_map/all_to_all | solution.py:44
  175.5 3.3 %shard_map.104.rest_0_ = bf16[16,8,4,512]{3,2,1,0:T(4,128)(2,1)} custom-call(s32[16]{0:T(128)S(1)} %min.18.slots, bf16[16,8,4,512]{3,2,1,0:T(4,128)(2,1)S(1)} %copy-done, bf16[8,16,512]{2,1,0:T(8,128)(2,1)S(1)} %bitcast.23, s32[8,64,1]{2,1,0:T(8,128)S(1)} %copy.33.limit_ref, bf16[8,128,1024]{2,1,0:T(8,128)(2,1)} %bitcast.27, ...), custom_call_target="tpu_custom_call", output_to_operand_aliasing={{}: (5, {})} | custom-call | flops 67108864 | bytes 786432 | tf_op jit(solution)/shard_map/pallas_call | solution.py:347
  178.8 0.2 all-gather.16.cloned.1.call-done
  179.0 3.3 %shard_map.105.carried_ref = bf16[16,8,4,512]{3,2,1,0:T(4,128)(2,1)} custom-call(s32[16]{0:T(128)S(1)} %min.18.slots, bf16[16,8,4,512]{3,2,1,0:T(4,128)(2,1)S(1)} %copy-done, bf16[8,16,512]{2,1,0:T(8,128)(2,1)S(1)} %bitcast.24, s32[8,64,1]{2,1,0:T(8,128)S(1)} %copy.33.limit_ref, bf16[8,128,1024]{2,1,0:T(8,128)(2,1)} %bitcast.28, ...), custom_call_target="tpu_custom_call", output_to_operand_aliasing={{}: (5, {})} | custom-call | flops 67108864 | bytes 786432 | tf_op jit(solution)/shard_map/pallas_call | solution.py:347
  182.3 4.5 %all-to-all-done.10.pages_ref = bf16[16,8,2048]{2,1,0:T(8,128)(2,1)S(1)} async-done(((bf16[16,8,2048]{2,1,0:T(8,128)(2,1)}), bf16[16,8,2048]{2,1,0:T(8,128)(2,1)S(1)}, u32[]{:S(2)}, u32[]{:S(2)}) %all-to-all-start.10) | async-done | bytes 524320 | tf_op jit(solution)/shard_map/all_to_all | solution.py:44
  186.8 1.6 shard_map.106
  (39 shorter events, 0.5 us)
Async XLA Ops:
  6.5 5.7 %copy-start.1 = (bf16[4,256,512]{2,1,0:T(8,128)(2,1)S(1)}, bf16[4,256,512]{2,1,0:T(8,128)(2,1)}, u32[]{:S(2)}) copy-start(bf16[4,256,512]{2,1,0:T(8,128)(2,1)} %param.8) | copy-start | bytes 3145732
  6.5 55.1 %all-gather.12.cloned.1.call-start = ((), (), s32[]{:S(2)}) async-start(), calls=%async_computation.12 | async-start | bytes 9437184 | tf_op jit(solution)/shard_map/all_gather | solution.py:407
  9.3 11.4 %copy-start.2 = (bf16[2,512,512]{2,1,0:T(8,128)(2,1)S(1)}, bf16[2,512,512]{2,1,0:T(8,128)(2,1)}, u32[]{:S(2)}) copy-start(bf16[2,512,512]{2,1,0:T(8,128)(2,1)} %get-tuple-element.64.both_ref) | copy-start | bytes 3145732
  9.3 2.9 %collective-permute-start = (bf16[512,512]{1,0:T(8,128)(2,1)S(1)}, bf16[512,512]{1,0:T(8,128)(2,1)S(1)}, u32[]{:S(2)}, u32[]{:S(2)}) collective-permute-start(bf16[512,512]{1,0:T(8,128)(2,1)S(1)} %get-tuple-element.59.mine_ref), channel_id=1, source_target_pairs={{0,16},{32,48},{64,80},{96,112},{1,17},{33,49},{65,81},{97,113},{2... | collective-permute-start | bytes 1572872 | tf_op jit(solution)/shard_map/ppermute | solution.py:408
  13.3 8.5 %collective-permute-start.1 = (bf16[128,512]{1,0:T(8,128)(2,1)S(1)}, bf16[128,512]{1,0:T(8,128)(2,1)S(1)}, u32[]{:S(2)}, u32[]{:S(2)}) collective-permute-start(bf16[128,512]{1,0:T(8,128)(2,1)S(1)} %get-tuple-element.61), channel_id=1, source_target_pairs={{0,32},{16,48},{1,33},{17,49},{2,34},{18,50},{3,35},{19,51},{4,36}... | collective-permute-start | bytes 393224 | tf_op jit(solution)/shard_map/ppermute | solution.py:431
  17.2 7.0 %collective-permute-start.2 = (bf16[128,512]{1,0:T(8,128)(2,1)S(1)}, bf16[128,512]{1,0:T(8,128)(2,1)S(1)}, u32[]{:S(2)}, u32[]{:S(2)}) collective-permute-start(bf16[128,512]{1,0:T(8,128)(2,1)S(1)} %get-tuple-element.62), channel_id=1, source_target_pairs={{0,64},{16,80},{1,65},{17,81},{2,66},{18,82},{3,67},{19,83},{4,68}... | collective-permute-start | bytes 393224 | tf_op jit(solution)/shard_map/ppermute | solution.py:431
  19.4 5.6 %collective-permute-start.3 = (bf16[128,512]{1,0:T(8,128)(2,1)S(1)}, bf16[128,512]{1,0:T(8,128)(2,1)S(1)}, u32[]{:S(2)}, u32[]{:S(2)}) collective-permute-start(bf16[128,512]{1,0:T(8,128)(2,1)S(1)} %get-tuple-element.63), channel_id=1, source_target_pairs={{0,96},{16,112},{1,97},{17,113},{2,98},{18,114},{3,99},{19,115},{4... | collective-permute-start | bytes 393224 | tf_op jit(solution)/shard_map/ppermute | solution.py:431
  47.8 15.0 %all-to-all-start.1 = ((bf16[16,40,512]{2,1,0:T(8,128)(2,1)}), bf16[16,40,512]{2,1,0:T(8,128)(2,1)S(1)}, u32[]{:S(2)}, u32[]{:S(2)}) async-start(bf16[16,40,512]{2,1,0:T(8,128)(2,1)} %shard_map.86), calls=%async_computation.1 | async-start | bytes 1310720 | tf_op jit(solution)/shard_map/all_to_all | solution.py:44
  51.5 46.9 %all-gather.10.cloned.1.call-start = ((), (), s32[]{:S(2)}) async-start(), calls=%async_computation.11 | async-start | bytes 4718592 | tf_op jit(solution)/shard_map/all_gather | solution.py:515
  64.1 15.2 %all-to-all-start.2 = ((bf16[16,8,640]{2,1,0:T(8,128)(2,1)}), bf16[16,8,640]{2,1,0:T(8,128)(2,1)S(1)}, u32[]{:S(2)}, u32[]{:S(2)}) async-start(bf16[16,8,640]{2,1,0:T(8,128)(2,1)} %get-tuple-element.72), calls=%async_computation.2 | async-start | bytes 327680 | tf_op jit(solution)/shard_map/all_to_all | solution.py:44
  71.1 79.5 %all-gather.14.cloned.1.call-start = ((), (), s32[]{:S(2)}) async-start(), calls=%async_computation.13 | async-start | bytes 2359296 | tf_op jit(solution)/shard_map/all_gather | solution.py:532
  91.9 13.1 %all-to-all-start.4 = ((bf16[16,8,1664]{2,1,0:T(8,128)(2,1)}), bf16[16,8,1664]{2,1,0:T(8,128)(2,1)S(1)}, u32[]{:S(2)}, u32[]{:S(2)}) async-start(bf16[16,8,1664]{2,1,0:T(8,128)(2,1)} %get-tuple-element.81), calls=%async_computation.4 | async-start | bytes 851968 | tf_op jit(solution)/shard_map/all_to_all | solution.py:44
  95.5 80.0 %all-gather.18.cloned.1.call-start = ((), (), s32[]{:S(2)}) async-start(), calls=%async_computation.15 | async-start | bytes 2359296 | tf_op jit(solution)/shard_map/all_gather | solution.py:532
  97.3 1.0 copy-start.3
  105.0 12.1 %copy-start.4 = (bf16[2,512,512]{2,1,0:T(8,128)(2,1)S(1)}, bf16[2,512,512]{2,1,0:T(8,128)(2,1)}, u32[]{:S(2)}) copy-start(bf16[2,512,512]{2,1,0:T(8,128)(2,1)} %copy-done.3) | copy-start | bytes 3145732
  118.7 13.1 %all-to-all-start.6 = ((bf16[16,8,1664]{2,1,0:T(8,128)(2,1)}), bf16[16,8,1664]{2,1,0:T(8,128)(2,1)S(1)}, u32[]{:S(2)}, u32[]{:S(2)}) async-start(bf16[16,8,1664]{2,1,0:T(8,128)(2,1)} %get-tuple-element.92), calls=%async_computation.6 | async-start | bytes 851968 | tf_op jit(solution)/shard_map/all_to_all | solution.py:44
  122.2 56.8 %all-gather.16.cloned.1.call-start = ((), (), s32[]{:S(2)}) async-start(), calls=%async_computation.14 | async-start | bytes 2359296 | tf_op jit(solution)/shard_map/all_gather | solution.py:532
  124.0 1.0 copy-start.5
  131.8 12.1 %copy-start.6 = (bf16[2,512,512]{2,1,0:T(8,128)(2,1)S(1)}, bf16[2,512,512]{2,1,0:T(8,128)(2,1)}, u32[]{:S(2)}) copy-start(bf16[2,512,512]{2,1,0:T(8,128)(2,1)} %copy-done.5) | copy-start | bytes 3145732
  132.3 13.2 %copy-start.8 = (s32[8,8,1]{1,2,0:T(1,128)S(1)}, s32[8,8,1]{1,2,0:T(1,128)}, u32[]{:S(2)}) copy-start(s32[8,8,1]{1,2,0:T(1,128)} %param.12) | copy-start | bytes 772
  143.9 5.7 %copy-start.9 = (s32[16,8]{0,1:T(8,128)S(1)}, s32[16,8]{0,1:T(8,128)}, u32[]{:S(2)}) copy-start(s32[16,8]{0,1:T(8,128)} %param.15) | copy-start | bytes 1540
  143.9 6.3 %copy-start.7 = (bf16[16,8,512]{2,1,0:T(8,128)(2,1)S(1)}, bf16[16,8,512]{2,1,0:T(8,128)(2,1)}, u32[]{:S(2)}) copy-start(bf16[16,8,512]{2,1,0:T(8,128)(2,1)} %param.14) | copy-start | bytes 393220
  143.9 6.7 %copy-start = (bf16[16,8,4,512]{3,2,1,0:T(4,128)(2,1)S(1)}, bf16[16,8,4,512]{3,2,1,0:T(4,128)(2,1)}, u32[]{:S(2)}) copy-start(bf16[16,8,4,512]{3,2,1,0:T(4,128)(2,1)} %q_ref.7) | copy-start | bytes 1572868
  146.0 13.1 %all-to-all-start.8 = ((bf16[16,8,1664]{2,1,0:T(8,128)(2,1)}), bf16[16,8,1664]{2,1,0:T(8,128)(2,1)S(1)}, u32[]{:S(2)}, u32[]{:S(2)}) async-start(bf16[16,8,1664]{2,1,0:T(8,128)(2,1)} %get-tuple-element.102), calls=%async_computation.8 | async-start | bytes 851968 | tf_op jit(solution)/shard_map/all_to_all | solution.py:44
  171.9 14.9 %all-to-all-start.10 = ((bf16[16,8,2048]{2,1,0:T(8,128)(2,1)}), bf16[16,8,2048]{2,1,0:T(8,128)(2,1)S(1)}, u32[]{:S(2)}, u32[]{:S(2)}) async-start(bf16[16,8,2048]{2,1,0:T(8,128)(2,1)} %shard_map.103), calls=%async_computation.10 | async-start | bytes 1048576 | tf_op jit(solution)/shard_map/all_to_all | solution.py:44
Sparse Core Ops, SparseCore 0:
  9.4 52.1 all-gather.11
  64.2 32.8 all-gather.9
  98.8 25.1 all-gather.13
  125.6 25.3 all-gather.17
  152.6 26.3 all-gather.15

commit v11 on v10

--- a/solution.py
+++ b/solution.py
@@ -275,13 +275,15 @@
             out_ref[place, :, i * lat : (i + 1) * lat] = part
 
 
-def attend(q, new, keys, limit, heads):
-    rows = q.shape[0]
+def own_rows(new, rows, heads):
     requests = new.shape[0]
     row = lax.broadcasted_iota(jnp.int32, (rows, requests), 0)
     start = lax.broadcasted_iota(jnp.int32, (rows, requests), 1) * heads
     pick = jnp.where((row >= start) & (row < start + heads), 1.0, 0.0).astype(bf16)
-    own = dot(pick, new)
+    return dot(pick, new)
+
+
+def attend(q, own, keys, limit):
     scores = dot_t(q, keys) * score_scale
     place = lax.broadcasted_iota(jnp.int32, scores.shape, 1)
     scores = jnp.where(place < limit, scores, -jnp.inf)
@@ -309,7 +311,8 @@
         q = q_ref[:, i].reshape(requests * heads, lat)
         copies[2 * i].wait()
         copies[2 * i + 1].wait()
-        result = attend(q, new_ref[i], keys[i], limit_ref[i], heads)
+        own = own_rows(new_ref[i], requests * heads, heads)
+        result = attend(q, own, keys[i], limit_ref[i])
         out_ref[:, i] = result.reshape(requests, heads, lat)
 
 
@@ -320,7 +323,8 @@
         at = 2 * i * lat
         pages = pages_ref[:, :, at : at + 2 * lat].astype(f32).reshape(PAGE, 2 * lat)
         keys = jnp.concatenate([pages[:, :lat], pages[:, lat:]], axis=0).astype(bf16)
-        result = attend(q, new_ref[layer + i], keys, limit_ref[layer + i], heads)
+        own = new_ref[i].astype(f32)
+        result = attend(q, own, keys, limit_ref[layer + i])
         out_ref[:, i] = result.reshape(requests, heads, lat)
 
 
@@ -337,7 +341,7 @@
     operands = scalars + [queries, new, limit, pages if last else held_in_hbm(pages)]
     if last:
         in_specs[:3] = [whole(operand.shape) for operand in operands[:3]]
-        operands[:3] = [in_vmem(operand) for operand in operands[:3]]
+        operands[0], operands[2] = in_vmem(queries), in_vmem(limit)
     aliases = {}
     if carried is not None:
         in_specs.append(in_hbm)
@@ -556,7 +560,8 @@
         return decode_pair(layer, slots, queries, new, limit, pages, carried, last)
 
     out = decode(0, pages[0], None)
-    got, out, hot = lax.optimization_barrier((got, out, in_vmem(hot)))
+    rows = jnp.repeat(new[layers - 2 :], queries.shape[2], axis=1)
+    got, out, hot, rows = lax.optimization_barrier((got, out, in_vmem(hot), in_vmem(rows)))
 
     got = exchanged(pair_step(got, mixing, segments), "segment")
     (sent,) = call(
@@ -569,7 +574,7 @@
     got = exchanged(sent, "wide")
     out = decode(4, pages[2], decode(2, pages[1], out))
     got, out = lax.optimization_barrier((got, out))
-    return decode(layers - 2, got, out, True)
+    return decode_pair(layers - 2, slots, queries, rows, limit, got, out, True)
 
 
 def solution(mesh):

time: 196 us -> 196 us (level)
  no operation moved by 1% of the time
where the time goes in v11:
time: 196 us; the launch traced here: 195 us
  blocking collectives  66.6 us (34%)
  waiting for transfers between devices  41.1 us (21%)
  Pallas kernels  36 us (18%)
  starting transfers between devices  33.9 us (17%)
  between operations  13.5 us (7%)
  local copies, waits for them, and re-layouts  3.26 us (2%)
    all_to_all x5, blocking collectives, exchanged(): return lax.all_to_all(sent, axis, 0, 0, tiled=True)  66.6 us
    all_to_all x6, waiting for transfers between devices, exchanged(): return lax.all_to_all(sent, axis, 0, 0, tiled=True)  25.9 us
    all_to_all x6, starting transfers between devices, exchanged(): return lax.all_to_all(sent, axis, 0, 0, tiled=True)  24.9 us
    pallas_call x14, Pallas kernels, call(): pl.pallas_call(body, grid_spec=pltpu.PrefetchScalarGridSpec(num_scalar_pr...  14.7 us
    pallas_call x4, Pallas kernels, decode_pair(): pl.pallas_call(functools.partial(last_decode_kernel if last else decode_k...  11.4 us
    all_gather x1, waiting for transfers between devices, shards(): every = lax.all_gather(both, 'segment', axis=0)  10.1 us
    pallas_call x7, Pallas kernels, resident(): pl.pallas_call(functools.partial(reside_kernel, lists), in_specs=[in_hbm]...  9.92 us
    ppermute x3, starting transfers between devices, shards(): lax.ppermute(home[hop], 'segment', [(0, 2 * hop), (1, 2 * hop + 1)])  7.45 us
  transfers between devices with their start and end apart: 15, of which 10 were waited for; matrix products, arithmetic and copies ran while one was open for 1% of the time, Pallas kernels for 16%

profile of v11, /device:TPU:0, one launch (start us, length us, event | category | flops | bytes accessed | tf_op | source)
XLA Modules:
  0.0 194.9 jit_solution(2703287185356060746)
XLA Ops:
  6.5 0.1 pad_add_fusion.where
  6.6 2.7 %shard_map.82 = (bf16[2,512,512]{2,1,0:T(8,128)(2,1)}, bf16[512,512]{1,0:T(8,128)(2,1)S(1)}) custom-call(s32[2]{0:T(128)S(1)} %pad_add_fusion.where, bf16[1,512,512]{2,1,0:T(8,128)(2,1)} %latent_ref.1, bf16[1,512]{1,0:T(2,128)(2,1)} %gain_ref.1, bf16[1,512,512]{2,1,0:T(8,128)(2,1)} %back_ref.1), custom_call_target="tpu_custom_call" | custom-call | bytes 3145728 | tf_op jit(solution)/shard_map/pallas_call | solution.py:66
  9.3 1.5 collective-permute-start
  10.8 1.5 collective-permute-done.lent_ref
  12.3 1.0 shard_map.83
  13.3 3.9 %collective-permute-start.1 = (bf16[128,512]{1,0:T(8,128)(2,1)S(1)}, bf16[128,512]{1,0:T(8,128)(2,1)S(1)}, u32[]{:S(2)}, u32[]{:S(2)}) collective-permute-start(bf16[128,512]{1,0:T(8,128)(2,1)S(1)} %get-tuple-element.62), channel_id=1, source_target_pairs={{0,32},{16,48},{1,33},{17,49},{2,34},{18,50},{3,35},{19,51},{4,36}... | collective-permute-start | bytes 393224 | tf_op jit(solution)/shard_map/ppermute | solution.py:435
  17.2 2.2 %collective-permute-start.2 = (bf16[128,512]{1,0:T(8,128)(2,1)S(1)}, bf16[128,512]{1,0:T(8,128)(2,1)S(1)}, u32[]{:S(2)}, u32[]{:S(2)}) collective-permute-start(bf16[128,512]{1,0:T(8,128)(2,1)S(1)} %get-tuple-element.63), channel_id=1, source_target_pairs={{0,64},{16,80},{1,65},{17,81},{2,66},{18,82},{3,67},{19,83},{4,68}... | collective-permute-start | bytes 393224 | tf_op jit(solution)/shard_map/ppermute | solution.py:435
  19.4 1.3 collective-permute-start.3
  20.7 1.0 shard_map.84.cross_ref
  21.8 2.5 %collective-permute-done.2.b_ref = bf16[128,512]{1,0:T(8,128)(2,1)S(1)} collective-permute-done((bf16[128,512]{1,0:T(8,128)(2,1)S(1)}, bf16[128,512]{1,0:T(8,128)(2,1)S(1)}, u32[]{:S(2)}, u32[]{:S(2)}) %collective-permute-start.2) | collective-permute-done | bytes 131104 | tf_op jit(solution)/shard_map/ppermute | solution.py:435
  24.2 0.8 collective-permute-done.3.c_ref
  25.0 0.7 shard_map.85
  25.8 21.0 %all_to_all.55.got_ref = bf16[16,8,2688]{2,1,0:T(8,128)(2,1)S(1)} all-to-all(bf16[16,8,2688]{2,1,0:T(8,128)(2,1)S(1)} %get-tuple-element.66), channel_id=1, replica_groups=mesh['segment'=8,'wide'=16] {'wide'}, dimensions={0} | all-to-all | bytes 1376256 | tf_op jit(solution)/shard_map/all_to_all | solution.py:44
  46.8 1.1 shard_map.86
  47.8 3.6 %all-to-all-start.1 = ((bf16[16,40,512]{2,1,0:T(8,128)(2,1)}), bf16[16,40,512]{2,1,0:T(8,128)(2,1)S(1)}, u32[]{:S(2)}, u32[]{:S(2)}) async-start(bf16[16,40,512]{2,1,0:T(8,128)(2,1)} %shard_map.86), calls=%async_computation.1 | async-start | bytes 1310720 | tf_op jit(solution)/shard_map/all_to_all | solution.py:44
  51.5 10.1 %all-gather.12.cloned.1.call-done.source_ref = bf16[16,512,512]{2,1,0:T(8,128)(2,1)} async-done(((bf16[2,512,512]{2,1,0:T(8,128)(2,1)}), bf16[16,512,512]{2,1,0:T(8,128)(2,1)}) %all-gather.12.cloned.1.call-update) | async-done | bytes 8388624 | tf_op jit(solution)/shard_map/all_gather | solution.py:411
  61.6 1.2 shard_map.87
  62.9 1.2 shard_map.88
  64.1 7.0 %all-to-all-start.2 = ((bf16[16,8,640]{2,1,0:T(8,128)(2,1)}), bf16[16,8,640]{2,1,0:T(8,128)(2,1)S(1)}, u32[]{:S(2)}, u32[]{:S(2)}) async-start(bf16[16,8,640]{2,1,0:T(8,128)(2,1)} %get-tuple-element.73), calls=%async_computation.2 | async-start | bytes 327680 | tf_op jit(solution)/shard_map/all_to_all | solution.py:44
  71.1 1.6 shard_map.89
  72.7 6.6 %all-to-all-done.2.got_ref = bf16[16,8,640]{2,1,0:T(8,128)(2,1)S(1)} async-done(((bf16[16,8,640]{2,1,0:T(8,128)(2,1)}), bf16[16,8,640]{2,1,0:T(8,128)(2,1)S(1)}, u32[]{:S(2)}, u32[]{:S(2)}) %all-to-all-start.2) | async-done | bytes 163872 | tf_op jit(solution)/shard_map/all_to_all | solution.py:44
  79.3 0.2 shard_map.90
  79.4 11.0 %all_to_all.56.got_ref = bf16[16,8,512]{2,1,0:T(8,128)(2,1)S(1)} all-to-all(bf16[16,8,512]{2,1,0:T(8,128)(2,1)S(1)} %shard_map.90), channel_id=1, replica_groups=mesh['segment'=8,'wide'=16] {'wide'}, dimensions={0} | all-to-all | bytes 262144 | tf_op jit(solution)/shard_map/all_to_all | solution.py:44
  90.5 1.4 shard_map.91
  91.9 3.6 %all-to-all-start.4 = ((bf16[16,8,1664]{2,1,0:T(8,128)(2,1)}), bf16[16,8,1664]{2,1,0:T(8,128)(2,1)S(1)}, u32[]{:S(2)}, u32[]{:S(2)}) async-start(bf16[16,8,1664]{2,1,0:T(8,128)(2,1)} %get-tuple-element.82), calls=%async_computation.4 | async-start | bytes 851968 | tf_op jit(solution)/shard_map/all_to_all | solution.py:44
  95.5 1.8 shard_map.93
  97.3 1.0 copy-done.3
  98.3 1.2 shard_map.92.cross_ref
  99.6 5.5 %all-to-all-done.4.got_ref = bf16[16,8,1664]{2,1,0:T(8,128)(2,1)S(1)} async-done(((bf16[16,8,1664]{2,1,0:T(8,128)(2,1)}), bf16[16,8,1664]{2,1,0:T(8,128)(2,1)S(1)}, u32[]{:S(2)}, u32[]{:S(2)}) %all-to-all-start.4) | async-done | bytes 426016 | tf_op jit(solution)/shard_map/all_to_all | solution.py:44
  105.0 0.5 shard_map.94
  105.5 11.6 %all_to_all.57.got_ref = bf16[16,8,1024]{2,1,0:T(8,128)(2,1)S(1)} all-to-all(bf16[16,8,1024]{2,1,0:T(8,128)(2,1)S(1)} %shard_map.94), channel_id=1, replica_groups=mesh['segment'=8,'wide'=16] {'wide'}, dimensions={0} | all-to-all | bytes 524288 | tf_op jit(solution)/shard_map/all_to_all | solution.py:44
  117.1 1.5 shard_map.95
  118.7 3.6 %all-to-all-start.6 = ((bf16[16,8,1664]{2,1,0:T(8,128)(2,1)}), bf16[16,8,1664]{2,1,0:T(8,128)(2,1)S(1)}, u32[]{:S(2)}, u32[]{:S(2)}) async-start(bf16[16,8,1664]{2,1,0:T(8,128)(2,1)} %get-tuple-element.93), calls=%async_computation.6 | async-start | bytes 851968 | tf_op jit(solution)/shard_map/all_to_all | solution.py:44
  122.3 1.7 shard_map.97
  124.0 1.0 copy-done.5
  125.0 1.2 shard_map.96.cross_ref
  126.3 5.5 %all-to-all-done.6.got_ref = bf16[16,8,1664]{2,1,0:T(8,128)(2,1)S(1)} async-done(((bf16[16,8,1664]{2,1,0:T(8,128)(2,1)}), bf16[16,8,1664]{2,1,0:T(8,128)(2,1)S(1)}, u32[]{:S(2)}, u32[]{:S(2)}) %all-to-all-start.6) | async-done | bytes 426016 | tf_op jit(solution)/shard_map/all_to_all | solution.py:44
  131.8 0.5 shard_map.98
  132.3 11.6 %all_to_all.58.got_ref = bf16[16,8,1024]{2,1,0:T(8,128)(2,1)S(1)} all-to-all(bf16[16,8,1024]{2,1,0:T(8,128)(2,1)S(1)} %shard_map.98), channel_id=1, replica_groups=mesh['segment'=8,'wide'=16] {'wide'}, dimensions={0} | all-to-all | bytes 524288 | tf_op jit(solution)/shard_map/all_to_all | solution.py:44
  143.9 1.5 shard_map.99
  145.5 0.1 select_reduce_fusion.1
  145.6 0.2 convert_reduce_fusion
  145.8 0.1 copy.26
  145.9 0.1 slice.7
  145.9 0.1 min.16.slots
  146.0 3.6 %all-to-all-start.8 = ((bf16[16,8,1664]{2,1,0:T(8,128)(2,1)}), bf16[16,8,1664]{2,1,0:T(8,128)(2,1)S(1)}, u32[]{:S(2)}, u32[]{:S(2)}) async-start(bf16[16,8,1664]{2,1,0:T(8,128)(2,1)} %get-tuple-element.103), calls=%async_computation.8 | async-start | bytes 851968 | tf_op jit(solution)/shard_map/all_to_all | solution.py:44
  149.7 0.1 copy.28
  149.8 0.5 copy.29.limit_ref
  150.3 0.1 copy.30
  150.4 0.1 eq.32
  150.4 0.1 fusion.1
  150.5 0.1 reshape.47
  150.7 3.3 %shard_map.101.rest_0_ = bf16[16,8,4,512]{3,2,1,0:T(4,128)(2,1)} custom-call(s32[16]{0:T(128)S(1)} %min.16.slots, bf16[16,8,4,512]{3,2,1,0:T(4,128)(2,1)S(1)} %copy-done, bf16[8,16,512]{2,1,0:T(8,128)(2,1)S(1)} %bitcast.23, s32[8,64,1]{2,1,0:T(8,128)S(1)} %copy.29.limit_ref, bf16[8,128,1024]{2,1,0:T(8,128)(2,1)} %bitcast.26), custom_call_target="tpu_custom_call" | custom-call | flops 67108864 | bytes 786432 | tf_op jit(solution)/shard_map/pallas_call | solution.py:351
  154.0 1.2 shard_map.100.cross_ref
  155.2 3.9 %all-to-all-done.8.got_ref = bf16[16,8,1664]{2,1,0:T(8,128)(2,1)S(1)} async-done(((bf16[16,8,1664]{2,1,0:T(8,128)(2,1)}), bf16[16,8,1664]{2,1,0:T(8,128)(2,1)S(1)}, u32[]{:S(2)}, u32[]{:S(2)}) %all-to-all-start.8) | async-done | bytes 426016 | tf_op jit(solution)/shard_map/all_to_all | solution.py:44
  159.2 0.5 shard_map.102
  159.7 11.3 %all_to_all.59.got_ref = bf16[8,8,1024]{2,1,0:T(8,128)(2,1)S(1)} all-to-all(bf16[8,8,1024]{2,1,0:T(8,128)(2,1)S(1)} %shard_map.102), channel_id=1, replica_groups=mesh['segment'=8,'wide'=16] {'segment'}, dimensions={0} | all-to-all | bytes 262144 | tf_op jit(solution)/shard_map/all_to_all | solution.py:44
  171.0 0.9 shard_map.103
  171.9 3.6 %all-to-all-start.10 = ((bf16[16,8,2048]{2,1,0:T(8,128)(2,1)}), bf16[16,8,2048]{2,1,0:T(8,128)(2,1)S(1)}, u32[]{:S(2)}, u32[]{:S(2)}) async-start(bf16[16,8,2048]{2,1,0:T(8,128)(2,1)} %shard_map.103), calls=%async_computation.10 | async-start | bytes 1048576 | tf_op jit(solution)/shard_map/all_to_all | solution.py:44
  175.5 3.3 %shard_map.104.rest_0_ = bf16[16,8,4,512]{3,2,1,0:T(4,128)(2,1)} custom-call(s32[16]{0:T(128)S(1)} %min.16.slots, bf16[16,8,4,512]{3,2,1,0:T(4,128)(2,1)S(1)} %copy-done, bf16[8,16,512]{2,1,0:T(8,128)(2,1)S(1)} %bitcast.24, s32[8,64,1]{2,1,0:T(8,128)S(1)} %copy.29.limit_ref, bf16[8,128,1024]{2,1,0:T(8,128)(2,1)} %bitcast.27, ...), custom_call_target="tpu_custom_call", output_to_operand_aliasing={{}: (5, {})} | custom-call | flops 67108864 | bytes 786432 | tf_op jit(solution)/shard_map/pallas_call | solution.py:351
  178.8 0.2 all-gather.16.cloned.1.call-done
  179.0 3.3 %shard_map.105.carried_ref = bf16[16,8,4,512]{3,2,1,0:T(4,128)(2,1)} custom-call(s32[16]{0:T(128)S(1)} %min.16.slots, bf16[16,8,4,512]{3,2,1,0:T(4,128)(2,1)S(1)} %copy-done, bf16[8,16,512]{2,1,0:T(8,128)(2,1)S(1)} %bitcast.25, s32[8,64,1]{2,1,0:T(8,128)S(1)} %copy.29.limit_ref, bf16[8,128,1024]{2,1,0:T(8,128)(2,1)} %bitcast.28, ...), custom_call_target="tpu_custom_call", output_to_operand_aliasing={{}: (5, {})} | custom-call | flops 67108864 | bytes 786432 | tf_op jit(solution)/shard_map/pallas_call | solution.py:351
  182.3 4.5 %all-to-all-done.10.pages_ref = bf16[16,8,2048]{2,1,0:T(8,128)(2,1)S(1)} async-done(((bf16[16,8,2048]{2,1,0:T(8,128)(2,1)}), bf16[16,8,2048]{2,1,0:T(8,128)(2,1)S(1)}, u32[]{:S(2)}, u32[]{:S(2)}) %all-to-all-start.10) | async-done | bytes 524320 | tf_op jit(solution)/shard_map/all_to_all | solution.py:44
  186.8 1.6 shard_map.106
  (42 shorter events, 0.6 us)
Async XLA Ops:
  6.5 5.7 %copy-start.1 = (bf16[4,256,512]{2,1,0:T(8,128)(2,1)S(1)}, bf16[4,256,512]{2,1,0:T(8,128)(2,1)}, u32[]{:S(2)}) copy-start(bf16[4,256,512]{2,1,0:T(8,128)(2,1)} %param.8) | copy-start | bytes 3145732
  6.5 55.1 %all-gather.12.cloned.1.call-start = ((), (), s32[]{:S(2)}) async-start(), calls=%async_computation.12 | async-start | bytes 9437184 | tf_op jit(solution)/shard_map/all_gather | solution.py:411
  9.3 11.4 %copy-start.2 = (bf16[2,512,512]{2,1,0:T(8,128)(2,1)S(1)}, bf16[2,512,512]{2,1,0:T(8,128)(2,1)}, u32[]{:S(2)}) copy-start(bf16[2,512,512]{2,1,0:T(8,128)(2,1)} %get-tuple-element.65.both_ref) | copy-start | bytes 3145732
  9.3 2.9 %collective-permute-start = (bf16[512,512]{1,0:T(8,128)(2,1)S(1)}, bf16[512,512]{1,0:T(8,128)(2,1)S(1)}, u32[]{:S(2)}, u32[]{:S(2)}) collective-permute-start(bf16[512,512]{1,0:T(8,128)(2,1)S(1)} %get-tuple-element.60.mine_ref), channel_id=1, source_target_pairs={{0,16},{32,48},{64,80},{96,112},{1,17},{33,49},{65,81},{97,113},{2... | collective-permute-start | bytes 1572872 | tf_op jit(solution)/shard_map/ppermute | solution.py:412
  13.3 8.5 %collective-permute-start.1 = (bf16[128,512]{1,0:T(8,128)(2,1)S(1)}, bf16[128,512]{1,0:T(8,128)(2,1)S(1)}, u32[]{:S(2)}, u32[]{:S(2)}) collective-permute-start(bf16[128,512]{1,0:T(8,128)(2,1)S(1)} %get-tuple-element.62), channel_id=1, source_target_pairs={{0,32},{16,48},{1,33},{17,49},{2,34},{18,50},{3,35},{19,51},{4,36}... | collective-permute-start | bytes 393224 | tf_op jit(solution)/shard_map/ppermute | solution.py:435
  17.2 7.0 %collective-permute-start.2 = (bf16[128,512]{1,0:T(8,128)(2,1)S(1)}, bf16[128,512]{1,0:T(8,128)(2,1)S(1)}, u32[]{:S(2)}, u32[]{:S(2)}) collective-permute-start(bf16[128,512]{1,0:T(8,128)(2,1)S(1)} %get-tuple-element.63), channel_id=1, source_target_pairs={{0,64},{16,80},{1,65},{17,81},{2,66},{18,82},{3,67},{19,83},{4,68}... | collective-permute-start | bytes 393224 | tf_op jit(solution)/shard_map/ppermute | solution.py:435
  19.4 5.6 %collective-permute-start.3 = (bf16[128,512]{1,0:T(8,128)(2,1)S(1)}, bf16[128,512]{1,0:T(8,128)(2,1)S(1)}, u32[]{:S(2)}, u32[]{:S(2)}) collective-permute-start(bf16[128,512]{1,0:T(8,128)(2,1)S(1)} %get-tuple-element.64), channel_id=1, source_target_pairs={{0,96},{16,112},{1,97},{17,113},{2,98},{18,114},{3,99},{19,115},{4... | collective-permute-start | bytes 393224 | tf_op jit(solution)/shard_map/ppermute | solution.py:435
  47.8 15.0 %all-to-all-start.1 = ((bf16[16,40,512]{2,1,0:T(8,128)(2,1)}), bf16[16,40,512]{2,1,0:T(8,128)(2,1)S(1)}, u32[]{:S(2)}, u32[]{:S(2)}) async-start(bf16[16,40,512]{2,1,0:T(8,128)(2,1)} %shard_map.86), calls=%async_computation.1 | async-start | bytes 1310720 | tf_op jit(solution)/shard_map/all_to_all | solution.py:44
  51.5 46.9 %all-gather.10.cloned.1.call-start = ((), (), s32[]{:S(2)}) async-start(), calls=%async_computation.11 | async-start | bytes 4718592 | tf_op jit(solution)/shard_map/all_gather | solution.py:519
  64.1 15.2 %all-to-all-start.2 = ((bf16[16,8,640]{2,1,0:T(8,128)(2,1)}), bf16[16,8,640]{2,1,0:T(8,128)(2,1)S(1)}, u32[]{:S(2)}, u32[]{:S(2)}) async-start(bf16[16,8,640]{2,1,0:T(8,128)(2,1)} %get-tuple-element.73), calls=%async_computation.2 | async-start | bytes 327680 | tf_op jit(solution)/shard_map/all_to_all | solution.py:44
  71.1 79.6 %all-gather.14.cloned.1.call-start = ((), (), s32[]{:S(2)}) async-start(), calls=%async_computation.13 | async-start | bytes 2359296 | tf_op jit(solution)/shard_map/all_gather | solution.py:536
  91.9 13.1 %all-to-all-start.4 = ((bf16[16,8,1664]{2,1,0:T(8,128)(2,1)}), bf16[16,8,1664]{2,1,0:T(8,128)(2,1)S(1)}, u32[]{:S(2)}, u32[]{:S(2)}) async-start(bf16[16,8,1664]{2,1,0:T(8,128)(2,1)} %get-tuple-element.82), calls=%async_computation.4 | async-start | bytes 851968 | tf_op jit(solution)/shard_map/all_to_all | solution.py:44
  95.5 80.0 %all-gather.18.cloned.1.call-start = ((), (), s32[]{:S(2)}) async-start(), calls=%async_computation.15 | async-start | bytes 2359296 | tf_op jit(solution)/shard_map/all_gather | solution.py:536
  97.3 1.0 copy-start.3
  105.0 12.1 %copy-start.4 = (bf16[2,512,512]{2,1,0:T(8,128)(2,1)S(1)}, bf16[2,512,512]{2,1,0:T(8,128)(2,1)}, u32[]{:S(2)}) copy-start(bf16[2,512,512]{2,1,0:T(8,128)(2,1)} %copy-done.3) | copy-start | bytes 3145732
  118.7 13.1 %all-to-all-start.6 = ((bf16[16,8,1664]{2,1,0:T(8,128)(2,1)}), bf16[16,8,1664]{2,1,0:T(8,128)(2,1)S(1)}, u32[]{:S(2)}, u32[]{:S(2)}) async-start(bf16[16,8,1664]{2,1,0:T(8,128)(2,1)} %get-tuple-element.93), calls=%async_computation.6 | async-start | bytes 851968 | tf_op jit(solution)/shard_map/all_to_all | solution.py:44
  122.2 56.8 %all-gather.16.cloned.1.call-start = ((), (), s32[]{:S(2)}) async-start(), calls=%async_computation.14 | async-start | bytes 2359296 | tf_op jit(solution)/shard_map/all_gather | solution.py:536
  124.0 1.0 copy-start.5
  131.8 12.1 %copy-start.6 = (bf16[2,512,512]{2,1,0:T(8,128)(2,1)S(1)}, bf16[2,512,512]{2,1,0:T(8,128)(2,1)}, u32[]{:S(2)}) copy-start(bf16[2,512,512]{2,1,0:T(8,128)(2,1)} %copy-done.5) | copy-start | bytes 3145732
  132.3 13.2 %copy-start.8 = (s32[8,8,1]{1,2,0:T(1,128)S(1)}, s32[8,8,1]{1,2,0:T(1,128)}, u32[]{:S(2)}) copy-start(s32[8,8,1]{1,2,0:T(1,128)} %param.12) | copy-start | bytes 772
  143.9 5.7 %copy-start.9 = (s32[16,8]{0,1:T(8,128)S(1)}, s32[16,8]{0,1:T(8,128)}, u32[]{:S(2)}) copy-start(s32[16,8]{0,1:T(8,128)} %param.15) | copy-start | bytes 1540
  143.9 6.3 %copy-start.7 = (bf16[16,8,512]{2,1,0:T(8,128)(2,1)S(1)}, bf16[16,8,512]{2,1,0:T(8,128)(2,1)}, u32[]{:S(2)}) copy-start(bf16[16,8,512]{2,1,0:T(8,128)(2,1)} %param.14) | copy-start | bytes 393220
  143.9 6.8 %copy-start = (bf16[16,8,4,512]{3,2,1,0:T(4,128)(2,1)S(1)}, bf16[16,8,4,512]{3,2,1,0:T(4,128)(2,1)}, u32[]{:S(2)}) copy-start(bf16[16,8,4,512]{3,2,1,0:T(4,128)(2,1)} %q_ref.7) | copy-start | bytes 1572868
  146.0 13.1 %all-to-all-start.8 = ((bf16[16,8,1664]{2,1,0:T(8,128)(2,1)}), bf16[16,8,1664]{2,1,0:T(8,128)(2,1)S(1)}, u32[]{:S(2)}, u32[]{:S(2)}) async-start(bf16[16,8,1664]{2,1,0:T(8,128)(2,1)} %get-tuple-element.103), calls=%async_computation.8 | async-start | bytes 851968 | tf_op jit(solution)/shard_map/all_to_all | solution.py:44
  171.9 14.9 %all-to-all-start.10 = ((bf16[16,8,2048]{2,1,0:T(8,128)(2,1)}), bf16[16,8,2048]{2,1,0:T(8,128)(2,1)S(1)}, u32[]{:S(2)}, u32[]{:S(2)}) async-start(bf16[16,8,2048]{2,1,0:T(8,128)(2,1)} %shard_map.103), calls=%async_computation.10 | async-start | bytes 1048576 | tf_op jit(solution)/shard_map/all_to_all | solution.py:44
Sparse Core Ops, SparseCore 0:
  9.4 52.1 all-gather.11
  64.2 32.8 all-gather.9
  98.8 25.1 all-gather.13
  125.6 25.3 all-gather.17
  152.6 26.3 all-gather.15
